TPU v7x, 32 devices: a whole 2x2x4 slice. The times are simulated.
32 devices in a mesh: depth: 4 (over y, x), tile: 8 (over z, core).
Axes of the slice: x: 2, y: 2, z: 4, core: 2. Of those that a mesh axis runs over, the one named last changes fastest.
Arguments:
- field: float32 [64, 256, 1024], P('depth', None, 'tile'), may hold values from -6 to 6
- light_vectors: float32 [16, 3], replicated, may hold values from -4 to 4
- transfer: float32 [16, 4, 8], replicated, may hold values from 0.05 to 1
- light_index: int32 [4], replicated, may hold values from 0 to 15
- flips: int32 [8], P('tile'), may hold values from 0 to 1
Outputs:
- frames: float32 [4, 4, 256, 1024], P(None, None, 'depth', 'tile')
All inputs are finite; a program needn't handle non-finite values.
Results may differ from a plain program's by a relative error of at most 0.0003.
Values sent between devices are 32-bit elements; how exact they have to be, the bound alone decides.
No kernel may reach another device: no remote copies, remote signals or barrier semaphores. Data moves between devices by JAX's collectives and lax.ppermute only.
A program may use at most 128 MiB of HBM per device.

v0:
```python
import functools

import jax
import jax.numpy as jnp
from jax import lax
from jax.experimental import pallas as pl
from jax.experimental.pallas import tpu as pltpu
from jax.sharding import PartitionSpec as P

AMBIENT = 0.3
OPACITY = 2.0
SUB = 8
VMEM = pltpu.VMEM
SMEM = pltpu.SMEM


def edge_kernel(parts, field_ref, out_ref):
    cells, _, cols = field_ref.shape
    rows = out_ref.shape[0]
    lane_pair = lax.broadcasted_iota(jnp.int32, (SUB, cols), 1) // 2

    def tile(i, carry):
        acc = jnp.zeros((SUB, cols), jnp.float32)
        for part in range(parts):
            for z in range(cells):
                slot = part * cells + z
                start = pl.multiple_of(part * rows + i * SUB, SUB)
                value = field_ref[z, pl.ds(start, SUB), :]
                moved = pltpu.roll(value, (2 * slot + 1) % cols, 1)
                acc = jnp.where(lane_pair == slot, moved, acc)
        out_ref[pl.ds(pl.multiple_of(i * SUB, SUB), SUB), :] = acc
        return carry

    lax.fori_loop(0, rows // SUB, tile, 0)


def pack_kernel(parts, scal_ref, field_ref, *refs):
    outs, (extra_ref, sems) = refs[:parts], refs[parts:]
    cells, all_rows, cols = field_ref.shape
    rows = all_rows // parts
    me = scal_ref[0]
    copies = []
    for m in range(parts):
        low = pl.multiple_of((me ^ m) * rows, SUB)
        centre = outs[m].at[pl.ds(2 * cells, cells * rows), :].reshape(cells, rows, cols)
        copies.append(pltpu.make_async_copy(field_ref.at[:, pl.ds(low, rows), :], centre, sems.at[0, m]))
        copies[-1].start()
    for m in range(parts):
        part = me ^ m
        low = part * rows
        above = jnp.where(part > 0, 1.0, 0.0)
        below = jnp.where(part < parts - 1, 1.0, 0.0)
        for z in range(cells):
            extra_ref[m, z : z + 1, :] = field_ref[z, pl.ds(jnp.maximum(low - 1, 0), 1), :] * above
            extra_ref[m, cells + z : cells + z + 1, :] = (
                field_ref[z, pl.ds(jnp.minimum(low + rows, all_rows - 1), 1), :] * below
            )
        copies.append(pltpu.make_async_copy(extra_ref.at[m], outs[m].at[pl.ds(0, 2 * cells), :], sems.at[1, m]))
        copies[-1].start()
    for copy in copies:
        copy.wait()


def shade_kernel(parts, cells, passes, knots, unroll, scal_ref, lights_ref, curves_ref, lateral_ref, *refs):
    bricks, (out_ref, cell_ref, ends_ref) = refs[:parts], refs[parts:]
    cols = bricks[0].shape[1]
    rows = out_ref.shape[2]
    depth = parts * cells
    me = scal_ref[0]
    flip = scal_ref[1]
    step = 1 - 2 * flip
    first = flip * (depth - 1)
    scale = OPACITY / depth
    lane = lax.broadcasted_iota(jnp.int32, (SUB, cols), 1)
    sublane = lax.broadcasted_iota(jnp.int32, (SUB, cols), 0)
    is_first = lane == 0
    is_last = lane == cols - 1

    def bends(index, channel, factor):
        points = [curves_ref[index, channel * knots + k] * factor for k in range(knots)]
        slopes = [points[k + 1] - points[k] for k in range(knots - 1)]
        return [points[0], slopes[0]] + [slopes[k] - slopes[k - 1] for k in range(1, knots - 1)]

    chosen = [scal_ref[2 + p] for p in range(passes)]
    vectors = [[lights_ref[chosen[p], axis] for axis in range(3)] for p in range(passes)]
    curves = [bends(chosen[p], 3, scale) for p in range(passes)]

    ends_ref[0, 1] = jnp.zeros((rows, cols), jnp.float32)
    ends_ref[parts + 1, 0] = jnp.zeros((rows, cols), jnp.float32)
    for m in range(parts):
        ends_ref[(me ^ m) + 1, 0] = bricks[m][2 * cells : 2 * cells + rows, :]
        ends_ref[(me ^ m) + 1, 1] = bricks[m][(cells - 1) * rows + 2 * cells : cells * rows + 2 * cells, :]

    def row_tile(i, carry):
        base = pl.multiple_of(i * SUB, SUB)
        at = pl.ds(base, SUB)
        is_top = jnp.logical_and(sublane == 0, i == 0)
        is_bottom = jnp.logical_and(sublane == SUB - 1, i == rows // SUB - 1)
        for m in range(parts):
            part = me ^ m
            brick = bricks[m]
            sides = pltpu.roll(lateral_ref[part, at, :], (cols - 1 - 2 * cells * me) % cols, 1)
            line = [ends_ref[part, 1, at, :]]
            line += [brick[pl.ds(2 * cells + z * rows + base, SUB), :] for z in range(cells)]
            line += [ends_ref[part + 2, 0, at, :]]
            for z in range(cells):
                here = line[z + 1]
                start = 2 * cells + z * rows + base
                upper = jnp.where(is_top, brick[z : z + 1, :], brick[pl.ds(start - 1, SUB), :])
                lower = jnp.where(is_bottom, brick[cells + z : cells + z + 1, :], brick[pl.ds(start + 1, SUB), :])
                edge = pltpu.roll(sides, (cols - 2 * z) % cols, 1) if z else sides
                grad_x = pltpu.roll(jnp.where(is_first, edge, here), cols - 1, 1) - pltpu.roll(
                    jnp.where(is_last, edge, here), 1, 1
                )
                grad_y = lower - upper
                grad_z = line[z + 2] - line[z]
                inverse = lax.rsqrt(grad_x * grad_x + grad_y * grad_y + grad_z * grad_z + 4.0)
                half = 0.5 * (knots - 1)
                position = half + half * jnp.tanh(0.5 * here)
                spot = part * cells + z
                cell_ref[0, spot] = grad_x * inverse
                cell_ref[1, spot] = grad_y * inverse
                cell_ref[2, spot] = grad_z * inverse
                cell_ref[3, spot] = position
                for k in range(1, knots - 1):
                    cell_ref[3 + k, spot] = jnp.maximum(position - k, 0.0)

        zero = jnp.zeros((SUB, cols), jnp.float32)
        for p in range(passes):
            vector = [jnp.full((SUB, cols), v) for v in vectors[p]]
            curve = [jnp.full((SUB, cols), v) for v in curves[p]]

            def march(g, state):
                keep, sums = state
                for u in range(unroll):
                    z = first + step * (g * unroll + u)
                    hinges = [cell_ref[3 + k, z] for k in range(knots - 1)]
                    terms = [curve[0]] + [curve[k + 1] * hinges[k] for k in range(knots - 1)]
                    while len(terms) > 1:
                        terms = [sum(terms[j : j + 2][1:], terms[j]) for j in range(0, len(terms), 2)]
                    opacity = terms[0]
                    facing = cell_ref[0, z] * vector[0] + cell_ref[1, z] * vector[1] + cell_ref[2, z] * vector[2]
                    taken = keep * opacity
                    weight = taken * (AMBIENT + jnp.abs(facing))
                    keep = keep - taken
                    sums = [sums[0] + weight] + [sums[k + 1] + weight * hinges[k] for k in range(knots - 1)]
                return keep, sums

            keep, sums = lax.fori_loop(0, depth // unroll, march, (jnp.ones((SUB, cols), jnp.float32), [zero] * knots))
            for channel in range(3):
                tint = bends(chosen[p], channel, 1.0)
                color = tint[0] * sums[0]
                for k in range(1, knots):
                    color = color + tint[k] * sums[k]
                out_ref[p, channel, at, :] = color
            out_ref[p, 3, at, :] = 1.0 - keep
        return carry

    lax.fori_loop(0, rows // SUB, row_tile, 0)


def swap_along(block, axis, mask):
    return lax.ppermute(block, axis, [(i, i ^ mask) for i in range(lax.axis_size(axis))])


def on_device(field, light_vectors, transfer, light_index, flips):
    parts = lax.axis_size("depth")
    cells, all_rows, cols = field.shape
    rows = all_rows // parts
    passes = light_index.shape[0]
    lights, channels, knots = transfer.shape
    message = cells * rows + 2 * cells + SUB
    scal = jnp.concatenate([lax.axis_index("depth").astype(jnp.int32)[None], flips, light_index])

    packed = pl.pallas_call(
        functools.partial(pack_kernel, parts),
        out_shape=[jax.ShapeDtypeStruct((message, cols), jnp.float32)] * parts,
        in_specs=[pl.BlockSpec(memory_space=SMEM), pl.BlockSpec(memory_space=VMEM)],
        out_specs=[pl.BlockSpec(memory_space=pl.ANY)] * parts,
        scratch_shapes=[VMEM((parts, 2 * cells, cols), jnp.float32), pltpu.SemaphoreType.DMA((2, parts))],
        name="pack",
    )(scal, field)
    bricks = [packed[0]] + [swap_along(packed[m], "depth", m) for m in range(1, parts)]

    edges = pl.pallas_call(
        functools.partial(edge_kernel, parts),
        out_shape=jax.ShapeDtypeStruct((rows, cols), jnp.float32),
        in_specs=[pl.BlockSpec(memory_space=VMEM)],
        out_specs=pl.BlockSpec(memory_space=VMEM),
        name="edges",
    )(field)
    around = lax.all_gather(edges, "tile")
    tile, tiles = lax.axis_index("tile"), lax.axis_size("tile")
    left = jnp.where(tile > 0, lax.dynamic_index_in_dim(around, jnp.maximum(tile - 1, 0), 0, False), 0.0)
    right = jnp.where(tile < tiles - 1, lax.dynamic_index_in_dim(around, jnp.minimum(tile + 1, tiles - 1), 0, False), 0.0)
    sides = jnp.where(jnp.arange(cols) % 2 == 0, left, right)
    lateral = lax.all_gather(sides, "depth")
    return pl.pallas_call(
        functools.partial(shade_kernel, parts, cells, passes, knots, 32),
        out_shape=jax.ShapeDtypeStruct((passes, channels, rows, cols), jnp.float32),
        in_specs=[pl.BlockSpec(memory_space=SMEM)] * 3 + [pl.BlockSpec(memory_space=VMEM)] * (1 + parts),
        out_specs=pl.BlockSpec(memory_space=VMEM),
        scratch_shapes=[
            VMEM((knots + 2, parts * cells, SUB, cols), jnp.float32),
            VMEM((parts + 2, 2, rows, cols), jnp.float32),
        ],
        name="shade",
    )(scal, light_vectors, transfer.reshape(lights, channels * knots), lateral, *bricks)


def solution(mesh):
    in_specs = (P("depth", None, "tile"), P(), P(), P(), P("tile"))
    out_specs = P(None, None, "depth", "tile")
    return jax.shard_map(
        on_device, mesh=mesh, in_specs=in_specs, out_specs=out_specs, check_vma=False
    )
```

profile of v0, /device:TPU:0, one launch (start us, length us, event | category | flops | bytes accessed | tf_op | source)
XLA Modules:
  0.0 59.8 jit_solution(17536060774632616556)
XLA Ops:
  0.7 1.3 %pad_add_fusion.scal_ref = s32[6]{0:T(128)} fusion(s32[4]{0:T(128)} %param.8, s32[1]{0:T(128)S(6)} %copy.12, s32[1]{0:T(128)} %bitcast), kind=kLoop, calls=%fused_computation.3 | loop fusion | flops 12 | bytes 48 | tf_op jit(solution)/shard_map/concatenate | solution.py:173
  1.9 0.0 copy-start.4
  1.9 0.0 copy-start.3
  1.9 3.1 %pack.1 = (f32[1064,128]{1,0:T(8,128)}, f32[1064,128]{1,0:T(8,128)}, f32[1064,128]{1,0:T(8,128)}, f32[1064,128]{1,0:T(8,128)}) custom-call(s32[6]{0:T(128)} %pad_add_fusion.scal_ref, f32[16,256,128]{2,1,0:T(8,128)} %field_ref.3), custom_call_target="tpu_custom_call" | custom-call | tf_op jit(solution)/shard_map/pack/pallas_call | solution.py:175
  5.0 3.0 %collective-permute-start = (f32[1064,128]{1,0:T(8,128)}, f32[1064,128]{1,0:T(8,128)S(1)}, u32[]{:S(2)}, u32[]{:S(2)}) collective-permute-start(f32[1064,128]{1,0:T(8,128)} %get-tuple-element.10), channel_id=1, source_target_pairs={{0,8},{8,0},{16,24},{24,16},{1,9},{9,1},{17,25},{25,17},{2,10},{10... | collective-permute-start | bytes 1634312 | tf_op jit(solution)/shard_map/ppermute | solution.py:163
  8.0 1.5 %collective-permute-start.1 = (f32[1064,128]{1,0:T(8,128)}, f32[1064,128]{1,0:T(8,128)S(1)}, u32[]{:S(2)}, u32[]{:S(2)}) collective-permute-start(f32[1064,128]{1,0:T(8,128)} %get-tuple-element.11), channel_id=1, source_target_pairs={{0,16},{8,24},{16,0},{24,8},{1,17},{9,25},{17,1},{25,9},{2,18},{10... | collective-permute-start | bytes 1634312 | tf_op jit(solution)/shard_map/ppermute | solution.py:163
  9.5 0.0 collective-permute-start.2
  9.5 3.3 %edges.1 = f32[64,128]{1,0:T(8,128)} custom-call(f32[16,256,128]{2,1,0:T(8,128)} %field_ref.3), custom_call_target="tpu_custom_call" | custom-call | tf_op jit(solution)/shard_map/edges/pallas_call | solution.py:185
  12.8 0.0 copy-done.4
  12.8 0.7 %copy.10.lights_ref = f32[16,3]{1,0:T(8,128)} copy(f32[16,3]{0,1:T(4,128)S(1)} %copy-done.4) | data formatting | bytes 384 | tf_op args[1]
  13.5 0.0 copy-done.3
  13.5 0.6 %copy.11.curves_ref = f32[16,32]{1,0:T(8,128)} copy(f32[16,32]{0,1:T(8,128)S(1)} %bitcast.4) | data formatting | bytes 4096 | tf_op jit(solution)/shard_map/reshape | solution.py:208
  14.2 15.1 %all-gather = f32[512,128]{1,0:T(8,128)S(1)} all-gather(f32[64,128]{1,0:T(8,128)} %edges.1), channel_id=2, replica_groups=mesh['depth'=4,'tile'=8] {'tile'}, dimensions={0}, use_global_device_ids=true | all-gather | bytes 294912 | tf_op jit(solution)/shard_map/all_gather | solution.py:192
  29.3 9.2 %all_gather.12.lateral_ref = f32[4,64,128]{2,1,0:T(8,128)} all-gather(f32[1,64,128]{2,1,0:T(8,128)S(1)} %select_select_fusion), channel_id=1, replica_groups=mesh['depth'=4,'tile'=8] {'depth'}, dimensions={0}, use_global_device_ids=true | all-gather | bytes 163840 | tf_op jit(solution)/shard_map/all_gather | solution.py:197
  38.4 0.0 collective-permute-done.refs_1_
  38.4 0.0 copy-start
  38.4 0.0 collective-permute-done.1.refs_2_
  38.5 0.0 copy-start.1
  38.5 0.0 collective-permute-done.2.refs_3_
  38.5 0.0 copy-start.2
  38.5 0.7 %copy-done = f32[1064,128]{1,0:T(8,128)} copy-done((f32[1064,128]{1,0:T(8,128)}, f32[1064,128]{1,0:T(8,128)S(1)}, u32[]{:S(2)}) %copy-start) | copy-done | bytes 544792
  39.2 0.2 copy-done.1
  39.4 0.2 copy-done.2
  39.6 20.2 %shade.1 = f32[4,4,64,128]{3,2,1,0:T(8,128)} custom-call(s32[6]{0:T(128)} %pad_add_fusion.scal_ref, f32[16,3]{1,0:T(8,128)} %copy.10.lights_ref, f32[16,32]{1,0:T(8,128)} %copy.11.curves_ref, f32[4,64,128]{2,1,0:T(8,128)} %all_gather.12.lateral_ref, f32[1064,128]{1,0:T(8,128)} %get-tuple-element.9.refs_0_, f32[1064,128]{1,0:T(8,128)} %copy-done, ...), custom_call_target="tpu_custom_call" | custom-call | tf_op jit(solution)/shard_map/shade/pallas_call | solution.py:198
  (2 shorter events, 0.0 us)
Async XLA Ops:
  1.9 10.9 %copy-start.4 = (f32[16,3]{0,1:T(4,128)S(1)}, f32[16,3]{0,1:T(4,128)}, u32[]{:S(2)}) copy-start(f32[16,3]{0,1:T(4,128)} %param.6) | copy-start | bytes 580
  1.9 11.6 %copy-start.3 = (f32[16,4,8]{0,2,1:T(8,128)S(1)}, f32[16,4,8]{0,2,1:T(8,128)}, u32[]{:S(2)}) copy-start(f32[16,4,8]{0,2,1:T(8,128)} %param.7) | copy-start | bytes 6148
  5.0 33.4 %collective-permute-start = (f32[1064,128]{1,0:T(8,128)}, f32[1064,128]{1,0:T(8,128)S(1)}, u32[]{:S(2)}, u32[]{:S(2)}) collective-permute-start(f32[1064,128]{1,0:T(8,128)} %get-tuple-element.10), channel_id=1, source_target_pairs={{0,8},{8,0},{16,24},{24,16},{1,9},{9,1},{17,25},{25,17},{2,10},{10... | collective-permute-start | bytes 1634312 | tf_op jit(solution)/shard_map/ppermute | solution.py:163
  8.0 30.5 %collective-permute-start.1 = (f32[1064,128]{1,0:T(8,128)}, f32[1064,128]{1,0:T(8,128)S(1)}, u32[]{:S(2)}, u32[]{:S(2)}) collective-permute-start(f32[1064,128]{1,0:T(8,128)} %get-tuple-element.11), channel_id=1, source_target_pairs={{0,16},{8,24},{16,0},{24,8},{1,17},{9,25},{17,1},{25,9},{2,18},{10... | collective-permute-start | bytes 1634312 | tf_op jit(solution)/shard_map/ppermute | solution.py:163
  9.5 29.0 %collective-permute-start.2 = (f32[1064,128]{1,0:T(8,128)}, f32[1064,128]{1,0:T(8,128)S(1)}, u32[]{:S(2)}, u32[]{:S(2)}) collective-permute-start(f32[1064,128]{1,0:T(8,128)} %get-tuple-element.12), channel_id=1, source_target_pairs={{0,24},{8,16},{16,8},{24,0},{1,25},{9,17},{17,9},{25,1},{2,26},{10... | collective-permute-start | bytes 1634312 | tf_op jit(solution)/shard_map/ppermute | solution.py:163
  38.4 0.8 %copy-start = (f32[1064,128]{1,0:T(8,128)}, f32[1064,128]{1,0:T(8,128)S(1)}, u32[]{:S(2)}) copy-start(f32[1064,128]{1,0:T(8,128)S(1)} %collective-permute-done.refs_1_) | copy-start | bytes 1634308
  38.5 1.0 %copy-start.1 = (f32[1064,128]{1,0:T(8,128)}, f32[1064,128]{1,0:T(8,128)S(1)}, u32[]{:S(2)}) copy-start(f32[1064,128]{1,0:T(8,128)S(1)} %collective-permute-done.1.refs_2_) | copy-start | bytes 1634308
  38.5 1.2 %copy-start.2 = (f32[1064,128]{1,0:T(8,128)}, f32[1064,128]{1,0:T(8,128)S(1)}, u32[]{:S(2)}) copy-start(f32[1064,128]{1,0:T(8,128)S(1)} %collective-permute-done.2.refs_3_) | copy-start | bytes 1634308
where the time goes:
time: 60.1 us; the launch traced here: 59.8 us
  Pallas kernels  26.5 us (44%)
  blocking collectives  24.2 us (40%)
  starting transfers between devices  4.54 us (8%)
  local copies, waits for them, and re-layouts  2.5 us (4%)
  other arithmetic  1.28 us (2%)
  between operations  0.71 us (1%)
    pallas_call x1, Pallas kernels, on_device(): pl.pallas_call(functools.partial(shade_kernel, parts, cells, passes, knot...  20.2 us
    all_gather x1, blocking collectives, on_device(): around = lax.all_gather(edges, 'tile')  15.1 us
    all_gather x1, blocking collectives, on_device(): lateral = lax.all_gather(sides, 'depth')  9.16 us
    ppermute x3, starting transfers between devices, swap_along(): lax.ppermute(block, axis, [(i, i ^ mask) for i in range(lax.axis_size(axi...  4.54 us
    pallas_call x1, Pallas kernels, on_device(): pl.pallas_call(functools.partial(edge_kernel, parts), out_shape=jax.Shape...  3.3 us
    pallas_call x1, Pallas kernels, on_device(): pl.pallas_call(functools.partial(pack_kernel, parts), out_shape=[jax.Shap...  3.06 us
    unnamed x11, local copies, waits for them, and re-layouts  1.85 us
    concatenate x1, other arithmetic, on_device(): jnp.concatenate([lax.axis_index('depth').astype(jnp.int32)[None], flips,...  1.27 us
  transfers between devices with their start and end apart: 3, of which 0 were waited for; matrix products, arithmetic and copies ran while one was open for 2% of the time, Pallas kernels for 6%

commit v1 on v0

v1 whole, which is shorter than its diff:
```python
import functools

import jax
import jax.numpy as jnp
from jax import lax
from jax.experimental import pallas as pl
from jax.experimental.pallas import tpu as pltpu
from jax.sharding import PartitionSpec as P

AMBIENT = 0.3
OPACITY = 2.0
SUB = 8
VMEM = pltpu.VMEM
SMEM = pltpu.SMEM


def edge_kernel(parts, field_ref, out_ref):
    cells, _, cols = field_ref.shape
    rows = out_ref.shape[0]
    lane_pair = lax.broadcasted_iota(jnp.int32, (SUB, cols), 1) // 2

    def tile(i, carry):
        acc = jnp.zeros((SUB, cols), jnp.float32)
        for part in range(parts):
            for z in range(cells):
                slot = part * cells + z
                start = pl.multiple_of(part * rows + i * SUB, SUB)
                value = field_ref[z, pl.ds(start, SUB), :]
                moved = pltpu.roll(value, (2 * slot + 1) % cols, 1)
                acc = jnp.where(lane_pair == slot, moved, acc)
        out_ref[pl.ds(pl.multiple_of(i * SUB, SUB), SUB), :] = acc
        return carry

    lax.fori_loop(0, rows // SUB, tile, 0)


def pack_kernel(parts, field_ref, *refs):
    outs, (near_ref, extra_ref, sems) = refs[:parts], refs[parts:]
    cells, all_rows, cols = field_ref.shape
    rows = all_rows // parts
    me = lax.axis_index("depth")
    copies, nears = [], []
    for m in range(parts):
        low = pl.multiple_of((me ^ m) * rows, SUB)
        centre = outs[m].at[pl.ds(2 * cells, cells * rows), :].reshape(cells, rows, cols)
        before = pl.multiple_of(jnp.maximum(low - SUB, 0), SUB)
        after = pl.multiple_of(jnp.minimum(low + rows, all_rows - SUB), SUB)
        for side, start in enumerate((before, after)):
            nears.append(
                pltpu.make_async_copy(field_ref.at[:, pl.ds(start, SUB), :], near_ref.at[m, side], sems.at[1 + side, m])
            )
            nears[-1].start()
        copies.append(pltpu.make_async_copy(field_ref.at[:, pl.ds(low, rows), :], centre, sems.at[0, m]))
        copies[-1].start()
    for m in range(parts):
        part = me ^ m
        above = jnp.where(part > 0, 1.0, 0.0)
        below = jnp.where(part < parts - 1, 1.0, 0.0)
        nears[2 * m].wait()
        nears[2 * m + 1].wait()
        for z in range(cells):
            extra_ref[m, z : z + 1, :] = near_ref[m, 0, z, SUB - 1 : SUB, :] * above
            extra_ref[m, cells + z : cells + z + 1, :] = near_ref[m, 1, z, 0:1, :] * below
        copies.append(pltpu.make_async_copy(extra_ref.at[m], outs[m].at[pl.ds(0, 2 * cells), :], sems.at[3, m]))
        copies[-1].start()
    for copy in copies:
        copy.wait()


def shade_kernel(parts, cells, passes, knots, unroll, index_ref, flip_ref, lights_ref, curves_ref, *refs):
    bricks, laterals, (out_ref, cell_ref, ends_ref) = refs[:parts], refs[parts : 2 * parts], refs[2 * parts :]
    cols = bricks[0].shape[1]
    rows = out_ref.shape[2]
    depth = parts * cells
    me = lax.axis_index("depth")
    flip = flip_ref[0]
    step = 1 - 2 * flip
    first = flip * (depth - 1)
    scale = OPACITY / depth
    lane = lax.broadcasted_iota(jnp.int32, (SUB, cols), 1)
    sublane = lax.broadcasted_iota(jnp.int32, (SUB, cols), 0)
    is_first = lane == 0
    is_last = lane == cols - 1

    def bends(index, channel):
        points = [curves_ref[index, channel, k] for k in range(knots)]
        slopes = [points[k + 1] - points[k] for k in range(knots - 1)]
        return [points[0], slopes[0]] + [slopes[k] - slopes[k - 1] for k in range(1, knots - 1)]

    def segments(index, channel, factor):
        points = [curves_ref[index, channel, k] * factor for k in range(knots)]
        offset = jnp.zeros((SUB, cols), jnp.float32)
        slope = jnp.zeros((SUB, cols), jnp.float32)
        for k in range(knots - 1):
            rise = points[k + 1] - points[k]
            slope = jnp.where(lane == k, rise, slope)
            offset = jnp.where(lane == k, points[k] - k * rise, offset)
        return offset, slope

    chosen = [index_ref[p] for p in range(passes)]
    vectors = [[lights_ref[chosen[p], axis] for axis in range(3)] for p in range(passes)]
    tables = [segments(chosen[p], 3, scale) for p in range(passes)]

    ends_ref[0, 1] = jnp.zeros((rows, cols), jnp.float32)
    ends_ref[parts + 1, 0] = jnp.zeros((rows, cols), jnp.float32)
    for m in range(parts):
        ends_ref[(me ^ m) + 1, 0] = bricks[m][2 * cells : 2 * cells + rows, :]
        ends_ref[(me ^ m) + 1, 1] = bricks[m][(cells - 1) * rows + 2 * cells : cells * rows + 2 * cells, :]

    def row_tile(i, carry):
        base = pl.multiple_of(i * SUB, SUB)
        at = pl.ds(base, SUB)
        is_top = jnp.logical_and(sublane == 0, i == 0)
        is_bottom = jnp.logical_and(sublane == SUB - 1, i == rows // SUB - 1)
        for m in range(parts):
            part = me ^ m
            brick = bricks[m]
            sides = pltpu.roll(laterals[m][at, :], (cols - 1 - 2 * cells * me) % cols, 1)
            line = [ends_ref[part, 1, at, :]]
            line += [brick[pl.ds(2 * cells + z * rows + base, SUB), :] for z in range(cells)]
            line += [ends_ref[part + 2, 0, at, :]]
            for z in range(cells):
                here = line[z + 1]
                start = 2 * cells + z * rows + base
                upper = jnp.where(is_top, brick[z : z + 1, :], brick[pl.ds(start - 1, SUB), :])
                lower = jnp.where(is_bottom, brick[cells + z : cells + z + 1, :], brick[pl.ds(start + 1, SUB), :])
                edge = pltpu.roll(sides, (cols - 2 * z) % cols, 1) if z else sides
                grad_x = pltpu.roll(jnp.where(is_first, edge, here), cols - 1, 1) - pltpu.roll(
                    jnp.where(is_last, edge, here), 1, 1
                )
                grad_y = lower - upper
                grad_z = line[z + 2] - line[z]
                inverse = lax.rsqrt(grad_x * grad_x + grad_y * grad_y + grad_z * grad_z + 4.0)
                half = 0.5 * (knots - 1)
                position = half + half * jnp.tanh(0.5 * here)
                spot = part * cells + z
                cell_ref[0, spot] = grad_x * inverse
                cell_ref[1, spot] = grad_y * inverse
                cell_ref[2, spot] = grad_z * inverse
                cell_ref[3, spot] = position
                for k in range(1, knots - 1):
                    cell_ref[3 + k, spot] = jnp.maximum(position - k, 0.0)
                segment = jnp.minimum(position.astype(jnp.int32), knots - 2)
                for p, (offset, slope) in enumerate(tables):
                    found = jnp.take_along_axis(offset, segment, axis=1, mode="promise_in_bounds")
                    rise = jnp.take_along_axis(slope, segment, axis=1, mode="promise_in_bounds")
                    cell_ref[knots + 2 + p, spot] = found + rise * position

        zero = jnp.zeros((SUB, cols), jnp.float32)
        for low in range(0, passes, 2):
            group = range(low, min(low + 2, passes))
            vector = {p: [jnp.full((SUB, cols), v) for v in vectors[p]] for p in group}

            def march(g, state):
                for u in range(unroll):
                    z = first + step * (g * unroll + u)
                    hinges = [cell_ref[3 + k, z] for k in range(knots - 1)]
                    normal = [cell_ref[axis, z] for axis in range(3)]
                    following = []
                    for p, (keep, sums) in zip(group, state):
                        facing = normal[0] * vector[p][0] + normal[1] * vector[p][1] + normal[2] * vector[p][2]
                        taken = keep * cell_ref[knots + 2 + p, z]
                        weight = taken * (AMBIENT + jnp.abs(facing))
                        sums = [sums[0] + weight] + [sums[k + 1] + weight * hinges[k] for k in range(knots - 1)]
                        following.append((keep - taken, sums))
                    state = following
                return state

            initial = [(jnp.ones((SUB, cols), jnp.float32), [zero] * knots) for p in group]
            state = lax.fori_loop(0, depth // unroll, march, initial)
            for p, (keep, sums) in zip(group, state):
                for channel in range(3):
                    tint = bends(chosen[p], channel)
                    color = tint[0] * sums[0]
                    for k in range(1, knots):
                        color = color + tint[k] * sums[k]
                    out_ref[p, channel, at, :] = color
                out_ref[p, 3, at, :] = 1.0 - keep
        return carry

    lax.fori_loop(0, rows // SUB, row_tile, 0)


def shift_along(block, axis, amount):
    count = lax.axis_size(axis)
    route = [(i, i + amount) for i in range(count) if 0 <= i + amount < count]
    return lax.ppermute(block, axis, route)


def swap_along(block, axis, mask):
    return lax.ppermute(block, axis, [(i, i ^ mask) for i in range(lax.axis_size(axis))])


def on_device(field, light_vectors, transfer, light_index, flips):
    parts = lax.axis_size("depth")
    cells, all_rows, cols = field.shape
    rows = all_rows // parts
    passes = light_index.shape[0]
    lights, channels, knots = transfer.shape
    message = cells * rows + 2 * cells + SUB
    packed = pl.pallas_call(
        functools.partial(pack_kernel, parts),
        out_shape=[jax.ShapeDtypeStruct((message, cols), jnp.float32)] * parts,
        in_specs=[pl.BlockSpec(memory_space=pl.ANY)],
        out_specs=[pl.BlockSpec(memory_space=pl.ANY)] * parts,
        scratch_shapes=[
            VMEM((parts, 2, cells, SUB, cols), jnp.float32),
            VMEM((parts, 2 * cells, cols), jnp.float32),
            pltpu.SemaphoreType.DMA((4, parts)),
        ],
        name="pack",
    )(field)
    bricks = [packed[0]] + [swap_along(packed[m], "depth", m) for m in range(1, parts)]

    edges = pl.pallas_call(
        functools.partial(edge_kernel, parts),
        out_shape=jax.ShapeDtypeStruct((rows, cols), jnp.float32),
        in_specs=[pl.BlockSpec(memory_space=VMEM)],
        out_specs=pl.BlockSpec(memory_space=VMEM),
        name="edges",
    )(field)
    left = shift_along(edges, "tile", 1)
    right = shift_along(edges, "tile", -1)
    sides = jnp.where(jnp.arange(cols) % 2 == 0, left, right)
    laterals = [sides] + [swap_along(sides, "depth", m) for m in range(1, parts)]
    return pl.pallas_call(
        functools.partial(shade_kernel, parts, cells, passes, knots, 32),
        out_shape=jax.ShapeDtypeStruct((passes, channels, rows, cols), jnp.float32),
        in_specs=[pl.BlockSpec(memory_space=SMEM)] * 4 + [pl.BlockSpec(memory_space=VMEM)] * (2 * parts),
        out_specs=pl.BlockSpec(memory_space=VMEM),
        scratch_shapes=[
            VMEM((knots + 2 + passes, parts * cells, SUB, cols), jnp.float32),
            VMEM((parts + 2, 2, rows, cols), jnp.float32),
        ],
        name="shade",
    )(light_index, flips, light_vectors, transfer, *bricks, *laterals)


def solution(mesh):
    in_specs = (P("depth", None, "tile"), P(), P(), P(), P("tile"))
    out_specs = P(None, None, "depth", "tile")
    return jax.shard_map(
        on_device, mesh=mesh, in_specs=in_specs, out_specs=out_specs, check_vma=False
    )
```

time: 60.1 us -> 142 us (2.36)
  Pallas kernels: 26.5 us -> 111 us
  blocking collectives: 24.2 us -> 0 us
  waiting for transfers between devices: 0.01 us -> 14.6 us
  starting transfers between devices: 4.54 us -> 12.9 us
    pallas_call x1, Pallas kernels: 3.06 us -> 64.8 us  [on_device(): pl.pallas_call(functools.partial(pack_kernel, parts), out_shape=[jax.Shap...]
    all_gather x2 -> x0, blocking collectives: 24.2 us -> none  [the longest x1 15.1 us: on_device(): around = lax.all_gather(edges, 'tile')]
    pallas_call x1, Pallas kernels: 20.2 us -> 43.2 us  [on_device(): pl.pallas_call(functools.partial(shade_kernel, parts, cells, passes, knot...]
    ppermute x3 -> x6, waiting for transfers between devices: 0.01 us -> 10.3 us  [swap_along(): lax.ppermute(block, axis, [(i, i ^ mask) for i in range(lax.axis_size(axi...]
    ppermute x3 -> x6, starting transfers between devices: 4.54 us -> 10.3 us  [swap_along(): lax.ppermute(block, axis, [(i, i ^ mask) for i in range(lax.axis_size(axi...]
    ppermute x0 -> x2, waiting for transfers between devices: none -> 4.26 us  [shift_along(): return lax.ppermute(block, axis, route)]
    ppermute x0 -> x2, starting transfers between devices: none -> 2.57 us  [shift_along(): return lax.ppermute(block, axis, route)]
  transfers between devices with their start and end apart: 3 -> 8, of which waited for: 0 -> 3; matrix products, arithmetic and copies ran while one was open for 2% -> 1% of each run, Pallas kernels for 6% -> 2%
where the time goes in v1:
time: 142 us
  Pallas kernels  111 us (78%)
  waiting for transfers between devices  14.6 us (10%)
  starting transfers between devices  12.9 us (9%)
  local copies, waits for them, and re-layouts  2.52 us (2%)
    pallas_call x1, Pallas kernels, on_device(): pl.pallas_call(functools.partial(pack_kernel, parts), out_shape=[jax.Shap...  64.8 us
    pallas_call x1, Pallas kernels, on_device(): pl.pallas_call(functools.partial(shade_kernel, parts, cells, passes, knot...  43.2 us
    ppermute x6, starting transfers between devices, swap_along(): lax.ppermute(block, axis, [(i, i ^ mask) for i in range(lax.axis_size(axi...  10.3 us
    ppermute x6, waiting for transfers between devices, swap_along(): lax.ppermute(block, axis, [(i, i ^ mask) for i in range(lax.axis_size(axi...  10.3 us
    ppermute x2, waiting for transfers between devices, shift_along(): return lax.ppermute(block, axis, route)  4.26 us
    pallas_call x1, Pallas kernels, on_device(): pl.pallas_call(functools.partial(edge_kernel, parts), out_shape=jax.Shape...  3.3 us
  transfers between devices with their start and end apart: 8, of which 3 were waited for; matrix products, arithmetic and copies ran while one was open for 1% of the time, Pallas kernels for 2%

profile of v1, /device:TPU:0, one launch (start us, length us, event | category | flops | bytes accessed | tf_op | source)
XLA Modules:
  0.0 142.0 jit_solution(11333927757340239749)
XLA Ops:
  0.0 64.8 %pack.1 = (f32[1064,128]{1,0:T(8,128)}, f32[1064,128]{1,0:T(8,128)}, f32[1064,128]{1,0:T(8,128)}, f32[1064,128]{1,0:T(8,128)}) custom-call(f32[16,256,128]{2,1,0:T(8,128)} %field_ref.3), custom_call_target="tpu_custom_call" | custom-call | tf_op jit(solution)/shard_map/pack/pallas_call | solution.py:201
  64.8 3.0 %collective-permute-start = (f32[1064,128]{1,0:T(8,128)}, f32[1064,128]{1,0:T(8,128)S(1)}, u32[]{:S(2)}, u32[]{:S(2)}) collective-permute-start(f32[1064,128]{1,0:T(8,128)} %get-tuple-element.10), channel_id=1, source_target_pairs={{0,8},{8,0},{16,24},{24,16},{1,9},{9,1},{17,25},{25,17},{2,10},{10... | collective-permute-start | bytes 1634312 | tf_op jit(solution)/shard_map/ppermute | solution.py:191
  67.8 1.5 %collective-permute-start.1 = (f32[1064,128]{1,0:T(8,128)}, f32[1064,128]{1,0:T(8,128)S(1)}, u32[]{:S(2)}, u32[]{:S(2)}) collective-permute-start(f32[1064,128]{1,0:T(8,128)} %get-tuple-element.11), channel_id=1, source_target_pairs={{0,16},{8,24},{16,0},{24,8},{1,17},{9,25},{17,1},{25,9},{2,18},{10... | collective-permute-start | bytes 1634312 | tf_op jit(solution)/shard_map/ppermute | solution.py:191
  69.3 0.0 collective-permute-start.2
  69.3 3.3 %edges.1 = f32[64,128]{1,0:T(8,128)} custom-call(f32[16,256,128]{2,1,0:T(8,128)} %field_ref.3), custom_call_target="tpu_custom_call" | custom-call | tf_op jit(solution)/shard_map/edges/pallas_call | solution.py:215
  72.6 1.3 collective-permute-start.3
  73.9 1.3 collective-permute-start.4
  75.2 0.0 collective-permute-done.3
  75.2 4.3 %collective-permute-done.4 = f32[64,128]{1,0:T(8,128)S(1)} collective-permute-done((f32[64,128]{1,0:T(8,128)}, f32[64,128]{1,0:T(8,128)S(1)}, u32[]{:S(2)}, u32[]{:S(2)}) %collective-permute-start.4) | collective-permute-done | bytes 32800 | tf_op jit(solution)/shard_map/ppermute | solution.py:187
  79.5 1.6 %collective-permute-start.5 = (f32[64,128]{1,0:T(8,128)S(1)}, f32[64,128]{1,0:T(8,128)S(1)}, u32[]{:S(2)}, u32[]{:S(2)}) collective-permute-start(f32[64,128]{1,0:T(8,128)S(1)} %broadcast_select_fusion.refs_4_), channel_id=1, source_target_pairs={{0,8},{8,0},{16,24},{24,16},{1,9},{9,1},{17,25},{25,17},{2,10},{10... | collective-permute-start | bytes 98312 | tf_op jit(solution)/shard_map/ppermute | solution.py:191
  81.1 1.5 %collective-permute-start.6 = (f32[64,128]{1,0:T(8,128)S(1)}, f32[64,128]{1,0:T(8,128)S(1)}, u32[]{:S(2)}, u32[]{:S(2)}) collective-permute-start(f32[64,128]{1,0:T(8,128)S(1)} %broadcast_select_fusion.refs_4_), channel_id=1, source_target_pairs={{0,16},{8,24},{16,0},{24,8},{1,17},{9,25},{17,1},{25,9},{2,18},{10... | collective-permute-start | bytes 98312 | tf_op jit(solution)/shard_map/ppermute | solution.py:191
  82.6 10.2 %collective-permute-done.5.refs_5_ = f32[64,128]{1,0:T(8,128)S(1)} collective-permute-done((f32[64,128]{1,0:T(8,128)S(1)}, f32[64,128]{1,0:T(8,128)S(1)}, u32[]{:S(2)}, u32[]{:S(2)}) %collective-permute-start.5) | collective-permute-done | bytes 32800 | tf_op jit(solution)/shard_map/ppermute | solution.py:191
  92.8 2.7 %collective-permute-start.7 = (f32[64,128]{1,0:T(8,128)S(1)}, f32[64,128]{1,0:T(8,128)S(1)}, u32[]{:S(2)}, u32[]{:S(2)}) collective-permute-start(f32[64,128]{1,0:T(8,128)S(1)} %broadcast_select_fusion.refs_4_), channel_id=1, source_target_pairs={{0,24},{8,16},{16,8},{24,0},{1,25},{9,17},{17,9},{25,1},{2,26},{10... | collective-permute-start | bytes 98312 | tf_op jit(solution)/shard_map/ppermute | solution.py:191
  95.5 0.0 copy-done.7
  95.5 0.7 copy.7.curves_ref
  96.2 0.0 copy-done.8
  96.2 0.7 copy.6.lights_ref
  97.5 0.0 collective-permute-done.6.refs_6_
  97.5 0.0 copy-start.5
  97.5 0.1 collective-permute-done.7.refs_7_
  97.6 0.0 collective-permute-done.refs_1_
  97.6 0.0 collective-permute-done.1.refs_2_
  97.6 0.0 copy-start.1
  97.6 0.0 collective-permute-done.2.refs_3_
  97.6 0.0 copy-start.2
  97.7 0.0 copy-done.3
  97.7 0.4 copy-done.5
  98.1 0.1 copy-done.6
  98.2 0.2 copy-done
  98.4 0.2 copy-done.1
  98.6 0.2 copy-done.2
  98.8 43.2 %shade.1 = f32[4,4,64,128]{3,2,1,0:T(8,128)} custom-call(s32[4]{0:T(128)} %index_ref.1, s32[1]{0:T(128)S(6)} %copy.8.flip_ref, f32[16,3]{1,0:T(8,128)} %copy.6.lights_ref, f32[16,4,8]{2,1,0:T(4,128)} %copy.7.curves_ref, f32[1064,128]{1,0:T(8,128)} %get-tuple-element.9.refs_0_, f32[1064,128]{1,0:T(8,128)} %copy-done, f32[1064,128]{1,0:T(8,128)} %copy-done.1, ...), custom_call_target="tpu_custom_call" | custom-call | tf_op jit(solution)/shard_map/shade/pallas_call | solution.py:226
  (9 shorter events, 0.0 us)
Async XLA Ops:
  0.0 95.5 %copy-start.7 = (f32[16,4,8]{0,2,1:T(8,128)S(1)}, f32[16,4,8]{0,2,1:T(8,128)}, u32[]{:S(2)}) copy-start(f32[16,4,8]{0,2,1:T(8,128)} %param.7) | copy-start | bytes 6148
  0.0 96.2 %copy-start.8 = (f32[16,3]{0,1:T(4,128)S(1)}, f32[16,3]{0,1:T(4,128)}, u32[]{:S(2)}) copy-start(f32[16,3]{0,1:T(4,128)} %param.6) | copy-start | bytes 580
  64.8 32.8 %collective-permute-start = (f32[1064,128]{1,0:T(8,128)}, f32[1064,128]{1,0:T(8,128)S(1)}, u32[]{:S(2)}, u32[]{:S(2)}) collective-permute-start(f32[1064,128]{1,0:T(8,128)} %get-tuple-element.10), channel_id=1, source_target_pairs={{0,8},{8,0},{16,24},{24,16},{1,9},{9,1},{17,25},{25,17},{2,10},{10... | collective-permute-start | bytes 1634312 | tf_op jit(solution)/shard_map/ppermute | solution.py:191
  67.8 29.8 %collective-permute-start.1 = (f32[1064,128]{1,0:T(8,128)}, f32[1064,128]{1,0:T(8,128)S(1)}, u32[]{:S(2)}, u32[]{:S(2)}) collective-permute-start(f32[1064,128]{1,0:T(8,128)} %get-tuple-element.11), channel_id=1, source_target_pairs={{0,16},{8,24},{16,0},{24,8},{1,17},{9,25},{17,1},{25,9},{2,18},{10... | collective-permute-start | bytes 1634312 | tf_op jit(solution)/shard_map/ppermute | solution.py:191
  69.3 28.3 %collective-permute-start.2 = (f32[1064,128]{1,0:T(8,128)}, f32[1064,128]{1,0:T(8,128)S(1)}, u32[]{:S(2)}, u32[]{:S(2)}) collective-permute-start(f32[1064,128]{1,0:T(8,128)} %get-tuple-element.12), channel_id=1, source_target_pairs={{0,24},{8,16},{16,8},{24,0},{1,25},{9,17},{17,9},{25,1},{2,26},{10... | collective-permute-start | bytes 1634312 | tf_op jit(solution)/shard_map/ppermute | solution.py:191
  72.6 2.6 %collective-permute-start.3 = (f32[64,128]{1,0:T(8,128)}, f32[64,128]{1,0:T(8,128)S(1)}, u32[]{:S(2)}, u32[]{:S(2)}) collective-permute-start(f32[64,128]{1,0:T(8,128)} %edges.1), channel_id=1, source_target_pairs={{0,1},{1,2},{2,3},{3,4},{4,5},{5,6},{6,7},{8,9},{9,10},{10,11},{11... | collective-permute-start | bytes 98312 | tf_op jit(solution)/shard_map/ppermute | solution.py:187
  73.9 5.6 %collective-permute-start.4 = (f32[64,128]{1,0:T(8,128)}, f32[64,128]{1,0:T(8,128)S(1)}, u32[]{:S(2)}, u32[]{:S(2)}) collective-permute-start(f32[64,128]{1,0:T(8,128)} %edges.1), channel_id=1, source_target_pairs={{1,0},{2,1},{3,2},{4,3},{5,4},{6,5},{7,6},{9,8},{10,9},{11,10},{12... | collective-permute-start | bytes 98312 | tf_op jit(solution)/shard_map/ppermute | solution.py:187
  79.5 18.1 %copy-start.3 = (f32[64,128]{1,0:T(8,128)}, f32[64,128]{1,0:T(8,128)S(1)}, u32[]{:S(2)}) copy-start(f32[64,128]{1,0:T(8,128)S(1)} %broadcast_select_fusion.refs_4_) | copy-start | bytes 98308
  79.5 13.3 %collective-permute-start.5 = (f32[64,128]{1,0:T(8,128)S(1)}, f32[64,128]{1,0:T(8,128)S(1)}, u32[]{:S(2)}, u32[]{:S(2)}) collective-permute-start(f32[64,128]{1,0:T(8,128)S(1)} %broadcast_select_fusion.refs_4_), channel_id=1, source_target_pairs={{0,8},{8,0},{16,24},{24,16},{1,9},{9,1},{17,25},{25,17},{2,10},{10... | collective-permute-start | bytes 98312 | tf_op jit(solution)/shard_map/ppermute | solution.py:191
  81.1 16.4 %collective-permute-start.6 = (f32[64,128]{1,0:T(8,128)S(1)}, f32[64,128]{1,0:T(8,128)S(1)}, u32[]{:S(2)}, u32[]{:S(2)}) collective-permute-start(f32[64,128]{1,0:T(8,128)S(1)} %broadcast_select_fusion.refs_4_), channel_id=1, source_target_pairs={{0,16},{8,24},{16,0},{24,8},{1,17},{9,25},{17,1},{25,9},{2,18},{10... | collective-permute-start | bytes 98312 | tf_op jit(solution)/shard_map/ppermute | solution.py:191
  92.8 4.9 %copy-start.4 = (f32[64,128]{1,0:T(8,128)}, f32[64,128]{1,0:T(8,128)S(1)}, u32[]{:S(2)}) copy-start(f32[64,128]{1,0:T(8,128)S(1)} %collective-permute-done.5.refs_5_) | copy-start | bytes 98308
  92.8 4.8 %collective-permute-start.7 = (f32[64,128]{1,0:T(8,128)S(1)}, f32[64,128]{1,0:T(8,128)S(1)}, u32[]{:S(2)}, u32[]{:S(2)}) collective-permute-start(f32[64,128]{1,0:T(8,128)S(1)} %broadcast_select_fusion.refs_4_), channel_id=1, source_target_pairs={{0,24},{8,16},{16,8},{24,0},{1,25},{9,17},{17,9},{25,1},{2,26},{10... | collective-permute-start | bytes 98312 | tf_op jit(solution)/shard_map/ppermute | solution.py:191
  97.5 0.6 copy-start.5
  97.6 0.6 copy-start.6
  97.6 0.8 copy-start
  97.6 1.0 copy-start.1
  97.6 1.2 copy-start.2

commit v2 on v1

--- a/solution.py
+++ b/solution.py
@@ -14,7 +14,7 @@
 SMEM = pltpu.SMEM
 
 
-def edge_kernel(parts, field_ref, out_ref):
+def edge_kernel(parts, field_ref, _, out_ref):
     cells, _, cols = field_ref.shape
     rows = out_ref.shape[0]
     lane_pair = lax.broadcasted_iota(jnp.int32, (SUB, cols), 1) // 2
@@ -35,40 +35,34 @@
 
 
 def pack_kernel(parts, field_ref, *refs):
-    outs, (near_ref, extra_ref, sems) = refs[:parts], refs[parts:]
+    outs, (extra_ref, sems) = refs[:parts], refs[parts:]
     cells, all_rows, cols = field_ref.shape
     rows = all_rows // parts
     me = lax.axis_index("depth")
-    copies, nears = [], []
+    copies = []
     for m in range(parts):
         low = pl.multiple_of((me ^ m) * rows, SUB)
         centre = outs[m].at[pl.ds(2 * cells, cells * rows), :].reshape(cells, rows, cols)
-        before = pl.multiple_of(jnp.maximum(low - SUB, 0), SUB)
-        after = pl.multiple_of(jnp.minimum(low + rows, all_rows - SUB), SUB)
-        for side, start in enumerate((before, after)):
-            nears.append(
-                pltpu.make_async_copy(field_ref.at[:, pl.ds(start, SUB), :], near_ref.at[m, side], sems.at[1 + side, m])
-            )
-            nears[-1].start()
         copies.append(pltpu.make_async_copy(field_ref.at[:, pl.ds(low, rows), :], centre, sems.at[0, m]))
         copies[-1].start()
     for m in range(parts):
         part = me ^ m
+        low = part * rows
         above = jnp.where(part > 0, 1.0, 0.0)
         below = jnp.where(part < parts - 1, 1.0, 0.0)
-        nears[2 * m].wait()
-        nears[2 * m + 1].wait()
         for z in range(cells):
-            extra_ref[m, z : z + 1, :] = near_ref[m, 0, z, SUB - 1 : SUB, :] * above
-            extra_ref[m, cells + z : cells + z + 1, :] = near_ref[m, 1, z, 0:1, :] * below
-        copies.append(pltpu.make_async_copy(extra_ref.at[m], outs[m].at[pl.ds(0, 2 * cells), :], sems.at[3, m]))
+            extra_ref[m, z : z + 1, :] = field_ref[z, pl.ds(jnp.maximum(low - 1, 0), 1), :] * above
+            extra_ref[m, cells + z : cells + z + 1, :] = (
+                field_ref[z, pl.ds(jnp.minimum(low + rows, all_rows - 1), 1), :] * below
+            )
+        copies.append(pltpu.make_async_copy(extra_ref.at[m], outs[m].at[pl.ds(0, 2 * cells), :], sems.at[1, m]))
         copies[-1].start()
     for copy in copies:
         copy.wait()
 
 
 def shade_kernel(parts, cells, passes, knots, unroll, index_ref, flip_ref, lights_ref, curves_ref, *refs):
-    bricks, laterals, (out_ref, cell_ref, ends_ref) = refs[:parts], refs[parts : 2 * parts], refs[2 * parts :]
+    bricks, laterals, (out_ref, cell_ref, ends_ref) = refs[:parts], refs[parts : 2 * parts - 1], refs[2 * parts - 1 :]
     cols = bricks[0].shape[1]
     rows = out_ref.shape[2]
     depth = parts * cells
@@ -87,19 +81,9 @@
         slopes = [points[k + 1] - points[k] for k in range(knots - 1)]
         return [points[0], slopes[0]] + [slopes[k] - slopes[k - 1] for k in range(1, knots - 1)]
 
-    def segments(index, channel, factor):
-        points = [curves_ref[index, channel, k] * factor for k in range(knots)]
-        offset = jnp.zeros((SUB, cols), jnp.float32)
-        slope = jnp.zeros((SUB, cols), jnp.float32)
-        for k in range(knots - 1):
-            rise = points[k + 1] - points[k]
-            slope = jnp.where(lane == k, rise, slope)
-            offset = jnp.where(lane == k, points[k] - k * rise, offset)
-        return offset, slope
-
     chosen = [index_ref[p] for p in range(passes)]
     vectors = [[lights_ref[chosen[p], axis] for axis in range(3)] for p in range(passes)]
-    tables = [segments(chosen[p], 3, scale) for p in range(passes)]
+    curves = [[value * scale for value in bends(chosen[p], 3)] for p in range(passes)]
 
     ends_ref[0, 1] = jnp.zeros((rows, cols), jnp.float32)
     ends_ref[parts + 1, 0] = jnp.zeros((rows, cols), jnp.float32)
@@ -115,7 +99,8 @@
         for m in range(parts):
             part = me ^ m
             brick = bricks[m]
-            sides = pltpu.roll(laterals[m][at, :], (cols - 1 - 2 * cells * me) % cols, 1)
+            got = laterals[m][at, :] if m < parts - 1 else brick[pl.ds((2 + rows) * cells + base, SUB), :]
+            sides = pltpu.roll(got, (cols - 1 - 2 * cells * me) % cols, 1)
             line = [ends_ref[part, 1, at, :]]
             line += [brick[pl.ds(2 * cells + z * rows + base, SUB), :] for z in range(cells)]
             line += [ends_ref[part + 2, 0, at, :]]
@@ -140,16 +125,12 @@
                 cell_ref[3, spot] = position
                 for k in range(1, knots - 1):
                     cell_ref[3 + k, spot] = jnp.maximum(position - k, 0.0)
-                segment = jnp.minimum(position.astype(jnp.int32), knots - 2)
-                for p, (offset, slope) in enumerate(tables):
-                    found = jnp.take_along_axis(offset, segment, axis=1, mode="promise_in_bounds")
-                    rise = jnp.take_along_axis(slope, segment, axis=1, mode="promise_in_bounds")
-                    cell_ref[knots + 2 + p, spot] = found + rise * position
 
         zero = jnp.zeros((SUB, cols), jnp.float32)
         for low in range(0, passes, 2):
             group = range(low, min(low + 2, passes))
             vector = {p: [jnp.full((SUB, cols), v) for v in vectors[p]] for p in group}
+            curve = {p: [jnp.full((SUB, cols), v) for v in curves[p]] for p in group}
 
             def march(g, state):
                 for u in range(unroll):
@@ -159,7 +140,10 @@
                     following = []
                     for p, (keep, sums) in zip(group, state):
                         facing = normal[0] * vector[p][0] + normal[1] * vector[p][1] + normal[2] * vector[p][2]
-                        taken = keep * cell_ref[knots + 2 + p, z]
+                        terms = [curve[p][0]] + [curve[p][k + 1] * hinges[k] for k in range(knots - 1)]
+                        while len(terms) > 1:
+                            terms = [sum(terms[j : j + 2][1:], terms[j]) for j in range(0, len(terms), 2)]
+                        taken = keep * terms[0]
                         weight = taken * (AMBIENT + jnp.abs(facing))
                         sums = [sums[0] + weight] + [sums[k + 1] + weight * hinges[k] for k in range(knots - 1)]
                         following.append((keep - taken, sums))
@@ -197,39 +181,39 @@
     rows = all_rows // parts
     passes = light_index.shape[0]
     lights, channels, knots = transfer.shape
-    message = cells * rows + 2 * cells + SUB
+    message = cells * rows + 2 * cells
+    tails = [SUB] * (parts - 1) + [rows]
+
     packed = pl.pallas_call(
         functools.partial(pack_kernel, parts),
-        out_shape=[jax.ShapeDtypeStruct((message, cols), jnp.float32)] * parts,
-        in_specs=[pl.BlockSpec(memory_space=pl.ANY)],
+        out_shape=[jax.ShapeDtypeStruct((message + tail, cols), jnp.float32) for tail in tails],
+        in_specs=[pl.BlockSpec(memory_space=VMEM)],
         out_specs=[pl.BlockSpec(memory_space=pl.ANY)] * parts,
-        scratch_shapes=[
-            VMEM((parts, 2, cells, SUB, cols), jnp.float32),
-            VMEM((parts, 2 * cells, cols), jnp.float32),
-            pltpu.SemaphoreType.DMA((4, parts)),
-        ],
+        scratch_shapes=[VMEM((parts, 2 * cells, cols), jnp.float32), pltpu.SemaphoreType.DMA((2, parts))],
         name="pack",
     )(field)
-    bricks = [packed[0]] + [swap_along(packed[m], "depth", m) for m in range(1, parts)]
+    bricks = [packed[0]] + [swap_along(packed[m], "depth", m) for m in range(1, parts - 1)]
 
     edges = pl.pallas_call(
         functools.partial(edge_kernel, parts),
         out_shape=jax.ShapeDtypeStruct((rows, cols), jnp.float32),
-        in_specs=[pl.BlockSpec(memory_space=VMEM)],
+        in_specs=[pl.BlockSpec(memory_space=VMEM), pl.BlockSpec(memory_space=pl.ANY)],
         out_specs=pl.BlockSpec(memory_space=VMEM),
         name="edges",
-    )(field)
+    )(field, packed[0])
     left = shift_along(edges, "tile", 1)
     right = shift_along(edges, "tile", -1)
     sides = jnp.where(jnp.arange(cols) % 2 == 0, left, right)
-    laterals = [sides] + [swap_along(sides, "depth", m) for m in range(1, parts)]
+    laterals = [sides] + [swap_along(sides, "depth", m) for m in range(1, parts - 1)]
+    far = lax.dynamic_update_slice(packed[-1], sides, (message, 0))
+    bricks.append(swap_along(far, "depth", parts - 1))
     return pl.pallas_call(
-        functools.partial(shade_kernel, parts, cells, passes, knots, 32),
+        functools.partial(shade_kernel, parts, cells, passes, knots, parts * cells),
         out_shape=jax.ShapeDtypeStruct((passes, channels, rows, cols), jnp.float32),
-        in_specs=[pl.BlockSpec(memory_space=SMEM)] * 4 + [pl.BlockSpec(memory_space=VMEM)] * (2 * parts),
+        in_specs=[pl.BlockSpec(memory_space=SMEM)] * 4 + [pl.BlockSpec(memory_space=VMEM)] * (2 * parts - 1),
         out_specs=pl.BlockSpec(memory_space=VMEM),
         scratch_shapes=[
-            VMEM((knots + 2 + passes, parts * cells, SUB, cols), jnp.float32),
+            VMEM((knots + 2, parts * cells, SUB, cols), jnp.float32),
             VMEM((parts + 2, 2, rows, cols), jnp.float32),
         ],
         name="shade",

time: 142 us -> 64.7 us (0.46)
  Pallas kernels: 111 us -> 25.6 us
  waiting for transfers between devices: 14.6 us -> 24.7 us
  starting transfers between devices: 12.9 us -> 10.2 us
    pallas_call x1, Pallas kernels: 64.8 us -> 3.02 us  [on_device(): pl.pallas_call(functools.partial(pack_kernel, parts), out_shape=[jax.Shap...]
    pallas_call x1, Pallas kernels: 43.2 us -> 19.2 us  [on_device(): pl.pallas_call(functools.partial(shade_kernel, parts, cells, passes, knot...]
    ppermute x6 -> x5, waiting for transfers between devices: 10.3 us -> 20.5 us  [swap_along(): lax.ppermute(block, axis, [(i, i ^ mask) for i in range(lax.axis_size(axi...]
    ppermute x6 -> x5, starting transfers between devices: 10.3 us -> 6.56 us  [swap_along(): lax.ppermute(block, axis, [(i, i ^ mask) for i in range(lax.axis_size(axi...]
    unnamed x20 -> x24, local copies, waits for them, and re-layouts: 2.52 us -> 3.14 us
  transfers between devices with their start and end apart: 8 -> 7, of which waited for: 3 -> 3; matrix products, arithmetic and copies ran while one was open for 1% -> 2% of each run, Pallas kernels for 2% -> 0%
where the time goes in v2:
time: 64.7 us; the launch traced here: 64.4 us
  Pallas kernels  25.6 us (40%)
  waiting for transfers between devices  24.7 us (38%)
  starting transfers between devices  10.2 us (16%)
  local copies, waits for them, and re-layouts  3.14 us (5%)
  between operations  0.77 us (1%)
    ppermute x5, waiting for transfers between devices, swap_along(): lax.ppermute(block, axis, [(i, i ^ mask) for i in range(lax.axis_size(axi...  20.5 us
    pallas_call x1, Pallas kernels, on_device(): pl.pallas_call(functools.partial(shade_kernel, parts, cells, passes, knot...  19.2 us
    ppermute x5, starting transfers between devices, swap_along(): lax.ppermute(block, axis, [(i, i ^ mask) for i in range(lax.axis_size(axi...  6.56 us
    ppermute x2, waiting for transfers between devices, shift_along(): return lax.ppermute(block, axis, route)  4.18 us
    ppermute x2, starting transfers between devices, shift_along(): return lax.ppermute(block, axis, route)  3.64 us
    pallas_call x1, Pallas kernels, on_device(): pl.pallas_call(functools.partial(edge_kernel, parts), out_shape=jax.Shape...  3.42 us
    unnamed x24, local copies, waits for them, and re-layouts  3.14 us
    pallas_call x1, Pallas kernels, on_device(): pl.pallas_call(functools.partial(pack_kernel, parts), out_shape=[jax.Shap...  3.02 us
  transfers between devices with their start and end apart: 7, of which 3 were waited for; matrix products, arithmetic and copies ran while one was open for 2% of the time, Pallas kernels for 0%

profile of v2, /device:TPU:0, one launch (start us, length us, event | category | flops | bytes accessed | tf_op | source)
XLA Modules:
  0.0 64.4 jit_solution(16191275982052503940)
XLA Ops:
  0.0 3.0 %pack.1 = (f32[1064,128]{1,0:T(8,128)}, f32[1064,128]{1,0:T(8,128)}, f32[1064,128]{1,0:T(8,128)}, f32[1120,128]{1,0:T(8,128)}) custom-call(f32[16,256,128]{2,1,0:T(8,128)} %field_ref.3), custom_call_target="tpu_custom_call" | custom-call | tf_op jit(solution)/shard_map/pack/pallas_call | solution.py:187
  3.0 0.0 copy-start.8
  3.0 0.0 copy-start.10
  3.0 0.0 copy-start.9
  3.1 3.4 %edges.1 = f32[64,128]{1,0:T(8,128)} custom-call(f32[16,256,128]{2,1,0:T(8,128)} %field_ref.3, f32[1064,128]{1,0:T(8,128)} %get-tuple-element.9._.refs_0_), custom_call_target="tpu_custom_call" | custom-call | tf_op jit(solution)/shard_map/edges/pallas_call | solution.py:197
  6.5 2.3 %collective-permute-start.2 = (f32[64,128]{1,0:T(8,128)}, f32[64,128]{1,0:T(8,128)S(1)}, u32[]{:S(2)}, u32[]{:S(2)}) collective-permute-start(f32[64,128]{1,0:T(8,128)} %edges.1), channel_id=1, source_target_pairs={{0,1},{1,2},{2,3},{3,4},{4,5},{5,6},{6,7},{8,9},{9,10},{10,11},{11... | collective-permute-start | bytes 98312 | tf_op jit(solution)/shard_map/ppermute | solution.py:171
  8.8 1.3 %collective-permute-start.3 = (f32[64,128]{1,0:T(8,128)}, f32[64,128]{1,0:T(8,128)S(1)}, u32[]{:S(2)}, u32[]{:S(2)}) collective-permute-start(f32[64,128]{1,0:T(8,128)} %edges.1), channel_id=1, source_target_pairs={{1,0},{2,1},{3,2},{4,3},{5,4},{6,5},{7,6},{9,8},{10,9},{11,10},{12... | collective-permute-start | bytes 98312 | tf_op jit(solution)/shard_map/ppermute | solution.py:171
  10.1 0.0 collective-permute-done.2
  10.2 4.2 %collective-permute-done.3 = f32[64,128]{1,0:T(8,128)S(1)} collective-permute-done((f32[64,128]{1,0:T(8,128)}, f32[64,128]{1,0:T(8,128)S(1)}, u32[]{:S(2)}, u32[]{:S(2)}) %collective-permute-start.3) | collective-permute-done | bytes 32800 | tf_op jit(solution)/shard_map/ppermute | solution.py:171
  14.3 0.0 copy-done.8
  14.3 0.0 copy-start.3
  14.4 2.5 %collective-permute-start.4 = (f32[1120,128]{1,0:T(8,128)S(1)}, f32[1120,128]{1,0:T(8,128)S(1)}, u32[]{:S(2)}, u32[]{:S(2)}) collective-permute-start(f32[1120,128]{1,0:T(8,128)S(1)} %get-tuple-element.13), channel_id=1, source_target_pairs={{0,24},{8,16},{16,8},{24,0},{1,25},{9,17},{17,9},{25,1},{2,26},{10... | collective-permute-start | bytes 1720328 | tf_op jit(solution)/shard_map/ppermute | solution.py:175
  16.9 0.0 copy-done.10
  16.9 0.5 collective-permute-start
  17.4 0.0 copy-done.9
  17.4 0.5 collective-permute-start.1
  17.9 1.5 %collective-permute-start.5 = (f32[64,128]{1,0:T(8,128)S(1)}, f32[64,128]{1,0:T(8,128)S(1)}, u32[]{:S(2)}, u32[]{:S(2)}) collective-permute-start(f32[64,128]{1,0:T(8,128)S(1)} %get-tuple-element.14.refs_4_), channel_id=1, source_target_pairs={{0,8},{8,0},{16,24},{24,16},{1,9},{9,1},{17,25},{25,17},{2,10},{10... | collective-permute-start | bytes 98312 | tf_op jit(solution)/shard_map/ppermute | solution.py:175
  19.4 1.5 %collective-permute-start.6 = (f32[64,128]{1,0:T(8,128)S(1)}, f32[64,128]{1,0:T(8,128)S(1)}, u32[]{:S(2)}, u32[]{:S(2)}) collective-permute-start(f32[64,128]{1,0:T(8,128)S(1)} %get-tuple-element.14.refs_4_), channel_id=1, source_target_pairs={{0,16},{8,24},{16,0},{24,8},{1,17},{9,25},{17,1},{25,9},{2,18},{10... | collective-permute-start | bytes 98312 | tf_op jit(solution)/shard_map/ppermute | solution.py:175
  20.9 0.0 copy-done.6
  20.9 0.7 %copy.7.curves_ref = f32[16,4,8]{2,1,0:T(4,128)} copy(f32[16,4,8]{0,2,1:T(8,128)S(1)} %copy-done.6) | data formatting | bytes 4096 | tf_op args[2]
  21.6 0.7 %copy.6.lights_ref = f32[16,3]{1,0:T(8,128)} copy(f32[16,3]{0,1:T(4,128)S(1)} %copy-done.7) | data formatting | bytes 384 | tf_op args[1]
  22.9 19.0 %collective-permute-done.5.refs_5_ = f32[64,128]{1,0:T(8,128)S(1)} collective-permute-done((f32[64,128]{1,0:T(8,128)S(1)}, f32[64,128]{1,0:T(8,128)S(1)}, u32[]{:S(2)}, u32[]{:S(2)}) %collective-permute-start.5) | collective-permute-done | bytes 32800 | tf_op jit(solution)/shard_map/ppermute | solution.py:175
  41.9 1.5 %collective-permute-done.6.refs_6_ = f32[64,128]{1,0:T(8,128)S(1)} collective-permute-done((f32[64,128]{1,0:T(8,128)S(1)}, f32[64,128]{1,0:T(8,128)S(1)}, u32[]{:S(2)}, u32[]{:S(2)}) %collective-permute-start.6) | collective-permute-done | bytes 32800 | tf_op jit(solution)/shard_map/ppermute | solution.py:175
  43.5 0.0 collective-permute-done.refs_1_
  43.5 0.0 collective-permute-done.1.refs_2_
  43.5 0.0 copy-start.2
  43.5 0.0 collective-permute-done.4.refs_3_
  43.5 0.6 copy-done.5
  44.1 0.2 copy-done.1
  44.3 0.2 copy-done.2
  44.4 0.8 %copy-done = f32[1120,128]{1,0:T(8,128)} copy-done((f32[1120,128]{1,0:T(8,128)}, f32[1120,128]{1,0:T(8,128)S(1)}, u32[]{:S(2)}) %copy-start) | copy-done | bytes 573464
  45.3 19.2 %shade.1 = f32[4,4,64,128]{3,2,1,0:T(8,128)} custom-call(s32[4]{0:T(128)} %index_ref.1, s32[1]{0:T(128)S(6)} %copy.9.flip_ref, f32[16,3]{1,0:T(8,128)} %copy.6.lights_ref, f32[16,4,8]{2,1,0:T(4,128)} %copy.7.curves_ref, f32[1064,128]{1,0:T(8,128)} %get-tuple-element.9._.refs_0_, f32[1064,128]{1,0:T(8,128)} %copy-done.1, f32[1064,128]{1,0:T(8,128)} %copy-done.2, ...), custom_call_target="tpu_custom_call" | custom-call | tf_op jit(solution)/shard_map/shade/pallas_call | solution.py:210
  (11 shorter events, 0.0 us)
Async XLA Ops:
  0.0 20.9 %copy-start.6 = (f32[16,4,8]{0,2,1:T(8,128)S(1)}, f32[16,4,8]{0,2,1:T(8,128)}, u32[]{:S(2)}) copy-start(f32[16,4,8]{0,2,1:T(8,128)} %param.7) | copy-start | bytes 6148
  0.0 21.6 %copy-start.7 = (f32[16,3]{0,1:T(4,128)S(1)}, f32[16,3]{0,1:T(4,128)}, u32[]{:S(2)}) copy-start(f32[16,3]{0,1:T(4,128)} %param.6) | copy-start | bytes 580
  3.0 11.3 %copy-start.8 = (f32[1120,128]{1,0:T(8,128)S(1)}, f32[1120,128]{1,0:T(8,128)}, u32[]{:S(2)}) copy-start(f32[1120,128]{1,0:T(8,128)} %get-tuple-element.12) | copy-start | bytes 1720324
  3.0 13.8 %copy-start.10 = (f32[1064,128]{1,0:T(8,128)S(1)}, f32[1064,128]{1,0:T(8,128)}, u32[]{:S(2)}) copy-start(f32[1064,128]{1,0:T(8,128)} %get-tuple-element.10) | copy-start | bytes 1634308
  3.0 14.4 %copy-start.9 = (f32[1064,128]{1,0:T(8,128)S(1)}, f32[1064,128]{1,0:T(8,128)}, u32[]{:S(2)}) copy-start(f32[1064,128]{1,0:T(8,128)} %get-tuple-element.11) | copy-start | bytes 1634308
  6.5 3.7 %collective-permute-start.2 = (f32[64,128]{1,0:T(8,128)}, f32[64,128]{1,0:T(8,128)S(1)}, u32[]{:S(2)}, u32[]{:S(2)}) collective-permute-start(f32[64,128]{1,0:T(8,128)} %edges.1), channel_id=1, source_target_pairs={{0,1},{1,2},{2,3},{3,4},{4,5},{5,6},{6,7},{8,9},{9,10},{10,11},{11... | collective-permute-start | bytes 98312 | tf_op jit(solution)/shard_map/ppermute | solution.py:171
  8.8 5.5 %collective-permute-start.3 = (f32[64,128]{1,0:T(8,128)}, f32[64,128]{1,0:T(8,128)S(1)}, u32[]{:S(2)}, u32[]{:S(2)}) collective-permute-start(f32[64,128]{1,0:T(8,128)} %edges.1), channel_id=1, source_target_pairs={{1,0},{2,1},{3,2},{4,3},{5,4},{6,5},{7,6},{9,8},{10,9},{11,10},{12... | collective-permute-start | bytes 98312 | tf_op jit(solution)/shard_map/ppermute | solution.py:171
  14.3 29.1 %copy-start.3 = (f32[64,128]{1,0:T(8,128)}, f32[64,128]{1,0:T(8,128)S(1)}, u32[]{:S(2)}) copy-start(f32[64,128]{1,0:T(8,128)S(1)} %get-tuple-element.14.refs_4_) | copy-start | bytes 98308
  14.4 29.1 %collective-permute-start.4 = (f32[1120,128]{1,0:T(8,128)S(1)}, f32[1120,128]{1,0:T(8,128)S(1)}, u32[]{:S(2)}, u32[]{:S(2)}) collective-permute-start(f32[1120,128]{1,0:T(8,128)S(1)} %get-tuple-element.13), channel_id=1, source_target_pairs={{0,24},{8,16},{16,8},{24,0},{1,25},{9,17},{17,9},{25,1},{2,26},{10... | collective-permute-start | bytes 1720328 | tf_op jit(solution)/shard_map/ppermute | solution.py:175
  16.9 26.6 %collective-permute-start = (f32[1064,128]{1,0:T(8,128)S(1)}, f32[1064,128]{1,0:T(8,128)S(1)}, u32[]{:S(2)}, u32[]{:S(2)}) collective-permute-start(f32[1064,128]{1,0:T(8,128)S(1)} %copy-done.10), channel_id=1, source_target_pairs={{0,8},{8,0},{16,24},{24,16},{1,9},{9,1},{17,25},{25,17},{2,10},{10... | collective-permute-start | bytes 1634312 | tf_op jit(solution)/shard_map/ppermute | solution.py:175
  17.4 26.1 %collective-permute-start.1 = (f32[1064,128]{1,0:T(8,128)S(1)}, f32[1064,128]{1,0:T(8,128)S(1)}, u32[]{:S(2)}, u32[]{:S(2)}) collective-permute-start(f32[1064,128]{1,0:T(8,128)S(1)} %copy-done.9), channel_id=1, source_target_pairs={{0,16},{8,24},{16,0},{24,8},{1,17},{9,25},{17,1},{25,9},{2,18},{10... | collective-permute-start | bytes 1634312 | tf_op jit(solution)/shard_map/ppermute | solution.py:175
  17.9 24.0 %collective-permute-start.5 = (f32[64,128]{1,0:T(8,128)S(1)}, f32[64,128]{1,0:T(8,128)S(1)}, u32[]{:S(2)}, u32[]{:S(2)}) collective-permute-start(f32[64,128]{1,0:T(8,128)S(1)} %get-tuple-element.14.refs_4_), channel_id=1, source_target_pairs={{0,8},{8,0},{16,24},{24,16},{1,9},{9,1},{17,25},{25,17},{2,10},{10... | collective-permute-start | bytes 98312 | tf_op jit(solution)/shard_map/ppermute | solution.py:175
  19.4 24.0 %collective-permute-start.6 = (f32[64,128]{1,0:T(8,128)S(1)}, f32[64,128]{1,0:T(8,128)S(1)}, u32[]{:S(2)}, u32[]{:S(2)}) collective-permute-start(f32[64,128]{1,0:T(8,128)S(1)} %get-tuple-element.14.refs_4_), channel_id=1, source_target_pairs={{0,16},{8,24},{16,0},{24,8},{1,17},{9,25},{17,1},{25,9},{2,18},{10... | collective-permute-start | bytes 98312 | tf_op jit(solution)/shard_map/ppermute | solution.py:175
  41.9 1.6 %copy-start.4 = (f32[64,128]{1,0:T(8,128)}, f32[64,128]{1,0:T(8,128)S(1)}, u32[]{:S(2)}) copy-start(f32[64,128]{1,0:T(8,128)S(1)} %collective-permute-done.5.refs_5_) | copy-start | bytes 98308
  43.5 0.6 copy-start.5
  43.5 0.8 %copy-start.1 = (f32[1064,128]{1,0:T(8,128)}, f32[1064,128]{1,0:T(8,128)S(1)}, u32[]{:S(2)}) copy-start(f32[1064,128]{1,0:T(8,128)S(1)} %collective-permute-done.refs_1_) | copy-start | bytes 1634308
  43.5 1.0 %copy-start.2 = (f32[1064,128]{1,0:T(8,128)}, f32[1064,128]{1,0:T(8,128)S(1)}, u32[]{:S(2)}) copy-start(f32[1064,128]{1,0:T(8,128)S(1)} %collective-permute-done.1.refs_2_) | copy-start | bytes 1634308
  44.4 0.8 %copy-start = (f32[1120,128]{1,0:T(8,128)}, f32[1120,128]{1,0:T(8,128)S(1)}, u32[]{:S(2)}) copy-start(f32[1120,128]{1,0:T(8,128)S(1)} %collective-permute-done.4.refs_3_) | copy-start | bytes 1720324

commit v3 on v2

v3 whole, which is shorter than its diff:
```python
import functools

import jax
import jax.numpy as jnp
from jax import lax
from jax.experimental import pallas as pl
from jax.experimental.pallas import tpu as pltpu
from jax.sharding import PartitionSpec as P

AMBIENT = 0.3
OPACITY = 2.0
SUB = 8
VMEM = pltpu.VMEM
SMEM = pltpu.SMEM
MIB = 1 << 20


def edge_kernel(parts, field_ref, _, out_ref):
    cells, _, cols = field_ref.shape
    rows = out_ref.shape[0]
    lane_pair = lax.broadcasted_iota(jnp.int32, (SUB, cols), 1) // 2

    def tile(i, carry):
        acc = jnp.zeros((SUB, cols), jnp.float32)
        for part in range(parts):
            for z in range(cells):
                slot = part * cells + z
                start = pl.multiple_of(part * rows + i * SUB, SUB)
                value = field_ref[z, pl.ds(start, SUB), :]
                moved = pltpu.roll(value, (2 * slot + 1) % cols, 1)
                acc = jnp.where(lane_pair == slot, moved, acc)
        out_ref[pl.ds(pl.multiple_of(i * SUB, SUB), SUB), :] = acc
        return carry

    lax.fori_loop(0, rows // SUB, tile, 0)


def pack_kernel(parts, field_ref, *outs):
    cells, all_rows, cols = field_ref.shape
    rows = all_rows // parts
    me = lax.axis_index("depth")
    for m in range(parts):
        part = me ^ m
        low = pl.multiple_of(part * rows, SUB)
        above = jnp.where(part > 0, 1.0, 0.0)
        below = jnp.where(part < parts - 1, 1.0, 0.0)
        head = outs[m]
        for z in range(cells):
            head[z : z + 1, :] = field_ref[z, pl.ds(jnp.maximum(low - 1, 0), 1), :] * above
            head[cells + z : cells + z + 1, :] = field_ref[z, pl.ds(jnp.minimum(low + rows, all_rows - 1), 1), :] * below
        for z in range(cells):
            values = field_ref[z, pl.ds(low, rows), :]
            if m < parts - 1:
                head[2 * cells + z * rows : 2 * cells + (z + 1) * rows, :] = values
            elif z == 0:
                head[2 * cells : 2 * cells + rows, :] = values
            elif z == cells - 1:
                head[2 * cells + rows : 2 * cells + 2 * rows, :] = values
            else:
                outs[parts][z * rows : (z + 1) * rows, :] = values


def brick_views(parts, cells, rows, refs):
    views = []
    for m in range(parts - 1):
        head, lateral = refs[2 * m], refs[2 * m + 1]
        views.append((head, [(head, 2 * cells + z * rows) for z in range(cells)], lateral))
    return views


def far_view(cells, rows, head, body):
    places = [(head, 2 * cells)] + [(body, z * rows) for z in range(1, cells - 1)] + [(head, 2 * cells + rows)]
    return head, places, body


def fill_ends(parts, cells, rows, heads, ends_ref):
    me = lax.axis_index("depth")
    ends_ref[0, 1] = jnp.zeros_like(ends_ref[0, 1])
    ends_ref[parts + 1, 0] = jnp.zeros_like(ends_ref[0, 0])
    for m in range(parts):
        last = (cells - 1) * rows if m < parts - 1 else rows
        ends_ref[(me ^ m) + 1, 0] = heads[m][2 * cells : 2 * cells + rows, :]
        ends_ref[(me ^ m) + 1, 1] = heads[m][2 * cells + last : 2 * cells + last + rows, :]


def tables(light_refs, passes, parts, cells):
    index_ref, lights_ref, curves_ref = light_refs
    knots = curves_ref.shape[2]

    def bends(index, channel):
        points = [curves_ref[index, channel, k] for k in range(knots)]
        slopes = [points[k + 1] - points[k] for k in range(knots - 1)]
        return [points[0], slopes[0]] + [slopes[k] - slopes[k - 1] for k in range(1, knots - 1)]

    chosen = [index_ref[p] for p in range(passes)]
    vectors = [[lights_ref[index, axis] for axis in range(3)] for index in chosen]
    scale = OPACITY / (parts * cells)
    curves = [[value * scale for value in bends(index, 3)] for index in chosen]
    tints = [[bends(index, channel) for channel in range(3)] for index in chosen]
    return vectors, curves, tints


def prepare_steps(m, view, base, cells, rows, knots, cols, ends_ref, cell_ref):
    head, places, lateral = view
    me = lax.axis_index("depth")
    part = me ^ m
    at = pl.ds(base, SUB)
    lane = lax.broadcasted_iota(jnp.int32, (SUB, cols), 1)
    sublane = lax.broadcasted_iota(jnp.int32, (SUB, cols), 0)
    is_first = lane == 0
    is_last = lane == cols - 1
    is_top = jnp.logical_and(sublane == 0, base == 0)
    is_bottom = jnp.logical_and(sublane == SUB - 1, base == rows - SUB)
    sides = pltpu.roll(lateral[at, :], (cols - 1 - 2 * cells * me) % cols, 1)

    def layer(z):
        if z < 0:
            return ends_ref[part, 1, at, :]
        if z == cells:
            return ends_ref[part + 2, 0, at, :]
        ref, low = places[z]
        return ref[pl.ds(low + base, SUB), :]

    def step(z):
        ref, low = places[z]
        here = layer(z)
        upper = jnp.where(is_top, head[z : z + 1, :], ref[pl.ds(low + base - 1, SUB), :])
        lower = jnp.where(is_bottom, head[cells + z : cells + z + 1, :], ref[pl.ds(low + base + 1, SUB), :])
        edge = pltpu.roll(sides, (cols - 2 * z) % cols, 1) if z else sides
        grad_x = pltpu.roll(jnp.where(is_first, edge, here), cols - 1, 1) - pltpu.roll(
            jnp.where(is_last, edge, here), 1, 1
        )
        grad_y = lower - upper
        grad_z = layer(z + 1) - layer(z - 1)
        inverse = lax.rsqrt(grad_x * grad_x + grad_y * grad_y + grad_z * grad_z + 4.0)
        half = 0.5 * (knots - 1)
        position = half + half * jnp.tanh(0.5 * here)
        cell_ref[0, z] = grad_x * inverse
        cell_ref[1, z] = grad_y * inverse
        cell_ref[2, z] = grad_z * inverse
        cell_ref[3, z] = position
        for k in range(1, knots - 1):
            cell_ref[3 + k, z] = jnp.maximum(position - k, 0.0)

    return [functools.partial(step, z) for z in range(cells)]


def tree(terms):
    while len(terms) > 1:
        terms = [sum(terms[j + 1 : j + 2], terms[j]) for j in range(0, len(terms), 2)]
    return terms[0]


def march_unit(flip, vectors, curves, cells, knots, cols, cell_ref, beside):
    passes = len(vectors)
    shape = (SUB, cols)
    zero = jnp.zeros(shape, jnp.float32)
    result = []
    beside = list(beside)
    for low in range(0, passes, 2):
        group = range(low, min(low + 2, passes))
        vector = {p: [jnp.full(shape, v) for v in vectors[p]] for p in group}
        curve = {p: [jnp.full(shape, v) for v in curves[p]] for p in group}
        state = {p: (jnp.ones(shape, jnp.float32), [zero] * knots) for p in group}
        share = -(-len(beside) * 2 // max(passes - low, 1))
        mine, beside = beside[:share], beside[share:]
        for u in range(cells):
            for step in mine[u * share // cells : (u + 1) * share // cells]:
                step()
            z = u + flip * (cells - 1 - 2 * u)
            hinges = [cell_ref[3 + k, z] for k in range(knots - 1)]
            normal = [cell_ref[axis, z] for axis in range(3)]
            for p in group:
                keep, sums = state[p]
                opacity = tree([curve[p][0]] + [curve[p][k + 1] * hinges[k] for k in range(knots - 1)])
                facing = normal[0] * vector[p][0] + normal[1] * vector[p][1] + normal[2] * vector[p][2]
                taken = keep * opacity
                weight = taken * (AMBIENT + jnp.abs(facing))
                sums = [sums[0] + weight] + [sums[k + 1] + weight * hinges[k] for k in range(knots - 1)]
                state[p] = (keep - taken, sums)
        result += [[state[p][0]] + state[p][1] for p in group]
    return result


def near_kernel(parts, cells, index_ref, flip_ref, lights_ref, curves_ref, *refs):
    inputs, far_head, out_ref, ends_ref, cell_refs = refs[: 2 * parts - 2], refs[2 * parts - 2], refs[2 * parts - 1], refs[2 * parts], refs[2 * parts + 1 :]
    rows, cols = out_ref.shape[2:]
    knots = curves_ref.shape[2]
    passes = index_ref.shape[0]
    flip = flip_ref[0]
    vectors, curves, _ = tables((index_ref, lights_ref, curves_ref), passes, parts, cells)
    views = brick_views(parts, cells, rows, inputs)
    fill_ends(parts, cells, rows, [view[0] for view in views] + [far_head], ends_ref)
    count = parts - 1
    tiles = rows // SUB

    def prepare(m, base):
        return prepare_steps(m, views[m], base, cells, rows, knots, cols, ends_ref, cell_refs[m])

    for step in prepare(0, 0):
        step()

    def tile(i, carry):
        base = pl.multiple_of(i * SUB, SUB)
        after = pl.multiple_of(jnp.minimum(i + 1, tiles - 1) * SUB, SUB)
        for m in range(count):
            beside = prepare(m + 1, base) if m + 1 < count else prepare(0, after)
            result = march_unit(flip, vectors, curves, cells, knots, cols, cell_refs[m], beside)
            for p in range(passes):
                for j in range(knots + 1):
                    out_ref[m, p * (knots + 1) + j, pl.ds(base, SUB), :] = result[p][j]
        return carry

    lax.fori_loop(0, tiles, tile, 0)


def over_either(first_leads, one, other):
    shape = one[0].shape
    unit = jnp.ones(shape, jnp.float32)
    scale_one = jnp.where(first_leads, unit, other[0])
    scale_other = jnp.where(first_leads, one[0], unit)
    return [one[0] * other[0]] + [scale_one * a + scale_other * b for a, b in zip(one[1:], other[1:])]


def far_kernel(parts, cells, index_ref, flip_ref, lights_ref, curves_ref, *refs):
    heads, body, states, out_ref, ends_ref, cell_refs = refs[:parts], refs[parts], refs[parts + 1], refs[parts + 2], refs[parts + 3], refs[parts + 4 :]
    rows, cols = out_ref.shape[2:]
    knots = curves_ref.shape[2]
    passes = index_ref.shape[0]
    flip = flip_ref[0]
    me = lax.axis_index("depth")
    vectors, curves, tints = tables((index_ref, lights_ref, curves_ref), passes, parts, cells)
    view = far_view(cells, rows, heads[-1], body)
    fill_ends(parts, cells, rows, heads, ends_ref)
    tiles = rows // SUB

    def prepare(base, slot):
        return prepare_steps(parts - 1, view, base, cells, rows, knots, cols, ends_ref, cell_refs[slot])

    def finish(result, base):
        at = pl.ds(base, SUB)
        for p in range(passes):
            images = [[states[m, p * (knots + 1) + j, at, :] for j in range(knots + 1)] for m in range(parts - 1)]
            images.append(result[p])
            bit = 0
            while len(images) > 1:
                leads = ((me >> bit) & 1) == flip
                images = [over_either(leads, images[j], images[j + 1]) for j in range(0, len(images), 2)]
                bit += 1
            keep, sums = images[0][0], images[0][1:]
            for channel in range(3):
                out_ref[p, channel, at, :] = tree([tints[p][channel][k] * sums[k] for k in range(knots)])
            out_ref[p, 3, at, :] = 1.0 - keep

    for step in prepare(0, 0):
        step()

    def pair(i, carry):
        for slot in range(2):
            base = pl.multiple_of((2 * i + slot) * SUB, SUB)
            after = pl.multiple_of(jnp.minimum(2 * i + slot + 1, tiles - 1) * SUB, SUB)
            result = march_unit(flip, vectors, curves, cells, knots, cols, cell_refs[slot], prepare(after, 1 - slot))
            finish(result, base)
        return carry

    lax.fori_loop(0, tiles // 2, pair, 0)


def shift_along(block, axis, amount):
    count = lax.axis_size(axis)
    route = [(i, i + amount) for i in range(count) if 0 <= i + amount < count]
    return lax.ppermute(block, axis, route)


def swap_along(block, axis, mask):
    return lax.ppermute(block, axis, [(i, i ^ mask) for i in range(lax.axis_size(axis))])


def estimate(micros):
    return pl.CostEstimate(flops=0, transcendentals=0, bytes_accessed=int(micros * 3_690_000))


def on_device(field, light_vectors, transfer, light_index, flips):
    parts = lax.axis_size("depth")
    cells, all_rows, cols = field.shape
    rows = all_rows // parts
    passes = light_index.shape[0]
    channels, knots = transfer.shape[1:]
    in_vmem = pl.BlockSpec(memory_space=VMEM)
    in_smem = pl.BlockSpec(memory_space=SMEM)

    near_rows = 2 * cells + cells * rows + SUB
    head_rows = 2 * cells + 2 * rows + SUB
    body_rows = (cells - 1) * rows + SUB
    shapes = [(near_rows, cols)] * (parts - 1) + [(head_rows, cols), (body_rows, cols)]
    *near, far_head, far_body = pl.pallas_call(
        functools.partial(pack_kernel, parts),
        out_shape=[jax.ShapeDtypeStruct(shape, jnp.float32) for shape in shapes],
        in_specs=[in_vmem],
        out_specs=[in_vmem] * (parts + 1),
        compiler_params=pltpu.CompilerParams(vmem_limit_bytes=12 * MIB),
        cost_estimate=estimate(1),
        name="pack",
    )(field)
    far_head = swap_along(far_head, "depth", parts - 1)
    own = near[0]
    near = [own] + [swap_along(near[m], "depth", m) for m in range(1, parts - 1)]

    edges = pl.pallas_call(
        functools.partial(edge_kernel, parts),
        out_shape=jax.ShapeDtypeStruct((rows, cols), jnp.float32),
        in_specs=[in_vmem, pl.BlockSpec(memory_space=pl.ANY)],
        out_specs=in_vmem,
        compiler_params=pltpu.CompilerParams(vmem_limit_bytes=8 * MIB),
        cost_estimate=estimate(1),
        name="edges",
    )(field, own)
    left = shift_along(edges, "tile", 1)
    right = shift_along(edges, "tile", -1)
    sides = jnp.where(jnp.arange(cols) % 2 == 0, left, right)
    laterals = [sides] + [swap_along(sides, "depth", m) for m in range(1, parts - 1)]
    far_body = swap_along(lax.dynamic_update_slice(far_body, sides, (0, 0)), "depth", parts - 1)

    lights = (light_index, flips, light_vectors, transfer)
    cell_shape = VMEM((knots + 2, cells, SUB, cols), jnp.float32)
    ends_shape = VMEM((parts + 2, 2, rows, cols), jnp.float32)
    states = pl.pallas_call(
        functools.partial(near_kernel, parts, cells),
        out_shape=jax.ShapeDtypeStruct((parts - 1, passes * (knots + 1), rows, cols), jnp.float32),
        in_specs=[in_smem] * 4 + [in_vmem] * (2 * parts - 1),
        out_specs=in_vmem,
        scratch_shapes=[ends_shape] + [cell_shape] * (parts - 1),
        compiler_params=pltpu.CompilerParams(vmem_limit_bytes=16 * MIB),
        cost_estimate=estimate(60),
        name="near",
    )(*lights, *[ref for both in zip(near, laterals) for ref in both], far_head)
    return pl.pallas_call(
        functools.partial(far_kernel, parts, cells),
        out_shape=jax.ShapeDtypeStruct((passes, channels, rows, cols), jnp.float32),
        in_specs=[in_smem] * 4 + [in_vmem] * (parts + 2),
        out_specs=in_vmem,
        scratch_shapes=[ends_shape] + [cell_shape] * 2,
        compiler_params=pltpu.CompilerParams(vmem_limit_bytes=16 * MIB),
        cost_estimate=estimate(5),
        name="far",
    )(*lights, *near, far_head, far_body, states)


def solution(mesh):
    in_specs = (P("depth", None, "tile"), P(), P(), P(), P("tile"))
    out_specs = P(None, None, "depth", "tile")
    return jax.shard_map(
        on_device, mesh=mesh, in_specs=in_specs, out_specs=out_specs, check_vma=False
    )
```

time: 64.7 us -> 64 us (0.989)
  Pallas kernels: 25.6 us -> 22.1 us
  starting transfers between devices: 10.2 us -> 12.3 us
  local copies, waits for them, and re-layouts: 3.14 us -> 1.76 us
  waiting for transfers between devices: 24.7 us -> 25.8 us
    ppermute x5 -> x6, waiting for transfers between devices: 20.5 us -> 25.8 us  [swap_along(): lax.ppermute(block, axis, [(i, i ^ mask) for i in range(lax.axis_size(axi...]
    ppermute x2, waiting for transfers between devices: 4.18 us -> 0.01 us  [shift_along(): return lax.ppermute(block, axis, route)]
    pallas_call x1, Pallas kernels: 3.42 us -> 1.09 us  [on_device(): pl.pallas_call(functools.partial(edge_kernel, parts), out_shape=jax.Shape...]
    pallas_call x1, Pallas kernels: 3.02 us -> 0.96 us  [on_device(): pl.pallas_call(functools.partial(pack_kernel, parts), out_shape=[jax.Shap...]
    ppermute x5 -> x6, starting transfers between devices: 6.56 us -> 7.97 us  [swap_along(): lax.ppermute(block, axis, [(i, i ^ mask) for i in range(lax.axis_size(axi...]
    unnamed x24 -> x10, local copies, waits for them, and re-layouts: 3.14 us -> 1.76 us
    pallas_call x1 -> x2, Pallas kernels: 19.2 us -> 20.1 us  [the longest x1 12.9 us: on_device(): pl.pallas_call(functools.partial(near_kernel, parts, cells), out_shape=ja...]
    ppermute x2, starting transfers between devices: 3.64 us -> 4.32 us  [shift_along(): return lax.ppermute(block, axis, route)]
  transfers between devices with their start and end apart: 7 -> 8, of which waited for: 3 -> 2; matrix products, arithmetic and copies ran while one was open for 2% -> 1% of each run, Pallas kernels for 0% -> 20%
where the time goes in v3:
time: 64 us; the launch traced here: 63.4 us
  waiting for transfers between devices  25.8 us (40%)
  Pallas kernels  22.1 us (35%)
  starting transfers between devices  12.3 us (19%)
  local copies, waits for them, and re-layouts  1.76 us (3%)
  between operations  0.72 us (1%)
    ppermute x6, waiting for transfers between devices, swap_along(): lax.ppermute(block, axis, [(i, i ^ mask) for i in range(lax.axis_size(axi...  25.8 us
    pallas_call x1, Pallas kernels, on_device(): pl.pallas_call(functools.partial(near_kernel, parts, cells), out_shape=ja...  12.9 us
    ppermute x6, starting transfers between devices, swap_along(): lax.ppermute(block, axis, [(i, i ^ mask) for i in range(lax.axis_size(axi...  7.97 us
    pallas_call x1, Pallas kernels, on_device(): pl.pallas_call(functools.partial(far_kernel, parts, cells), out_shape=jax...  7.16 us
    ppermute x2, starting transfers between devices, shift_along(): return lax.ppermute(block, axis, route)  4.32 us
    unnamed x10, local copies, waits for them, and re-layouts  1.76 us
  transfers between devices with their start and end apart: 8, of which 2 were waited for; matrix products, arithmetic and copies ran while one was open for 1% of the time, Pallas kernels for 20%

profile of v3, /device:TPU:0, one launch (start us, length us, event | category | flops | bytes accessed | tf_op | source)
XLA Modules:
  0.0 63.4 jit_solution(3528352604240091556)
XLA Ops:
  0.0 0.0 copy-start
  0.0 1.6 %copy-done = f32[16,256,128]{2,1,0:T(8,128)S(1)} copy-done((f32[16,256,128]{2,1,0:T(8,128)S(1)}, f32[16,256,128]{2,1,0:T(8,128)}, u32[]{:S(2)}) %copy-start) | copy-done | bytes 2097176
  1.6 0.0 copy-start.3
  1.6 0.0 copy-start.2
  1.6 0.0 copy-start.1
  1.6 1.0 %pack.1 = (f32[1064,128]{1,0:T(8,128)S(1)}, f32[1064,128]{1,0:T(8,128)S(1)}, f32[1064,128]{1,0:T(8,128)S(1)}, f32[168,128]{1,0:T(8,128)S(1)}, f32[968,128]{1,0:T(8,128)}) custom-call(f32[16,256,128]{2,1,0:T(8,128)S(1)} %copy-done), custom_call_target="tpu_custom_call" | custom-call | bytes 3690000 | tf_op jit(solution)/shard_map/pack/pallas_call | solution.py:296
  2.6 1.1 %edges.1 = f32[64,128]{1,0:T(8,128)S(1)} custom-call(f32[16,256,128]{2,1,0:T(8,128)S(1)} %copy-done, f32[1064,128]{1,0:T(8,128)S(1)} %get-tuple-element.10._.refs_0_), custom_call_target="tpu_custom_call" | custom-call | bytes 3690000 | tf_op jit(solution)/shard_map/edges/pallas_call | solution.py:309
  3.7 1.3 %collective-permute-start.4 = (f32[64,128]{1,0:T(8,128)S(1)}, f32[64,128]{1,0:T(8,128)S(1)}, u32[]{:S(2)}, u32[]{:S(2)}) collective-permute-start(f32[64,128]{1,0:T(8,128)S(1)} %edges.1), channel_id=1, source_target_pairs={{1,0},{2,1},{3,2},{4,3},{5,4},{6,5},{7,6},{9,8},{10,9},{11,10},{12... | collective-permute-start | bytes 98312 | tf_op jit(solution)/shard_map/ppermute | solution.py:272
  5.0 3.0 %collective-permute-start.3 = (f32[64,128]{1,0:T(8,128)S(1)}, f32[64,128]{1,0:T(8,128)S(1)}, u32[]{:S(2)}, u32[]{:S(2)}) collective-permute-start(f32[64,128]{1,0:T(8,128)S(1)} %edges.1), channel_id=1, source_target_pairs={{0,1},{1,2},{2,3},{3,4},{4,5},{5,6},{6,7},{8,9},{9,10},{10,11},{11... | collective-permute-start | bytes 98312 | tf_op jit(solution)/shard_map/ppermute | solution.py:272
  8.0 3.0 %collective-permute-start = (f32[1064,128]{1,0:T(8,128)S(1)}, f32[1064,128]{1,0:T(8,128)S(1)}, u32[]{:S(2)}, u32[]{:S(2)}) collective-permute-start(f32[1064,128]{1,0:T(8,128)S(1)} %get-tuple-element.11), channel_id=1, source_target_pairs={{0,8},{8,0},{16,24},{24,16},{1,9},{9,1},{17,25},{25,17},{2,10},{10... | collective-permute-start | bytes 1634312 | tf_op jit(solution)/shard_map/ppermute | solution.py:276
  11.0 1.5 %collective-permute-start.1 = (f32[1064,128]{1,0:T(8,128)S(1)}, f32[1064,128]{1,0:T(8,128)S(1)}, u32[]{:S(2)}, u32[]{:S(2)}) collective-permute-start(f32[1064,128]{1,0:T(8,128)S(1)} %get-tuple-element.12), channel_id=1, source_target_pairs={{0,16},{8,24},{16,0},{24,8},{1,17},{9,25},{17,1},{25,9},{2,18},{10... | collective-permute-start | bytes 1634312 | tf_op jit(solution)/shard_map/ppermute | solution.py:276
  12.5 0.0 collective-permute-done.4
  12.5 0.0 collective-permute-done.3
  12.5 0.6 constant_dynamic-update-slice_fusion
  13.2 0.2 collective-permute-start.5
  13.4 2.7 %collective-permute-start.2 = (f32[168,128]{1,0:T(8,128)S(1)}, f32[168,128]{1,0:T(8,128)S(1)}, u32[]{:S(2)}, u32[]{:S(2)}) collective-permute-start(f32[168,128]{1,0:T(8,128)S(1)} %get-tuple-element.13), channel_id=1, source_target_pairs={{0,24},{8,16},{16,8},{24,0},{1,25},{9,17},{17,9},{25,1},{2,26},{10... | collective-permute-start | bytes 258056 | tf_op jit(solution)/shard_map/ppermute | solution.py:276
  16.1 0.5 collective-permute-start.7
  16.6 22.7 %collective-permute-done.7.refs_5_ = f32[64,128]{1,0:T(8,128)S(1)} collective-permute-done((f32[64,128]{1,0:T(8,128)S(1)}, f32[64,128]{1,0:T(8,128)S(1)}, u32[]{:S(2)}, u32[]{:S(2)}) %collective-permute-start.7) | collective-permute-done | bytes 32800 | tf_op jit(solution)/shard_map/ppermute | solution.py:276
  39.4 0.0 collective-permute-start.6
  40.0 0.0 copy-done.3
  40.0 0.1 copy.8.lights_ref
  40.1 0.0 copy-done.2
  40.1 0.1 copy.9.curves_ref
  40.2 3.1 %collective-permute-done.6.refs_3_ = f32[64,128]{1,0:T(8,128)S(1)} collective-permute-done((f32[64,128]{1,0:T(8,128)S(1)}, f32[64,128]{1,0:T(8,128)S(1)}, u32[]{:S(2)}, u32[]{:S(2)}) %collective-permute-start.6) | collective-permute-done | bytes 32800 | tf_op jit(solution)/shard_map/ppermute | solution.py:276
  43.3 0.0 collective-permute-done.2.refs_6_.refs_3_
  43.3 0.0 collective-permute-done.refs_2_.refs_1_
  43.3 0.0 collective-permute-done.1.refs_4_.refs_2_
  43.3 0.0 copy-done.1
  43.3 12.9 %near.1.refs_5_ = f32[3,36,64,128]{3,2,1,0:T(8,128)S(1)} custom-call(s32[4]{0:T(128)S(1)} %copy-done.1, s32[1]{0:T(128)S(6)} %copy.11.flip_ref, f32[16,3]{1,0:T(8,128)S(1)} %copy.8.lights_ref, f32[16,4,8]{2,1,0:T(4,128)S(1)} %copy.9.curves_ref, f32[1064,128]{1,0:T(8,128)S(1)} %get-tuple-element.10._.refs_0_, f32[64,128]{1,0:T(8,128)S(1)} %get-tuple-element.16.refs_1_, ...), custom_call_target="tpu_custom_call" | custom-call | bytes 221400000 | tf_op jit(solution)/shard_map/near/pallas_call | solution.py:327
  56.2 0.0 collective-permute-done.5.refs_4_
  56.2 7.2 %far.1 = f32[4,4,64,128]{3,2,1,0:T(8,128)} custom-call(s32[4]{0:T(128)S(1)} %copy-done.1, s32[1]{0:T(128)S(6)} %copy.11.flip_ref, f32[16,3]{1,0:T(8,128)S(1)} %copy.8.lights_ref, f32[16,4,8]{2,1,0:T(4,128)S(1)} %copy.9.curves_ref, f32[1064,128]{1,0:T(8,128)S(1)} %get-tuple-element.10._.refs_0_, f32[1064,128]{1,0:T(8,128)S(1)} %collective-permute-done.refs_2_.refs_1_, ...), custom_call_target="tpu_custom_call" | custom-call | bytes 18450000 | tf_op jit(solution)/shard_map/far/pallas_call | solution.py:337
  (1 shorter events, 0.0 us)
Async XLA Ops:
  0.0 1.6 %copy-start = (f32[16,256,128]{2,1,0:T(8,128)S(1)}, f32[16,256,128]{2,1,0:T(8,128)}, u32[]{:S(2)}) copy-start(f32[16,256,128]{2,1,0:T(8,128)} %field_ref.3) | copy-start | bytes 6291460
  1.6 38.4 %copy-start.3 = (f32[16,3]{0,1:T(4,128)S(1)}, f32[16,3]{0,1:T(4,128)}, u32[]{:S(2)}) copy-start(f32[16,3]{0,1:T(4,128)} %param.6) | copy-start | bytes 580
  1.6 38.5 %copy-start.2 = (f32[16,4,8]{0,2,1:T(8,128)S(1)}, f32[16,4,8]{0,2,1:T(8,128)}, u32[]{:S(2)}) copy-start(f32[16,4,8]{0,2,1:T(8,128)} %param.7) | copy-start | bytes 6148
  1.6 41.7 %copy-start.1 = (s32[4]{0:T(128)S(1)}, s32[4]{0:T(128)}, u32[]{:S(2)}) copy-start(s32[4]{0:T(128)} %index_ref.3) | copy-start | bytes 52
  3.7 8.9 %collective-permute-start.4 = (f32[64,128]{1,0:T(8,128)S(1)}, f32[64,128]{1,0:T(8,128)S(1)}, u32[]{:S(2)}, u32[]{:S(2)}) collective-permute-start(f32[64,128]{1,0:T(8,128)S(1)} %edges.1), channel_id=1, source_target_pairs={{1,0},{2,1},{3,2},{4,3},{5,4},{6,5},{7,6},{9,8},{10,9},{11,10},{12... | collective-permute-start | bytes 98312 | tf_op jit(solution)/shard_map/ppermute | solution.py:272
  5.0 7.6 %collective-permute-start.3 = (f32[64,128]{1,0:T(8,128)S(1)}, f32[64,128]{1,0:T(8,128)S(1)}, u32[]{:S(2)}, u32[]{:S(2)}) collective-permute-start(f32[64,128]{1,0:T(8,128)S(1)} %edges.1), channel_id=1, source_target_pairs={{0,1},{1,2},{2,3},{3,4},{4,5},{5,6},{6,7},{8,9},{9,10},{10,11},{11... | collective-permute-start | bytes 98312 | tf_op jit(solution)/shard_map/ppermute | solution.py:272
  8.0 35.3 %collective-permute-start = (f32[1064,128]{1,0:T(8,128)S(1)}, f32[1064,128]{1,0:T(8,128)S(1)}, u32[]{:S(2)}, u32[]{:S(2)}) collective-permute-start(f32[1064,128]{1,0:T(8,128)S(1)} %get-tuple-element.11), channel_id=1, source_target_pairs={{0,8},{8,0},{16,24},{24,16},{1,9},{9,1},{17,25},{25,17},{2,10},{10... | collective-permute-start | bytes 1634312 | tf_op jit(solution)/shard_map/ppermute | solution.py:276
  11.0 32.3 %collective-permute-start.1 = (f32[1064,128]{1,0:T(8,128)S(1)}, f32[1064,128]{1,0:T(8,128)S(1)}, u32[]{:S(2)}, u32[]{:S(2)}) collective-permute-start(f32[1064,128]{1,0:T(8,128)S(1)} %get-tuple-element.12), channel_id=1, source_target_pairs={{0,16},{8,24},{16,0},{24,8},{1,17},{9,25},{17,1},{25,9},{2,18},{10... | collective-permute-start | bytes 1634312 | tf_op jit(solution)/shard_map/ppermute | solution.py:276
  13.2 43.1 %collective-permute-start.5 = (f32[968,128]{1,0:T(8,128)}, f32[968,128]{1,0:T(8,128)S(1)}, u32[]{:S(2)}, u32[]{:S(2)}) collective-permute-start(f32[968,128]{1,0:T(8,128)} %get-tuple-element.15), channel_id=1, source_target_pairs={{0,24},{8,16},{16,8},{24,0},{1,25},{9,17},{17,9},{25,1},{2,26},{10... | collective-permute-start | bytes 1486856 | tf_op jit(solution)/shard_map/ppermute | solution.py:276
  13.4 29.9 %collective-permute-start.2 = (f32[168,128]{1,0:T(8,128)S(1)}, f32[168,128]{1,0:T(8,128)S(1)}, u32[]{:S(2)}, u32[]{:S(2)}) collective-permute-start(f32[168,128]{1,0:T(8,128)S(1)} %get-tuple-element.13), channel_id=1, source_target_pairs={{0,24},{8,16},{16,8},{24,0},{1,25},{9,17},{17,9},{25,1},{2,26},{10... | collective-permute-start | bytes 258056 | tf_op jit(solution)/shard_map/ppermute | solution.py:276
  16.1 23.2 %collective-permute-start.7 = (f32[64,128]{1,0:T(8,128)S(1)}, f32[64,128]{1,0:T(8,128)S(1)}, u32[]{:S(2)}, u32[]{:S(2)}) collective-permute-start(f32[64,128]{1,0:T(8,128)S(1)} %get-tuple-element.16.refs_1_), channel_id=1, source_target_pairs={{0,16},{8,24},{16,0},{24,8},{1,17},{9,25},{17,1},{25,9},{2,18},{10... | collective-permute-start | bytes 98312 | tf_op jit(solution)/shard_map/ppermute | solution.py:276
  39.4 3.9 %collective-permute-start.6 = (f32[64,128]{1,0:T(8,128)S(1)}, f32[64,128]{1,0:T(8,128)S(1)}, u32[]{:S(2)}, u32[]{:S(2)}) collective-permute-start(f32[64,128]{1,0:T(8,128)S(1)} %get-tuple-element.16.refs_1_), channel_id=1, source_target_pairs={{0,8},{8,0},{16,24},{24,16},{1,9},{9,1},{17,25},{25,17},{2,10},{10... | collective-permute-start | bytes 98312 | tf_op jit(solution)/shard_map/ppermute | solution.py:276

commit v4 on v3

--- a/solution.py
+++ b/solution.py
@@ -277,7 +277,7 @@
 
 
 def estimate(micros):
-    return pl.CostEstimate(flops=0, transcendentals=0, bytes_accessed=int(micros * 3_690_000))
+    return pl.CostEstimate(flops=int(micros * 1_000_000_000), transcendentals=0, bytes_accessed=0)
 
 
 def on_device(field, light_vectors, transfer, light_index, flips):
@@ -319,7 +319,8 @@
     right = shift_along(edges, "tile", -1)
     sides = jnp.where(jnp.arange(cols) % 2 == 0, left, right)
     laterals = [sides] + [swap_along(sides, "depth", m) for m in range(1, parts - 1)]
-    far_body = swap_along(lax.dynamic_update_slice(far_body, sides, (0, 0)), "depth", parts - 1)
+    *laterals, far_body = lax.optimization_barrier((*laterals, lax.dynamic_update_slice(far_body, sides, (0, 0))))
+    far_body = swap_along(far_body, "depth", parts - 1)
 
     lights = (light_index, flips, light_vectors, transfer)
     cell_shape = VMEM((knots + 2, cells, SUB, cols), jnp.float32)

time: 64 us -> 43.9 us (0.69)
  waiting for transfers between devices: 25.8 us -> 5.69 us
  starting transfers between devices: 12.3 us -> 13.2 us
    ppermute x6, waiting for transfers between devices: 25.8 us -> 4.95 us  [swap_along(): lax.ppermute(block, axis, [(i, i ^ mask) for i in range(lax.axis_size(axi...]
    ppermute x6, starting transfers between devices: 7.97 us -> 8.9 us  [swap_along(): lax.ppermute(block, axis, [(i, i ^ mask) for i in range(lax.axis_size(axi...]
    pallas_call x1, Pallas kernels: 0.96 us -> 0.18 us  [on_device(): pl.pallas_call(functools.partial(pack_kernel, parts), out_shape=[jax.Shap...]
    ppermute x2, waiting for transfers between devices: 0.01 us -> 0.74 us  [shift_along(): return lax.ppermute(block, axis, route)]
  transfers between devices with their start and end apart: 8 -> 8, of which waited for: 2 -> 2; matrix products, arithmetic and copies ran while one was open for 1% -> 0% of each run, Pallas kernels for 20% -> 34%
where the time goes in v4:
time: 43.9 us; the launch traced here: 43.7 us
  Pallas kernels  22.3 us (51%)
  starting transfers between devices  13.2 us (30%)
  waiting for transfers between devices  5.69 us (13%)
  local copies, waits for them, and re-layouts  1.76 us (4%)
  between operations  0.73 us (2%)
    pallas_call x1, Pallas kernels, on_device(): pl.pallas_call(functools.partial(near_kernel, parts, cells), out_shape=ja...  13.6 us
    ppermute x6, starting transfers between devices, swap_along(): lax.ppermute(block, axis, [(i, i ^ mask) for i in range(lax.axis_size(axi...  8.9 us
    pallas_call x1, Pallas kernels, on_device(): pl.pallas_call(functools.partial(far_kernel, parts, cells), out_shape=jax...  7.46 us
    ppermute x6, waiting for transfers between devices, swap_along(): lax.ppermute(block, axis, [(i, i ^ mask) for i in range(lax.axis_size(axi...  4.95 us
    ppermute x2, starting transfers between devices, shift_along(): return lax.ppermute(block, axis, route)  4.32 us
    unnamed x10, local copies, waits for them, and re-layouts  1.76 us
    pallas_call x1, Pallas kernels, on_device(): pl.pallas_call(functools.partial(edge_kernel, parts), out_shape=jax.Shape...  1.09 us
  transfers between devices with their start and end apart: 8, of which 2 were waited for; matrix products, arithmetic and copies ran while one was open for 0% of the time, Pallas kernels for 34%

profile of v4, /device:TPU:0, one launch (start us, length us, event | category | flops | bytes accessed | tf_op | source)
XLA Modules:
  0.0 43.7 jit_solution(891825384328694375)
XLA Ops:
  0.0 0.0 copy-start
  0.0 1.6 %copy-done = f32[16,256,128]{2,1,0:T(8,128)S(1)} copy-done((f32[16,256,128]{2,1,0:T(8,128)S(1)}, f32[16,256,128]{2,1,0:T(8,128)}, u32[]{:S(2)}) %copy-start) | copy-done | bytes 2097176
  1.6 0.0 copy-start.3
  1.6 0.0 copy-start.2
  1.6 0.0 copy-start.1
  1.6 0.2 pack.1
  1.8 3.0 %collective-permute-start = (f32[1064,128]{1,0:T(8,128)S(1)}, f32[1064,128]{1,0:T(8,128)S(1)}, u32[]{:S(2)}, u32[]{:S(2)}) collective-permute-start(f32[1064,128]{1,0:T(8,128)S(1)} %get-tuple-element.15), channel_id=1, source_target_pairs={{0,8},{8,0},{16,24},{24,16},{1,9},{9,1},{17,25},{25,17},{2,10},{10... | collective-permute-start | bytes 1634312 | tf_op jit(solution)/shard_map/ppermute | solution.py:276
  4.8 1.5 %collective-permute-start.1 = (f32[1064,128]{1,0:T(8,128)S(1)}, f32[1064,128]{1,0:T(8,128)S(1)}, u32[]{:S(2)}, u32[]{:S(2)}) collective-permute-start(f32[1064,128]{1,0:T(8,128)S(1)} %get-tuple-element.16), channel_id=1, source_target_pairs={{0,16},{8,24},{16,0},{24,8},{1,17},{9,25},{17,1},{25,9},{2,18},{10... | collective-permute-start | bytes 1634312 | tf_op jit(solution)/shard_map/ppermute | solution.py:276
  6.3 1.1 %edges.1 = f32[64,128]{1,0:T(8,128)S(1)} custom-call(f32[16,256,128]{2,1,0:T(8,128)S(1)} %copy-done, f32[1064,128]{1,0:T(8,128)S(1)} %get-tuple-element.14._.refs_0_), custom_call_target="tpu_custom_call" | custom-call | flops 1000000000 | tf_op jit(solution)/shard_map/edges/pallas_call | solution.py:309
  7.4 1.3 %collective-permute-start.4 = (f32[64,128]{1,0:T(8,128)S(1)}, f32[64,128]{1,0:T(8,128)S(1)}, u32[]{:S(2)}, u32[]{:S(2)}) collective-permute-start(f32[64,128]{1,0:T(8,128)S(1)} %edges.1), channel_id=1, source_target_pairs={{1,0},{2,1},{3,2},{4,3},{5,4},{6,5},{7,6},{9,8},{10,9},{11,10},{12... | collective-permute-start | bytes 98312 | tf_op jit(solution)/shard_map/ppermute | solution.py:272
  8.7 3.0 %collective-permute-start.3 = (f32[64,128]{1,0:T(8,128)S(1)}, f32[64,128]{1,0:T(8,128)S(1)}, u32[]{:S(2)}, u32[]{:S(2)}) collective-permute-start(f32[64,128]{1,0:T(8,128)S(1)} %edges.1), channel_id=1, source_target_pairs={{0,1},{1,2},{2,3},{3,4},{4,5},{5,6},{6,7},{8,9},{9,10},{10,11},{11... | collective-permute-start | bytes 98312 | tf_op jit(solution)/shard_map/ppermute | solution.py:272
  11.7 0.1 collective-permute-start.2
  11.8 0.0 collective-permute-done.4
  11.8 0.7 %collective-permute-done.3 = f32[64,128]{1,0:T(8,128)S(1)} collective-permute-done((f32[64,128]{1,0:T(8,128)S(1)}, f32[64,128]{1,0:T(8,128)S(1)}, u32[]{:S(2)}, u32[]{:S(2)}) %collective-permute-start.3) | collective-permute-done | bytes 32800 | tf_op jit(solution)/shard_map/ppermute | solution.py:272
  12.6 1.3 %collective-permute-start.6 = (f32[64,128]{1,0:T(8,128)S(1)}, f32[64,128]{1,0:T(8,128)S(1)}, u32[]{:S(2)}, u32[]{:S(2)}) collective-permute-start(f32[64,128]{1,0:T(8,128)S(1)} %get-tuple-element.20.refs_1_), channel_id=1, source_target_pairs={{0,16},{8,24},{16,0},{24,8},{1,17},{9,25},{17,1},{25,9},{2,18},{10... | collective-permute-start | bytes 98312 | tf_op jit(solution)/shard_map/ppermute | solution.py:276
  13.9 1.5 %collective-permute-start.5 = (f32[64,128]{1,0:T(8,128)S(1)}, f32[64,128]{1,0:T(8,128)S(1)}, u32[]{:S(2)}, u32[]{:S(2)}) collective-permute-start(f32[64,128]{1,0:T(8,128)S(1)} %get-tuple-element.20.refs_1_), channel_id=1, source_target_pairs={{0,8},{8,0},{16,24},{24,16},{1,9},{9,1},{17,25},{25,17},{2,10},{10... | collective-permute-start | bytes 98312 | tf_op jit(solution)/shard_map/ppermute | solution.py:276
  16.0 0.0 copy-done.3
  16.1 0.1 copy.8.lights_ref
  16.1 0.0 copy-done.2
  16.1 0.1 copy.9.curves_ref
  16.2 4.9 %collective-permute-done.6.refs_5_ = f32[64,128]{1,0:T(8,128)S(1)} collective-permute-done((f32[64,128]{1,0:T(8,128)S(1)}, f32[64,128]{1,0:T(8,128)S(1)}, u32[]{:S(2)}, u32[]{:S(2)}) %collective-permute-start.6) | collective-permute-done | bytes 32800 | tf_op jit(solution)/shard_map/ppermute | solution.py:276
  21.2 0.0 collective-permute-done.5.refs_3_
  21.2 1.5 %collective-permute-start.7 = (f32[968,128]{1,0:T(8,128)S(1)}, f32[968,128]{1,0:T(8,128)S(1)}, u32[]{:S(2)}, u32[]{:S(2)}) collective-permute-start(f32[968,128]{1,0:T(8,128)S(1)} %get-tuple-element.19), channel_id=1, source_target_pairs={{0,24},{8,16},{16,8},{24,0},{1,25},{9,17},{17,9},{25,1},{2,26},{10... | collective-permute-start | bytes 1486856 | tf_op jit(solution)/shard_map/ppermute | solution.py:276
  22.7 0.0 collective-permute-done.2.refs_6_.refs_3_
  22.7 0.0 collective-permute-done.refs_2_.refs_1_
  22.7 0.0 collective-permute-done.1.refs_4_.refs_2_
  22.7 0.0 copy-done.1
  22.7 13.6 %near.1.refs_5_ = f32[3,36,64,128]{3,2,1,0:T(8,128)S(1)} custom-call(s32[4]{0:T(128)S(1)} %copy-done.1, s32[1]{0:T(128)S(6)} %copy.11.flip_ref, f32[16,3]{1,0:T(8,128)S(1)} %copy.8.lights_ref, f32[16,4,8]{2,1,0:T(4,128)S(1)} %copy.9.curves_ref, f32[1064,128]{1,0:T(8,128)S(1)} %get-tuple-element.14._.refs_0_, f32[64,128]{1,0:T(8,128)S(1)} %get-tuple-element.20.refs_1_, ...), custom_call_target="tpu_custom_call" | custom-call | flops 60000002048 | tf_op jit(solution)/shard_map/near/pallas_call | solution.py:328
  36.3 0.0 collective-permute-done.7.refs_4_
  36.3 7.5 %far.1 = f32[4,4,64,128]{3,2,1,0:T(8,128)} custom-call(s32[4]{0:T(128)S(1)} %copy-done.1, s32[1]{0:T(128)S(6)} %copy.11.flip_ref, f32[16,3]{1,0:T(8,128)S(1)} %copy.8.lights_ref, f32[16,4,8]{2,1,0:T(4,128)S(1)} %copy.9.curves_ref, f32[1064,128]{1,0:T(8,128)S(1)} %get-tuple-element.14._.refs_0_, f32[1064,128]{1,0:T(8,128)S(1)} %collective-permute-done.refs_2_.refs_1_, ...), custom_call_target="tpu_custom_call" | custom-call | flops 5000000000 | tf_op jit(solution)/shard_map/far/pallas_call | solution.py:338
  (2 shorter events, 0.0 us)
Async XLA Ops:
  0.0 1.6 %copy-start = (f32[16,256,128]{2,1,0:T(8,128)S(1)}, f32[16,256,128]{2,1,0:T(8,128)}, u32[]{:S(2)}) copy-start(f32[16,256,128]{2,1,0:T(8,128)} %field_ref.3) | copy-start | bytes 6291460
  1.6 14.5 %copy-start.3 = (f32[16,3]{0,1:T(4,128)S(1)}, f32[16,3]{0,1:T(4,128)}, u32[]{:S(2)}) copy-start(f32[16,3]{0,1:T(4,128)} %param.6) | copy-start | bytes 580
  1.6 14.6 %copy-start.2 = (f32[16,4,8]{0,2,1:T(8,128)S(1)}, f32[16,4,8]{0,2,1:T(8,128)}, u32[]{:S(2)}) copy-start(f32[16,4,8]{0,2,1:T(8,128)} %param.7) | copy-start | bytes 6148
  1.6 21.1 %copy-start.1 = (s32[4]{0:T(128)S(1)}, s32[4]{0:T(128)}, u32[]{:S(2)}) copy-start(s32[4]{0:T(128)} %index_ref.3) | copy-start | bytes 52
  1.8 20.9 %collective-permute-start = (f32[1064,128]{1,0:T(8,128)S(1)}, f32[1064,128]{1,0:T(8,128)S(1)}, u32[]{:S(2)}, u32[]{:S(2)}) collective-permute-start(f32[1064,128]{1,0:T(8,128)S(1)} %get-tuple-element.15), channel_id=1, source_target_pairs={{0,8},{8,0},{16,24},{24,16},{1,9},{9,1},{17,25},{25,17},{2,10},{10... | collective-permute-start | bytes 1634312 | tf_op jit(solution)/shard_map/ppermute | solution.py:276
  4.8 17.9 %collective-permute-start.1 = (f32[1064,128]{1,0:T(8,128)S(1)}, f32[1064,128]{1,0:T(8,128)S(1)}, u32[]{:S(2)}, u32[]{:S(2)}) collective-permute-start(f32[1064,128]{1,0:T(8,128)S(1)} %get-tuple-element.16), channel_id=1, source_target_pairs={{0,16},{8,24},{16,0},{24,8},{1,17},{9,25},{17,1},{25,9},{2,18},{10... | collective-permute-start | bytes 1634312 | tf_op jit(solution)/shard_map/ppermute | solution.py:276
  7.4 4.4 %collective-permute-start.4 = (f32[64,128]{1,0:T(8,128)S(1)}, f32[64,128]{1,0:T(8,128)S(1)}, u32[]{:S(2)}, u32[]{:S(2)}) collective-permute-start(f32[64,128]{1,0:T(8,128)S(1)} %edges.1), channel_id=1, source_target_pairs={{1,0},{2,1},{3,2},{4,3},{5,4},{6,5},{7,6},{9,8},{10,9},{11,10},{12... | collective-permute-start | bytes 98312 | tf_op jit(solution)/shard_map/ppermute | solution.py:272
  8.7 3.9 %collective-permute-start.3 = (f32[64,128]{1,0:T(8,128)S(1)}, f32[64,128]{1,0:T(8,128)S(1)}, u32[]{:S(2)}, u32[]{:S(2)}) collective-permute-start(f32[64,128]{1,0:T(8,128)S(1)} %edges.1), channel_id=1, source_target_pairs={{0,1},{1,2},{2,3},{3,4},{4,5},{5,6},{6,7},{8,9},{9,10},{10,11},{11... | collective-permute-start | bytes 98312 | tf_op jit(solution)/shard_map/ppermute | solution.py:272
  11.7 10.9 %collective-permute-start.2 = (f32[168,128]{1,0:T(8,128)S(1)}, f32[168,128]{1,0:T(8,128)S(1)}, u32[]{:S(2)}, u32[]{:S(2)}) collective-permute-start(f32[168,128]{1,0:T(8,128)S(1)} %get-tuple-element.17), channel_id=1, source_target_pairs={{0,24},{8,16},{16,8},{24,0},{1,25},{9,17},{17,9},{25,1},{2,26},{10... | collective-permute-start | bytes 258056 | tf_op jit(solution)/shard_map/ppermute | solution.py:276
  12.6 8.6 %collective-permute-start.6 = (f32[64,128]{1,0:T(8,128)S(1)}, f32[64,128]{1,0:T(8,128)S(1)}, u32[]{:S(2)}, u32[]{:S(2)}) collective-permute-start(f32[64,128]{1,0:T(8,128)S(1)} %get-tuple-element.20.refs_1_), channel_id=1, source_target_pairs={{0,16},{8,24},{16,0},{24,8},{1,17},{9,25},{17,1},{25,9},{2,18},{10... | collective-permute-start | bytes 98312 | tf_op jit(solution)/shard_map/ppermute | solution.py:276
  13.9 7.3 %collective-permute-start.5 = (f32[64,128]{1,0:T(8,128)S(1)}, f32[64,128]{1,0:T(8,128)S(1)}, u32[]{:S(2)}, u32[]{:S(2)}) collective-permute-start(f32[64,128]{1,0:T(8,128)S(1)} %get-tuple-element.20.refs_1_), channel_id=1, source_target_pairs={{0,8},{8,0},{16,24},{24,16},{1,9},{9,1},{17,25},{25,17},{2,10},{10... | collective-permute-start | bytes 98312 | tf_op jit(solution)/shard_map/ppermute | solution.py:276
  21.2 15.1 %collective-permute-start.7 = (f32[968,128]{1,0:T(8,128)S(1)}, f32[968,128]{1,0:T(8,128)S(1)}, u32[]{:S(2)}, u32[]{:S(2)}) collective-permute-start(f32[968,128]{1,0:T(8,128)S(1)} %get-tuple-element.19), channel_id=1, source_target_pairs={{0,24},{8,16},{16,8},{24,0},{1,25},{9,17},{17,9},{25,1},{2,26},{10... | collective-permute-start | bytes 1486856 | tf_op jit(solution)/shard_map/ppermute | solution.py:276

commit v5 on v4

v5 whole, which is shorter than its diff:
```python
import functools

import jax
import jax.numpy as jnp
from jax import lax
from jax.experimental import pallas as pl
from jax.experimental.pallas import tpu as pltpu
from jax.sharding import PartitionSpec as P

AMBIENT = 0.3
OPACITY = 2.0
SUB = 8
VMEM = pltpu.VMEM
SMEM = pltpu.SMEM
MIB = 1 << 20


def near_pack_kernel(parts, field_ref, *refs):
    outs, (rim_ref, sems) = refs[: parts - 2], refs[parts - 2 :]
    cells, all_rows, cols = field_ref.shape
    rows = all_rows // parts
    me = lax.axis_index("depth")
    copies, rims = [], []
    for m in range(1, parts - 1):
        low = pl.multiple_of((me ^ m) * rows, SUB)
        before = pl.multiple_of(jnp.maximum(low - SUB, 0), SUB)
        after = pl.multiple_of(jnp.minimum(low + rows, all_rows - SUB), SUB)
        for side, start in enumerate((before, after)):
            source = field_ref.at[:, pl.ds(start, SUB), :]
            rims.append(pltpu.make_async_copy(source, rim_ref.at[m - 1, side], sems.at[side, m - 1]))
        centre = outs[m - 1].at[pl.ds(2 * cells, cells * rows), :].reshape(cells, rows, cols)
        copies.append(pltpu.make_async_copy(field_ref.at[:, pl.ds(low, rows), :], centre, sems.at[2, m - 1]))
    for copy in rims + copies:
        copy.start()
    for copy in rims:
        copy.wait()
    for m in range(1, parts - 1):
        part = me ^ m
        above = jnp.where(part > 0, 1.0, 0.0)
        below = jnp.where(part < parts - 1, 1.0, 0.0)
        for z in range(cells):
            outs[m - 1][z : z + 1, :] = rim_ref[m - 1, 0, z, SUB - 1 : SUB, :] * above
            outs[m - 1][cells + z : cells + z + 1, :] = rim_ref[m - 1, 1, z, 0:1, :] * below
    for copy in copies:
        copy.wait()


def edge_kernel(parts, field_ref, _, edge_ref, own_ref, head_ref, body_ref):
    cells, all_rows, cols = field_ref.shape
    rows = all_rows // parts
    me = lax.axis_index("depth")
    lane_pair = lax.broadcasted_iota(jnp.int32, (SUB, cols), 1) // 2

    def tile(i, carry):
        acc = jnp.zeros((SUB, cols), jnp.float32)
        for part in range(parts):
            for z in range(cells):
                slot = part * cells + z
                start = pl.multiple_of(part * rows + i * SUB, SUB)
                value = field_ref[z, pl.ds(start, SUB), :]
                moved = pltpu.roll(value, (2 * slot + 1) % cols, 1)
                acc = jnp.where(lane_pair == slot, moved, acc)
        edge_ref[pl.ds(pl.multiple_of(i * SUB, SUB), SUB), :] = acc
        return carry

    lax.fori_loop(0, rows // SUB, tile, 0)
    for m, head in ((0, own_ref), (parts - 1, head_ref)):
        part = me ^ m
        low = pl.multiple_of(part * rows, SUB)
        above = jnp.where(part > 0, 1.0, 0.0)
        below = jnp.where(part < parts - 1, 1.0, 0.0)
        for z in range(cells):
            head[z : z + 1, :] = field_ref[z, pl.ds(jnp.maximum(low - 1, 0), 1), :] * above
            head[cells + z : cells + z + 1, :] = field_ref[z, pl.ds(jnp.minimum(low + rows, all_rows - 1), 1), :] * below
        places = near_places(cells, rows, own_ref) if m == 0 else far_places(cells, rows, parts, head_ref, body_ref)
        for z in range(cells):
            ref, start = places[z]
            ref[start : start + rows, :] = field_ref[z, pl.ds(low, rows), :]


def side_kernel(parts, left_ref, right_ref, *outs):
    rows, cols = left_ref.shape
    group = rows // parts
    width = cols // parts
    me = lax.axis_index("depth")
    lane = lax.broadcasted_iota(jnp.int32, (rows, cols), 1)
    sides = jnp.where(lane % 2 == 0, left_ref[...], right_ref[...])
    for m in range(parts):
        acc = jnp.zeros((group, cols), jnp.float32)
        for j in range(parts):
            moved = pltpu.roll(sides[j * group : (j + 1) * group], (j - (me ^ m) + parts) * width % cols, 1)
            acc = jnp.where(lane[:group] // width == j, moved, acc)
        outs[m][...] = acc


def near_places(cells, rows, head):
    return [(head, 2 * cells + z * rows) for z in range(cells)]


def far_places(cells, rows, parts, head, body):
    skip = rows // parts
    middle = [(body, skip + (z - 1) * rows) for z in range(1, cells - 1)]
    return [(head, 2 * cells)] + middle + [(head, 2 * cells + rows)]


def fill_ends(parts, cells, rows, heads, ends_ref):
    me = lax.axis_index("depth")
    ends_ref[0, 1] = jnp.zeros_like(ends_ref[0, 1])
    ends_ref[parts + 1, 0] = jnp.zeros_like(ends_ref[0, 0])
    for m in range(parts):
        last = (cells - 1) * rows if m < parts - 1 else rows
        ends_ref[(me ^ m) + 1, 0] = heads[m][2 * cells : 2 * cells + rows, :]
        ends_ref[(me ^ m) + 1, 1] = heads[m][2 * cells + last : 2 * cells + last + rows, :]


def fill_table(index_ref, lights_ref, curves_ref, scale, table_ref):
    passes = index_ref.shape[0]
    channels, knots = curves_ref.shape[1:]
    shape = table_ref.shape[2:]
    for p in range(passes):
        chosen = index_ref[p]
        for axis in range(3):
            table_ref[p, axis] = jnp.full(shape, lights_ref[chosen, axis])
        for channel in range(channels):
            factor = scale if channel == channels - 1 else 1.0
            points = [curves_ref[chosen, channel, k] * factor for k in range(knots)]
            slopes = [points[k + 1] - points[k] for k in range(knots - 1)]
            bends = [points[0], slopes[0]] + [slopes[k] - slopes[k - 1] for k in range(1, knots - 1)]
            for k in range(knots):
                table_ref[p, 3 + channel * knots + k] = jnp.full(shape, bends[k])


def prepare_steps(m, zs, head, places, lateral, base, cells, rows, parts, knots, cols, ends_ref, cell_ref):
    me = lax.axis_index("depth")
    part = me ^ m
    at = pl.ds(base, SUB)
    lane = lax.broadcasted_iota(jnp.int32, (SUB, cols), 1)
    sublane = lax.broadcasted_iota(jnp.int32, (SUB, cols), 0)
    is_first = lane == 0
    is_last = lane == cols - 1
    is_top = jnp.logical_and(sublane == 0, base == 0)
    is_bottom = jnp.logical_and(sublane == SUB - 1, base == rows - SUB)
    group = rows // parts
    got = lateral[pl.ds(pl.multiple_of(base % group, SUB), SUB), :]
    sides = pltpu.roll(got, (2 * cols - 1 - base // group * (cols // parts)) % cols, 1)

    def layer(z):
        if z < 0:
            return ends_ref[part, 1, at, :]
        if z == cells:
            return ends_ref[part + 2, 0, at, :]
        ref, low = places[z]
        return ref[pl.ds(low + base, SUB), :]

    def step(z):
        ref, low = places[z]
        here = layer(z)
        upper = jnp.where(is_top, head[z : z + 1, :], ref[pl.ds(low + base - 1, SUB), :])
        lower = jnp.where(is_bottom, head[cells + z : cells + z + 1, :], ref[pl.ds(low + base + 1, SUB), :])
        edge = pltpu.roll(sides, (cols - 2 * z) % cols, 1) if z else sides
        grad_x = pltpu.roll(jnp.where(is_first, edge, here), cols - 1, 1) - pltpu.roll(
            jnp.where(is_last, edge, here), 1, 1
        )
        grad_y = lower - upper
        grad_z = layer(z + 1) - layer(z - 1)
        inverse = lax.rsqrt(grad_x * grad_x + grad_y * grad_y + grad_z * grad_z + 4.0)
        half = 0.5 * (knots - 1)
        position = half + half * jnp.tanh(0.5 * here)
        cell_ref[0, z] = grad_x * inverse
        cell_ref[1, z] = grad_y * inverse
        cell_ref[2, z] = grad_z * inverse
        cell_ref[3, z] = position
        for k in range(1, knots - 1):
            cell_ref[3 + k, z] = jnp.maximum(position - k, 0.0)

    return [functools.partial(step, z) for z in zs]


def tree(terms):
    while len(terms) > 1:
        terms = [sum(terms[j + 1 : j + 2], terms[j]) for j in range(0, len(terms), 2)]
    return terms[0]


def march_unit(flip, table_ref, zs, cells, knots, cell_ref, beside, inner=None):
    passes = table_ref.shape[0]
    shape = table_ref.shape[2:]
    zero = jnp.zeros(shape, jnp.float32)
    curve_at = 3 + 3 * knots
    result = []
    beside = list(beside)
    for low in range(0, passes, 2):
        group = range(low, min(low + 2, passes))
        vector = {p: [table_ref[p, axis] for axis in range(3)] for p in group}
        curve = {p: [table_ref[p, curve_at + k] for k in range(knots)] for p in group}
        state = {p: (jnp.ones(shape, jnp.float32), [zero] * knots) for p in group}
        share = -(-len(beside) * 2 // max(passes - low, 1))
        mine, beside = beside[:share], beside[share:]
        for u, spot in enumerate(zs):
            for step in mine[u * share // len(zs) : (u + 1) * share // len(zs)]:
                step()
            z = spot + flip * (cells - 1 - 2 * spot)
            hinges = [cell_ref[3 + k, z] for k in range(knots - 1)]
            normal = [cell_ref[axis, z] for axis in range(3)]
            for p in group:
                keep, sums = state[p]
                opacity = tree([curve[p][0]] + [curve[p][k + 1] * hinges[k] for k in range(knots - 1)])
                facing = normal[0] * vector[p][0] + normal[1] * vector[p][1] + normal[2] * vector[p][2]
                taken = keep * opacity
                weight = taken * (AMBIENT + jnp.abs(facing))
                sums = [sums[0] + weight] + [sums[k + 1] + weight * hinges[k] for k in range(knots - 1)]
                keep = keep - taken
                if inner is not None and u == 0:
                    keep, sums = keep * inner(p, 0), [total + keep * inner(p, j + 1) for j, total in enumerate(sums)]
                state[p] = (keep, sums)
        result += [[state[p][0]] + state[p][1] for p in group]
    return result


def own_kernel(parts, index_ref, flip_ref, lights_ref, curves_ref, own_ref, lateral_ref, out_ref, table_ref, *cell_refs):
    rows, cols = out_ref.shape[1:]
    knots = curves_ref.shape[2]
    passes = index_ref.shape[0]
    cells = cell_refs[0].shape[1]
    flip = flip_ref[0]
    tiles = rows // SUB
    inner = range(1, cells - 1)
    fill_table(index_ref, lights_ref, curves_ref, OPACITY / (parts * cells), table_ref)
    places = near_places(cells, rows, own_ref)

    def prepare(base, slot):
        return prepare_steps(
            0, inner, own_ref, places, lateral_ref, base, cells, rows, parts, knots, cols, None, cell_refs[slot]
        )

    for step in prepare(0, 0):
        step()

    def pair(i, carry):
        for slot in range(2):
            base = pl.multiple_of((2 * i + slot) * SUB, SUB)
            after = pl.multiple_of(jnp.minimum(2 * i + slot + 1, tiles - 1) * SUB, SUB)
            result = march_unit(flip, table_ref, inner, cells, knots, cell_refs[slot], prepare(after, 1 - slot))
            for p in range(passes):
                for j in range(knots + 1):
                    out_ref[p * (knots + 1) + j, pl.ds(base, SUB), :] = result[p][j]
        return carry

    lax.fori_loop(0, tiles // 2, pair, 0)


def near_kernel(parts, flip_ref, table_ref, inner_ref, *refs):
    count = parts - 1
    heads, laterals, out_ref, ends_ref = refs[:parts], refs[parts : 2 * parts - 1], refs[2 * parts - 1], refs[2 * parts]
    cell_refs = refs[2 * parts + 1 :]
    rows, cols = out_ref.shape[2:]
    cells = cell_refs[0].shape[1]
    passes = table_ref.shape[0]
    knots = inner_ref.shape[0] // passes - 1
    flip = flip_ref[0]
    tiles = rows // SUB
    zs = [(0, cells - 1)] + [range(cells)] * (count - 1)
    places = [near_places(cells, rows, head) for head in heads[:count]]
    fill_ends(parts, cells, rows, heads, ends_ref)

    def prepare(m, base):
        return prepare_steps(
            m, zs[m], heads[m], places[m], laterals[m], base, cells, rows, parts, knots, cols, ends_ref, cell_refs[m]
        )

    for step in prepare(0, 0):
        step()

    def tile(i, carry):
        base = pl.multiple_of(i * SUB, SUB)
        after = pl.multiple_of(jnp.minimum(i + 1, tiles - 1) * SUB, SUB)
        at = pl.ds(base, SUB)
        for m in range(count):
            beside = prepare(m + 1, base) if m + 1 < count else prepare(0, after)
            inner = (lambda p, j: inner_ref[p * (knots + 1) + j, at, :]) if m == 0 else None
            result = march_unit(flip, table_ref, zs[m], cells, knots, cell_refs[m], beside, inner)
            for p in range(passes):
                for j in range(knots + 1):
                    out_ref[m, p * (knots + 1) + j, at, :] = result[p][j]
        return carry

    lax.fori_loop(0, tiles, tile, 0)


def over_either(first_leads, one, other):
    shape = one[0].shape
    unit = jnp.ones(shape, jnp.float32)
    scale_one = jnp.where(first_leads, unit, other[0])
    scale_other = jnp.where(first_leads, one[0], unit)
    return [one[0] * other[0]] + [scale_one * a + scale_other * b for a, b in zip(one[1:], other[1:])]


def far_kernel(parts, flip_ref, table_ref, *refs):
    heads, body, states, out_ref, picture_ref, ends_ref, sems = refs[:parts], *refs[parts : parts + 6]
    cell_refs = refs[parts + 6 :]
    rows, cols = out_ref.shape[2:]
    cells = cell_refs[0].shape[1]
    passes = table_ref.shape[0]
    knots = states.shape[1] // passes - 1
    flip = flip_ref[0]
    me = lax.axis_index("depth")
    places = far_places(cells, rows, parts, heads[-1], body)
    fill_ends(parts, cells, rows, heads, ends_ref)
    tiles = rows // SUB

    def prepare(base, slot):
        return prepare_steps(
            parts - 1, range(cells), heads[-1], places, body, base, cells, rows, parts, knots, cols, ends_ref, cell_refs[slot]
        )

    def send(index):
        at = pl.ds(pl.multiple_of(index * SUB, SUB), SUB)
        return pltpu.make_async_copy(picture_ref.at[:, :, at, :], out_ref.at[:, :, at, :], sems.at[index])

    def finish(result, index):
        at = pl.ds(pl.multiple_of(index * SUB, SUB), SUB)
        for p in range(passes):
            images = [[states[m, p * (knots + 1) + j, at, :] for j in range(knots + 1)] for m in range(parts - 1)]
            images.append(result[p])
            bit = 0
            while len(images) > 1:
                leads = ((me >> bit) & 1) == flip
                images = [over_either(leads, images[j], images[j + 1]) for j in range(0, len(images), 2)]
                bit += 1
            keep, sums = images[0][0], images[0][1:]
            for channel in range(3):
                picture_ref[p, channel, at, :] = tree([table_ref[p, 3 + channel * knots + k] * sums[k] for k in range(knots)])
            picture_ref[p, 3, at, :] = 1.0 - keep
        send(index).start()

    for step in prepare(0, 0):
        step()

    def pair(i, carry):
        for slot in range(2):
            index = 2 * i + slot
            after = pl.multiple_of(jnp.minimum(index + 1, tiles - 1) * SUB, SUB)
            result = march_unit(flip, table_ref, range(cells), cells, knots, cell_refs[slot], prepare(after, 1 - slot))
            finish(result, index)
        return carry

    lax.fori_loop(0, tiles // 2, pair, 0)
    for index in range(tiles):
        send(index).wait()


def shift_along(block, axis, amount):
    count = lax.axis_size(axis)
    route = [(i, i + amount) for i in range(count) if 0 <= i + amount < count]
    return lax.ppermute(block, axis, route)


def swap_along(block, axis, mask):
    return lax.ppermute(block, axis, [(i, i ^ mask) for i in range(lax.axis_size(axis))])


def estimate(micros):
    return pl.CostEstimate(flops=int(micros * 1_000_000_000), transcendentals=0, bytes_accessed=0)


def on_device(field, light_vectors, transfer, light_index, flips):
    parts = lax.axis_size("depth")
    cells, all_rows, cols = field.shape
    rows = all_rows // parts
    passes = light_index.shape[0]
    channels, knots = transfer.shape[1:]
    tiles = rows // SUB
    values = passes * (knots + 1)
    in_vmem = pl.BlockSpec(memory_space=VMEM)
    in_smem = pl.BlockSpec(memory_space=SMEM)
    in_any = pl.BlockSpec(memory_space=pl.ANY)

    def array(*shape):
        return jax.ShapeDtypeStruct(shape, jnp.float32)

    def settings(mib, micros):
        return dict(
            compiler_params=pltpu.CompilerParams(vmem_limit_bytes=mib * MIB),
            cost_estimate=pl.CostEstimate(flops=int(micros * 1e9), transcendentals=0, bytes_accessed=0),
        )

    near_rows = 2 * cells + cells * rows + SUB
    head_rows = 2 * cells + 2 * rows + SUB
    skip = rows // parts
    body_rows = skip + (cells - 2) * rows + SUB
    packed = pl.pallas_call(
        functools.partial(near_pack_kernel, parts),
        out_shape=[array(near_rows, cols)] * (parts - 2),
        in_specs=[in_any],
        out_specs=[in_vmem] * (parts - 2),
        scratch_shapes=[VMEM((parts - 2, 2, cells, SUB, cols), jnp.float32), pltpu.SemaphoreType.DMA((3, parts - 2))],
        name="pack",
        **settings(8, 1),
    )(field)
    near = [swap_along(packed[m - 1], "depth", m) for m in range(1, parts - 1)]

    edges, own, far_head, far_body = pl.pallas_call(
        functools.partial(edge_kernel, parts),
        out_shape=[array(rows, cols), array(near_rows, cols), array(head_rows, cols), array(body_rows, cols)],
        in_specs=[in_vmem, in_any],
        out_specs=[in_vmem] * 4,
        name="edges",
        **settings(8, 1),
    )(field, packed[0])
    far_head = swap_along(far_head, "depth", parts - 1)
    sides = pl.pallas_call(
        functools.partial(side_kernel, parts),
        out_shape=[array(skip, cols)] * parts,
        in_specs=[in_vmem] * 2,
        out_specs=[in_vmem] * parts,
        name="sides",
        **settings(4, 0.1),
    )(shift_along(edges, "tile", 1), shift_along(edges, "tile", -1))
    laterals = [swap_along(sides[m], "depth", m) for m in range(1, parts - 1)]
    *laterals, far_body = lax.optimization_barrier((*laterals, lax.dynamic_update_slice(far_body, sides[-1], (0, 0))))
    far_body = swap_along(far_body, "depth", parts - 1)

    cell_shape = VMEM((knots + 2, cells, SUB, cols), jnp.float32)
    ends_shape = VMEM((parts + 2, 2, rows, cols), jnp.float32)
    inner, table = pl.pallas_call(
        functools.partial(own_kernel, parts),
        out_shape=[array(values, rows, cols), array(passes, 3 + channels * knots, SUB, cols)],
        in_specs=[in_smem] * 4 + [in_vmem] * 2,
        out_specs=[in_vmem] * 2,
        scratch_shapes=[cell_shape] * 2,
        name="own",
        **settings(8, 4),
    )(light_index, flips, light_vectors, transfer, own, sides[0])
    states = pl.pallas_call(
        functools.partial(near_kernel, parts),
        out_shape=array(parts - 1, values, rows, cols),
        in_specs=[in_smem] + [in_vmem] * (2 * parts + 1),
        out_specs=in_vmem,
        scratch_shapes=[ends_shape] + [cell_shape] * (parts - 1),
        name="near",
        **settings(16, 60),
    )(flips, table, inner, own, *near, far_head, sides[0], *laterals)
    return pl.pallas_call(
        functools.partial(far_kernel, parts),
        out_shape=array(passes, channels, rows, cols),
        in_specs=[in_smem] + [in_vmem] * (parts + 3),
        out_specs=in_any,
        scratch_shapes=[
            VMEM((passes, channels, rows, cols), jnp.float32),
            ends_shape,
            pltpu.SemaphoreType.DMA((tiles,)),
        ]
        + [cell_shape] * 2,
        name="far",
        **settings(16, 5),
    )(flips, table, own, *near, far_head, far_body, states)


def solution(mesh):
    in_specs = (P("depth", None, "tile"), P(), P(), P(), P("tile"))
    out_specs = P(None, None, "depth", "tile")
    return jax.shard_map(
        on_device, mesh=mesh, in_specs=in_specs, out_specs=out_specs, check_vma=False
    )
```

time: 43.9 us -> 41.4 us (0.943)
  waiting for transfers between devices: 5.69 us -> 3.79 us
  Pallas kernels: 22.3 us -> 21.7 us
    ppermute x6, waiting for transfers between devices: 4.95 us -> 3.79 us  [swap_along(): lax.ppermute(block, axis, [(i, i ^ mask) for i in range(lax.axis_size(axi...]
    ppermute x2, waiting for transfers between devices: 0.74 us -> 0.01 us  [shift_along(): return lax.ppermute(block, axis, route)]
    pallas_call x4 -> x6, Pallas kernels: 22.3 us -> 21.7 us  [the longest x1 9.36 us: on_device(): pl.pallas_call(functools.partial(near_kernel, parts), out_shape=array(par...]
  transfers between devices with their start and end apart: 8 -> 8, of which waited for: 2 -> 1; matrix products, arithmetic and copies ran while one was open for 0% -> 0% of each run, Pallas kernels for 34% -> 38%
where the time goes in v5:
time: 41.4 us; the launch traced here: 41.1 us
  Pallas kernels  21.7 us (52%)
  starting transfers between devices  13.1 us (32%)
  waiting for transfers between devices  3.79 us (9%)
  local copies, waits for them, and re-layouts  1.77 us (4%)
  between operations  0.77 us (2%)
    pallas_call x1, Pallas kernels, on_device(): pl.pallas_call(functools.partial(near_kernel, parts), out_shape=array(par...  9.36 us
    ppermute x6, starting transfers between devices, swap_along(): lax.ppermute(block, axis, [(i, i ^ mask) for i in range(lax.axis_size(axi...  8.79 us
    pallas_call x1, Pallas kernels, on_device(): pl.pallas_call(functools.partial(far_kernel, parts), out_shape=array(pass...  5.83 us
    pallas_call x1, Pallas kernels, on_device(): pl.pallas_call(functools.partial(own_kernel, parts), out_shape=[array(val...  4.99 us
    ppermute x2, starting transfers between devices, shift_along(): return lax.ppermute(block, axis, route)  4.32 us
    ppermute x6, waiting for transfers between devices, swap_along(): lax.ppermute(block, axis, [(i, i ^ mask) for i in range(lax.axis_size(axi...  3.79 us
    unnamed x10, local copies, waits for them, and re-layouts  1.77 us
    pallas_call x1, Pallas kernels, on_device(): pl.pallas_call(functools.partial(edge_kernel, parts), out_shape=[array(ro...  1.18 us
  transfers between devices with their start and end apart: 8, of which 1 were waited for; matrix products, arithmetic and copies ran while one was open for 0% of the time, Pallas kernels for 38%

profile of v5, /device:TPU:0, one launch (start us, length us, event | category | flops | bytes accessed | tf_op | source)
XLA Modules:
  0.0 41.1 jit_solution(1956946753568107327)
XLA Ops:
  0.0 0.0 copy-start
  0.0 1.6 %copy-done = f32[16,256,128]{2,1,0:T(8,128)S(1)} copy-done((f32[16,256,128]{2,1,0:T(8,128)S(1)}, f32[16,256,128]{2,1,0:T(8,128)}, u32[]{:S(2)}) %copy-start) | copy-done | bytes 2097176
  1.6 0.2 pack.1
  1.8 0.0 copy-start.3
  1.8 0.0 copy-start.2
  1.8 0.0 copy-start.1
  1.8 3.0 %collective-permute-start.3 = (f32[1064,128]{1,0:T(8,128)S(1)}, f32[1064,128]{1,0:T(8,128)S(1)}, u32[]{:S(2)}, u32[]{:S(2)}) collective-permute-start(f32[1064,128]{1,0:T(8,128)S(1)} %get-tuple-element.25), channel_id=1, source_target_pairs={{0,16},{8,24},{16,0},{24,8},{1,17},{9,25},{17,1},{25,9},{2,18},{10... | collective-permute-start | bytes 1634312 | tf_op jit(solution)/shard_map/ppermute | solution.py:359
  4.9 1.5 %collective-permute-start.2 = (f32[1064,128]{1,0:T(8,128)S(1)}, f32[1064,128]{1,0:T(8,128)S(1)}, u32[]{:S(2)}, u32[]{:S(2)}) collective-permute-start(f32[1064,128]{1,0:T(8,128)S(1)} %get-tuple-element.20._), channel_id=1, source_target_pairs={{0,8},{8,0},{16,24},{24,16},{1,9},{9,1},{17,25},{25,17},{2,10},{10... | collective-permute-start | bytes 1634312 | tf_op jit(solution)/shard_map/ppermute | solution.py:359
  6.4 1.2 %edges.1 = (f32[64,128]{1,0:T(8,128)S(1)}, f32[1064,128]{1,0:T(8,128)S(1)}, f32[168,128]{1,0:T(8,128)S(1)}, f32[920,128]{1,0:T(8,128)S(1)}) custom-call(f32[16,256,128]{2,1,0:T(8,128)S(1)} %copy-done, f32[1064,128]{1,0:T(8,128)S(1)} %get-tuple-element.20._), custom_call_target="tpu_custom_call" | custom-call | flops 1000000000 | tf_op jit(solution)/shard_map/edges/pallas_call | solution.py:402
  7.5 1.3 %collective-permute-start.1 = (f32[64,128]{1,0:T(8,128)S(1)}, f32[64,128]{1,0:T(8,128)S(1)}, u32[]{:S(2)}, u32[]{:S(2)}) collective-permute-start(f32[64,128]{1,0:T(8,128)S(1)} %get-tuple-element.22), channel_id=1, source_target_pairs={{1,0},{2,1},{3,2},{4,3},{5,4},{6,5},{7,6},{9,8},{10,9},{11,10},{12... | collective-permute-start | bytes 98312 | tf_op jit(solution)/shard_map/ppermute | solution.py:355
  8.8 3.0 %collective-permute-start = (f32[64,128]{1,0:T(8,128)S(1)}, f32[64,128]{1,0:T(8,128)S(1)}, u32[]{:S(2)}, u32[]{:S(2)}) collective-permute-start(f32[64,128]{1,0:T(8,128)S(1)} %get-tuple-element.22), channel_id=1, source_target_pairs={{0,1},{1,2},{2,3},{3,4},{4,5},{5,6},{6,7},{8,9},{9,10},{10,11},{11... | collective-permute-start | bytes 98312 | tf_op jit(solution)/shard_map/ppermute | solution.py:355
  11.9 0.1 collective-permute-start.4
  12.6 0.0 copy-done.3
  12.7 0.1 copy.6.lights_ref
  12.7 0.0 copy-done.2
  12.7 0.1 copy.7.curves_ref
  12.8 0.0 collective-permute-done.1.right_ref
  12.8 0.0 collective-permute-done.left_ref
  12.8 0.1 sides.1
  13.0 2.0 %collective-permute-start.5 = (f32[16,128]{1,0:T(8,128)S(1)}, f32[16,128]{1,0:T(8,128)S(1)}, u32[]{:S(2)}, u32[]{:S(2)}) collective-permute-start(f32[16,128]{1,0:T(8,128)S(1)} %get-tuple-element.27), channel_id=1, source_target_pairs={{0,8},{8,0},{16,24},{24,16},{1,9},{9,1},{17,25},{25,17},{2,10},{10... | collective-permute-start | bytes 24584 | tf_op jit(solution)/shard_map/ppermute | solution.py:359
  14.9 1.5 %collective-permute-start.6 = (f32[16,128]{1,0:T(8,128)S(1)}, f32[16,128]{1,0:T(8,128)S(1)}, u32[]{:S(2)}, u32[]{:S(2)}) collective-permute-start(f32[16,128]{1,0:T(8,128)S(1)} %get-tuple-element.28), channel_id=1, source_target_pairs={{0,16},{8,24},{16,0},{24,8},{1,17},{9,25},{17,1},{25,9},{2,18},{10... | collective-permute-start | bytes 24584 | tf_op jit(solution)/shard_map/ppermute | solution.py:359
  16.5 0.0 copy-done.1
  16.5 5.0 %own.1 = (f32[36,64,128]{2,1,0:T(8,128)S(1)}, f32[4,35,8,128]{3,2,1,0:T(8,128)S(1)}) custom-call(s32[4]{0:T(128)S(1)} %copy-done.1, s32[1]{0:T(128)S(6)} %copy.9.flip_ref, f32[16,3]{1,0:T(8,128)S(1)} %copy.6.lights_ref, f32[16,4,8]{2,1,0:T(4,128)S(1)} %copy.7.curves_ref, f32[1064,128]{1,0:T(8,128)S(1)} %get-tuple-element.21.own_ref.refs_0_, ...), custom_call_target="tpu_custom_call" | custom-call | flops 4000000000 | tf_op jit(solution)/shard_map/own/pallas_call | solution.py:425
  21.5 0.0 collective-permute-done.5.refs_5_
  21.5 0.0 collective-permute-done.6.refs_6_
  21.5 0.7 %collective-permute-start.7 = (f32[920,128]{1,0:T(8,128)S(1)}, f32[920,128]{1,0:T(8,128)S(1)}, u32[]{:S(2)}, u32[]{:S(2)}) collective-permute-start(f32[920,128]{1,0:T(8,128)S(1)} %constant_dynamic-update-slice_fusion), channel_id=1, source_target_pairs={{0,24},{8,16},{16,8},{24,0},{1,25},{9,17},{17,9},{25,1},{2,26},{10... | collective-permute-start | bytes 1413128 | tf_op jit(solution)/shard_map/ppermute | solution.py:359
  22.1 0.0 collective-permute-done.4.refs_3_
  22.1 0.0 collective-permute-done.3.refs_2_
  22.2 0.0 collective-permute-done.2.refs_1_
  22.2 9.4 %near.1.refs_5_ = f32[3,36,64,128]{3,2,1,0:T(8,128)S(1)} custom-call(s32[1]{0:T(128)S(6)} %copy.9.flip_ref, f32[4,35,8,128]{3,2,1,0:T(8,128)S(1)} %get-tuple-element.24.table_ref, f32[36,64,128]{2,1,0:T(8,128)S(1)} %get-tuple-element.32.inner_ref, f32[1064,128]{1,0:T(8,128)S(1)} %get-tuple-element.21.own_ref.refs_0_, ...), custom_call_target="tpu_custom_call" | custom-call | flops 60000002048 | tf_op jit(solution)/shard_map/near/pallas_call | solution.py:434
  31.5 3.8 %collective-permute-done.7.refs_4_ = f32[920,128]{1,0:T(8,128)S(1)} collective-permute-done((f32[920,128]{1,0:T(8,128)S(1)}, f32[920,128]{1,0:T(8,128)S(1)}, u32[]{:S(2)}, u32[]{:S(2)}) %collective-permute-start.7) | collective-permute-done | bytes 471072 | tf_op jit(solution)/shard_map/ppermute | solution.py:359
  35.3 5.8 %far.1 = f32[4,4,64,128]{3,2,1,0:T(8,128)} custom-call(s32[1]{0:T(128)S(6)} %copy.9.flip_ref, f32[4,35,8,128]{3,2,1,0:T(8,128)S(1)} %get-tuple-element.24.table_ref, f32[1064,128]{1,0:T(8,128)S(1)} %get-tuple-element.21.own_ref.refs_0_, f32[1064,128]{1,0:T(8,128)S(1)} %collective-permute-done.2.refs_1_, f32[1064,128]{1,0:T(8,128)S(1)} %collective-permute-done.3.refs_2_, ...), custom_call_target="tpu_custom_call" | custom-call | flops 5000000000 | tf_op jit(solution)/shard_map/far/pallas_call | solution.py:443
  (1 shorter events, 0.0 us)
Async XLA Ops:
  0.0 1.6 %copy-start = (f32[16,256,128]{2,1,0:T(8,128)S(1)}, f32[16,256,128]{2,1,0:T(8,128)}, u32[]{:S(2)}) copy-start(f32[16,256,128]{2,1,0:T(8,128)} %field_ref.3) | copy-start | bytes 6291460
  1.8 10.9 %copy-start.3 = (f32[16,3]{0,1:T(4,128)S(1)}, f32[16,3]{0,1:T(4,128)}, u32[]{:S(2)}) copy-start(f32[16,3]{0,1:T(4,128)} %param.6) | copy-start | bytes 580
  1.8 10.9 %copy-start.2 = (f32[16,4,8]{0,2,1:T(8,128)S(1)}, f32[16,4,8]{0,2,1:T(8,128)}, u32[]{:S(2)}) copy-start(f32[16,4,8]{0,2,1:T(8,128)} %param.7) | copy-start | bytes 6148
  1.8 14.6 %copy-start.1 = (s32[4]{0:T(128)S(1)}, s32[4]{0:T(128)}, u32[]{:S(2)}) copy-start(s32[4]{0:T(128)} %index_ref.1) | copy-start | bytes 52
  1.8 20.3 %collective-permute-start.3 = (f32[1064,128]{1,0:T(8,128)S(1)}, f32[1064,128]{1,0:T(8,128)S(1)}, u32[]{:S(2)}, u32[]{:S(2)}) collective-permute-start(f32[1064,128]{1,0:T(8,128)S(1)} %get-tuple-element.25), channel_id=1, source_target_pairs={{0,16},{8,24},{16,0},{24,8},{1,17},{9,25},{17,1},{25,9},{2,18},{10... | collective-permute-start | bytes 1634312 | tf_op jit(solution)/shard_map/ppermute | solution.py:359
  4.9 17.3 %collective-permute-start.2 = (f32[1064,128]{1,0:T(8,128)S(1)}, f32[1064,128]{1,0:T(8,128)S(1)}, u32[]{:S(2)}, u32[]{:S(2)}) collective-permute-start(f32[1064,128]{1,0:T(8,128)S(1)} %get-tuple-element.20._), channel_id=1, source_target_pairs={{0,8},{8,0},{16,24},{24,16},{1,9},{9,1},{17,25},{25,17},{2,10},{10... | collective-permute-start | bytes 1634312 | tf_op jit(solution)/shard_map/ppermute | solution.py:359
  7.5 5.3 %collective-permute-start.1 = (f32[64,128]{1,0:T(8,128)S(1)}, f32[64,128]{1,0:T(8,128)S(1)}, u32[]{:S(2)}, u32[]{:S(2)}) collective-permute-start(f32[64,128]{1,0:T(8,128)S(1)} %get-tuple-element.22), channel_id=1, source_target_pairs={{1,0},{2,1},{3,2},{4,3},{5,4},{6,5},{7,6},{9,8},{10,9},{11,10},{12... | collective-permute-start | bytes 98312 | tf_op jit(solution)/shard_map/ppermute | solution.py:355
  8.8 4.0 %collective-permute-start = (f32[64,128]{1,0:T(8,128)S(1)}, f32[64,128]{1,0:T(8,128)S(1)}, u32[]{:S(2)}, u32[]{:S(2)}) collective-permute-start(f32[64,128]{1,0:T(8,128)S(1)} %get-tuple-element.22), channel_id=1, source_target_pairs={{0,1},{1,2},{2,3},{3,4},{4,5},{5,6},{6,7},{8,9},{9,10},{10,11},{11... | collective-permute-start | bytes 98312 | tf_op jit(solution)/shard_map/ppermute | solution.py:355
  11.9 10.3 %collective-permute-start.4 = (f32[168,128]{1,0:T(8,128)S(1)}, f32[168,128]{1,0:T(8,128)S(1)}, u32[]{:S(2)}, u32[]{:S(2)}) collective-permute-start(f32[168,128]{1,0:T(8,128)S(1)} %get-tuple-element.26), channel_id=1, source_target_pairs={{0,24},{8,16},{16,8},{24,0},{1,25},{9,17},{17,9},{25,1},{2,26},{10... | collective-permute-start | bytes 258056 | tf_op jit(solution)/shard_map/ppermute | solution.py:359
  13.0 8.5 %collective-permute-start.5 = (f32[16,128]{1,0:T(8,128)S(1)}, f32[16,128]{1,0:T(8,128)S(1)}, u32[]{:S(2)}, u32[]{:S(2)}) collective-permute-start(f32[16,128]{1,0:T(8,128)S(1)} %get-tuple-element.27), channel_id=1, source_target_pairs={{0,8},{8,0},{16,24},{24,16},{1,9},{9,1},{17,25},{25,17},{2,10},{10... | collective-permute-start | bytes 24584 | tf_op jit(solution)/shard_map/ppermute | solution.py:359
  14.9 6.5 %collective-permute-start.6 = (f32[16,128]{1,0:T(8,128)S(1)}, f32[16,128]{1,0:T(8,128)S(1)}, u32[]{:S(2)}, u32[]{:S(2)}) collective-permute-start(f32[16,128]{1,0:T(8,128)S(1)} %get-tuple-element.28), channel_id=1, source_target_pairs={{0,16},{8,24},{16,0},{24,8},{1,17},{9,25},{17,1},{25,9},{2,18},{10... | collective-permute-start | bytes 24584 | tf_op jit(solution)/shard_map/ppermute | solution.py:359
  21.5 13.8 %collective-permute-start.7 = (f32[920,128]{1,0:T(8,128)S(1)}, f32[920,128]{1,0:T(8,128)S(1)}, u32[]{:S(2)}, u32[]{:S(2)}) collective-permute-start(f32[920,128]{1,0:T(8,128)S(1)} %constant_dynamic-update-slice_fusion), channel_id=1, source_target_pairs={{0,24},{8,16},{16,8},{24,0},{1,25},{9,17},{17,9},{25,1},{2,26},{10... | collective-permute-start | bytes 1413128 | tf_op jit(solution)/shard_map/ppermute | solution.py:359

commit v6 on v5

--- a/solution.py
+++ b/solution.py
@@ -15,37 +15,43 @@
 MIB = 1 << 20
 
 
-def near_pack_kernel(parts, field_ref, *refs):
-    outs, (rim_ref, sems) = refs[: parts - 2], refs[parts - 2 :]
+def pack_kernel(parts, field_ref, *refs):
+    outs, (rim_ref, sems) = refs[: parts - 1], refs[parts - 1 :]
     cells, all_rows, cols = field_ref.shape
     rows = all_rows // parts
     me = lax.axis_index("depth")
     copies, rims = [], []
-    for m in range(1, parts - 1):
-        low = pl.multiple_of((me ^ m) * rows, SUB)
+    for j, out in enumerate(outs):
+        low = pl.multiple_of((me ^ (j + 1)) * rows, SUB)
         before = pl.multiple_of(jnp.maximum(low - SUB, 0), SUB)
         after = pl.multiple_of(jnp.minimum(low + rows, all_rows - SUB), SUB)
         for side, start in enumerate((before, after)):
             source = field_ref.at[:, pl.ds(start, SUB), :]
-            rims.append(pltpu.make_async_copy(source, rim_ref.at[m - 1, side], sems.at[side, m - 1]))
-        centre = outs[m - 1].at[pl.ds(2 * cells, cells * rows), :].reshape(cells, rows, cols)
-        copies.append(pltpu.make_async_copy(field_ref.at[:, pl.ds(low, rows), :], centre, sems.at[2, m - 1]))
+            rims.append(pltpu.make_async_copy(source, rim_ref.at[j, side], sems.at[side, j]))
+        block = field_ref.at[:, pl.ds(low, rows), :]
+        if j < parts - 2:
+            centre = out.at[pl.ds(2 * cells, cells * rows), :].reshape(cells, rows, cols)
+            copies.append(pltpu.make_async_copy(block, centre, sems.at[2, j]))
+        else:
+            for side in range(2):
+                layer = out.at[pl.ds(2 * cells + side * rows, rows), :]
+                copies.append(pltpu.make_async_copy(block.at[side * (cells - 1)], layer, sems.at[2 + side, j]))
     for copy in rims + copies:
         copy.start()
     for copy in rims:
         copy.wait()
-    for m in range(1, parts - 1):
-        part = me ^ m
+    for j, out in enumerate(outs):
+        part = me ^ (j + 1)
         above = jnp.where(part > 0, 1.0, 0.0)
         below = jnp.where(part < parts - 1, 1.0, 0.0)
         for z in range(cells):
-            outs[m - 1][z : z + 1, :] = rim_ref[m - 1, 0, z, SUB - 1 : SUB, :] * above
-            outs[m - 1][cells + z : cells + z + 1, :] = rim_ref[m - 1, 1, z, 0:1, :] * below
+            out[z : z + 1, :] = rim_ref[j, 0, z, SUB - 1 : SUB, :] * above
+            out[cells + z : cells + z + 1, :] = rim_ref[j, 1, z, 0:1, :] * below
     for copy in copies:
         copy.wait()
 
 
-def edge_kernel(parts, field_ref, _, edge_ref, own_ref, head_ref, body_ref):
+def edge_kernel(parts, field_ref, _, edge_ref, own_ref, body_ref):
     cells, all_rows, cols = field_ref.shape
     rows = all_rows // parts
     me = lax.axis_index("depth")
@@ -64,21 +70,24 @@
         return carry
 
     lax.fori_loop(0, rows // SUB, tile, 0)
-    for m, head in ((0, own_ref), (parts - 1, head_ref)):
-        part = me ^ m
-        low = pl.multiple_of(part * rows, SUB)
-        above = jnp.where(part > 0, 1.0, 0.0)
-        below = jnp.where(part < parts - 1, 1.0, 0.0)
-        for z in range(cells):
-            head[z : z + 1, :] = field_ref[z, pl.ds(jnp.maximum(low - 1, 0), 1), :] * above
-            head[cells + z : cells + z + 1, :] = field_ref[z, pl.ds(jnp.minimum(low + rows, all_rows - 1), 1), :] * below
-        places = near_places(cells, rows, own_ref) if m == 0 else far_places(cells, rows, parts, head_ref, body_ref)
-        for z in range(cells):
-            ref, start = places[z]
-            ref[start : start + rows, :] = field_ref[z, pl.ds(low, rows), :]
-
-
-def side_kernel(parts, left_ref, right_ref, *outs):
+    low = pl.multiple_of(me * rows, SUB)
+    above = jnp.where(me > 0, 1.0, 0.0)
+    below = jnp.where(me < parts - 1, 1.0, 0.0)
+    for z in range(cells):
+        own_ref[z : z + 1, :] = field_ref[z, pl.ds(jnp.maximum(low - 1, 0), 1), :] * above
+        own_ref[cells + z : cells + z + 1, :] = field_ref[z, pl.ds(jnp.minimum(low + rows, all_rows - 1), 1), :] * below
+    far_low = pl.multiple_of((me ^ (parts - 1)) * rows, SUB)
+    own_places = near_places(cells, rows, own_ref)
+    body_places = far_places(cells, rows, parts, None, body_ref)
+    for z in range(cells):
+        ref, start = own_places[z]
+        ref[start : start + rows, :] = field_ref[z, pl.ds(low, rows), :]
+    for z in range(1, cells - 1):
+        ref, start = body_places[z]
+        ref[start : start + rows, :] = field_ref[z, pl.ds(far_low, rows), :]
+
+
+def side_kernel(parts, left_ref, right_ref, _, *outs):
     rows, cols = left_ref.shape
     group = rows // parts
     width = cols // parts
@@ -374,6 +383,7 @@
     in_vmem = pl.BlockSpec(memory_space=VMEM)
     in_smem = pl.BlockSpec(memory_space=SMEM)
     in_any = pl.BlockSpec(memory_space=pl.ANY)
+    in_hbm = pl.BlockSpec(memory_space=pltpu.HBM)
 
     def array(*shape):
         return jax.ShapeDtypeStruct(shape, jnp.float32)
@@ -388,37 +398,37 @@
     head_rows = 2 * cells + 2 * rows + SUB
     skip = rows // parts
     body_rows = skip + (cells - 2) * rows + SUB
-    packed = pl.pallas_call(
-        functools.partial(near_pack_kernel, parts),
-        out_shape=[array(near_rows, cols)] * (parts - 2),
-        in_specs=[in_any],
-        out_specs=[in_vmem] * (parts - 2),
-        scratch_shapes=[VMEM((parts - 2, 2, cells, SUB, cols), jnp.float32), pltpu.SemaphoreType.DMA((3, parts - 2))],
+    *packed, far_head = pl.pallas_call(
+        functools.partial(pack_kernel, parts),
+        out_shape=[array(near_rows, cols)] * (parts - 2) + [array(head_rows, cols)],
+        in_specs=[in_hbm],
+        out_specs=[in_vmem] * (parts - 1),
+        scratch_shapes=[VMEM((parts - 1, 2, cells, SUB, cols), jnp.float32), pltpu.SemaphoreType.DMA((4, parts - 1))],
         name="pack",
         **settings(8, 1),
     )(field)
     near = [swap_along(packed[m - 1], "depth", m) for m in range(1, parts - 1)]
 
-    edges, own, far_head, far_body = pl.pallas_call(
+    far_head = swap_along(far_head, "depth", parts - 1)
+
+    edges, own, far_body = pl.pallas_call(
         functools.partial(edge_kernel, parts),
-        out_shape=[array(rows, cols), array(near_rows, cols), array(head_rows, cols), array(body_rows, cols)],
+        out_shape=[array(rows, cols), array(near_rows, cols), array(body_rows, cols)],
         in_specs=[in_vmem, in_any],
-        out_specs=[in_vmem] * 4,
+        out_specs=[in_vmem] * 3,
         name="edges",
         **settings(8, 1),
     )(field, packed[0])
-    far_head = swap_along(far_head, "depth", parts - 1)
     sides = pl.pallas_call(
         functools.partial(side_kernel, parts),
         out_shape=[array(skip, cols)] * parts,
-        in_specs=[in_vmem] * 2,
+        in_specs=[in_vmem] * 2 + [in_any],
         out_specs=[in_vmem] * parts,
         name="sides",
         **settings(4, 0.1),
-    )(shift_along(edges, "tile", 1), shift_along(edges, "tile", -1))
+    )(shift_along(edges, "tile", 1), shift_along(edges, "tile", -1), far_head)
     laterals = [swap_along(sides[m], "depth", m) for m in range(1, parts - 1)]
-    *laterals, far_body = lax.optimization_barrier((*laterals, lax.dynamic_update_slice(far_body, sides[-1], (0, 0))))
-    far_body = swap_along(far_body, "depth", parts - 1)
+    far_body = swap_along(lax.dynamic_update_slice(far_body, sides[-1], (0, 0)), "depth", parts - 1)
 
     cell_shape = VMEM((knots + 2, cells, SUB, cols), jnp.float32)
     ends_shape = VMEM((parts + 2, 2, rows, cols), jnp.float32)

time: 41.4 us -> 37.8 us (0.913); the launches traced: 41.1 us -> 37.1 us
  waiting for transfers between devices: 3.79 us -> 0.27 us
  starting transfers between devices: 13.1 us -> 12.5 us
    ppermute x6, waiting for transfers between devices: 3.79 us -> 0.25 us  [swap_along(): lax.ppermute(block, axis, [(i, i ^ mask) for i in range(lax.axis_size(axi...]
    ppermute x6, starting transfers between devices: 8.79 us -> 8.15 us  [swap_along(): lax.ppermute(block, axis, [(i, i ^ mask) for i in range(lax.axis_size(axi...]
  transfers between devices with their start and end apart: 8 -> 8, of which waited for: 1 -> 1; matrix products, arithmetic and copies ran while one was open for 0% -> 0% of each run, Pallas kernels for 38% -> 42%
where the time goes in v6:
time: 37.8 us; the launch traced here: 37.1 us
  Pallas kernels  21.8 us (58%)
  starting transfers between devices  12.5 us (33%)
  local copies, waits for them, and re-layouts  1.77 us (5%)
  between operations  0.74 us (2%)
    pallas_call x1, Pallas kernels, on_device(): pl.pallas_call(functools.partial(near_kernel, parts), out_shape=array(par...  9.37 us
    ppermute x6, starting transfers between devices, swap_along(): lax.ppermute(block, axis, [(i, i ^ mask) for i in range(lax.axis_size(axi...  8.15 us
    pallas_call x1, Pallas kernels, on_device(): pl.pallas_call(functools.partial(far_kernel, parts), out_shape=array(pass...  5.83 us
    pallas_call x1, Pallas kernels, on_device(): pl.pallas_call(functools.partial(own_kernel, parts), out_shape=[array(val...  4.97 us
    ppermute x2, starting transfers between devices, shift_along(): return lax.ppermute(block, axis, route)  4.32 us
    unnamed x10, local copies, waits for them, and re-layouts  1.77 us
    pallas_call x1, Pallas kernels, on_device(): pl.pallas_call(functools.partial(edge_kernel, parts), out_shape=[array(ro...  1.16 us
  transfers between devices with their start and end apart: 8, of which 1 were waited for; matrix products, arithmetic and copies ran while one was open for 0% of the time, Pallas kernels for 42%

profile of v6, /device:TPU:0, one launch (start us, length us, event | category | flops | bytes accessed | tf_op | source)
XLA Modules:
  0.0 37.1 jit_solution(12493756285887809962)
XLA Ops:
  0.0 0.0 copy-start
  0.0 1.6 %copy-done = f32[16,256,128]{2,1,0:T(8,128)S(1)} copy-done((f32[16,256,128]{2,1,0:T(8,128)S(1)}, f32[16,256,128]{2,1,0:T(8,128)}, u32[]{:S(2)}) %copy-start) | copy-done | bytes 2097176
  1.6 0.4 %pack.1 = (f32[1064,128]{1,0:T(8,128)S(1)}, f32[1064,128]{1,0:T(8,128)S(1)}, f32[168,128]{1,0:T(8,128)S(1)}) custom-call(f32[16,256,128]{2,1,0:T(8,128)S(1)} %copy-done), custom_call_target="tpu_custom_call" | custom-call | flops 1000000000 | tf_op jit(solution)/shard_map/pack/pallas_call | solution.py:401
  2.0 0.0 copy-start.3
  2.0 0.0 copy-start.2
  2.0 0.0 copy-start.1
  2.0 4.0 %collective-permute-start.2 = (f32[168,128]{1,0:T(8,128)S(1)}, f32[168,128]{1,0:T(8,128)S(1)}, u32[]{:S(2)}, u32[]{:S(2)}) collective-permute-start(f32[168,128]{1,0:T(8,128)S(1)} %get-tuple-element.20), channel_id=1, source_target_pairs={{0,24},{8,16},{16,8},{24,0},{1,25},{9,17},{17,9},{25,1},{2,26},{10... | collective-permute-start | bytes 258056 | tf_op jit(solution)/shard_map/ppermute | solution.py:368
  6.0 0.5 %collective-permute-start.4 = (f32[1064,128]{1,0:T(8,128)S(1)}, f32[1064,128]{1,0:T(8,128)S(1)}, u32[]{:S(2)}, u32[]{:S(2)}) collective-permute-start(f32[1064,128]{1,0:T(8,128)S(1)} %get-tuple-element.23), channel_id=1, source_target_pairs={{0,16},{8,24},{16,0},{24,8},{1,17},{9,25},{17,1},{25,9},{2,18},{10... | collective-permute-start | bytes 1634312 | tf_op jit(solution)/shard_map/ppermute | solution.py:368
  6.5 0.1 collective-permute-start.3
  6.6 1.2 %edges.1 = (f32[64,128]{1,0:T(8,128)S(1)}, f32[1064,128]{1,0:T(8,128)S(1)}, f32[920,128]{1,0:T(8,128)S(1)}) custom-call(f32[16,256,128]{2,1,0:T(8,128)S(1)} %copy-done, f32[1064,128]{1,0:T(8,128)S(1)} %get-tuple-element.17._), custom_call_target="tpu_custom_call" | custom-call | flops 1000000000 | tf_op jit(solution)/shard_map/edges/pallas_call | solution.py:414
  7.8 1.3 %collective-permute-start.1 = (f32[64,128]{1,0:T(8,128)S(1)}, f32[64,128]{1,0:T(8,128)S(1)}, u32[]{:S(2)}, u32[]{:S(2)}) collective-permute-start(f32[64,128]{1,0:T(8,128)S(1)} %get-tuple-element.19), channel_id=1, source_target_pairs={{1,0},{2,1},{3,2},{4,3},{5,4},{6,5},{7,6},{9,8},{10,9},{11,10},{12... | collective-permute-start | bytes 98312 | tf_op jit(solution)/shard_map/ppermute | solution.py:364
  9.1 3.0 %collective-permute-start = (f32[64,128]{1,0:T(8,128)S(1)}, f32[64,128]{1,0:T(8,128)S(1)}, u32[]{:S(2)}, u32[]{:S(2)}) collective-permute-start(f32[64,128]{1,0:T(8,128)S(1)} %get-tuple-element.19), channel_id=1, source_target_pairs={{0,1},{1,2},{2,3},{3,4},{4,5},{5,6},{6,7},{8,9},{9,10},{10,11},{11... | collective-permute-start | bytes 98312 | tf_op jit(solution)/shard_map/ppermute | solution.py:364
  12.8 0.0 copy-done.3
  12.8 0.1 copy.6.lights_ref
  12.9 0.0 copy-done.2
  12.9 0.1 copy.7.curves_ref
  12.9 0.0 collective-permute-done.1.right_ref
  12.9 0.0 collective-permute-done.left_ref
  13.0 0.0 collective-permute-done.2._.refs_3_
  13.0 0.1 sides.1
  13.1 2.0 %collective-permute-start.6 = (f32[16,128]{1,0:T(8,128)S(1)}, f32[16,128]{1,0:T(8,128)S(1)}, u32[]{:S(2)}, u32[]{:S(2)}) collective-permute-start(f32[16,128]{1,0:T(8,128)S(1)} %get-tuple-element.27), channel_id=1, source_target_pairs={{0,8},{8,0},{16,24},{24,16},{1,9},{9,1},{17,25},{25,17},{2,10},{10... | collective-permute-start | bytes 24584 | tf_op jit(solution)/shard_map/ppermute | solution.py:368
  15.0 1.5 %collective-permute-start.7 = (f32[16,128]{1,0:T(8,128)S(1)}, f32[16,128]{1,0:T(8,128)S(1)}, u32[]{:S(2)}, u32[]{:S(2)}) collective-permute-start(f32[16,128]{1,0:T(8,128)S(1)} %get-tuple-element.28), channel_id=1, source_target_pairs={{0,16},{8,24},{16,0},{24,8},{1,17},{9,25},{17,1},{25,9},{2,18},{10... | collective-permute-start | bytes 24584 | tf_op jit(solution)/shard_map/ppermute | solution.py:368
  16.6 0.1 collective-permute-start.5
  16.6 0.0 copy-done.1
  16.6 5.0 %own.1 = (f32[36,64,128]{2,1,0:T(8,128)S(1)}, f32[4,35,8,128]{3,2,1,0:T(8,128)S(1)}) custom-call(s32[4]{0:T(128)S(1)} %copy-done.1, s32[1]{0:T(128)S(6)} %copy.9.flip_ref, f32[16,3]{1,0:T(8,128)S(1)} %copy.6.lights_ref, f32[16,4,8]{2,1,0:T(4,128)S(1)} %copy.7.curves_ref, f32[1064,128]{1,0:T(8,128)S(1)} %get-tuple-element.18.own_ref.refs_0_, ...), custom_call_target="tpu_custom_call" | custom-call | flops 4000000000 | tf_op jit(solution)/shard_map/own/pallas_call | solution.py:435
  21.6 0.0 collective-permute-done.6.refs_5_
  21.7 0.0 collective-permute-done.7.refs_6_
  21.7 0.0 collective-permute-done.4.refs_2_
  21.7 0.0 collective-permute-done.3.refs_1_
  21.7 9.4 %near.1.refs_5_ = f32[3,36,64,128]{3,2,1,0:T(8,128)S(1)} custom-call(s32[1]{0:T(128)S(6)} %copy.9.flip_ref, f32[4,35,8,128]{3,2,1,0:T(8,128)S(1)} %get-tuple-element.22.table_ref, f32[36,64,128]{2,1,0:T(8,128)S(1)} %get-tuple-element.26.inner_ref, f32[1064,128]{1,0:T(8,128)S(1)} %get-tuple-element.18.own_ref.refs_0_, ...), custom_call_target="tpu_custom_call" | custom-call | flops 60000002048 | tf_op jit(solution)/shard_map/near/pallas_call | solution.py:444
  31.0 0.2 collective-permute-done.5.refs_4_
  31.2 5.8 %far.1 = f32[4,4,64,128]{3,2,1,0:T(8,128)} custom-call(s32[1]{0:T(128)S(6)} %copy.9.flip_ref, f32[4,35,8,128]{3,2,1,0:T(8,128)S(1)} %get-tuple-element.22.table_ref, f32[1064,128]{1,0:T(8,128)S(1)} %get-tuple-element.18.own_ref.refs_0_, f32[1064,128]{1,0:T(8,128)S(1)} %collective-permute-done.3.refs_1_, f32[1064,128]{1,0:T(8,128)S(1)} %collective-permute-done.4.refs_2_, ...), custom_call_target="tpu_custom_call" | custom-call | flops 5000000000 | tf_op jit(solution)/shard_map/far/pallas_call | solution.py:453
  (1 shorter events, 0.0 us)
Async XLA Ops:
  0.0 1.6 %copy-start = (f32[16,256,128]{2,1,0:T(8,128)S(1)}, f32[16,256,128]{2,1,0:T(8,128)}, u32[]{:S(2)}) copy-start(f32[16,256,128]{2,1,0:T(8,128)} %field_ref.3) | copy-start | bytes 6291460
  2.0 10.8 %copy-start.3 = (f32[16,3]{0,1:T(4,128)S(1)}, f32[16,3]{0,1:T(4,128)}, u32[]{:S(2)}) copy-start(f32[16,3]{0,1:T(4,128)} %param.6) | copy-start | bytes 580
  2.0 10.9 %copy-start.2 = (f32[16,4,8]{0,2,1:T(8,128)S(1)}, f32[16,4,8]{0,2,1:T(8,128)}, u32[]{:S(2)}) copy-start(f32[16,4,8]{0,2,1:T(8,128)} %param.7) | copy-start | bytes 6148
  2.0 14.6 %copy-start.1 = (s32[4]{0:T(128)S(1)}, s32[4]{0:T(128)}, u32[]{:S(2)}) copy-start(s32[4]{0:T(128)} %index_ref.1) | copy-start | bytes 52
  2.0 11.0 %collective-permute-start.2 = (f32[168,128]{1,0:T(8,128)S(1)}, f32[168,128]{1,0:T(8,128)S(1)}, u32[]{:S(2)}, u32[]{:S(2)}) collective-permute-start(f32[168,128]{1,0:T(8,128)S(1)} %get-tuple-element.20), channel_id=1, source_target_pairs={{0,24},{8,16},{16,8},{24,0},{1,25},{9,17},{17,9},{25,1},{2,26},{10... | collective-permute-start | bytes 258056 | tf_op jit(solution)/shard_map/ppermute | solution.py:368
  6.0 15.7 %collective-permute-start.4 = (f32[1064,128]{1,0:T(8,128)S(1)}, f32[1064,128]{1,0:T(8,128)S(1)}, u32[]{:S(2)}, u32[]{:S(2)}) collective-permute-start(f32[1064,128]{1,0:T(8,128)S(1)} %get-tuple-element.23), channel_id=1, source_target_pairs={{0,16},{8,24},{16,0},{24,8},{1,17},{9,25},{17,1},{25,9},{2,18},{10... | collective-permute-start | bytes 1634312 | tf_op jit(solution)/shard_map/ppermute | solution.py:368
  6.5 15.2 %collective-permute-start.3 = (f32[1064,128]{1,0:T(8,128)S(1)}, f32[1064,128]{1,0:T(8,128)S(1)}, u32[]{:S(2)}, u32[]{:S(2)}) collective-permute-start(f32[1064,128]{1,0:T(8,128)S(1)} %get-tuple-element.17._), channel_id=1, source_target_pairs={{0,8},{8,0},{16,24},{24,16},{1,9},{9,1},{17,25},{25,17},{2,10},{10... | collective-permute-start | bytes 1634312 | tf_op jit(solution)/shard_map/ppermute | solution.py:368
  7.8 5.2 %collective-permute-start.1 = (f32[64,128]{1,0:T(8,128)S(1)}, f32[64,128]{1,0:T(8,128)S(1)}, u32[]{:S(2)}, u32[]{:S(2)}) collective-permute-start(f32[64,128]{1,0:T(8,128)S(1)} %get-tuple-element.19), channel_id=1, source_target_pairs={{1,0},{2,1},{3,2},{4,3},{5,4},{6,5},{7,6},{9,8},{10,9},{11,10},{12... | collective-permute-start | bytes 98312 | tf_op jit(solution)/shard_map/ppermute | solution.py:364
  9.1 3.9 %collective-permute-start = (f32[64,128]{1,0:T(8,128)S(1)}, f32[64,128]{1,0:T(8,128)S(1)}, u32[]{:S(2)}, u32[]{:S(2)}) collective-permute-start(f32[64,128]{1,0:T(8,128)S(1)} %get-tuple-element.19), channel_id=1, source_target_pairs={{0,1},{1,2},{2,3},{3,4},{4,5},{5,6},{6,7},{8,9},{9,10},{10,11},{11... | collective-permute-start | bytes 98312 | tf_op jit(solution)/shard_map/ppermute | solution.py:364
  13.1 8.6 %collective-permute-start.6 = (f32[16,128]{1,0:T(8,128)S(1)}, f32[16,128]{1,0:T(8,128)S(1)}, u32[]{:S(2)}, u32[]{:S(2)}) collective-permute-start(f32[16,128]{1,0:T(8,128)S(1)} %get-tuple-element.27), channel_id=1, source_target_pairs={{0,8},{8,0},{16,24},{24,16},{1,9},{9,1},{17,25},{25,17},{2,10},{10... | collective-permute-start | bytes 24584 | tf_op jit(solution)/shard_map/ppermute | solution.py:368
  15.0 6.6 %collective-permute-start.7 = (f32[16,128]{1,0:T(8,128)S(1)}, f32[16,128]{1,0:T(8,128)S(1)}, u32[]{:S(2)}, u32[]{:S(2)}) collective-permute-start(f32[16,128]{1,0:T(8,128)S(1)} %get-tuple-element.28), channel_id=1, source_target_pairs={{0,16},{8,24},{16,0},{24,8},{1,17},{9,25},{17,1},{25,9},{2,18},{10... | collective-permute-start | bytes 24584 | tf_op jit(solution)/shard_map/ppermute | solution.py:368
  16.6 14.7 %collective-permute-start.5 = (f32[920,128]{1,0:T(8,128)S(1)}, f32[920,128]{1,0:T(8,128)S(1)}, u32[]{:S(2)}, u32[]{:S(2)}) collective-permute-start(f32[920,128]{1,0:T(8,128)S(1)} %constant_dynamic-update-slice_fusion), channel_id=1, source_target_pairs={{0,24},{8,16},{16,8},{24,0},{1,25},{9,17},{17,9},{25,1},{2,26},{10... | collective-permute-start | bytes 1413128 | tf_op jit(solution)/shard_map/ppermute | solution.py:368

commit v7 on v6

--- a/solution.py
+++ b/solution.py
@@ -13,6 +13,7 @@
 VMEM = pltpu.VMEM
 SMEM = pltpu.SMEM
 MIB = 1 << 20
+FINE = 49152.0
 
 
 def pack_kernel(parts, field_ref, *refs):
@@ -122,24 +123,35 @@
         ends_ref[(me ^ m) + 1, 1] = heads[m][2 * cells + last : 2 * cells + last + rows, :]
 
 
-def fill_table(index_ref, lights_ref, curves_ref, scale, table_ref):
+def fill_weights(index_ref, curves_ref, scale, weight_ref):
     passes = index_ref.shape[0]
     channels, knots = curves_ref.shape[1:]
-    shape = table_ref.shape[2:]
-    for p in range(passes):
-        chosen = index_ref[p]
-        for axis in range(3):
-            table_ref[p, axis] = jnp.full(shape, lights_ref[chosen, axis])
-        for channel in range(channels):
-            factor = scale if channel == channels - 1 else 1.0
-            points = [curves_ref[chosen, channel, k] * factor for k in range(knots)]
-            slopes = [points[k + 1] - points[k] for k in range(knots - 1)]
-            bends = [points[0], slopes[0]] + [slopes[k] - slopes[k - 1] for k in range(1, knots - 1)]
+    shape = (2 * SUB, weight_ref.shape[1])
+    row = lax.broadcasted_iota(jnp.int32, shape, 0)
+    lane = lax.broadcasted_iota(jnp.int32, shape, 1)
+    block = knots * SUB
+    knot = lane // SUB
+    on_row = lane % SUB == row % SUB
+    zero = jnp.zeros(shape, jnp.float32)
+    for pair in range(passes * channels // 2):
+        halves = []
+        for channel in (2 * pair, 2 * pair + 1):
+            chosen = index_ref[channel // channels]
+            factor = scale if channel % channels == channels - 1 else 1.0
+            points = [curves_ref[chosen, channel % channels, k] * factor for k in range(knots)]
+            half = zero
             for k in range(knots):
-                table_ref[p, 3 + channel * knots + k] = jnp.full(shape, bends[k])
-
-
-def prepare_steps(m, zs, head, places, lateral, base, cells, rows, parts, knots, cols, ends_ref, cell_ref):
+                half = jnp.where(jnp.logical_or(knot == k, knot == k + 2 * knots), points[k], half)
+                if k + 1 < knots:
+                    half = jnp.where(knot == k + knots, points[k + 1] - points[k], half)
+            halves.append(half)
+        value = jnp.where(on_row, jnp.where(row < SUB, halves[0], halves[1]), zero)
+        coarse = value.astype(jnp.bfloat16).astype(jnp.float32)
+        value = jnp.where(lane < 2 * block, value, value - coarse)
+        weight_ref[2 * pair * SUB : 2 * (pair + 1) * SUB, :] = value.astype(jnp.bfloat16)
+
+
+def prepare_steps(m, zs, head, places, lateral, base, cells, rows, parts, cols, ends_ref, weight_ref, cell_ref, mixed_ref):
     me = lax.axis_index("depth")
     part = me ^ m
     at = pl.ds(base, SUB)
@@ -173,73 +185,80 @@
         grad_y = lower - upper
         grad_z = layer(z + 1) - layer(z - 1)
         inverse = lax.rsqrt(grad_x * grad_x + grad_y * grad_y + grad_z * grad_z + 4.0)
-        half = 0.5 * (knots - 1)
-        position = half + half * jnp.tanh(0.5 * here)
         cell_ref[0, z] = grad_x * inverse
         cell_ref[1, z] = grad_y * inverse
         cell_ref[2, z] = grad_z * inverse
-        cell_ref[3, z] = position
-        for k in range(1, knots - 1):
-            cell_ref[3 + k, z] = jnp.maximum(position - k, 0.0)
-
-    return [functools.partial(step, z) for z in zs]
-
-
-def tree(terms):
-    while len(terms) > 1:
-        terms = [sum(terms[j + 1 : j + 2], terms[j]) for j in range(0, len(terms), 2)]
-    return terms[0]
-
-
-def march_unit(flip, table_ref, zs, cells, knots, cell_ref, beside, inner=None):
-    passes = table_ref.shape[0]
-    shape = table_ref.shape[2:]
-    zero = jnp.zeros(shape, jnp.float32)
-    curve_at = 3 + 3 * knots
-    result = []
-    beside = list(beside)
-    for low in range(0, passes, 2):
-        group = range(low, min(low + 2, passes))
-        vector = {p: [table_ref[p, axis] for axis in range(3)] for p in group}
-        curve = {p: [table_ref[p, curve_at + k] for k in range(knots)] for p in group}
-        state = {p: (jnp.ones(shape, jnp.float32), [zero] * knots) for p in group}
-        share = -(-len(beside) * 2 // max(passes - low, 1))
-        mine, beside = beside[:share], beside[share:]
-        for u, spot in enumerate(zs):
-            for step in mine[u * share // len(zs) : (u + 1) * share // len(zs)]:
-                step()
-            z = spot + flip * (cells - 1 - 2 * spot)
-            hinges = [cell_ref[3 + k, z] for k in range(knots - 1)]
-            normal = [cell_ref[axis, z] for axis in range(3)]
-            for p in group:
-                keep, sums = state[p]
-                opacity = tree([curve[p][0]] + [curve[p][k + 1] * hinges[k] for k in range(knots - 1)])
-                facing = normal[0] * vector[p][0] + normal[1] * vector[p][1] + normal[2] * vector[p][2]
-                taken = keep * opacity
-                weight = taken * (AMBIENT + jnp.abs(facing))
-                sums = [sums[0] + weight] + [sums[k + 1] + weight * hinges[k] for k in range(knots - 1)]
-                keep = keep - taken
-                if inner is not None and u == 0:
-                    keep, sums = keep * inner(p, 0), [total + keep * inner(p, j + 1) for j, total in enumerate(sums)]
-                state[p] = (keep, sums)
-        result += [[state[p][0]] + state[p][1] for p in group]
-    return result
-
-
-def own_kernel(parts, index_ref, flip_ref, lights_ref, curves_ref, own_ref, lateral_ref, out_ref, table_ref, *cell_refs):
+        half = 0.5 * (knots - 1)
+        position = half + half * jnp.tanh(0.5 * here)
+        coarse = (position + FINE) - FINE
+        segment = jnp.minimum(jnp.floor(position), knots - 2.0)
+        rest = position - coarse
+        right = coarse - segment
+        left = 1.0 - right
+        zero = jnp.zeros_like(here)
+        is_at = [segment == k for k in range(knots - 1)]
+        tents = [jnp.where(is_at[0], left, zero)]
+        tents += [jnp.where(is_at[k], left, jnp.where(is_at[k - 1], right, zero)) for k in range(1, knots - 1)]
+        tents += [jnp.where(is_at[knots - 2], right, zero)]
+        rests = [jnp.where(is_at[k], rest, zero) for k in range(knots - 1)] + [zero]
+        return [jnp.concatenate(part, axis=0).astype(jnp.bfloat16) for part in (tents, rests)]
+
+    def two(first, second):
+        tents, rests = [jnp.concatenate(both, axis=1) for both in zip(step(first), step(second))]
+        right = jnp.concatenate([tents, rests, tents], axis=0)
+        mixed = jnp.dot(weight_ref[...], right, preferred_element_type=jnp.float32)
+        mixed_ref[first] = mixed[:, :cols]
+        mixed_ref[second] = mixed[:, cols:]
+
+    knots = weight_ref.shape[1] // (3 * SUB)
+    zs = list(zs)
+    return [functools.partial(two, *zs[i : i + 2]) for i in range(0, len(zs), 2)]
+
+
+def march_unit(flip, vector_ref, zs, cells, cell_ref, mixed_ref, beside, inner=None):
+    passes = vector_ref.shape[0]
+    channels = mixed_ref.shape[1] // (passes * SUB)
+    shape = vector_ref.shape[2:]
+    vectors = [[vector_ref[p, axis] for axis in range(3)] for p in range(passes)]
+    state = [(jnp.ones(shape, jnp.float32), [jnp.zeros(shape, jnp.float32)] * 3)] * passes
+    count = len(beside)
+    for u, spot in enumerate(zs):
+        for step in beside[u * count // len(zs) : (u + 1) * count // len(zs)]:
+            step()
+        z = spot + flip * (cells - 1 - 2 * spot)
+        normal = [cell_ref[axis, z] for axis in range(3)]
+        for p in range(passes):
+            keep, sums = state[p]
+            mixed = [mixed_ref[z, (p * channels + c) * SUB : (p * channels + c + 1) * SUB, :] for c in range(channels)]
+            facing = normal[0] * vectors[p][0] + normal[1] * vectors[p][1] + normal[2] * vectors[p][2]
+            taken = keep * mixed[3]
+            weight = taken * (AMBIENT + jnp.abs(facing))
+            sums = [total + weight * tint for total, tint in zip(sums, mixed)]
+            keep = keep - taken
+            if inner is not None and u == 0:
+                keep, sums = keep * inner(p, 0), [total + keep * inner(p, j + 1) for j, total in enumerate(sums)]
+            state[p] = (keep, sums)
+    return [[keep] + sums for keep, sums in state]
+
+
+def own_kernel(parts, index_ref, flip_ref, lights_ref, curves_ref, own_ref, lateral_ref, out_ref, vector_ref, weight_ref, *refs):
+    cell_refs, mixed_refs = refs[:2], refs[2:]
     rows, cols = out_ref.shape[1:]
-    knots = curves_ref.shape[2]
+    channels = curves_ref.shape[1]
     passes = index_ref.shape[0]
     cells = cell_refs[0].shape[1]
     flip = flip_ref[0]
     tiles = rows // SUB
     inner = range(1, cells - 1)
-    fill_table(index_ref, lights_ref, curves_ref, OPACITY / (parts * cells), table_ref)
+    for p in range(passes):
+        for axis in range(3):
+            vector_ref[p, axis] = jnp.full((SUB, cols), lights_ref[index_ref[p], axis])
+    fill_weights(index_ref, curves_ref, OPACITY / (parts * cells), weight_ref)
     places = near_places(cells, rows, own_ref)
 
     def prepare(base, slot):
         return prepare_steps(
-            0, inner, own_ref, places, lateral_ref, base, cells, rows, parts, knots, cols, None, cell_refs[slot]
+            0, inner, own_ref, places, lateral_ref, base, cells, rows, parts, cols, None, weight_ref, cell_refs[slot], mixed_refs[slot]
         )
 
     for step in prepare(0, 0):
@@ -249,23 +268,23 @@
         for slot in range(2):
             base = pl.multiple_of((2 * i + slot) * SUB, SUB)
             after = pl.multiple_of(jnp.minimum(2 * i + slot + 1, tiles - 1) * SUB, SUB)
-            result = march_unit(flip, table_ref, inner, cells, knots, cell_refs[slot], prepare(after, 1 - slot))
+            result = march_unit(flip, vector_ref, inner, cells, cell_refs[slot], mixed_refs[slot], prepare(after, 1 - slot))
             for p in range(passes):
-                for j in range(knots + 1):
-                    out_ref[p * (knots + 1) + j, pl.ds(base, SUB), :] = result[p][j]
+                for j in range(channels):
+                    out_ref[p * channels + j, pl.ds(base, SUB), :] = result[p][j]
         return carry
 
     lax.fori_loop(0, tiles // 2, pair, 0)
 
 
-def near_kernel(parts, flip_ref, table_ref, inner_ref, *refs):
+def near_kernel(parts, flip_ref, vector_ref, weight_ref, inner_ref, *refs):
     count = parts - 1
     heads, laterals, out_ref, ends_ref = refs[:parts], refs[parts : 2 * parts - 1], refs[2 * parts - 1], refs[2 * parts]
-    cell_refs = refs[2 * parts + 1 :]
+    cell_refs, mixed_refs = refs[2 * parts + 1 : 2 * parts + 1 + count], refs[2 * parts + 1 + count :]
     rows, cols = out_ref.shape[2:]
     cells = cell_refs[0].shape[1]
-    passes = table_ref.shape[0]
-    knots = inner_ref.shape[0] // passes - 1
+    passes = vector_ref.shape[0]
+    channels = inner_ref.shape[0] // passes
     flip = flip_ref[0]
     tiles = rows // SUB
     zs = [(0, cells - 1)] + [range(cells)] * (count - 1)
@@ -274,7 +293,7 @@
 
     def prepare(m, base):
         return prepare_steps(
-            m, zs[m], heads[m], places[m], laterals[m], base, cells, rows, parts, knots, cols, ends_ref, cell_refs[m]
+            m, zs[m], heads[m], places[m], laterals[m], base, cells, rows, parts, cols, ends_ref, weight_ref, cell_refs[m], mixed_refs[m]
         )
 
     for step in prepare(0, 0):
@@ -286,11 +305,11 @@
         at = pl.ds(base, SUB)
         for m in range(count):
             beside = prepare(m + 1, base) if m + 1 < count else prepare(0, after)
-            inner = (lambda p, j: inner_ref[p * (knots + 1) + j, at, :]) if m == 0 else None
-            result = march_unit(flip, table_ref, zs[m], cells, knots, cell_refs[m], beside, inner)
+            inner = (lambda p, j: inner_ref[p * channels + j, at, :]) if m == 0 else None
+            result = march_unit(flip, vector_ref, zs[m], cells, cell_refs[m], mixed_refs[m], beside, inner)
             for p in range(passes):
-                for j in range(knots + 1):
-                    out_ref[m, p * (knots + 1) + j, at, :] = result[p][j]
+                for j in range(channels):
+                    out_ref[m, p * channels + j, at, :] = result[p][j]
         return carry
 
     lax.fori_loop(0, tiles, tile, 0)
@@ -304,13 +323,12 @@
     return [one[0] * other[0]] + [scale_one * a + scale_other * b for a, b in zip(one[1:], other[1:])]
 
 
-def far_kernel(parts, flip_ref, table_ref, *refs):
+def far_kernel(parts, flip_ref, vector_ref, weight_ref, *refs):
     heads, body, states, out_ref, picture_ref, ends_ref, sems = refs[:parts], *refs[parts : parts + 6]
-    cell_refs = refs[parts + 6 :]
-    rows, cols = out_ref.shape[2:]
+    cell_refs, mixed_refs = refs[parts + 6 : parts + 8], refs[parts + 8 :]
+    channels, rows, cols = out_ref.shape[1:]
     cells = cell_refs[0].shape[1]
-    passes = table_ref.shape[0]
-    knots = states.shape[1] // passes - 1
+    passes = vector_ref.shape[0]
     flip = flip_ref[0]
     me = lax.axis_index("depth")
     places = far_places(cells, rows, parts, heads[-1], body)
@@ -319,7 +337,7 @@
 
     def prepare(base, slot):
         return prepare_steps(
-            parts - 1, range(cells), heads[-1], places, body, base, cells, rows, parts, knots, cols, ends_ref, cell_refs[slot]
+            parts - 1, range(cells), heads[-1], places, body, base, cells, rows, parts, cols, ends_ref, weight_ref, cell_refs[slot], mixed_refs[slot]
         )
 
     def send(index):
@@ -329,17 +347,16 @@
     def finish(result, index):
         at = pl.ds(pl.multiple_of(index * SUB, SUB), SUB)
         for p in range(passes):
-            images = [[states[m, p * (knots + 1) + j, at, :] for j in range(knots + 1)] for m in range(parts - 1)]
+            images = [[states[m, p * channels + j, at, :] for j in range(channels)] for m in range(parts - 1)]
             images.append(result[p])
             bit = 0
             while len(images) > 1:
                 leads = ((me >> bit) & 1) == flip
                 images = [over_either(leads, images[j], images[j + 1]) for j in range(0, len(images), 2)]
                 bit += 1
-            keep, sums = images[0][0], images[0][1:]
             for channel in range(3):
-                picture_ref[p, channel, at, :] = tree([table_ref[p, 3 + channel * knots + k] * sums[k] for k in range(knots)])
-            picture_ref[p, 3, at, :] = 1.0 - keep
+                picture_ref[p, channel, at, :] = images[0][channel + 1]
+            picture_ref[p, 3, at, :] = 1.0 - images[0][0]
         send(index).start()
 
     for step in prepare(0, 0):
@@ -349,7 +366,7 @@
         for slot in range(2):
             index = 2 * i + slot
             after = pl.multiple_of(jnp.minimum(index + 1, tiles - 1) * SUB, SUB)
-            result = march_unit(flip, table_ref, range(cells), cells, knots, cell_refs[slot], prepare(after, 1 - slot))
+            result = march_unit(flip, vector_ref, range(cells), cells, cell_refs[slot], mixed_refs[slot], prepare(after, 1 - slot))
             finish(result, index)
         return carry
 
@@ -379,7 +396,7 @@
     passes = light_index.shape[0]
     channels, knots = transfer.shape[1:]
     tiles = rows // SUB
-    values = passes * (knots + 1)
+    values = passes * channels
     in_vmem = pl.BlockSpec(memory_space=VMEM)
     in_smem = pl.BlockSpec(memory_space=SMEM)
     in_any = pl.BlockSpec(memory_space=pl.ANY)
@@ -430,40 +447,43 @@
     laterals = [swap_along(sides[m], "depth", m) for m in range(1, parts - 1)]
     far_body = swap_along(lax.dynamic_update_slice(far_body, sides[-1], (0, 0)), "depth", parts - 1)
 
-    cell_shape = VMEM((knots + 2, cells, SUB, cols), jnp.float32)
+    cell_shape = VMEM((3, cells, SUB, cols), jnp.float32)
+    mixed_shape = VMEM((cells, values * SUB, cols), jnp.float32)
     ends_shape = VMEM((parts + 2, 2, rows, cols), jnp.float32)
-    inner, table = pl.pallas_call(
+    weight_shape = jax.ShapeDtypeStruct((values * SUB, 3 * knots * SUB), jnp.bfloat16)
+    inner, vectors, weights = pl.pallas_call(
         functools.partial(own_kernel, parts),
-        out_shape=[array(values, rows, cols), array(passes, 3 + channels * knots, SUB, cols)],
+        out_shape=[array(values, rows, cols), array(passes, 3, SUB, cols), weight_shape],
         in_specs=[in_smem] * 4 + [in_vmem] * 2,
-        out_specs=[in_vmem] * 2,
-        scratch_shapes=[cell_shape] * 2,
+        out_specs=[in_vmem] * 3,
+        scratch_shapes=[cell_shape] * 2 + [mixed_shape] * 2,
         name="own",
-        **settings(8, 4),
+        **settings(12, 4),
     )(light_index, flips, light_vectors, transfer, own, sides[0])
     states = pl.pallas_call(
         functools.partial(near_kernel, parts),
         out_shape=array(parts - 1, values, rows, cols),
-        in_specs=[in_smem] + [in_vmem] * (2 * parts + 1),
+        in_specs=[in_smem] + [in_vmem] * (2 * parts + 2),
         out_specs=in_vmem,
-        scratch_shapes=[ends_shape] + [cell_shape] * (parts - 1),
+        scratch_shapes=[ends_shape] + [cell_shape] * (parts - 1) + [mixed_shape] * (parts - 1),
         name="near",
         **settings(16, 60),
-    )(flips, table, inner, own, *near, far_head, sides[0], *laterals)
+    )(flips, vectors, weights, inner, own, *near, far_head, sides[0], *laterals)
     return pl.pallas_call(
         functools.partial(far_kernel, parts),
         out_shape=array(passes, channels, rows, cols),
-        in_specs=[in_smem] + [in_vmem] * (parts + 3),
+        in_specs=[in_smem] + [in_vmem] * (parts + 4),
         out_specs=in_any,
         scratch_shapes=[
             VMEM((passes, channels, rows, cols), jnp.float32),
             ends_shape,
             pltpu.SemaphoreType.DMA((tiles,)),
         ]
-        + [cell_shape] * 2,
+        + [cell_shape] * 2
+        + [mixed_shape] * 2,
         name="far",
         **settings(16, 5),
-    )(flips, table, own, *near, far_head, far_body, states)
+    )(flips, vectors, weights, own, *near, far_head, far_body, states)
 
 
 def solution(mesh):

time: 37.8 us -> 35.6 us (0.942); the launches traced: 37.1 us -> 35.4 us
  Pallas kernels: 21.8 us -> 16.6 us
  waiting for transfers between devices: 0.27 us -> 3.81 us
    ppermute x6, waiting for transfers between devices: 0.25 us -> 3.79 us  [swap_along(): lax.ppermute(block, axis, [(i, i ^ mask) for i in range(lax.axis_size(axi...]
    pallas_call x1, Pallas kernels: 9.37 us -> 6.45 us  [on_device(): pl.pallas_call(functools.partial(near_kernel, parts), out_shape=array(par...]
    pallas_call x1, Pallas kernels: 5.83 us -> 4.14 us  [on_device(): pl.pallas_call(functools.partial(far_kernel, parts), out_shape=array(pass...]
    pallas_call x1, Pallas kernels: 4.97 us -> 4.34 us  [on_device(): pl.pallas_call(functools.partial(own_kernel, parts), out_shape=[array(val...]
  transfers between devices with their start and end apart: 8 -> 8, of which waited for: 1 -> 2; matrix products, arithmetic and copies ran while one was open for 0% -> 0% of each run, Pallas kernels for 42% -> 34%
where the time goes in v7:
time: 35.6 us; the launch traced here: 35.4 us
  Pallas kernels  16.6 us (47%)
  starting transfers between devices  12.5 us (35%)
  waiting for transfers between devices  3.81 us (11%)
  local copies, waits for them, and re-layouts  1.77 us (5%)
  between operations  0.75 us (2%)
    ppermute x6, starting transfers between devices, swap_along(): lax.ppermute(block, axis, [(i, i ^ mask) for i in range(lax.axis_size(axi...  8.15 us
    pallas_call x1, Pallas kernels, on_device(): pl.pallas_call(functools.partial(near_kernel, parts), out_shape=array(par...  6.45 us
    pallas_call x1, Pallas kernels, on_device(): pl.pallas_call(functools.partial(own_kernel, parts), out_shape=[array(val...  4.34 us
    ppermute x2, starting transfers between devices, shift_along(): return lax.ppermute(block, axis, route)  4.32 us
    pallas_call x1, Pallas kernels, on_device(): pl.pallas_call(functools.partial(far_kernel, parts), out_shape=array(pass...  4.14 us
    ppermute x6, waiting for transfers between devices, swap_along(): lax.ppermute(block, axis, [(i, i ^ mask) for i in range(lax.axis_size(axi...  3.79 us
    unnamed x10, local copies, waits for them, and re-layouts  1.77 us
    pallas_call x1, Pallas kernels, on_device(): pl.pallas_call(functools.partial(edge_kernel, parts), out_shape=[array(ro...  1.16 us
  transfers between devices with their start and end apart: 8, of which 2 were waited for; matrix products, arithmetic and copies ran while one was open for 0% of the time, Pallas kernels for 34%

profile of v7, /device:TPU:0, one launch (start us, length us, event | category | flops | bytes accessed | tf_op | source)
XLA Modules:
  0.0 35.4 jit_solution(13386034762086422324)
XLA Ops:
  0.0 0.0 copy-start
  0.0 1.6 %copy-done = f32[16,256,128]{2,1,0:T(8,128)S(1)} copy-done((f32[16,256,128]{2,1,0:T(8,128)S(1)}, f32[16,256,128]{2,1,0:T(8,128)}, u32[]{:S(2)}) %copy-start) | copy-done | bytes 2097176
  1.6 0.4 %pack.1 = (f32[1064,128]{1,0:T(8,128)S(1)}, f32[1064,128]{1,0:T(8,128)S(1)}, f32[168,128]{1,0:T(8,128)S(1)}) custom-call(f32[16,256,128]{2,1,0:T(8,128)S(1)} %copy-done), custom_call_target="tpu_custom_call" | custom-call | flops 1000000000 | tf_op jit(solution)/shard_map/pack/pallas_call | solution.py:418
  2.0 0.0 copy-start.3
  2.0 0.0 copy-start.2
  2.0 0.0 copy-start.1
  2.0 4.0 %collective-permute-start.2 = (f32[168,128]{1,0:T(8,128)S(1)}, f32[168,128]{1,0:T(8,128)S(1)}, u32[]{:S(2)}, u32[]{:S(2)}) collective-permute-start(f32[168,128]{1,0:T(8,128)S(1)} %get-tuple-element.21), channel_id=1, source_target_pairs={{0,24},{8,16},{16,8},{24,0},{1,25},{9,17},{17,9},{25,1},{2,26},{10... | collective-permute-start | bytes 258056 | tf_op jit(solution)/shard_map/ppermute | solution.py:385
  6.0 0.5 %collective-permute-start.4 = (f32[1064,128]{1,0:T(8,128)S(1)}, f32[1064,128]{1,0:T(8,128)S(1)}, u32[]{:S(2)}, u32[]{:S(2)}) collective-permute-start(f32[1064,128]{1,0:T(8,128)S(1)} %get-tuple-element.25), channel_id=1, source_target_pairs={{0,16},{8,24},{16,0},{24,8},{1,17},{9,25},{17,1},{25,9},{2,18},{10... | collective-permute-start | bytes 1634312 | tf_op jit(solution)/shard_map/ppermute | solution.py:385
  6.5 0.1 collective-permute-start.3
  6.6 1.2 %edges.1 = (f32[64,128]{1,0:T(8,128)S(1)}, f32[1064,128]{1,0:T(8,128)S(1)}, f32[920,128]{1,0:T(8,128)S(1)}) custom-call(f32[16,256,128]{2,1,0:T(8,128)S(1)} %copy-done, f32[1064,128]{1,0:T(8,128)S(1)} %get-tuple-element.18._), custom_call_target="tpu_custom_call" | custom-call | flops 1000000000 | tf_op jit(solution)/shard_map/edges/pallas_call | solution.py:431
  7.8 1.3 %collective-permute-start.1 = (f32[64,128]{1,0:T(8,128)S(1)}, f32[64,128]{1,0:T(8,128)S(1)}, u32[]{:S(2)}, u32[]{:S(2)}) collective-permute-start(f32[64,128]{1,0:T(8,128)S(1)} %get-tuple-element.20), channel_id=1, source_target_pairs={{1,0},{2,1},{3,2},{4,3},{5,4},{6,5},{7,6},{9,8},{10,9},{11,10},{12... | collective-permute-start | bytes 98312 | tf_op jit(solution)/shard_map/ppermute | solution.py:381
  9.1 3.0 %collective-permute-start = (f32[64,128]{1,0:T(8,128)S(1)}, f32[64,128]{1,0:T(8,128)S(1)}, u32[]{:S(2)}, u32[]{:S(2)}) collective-permute-start(f32[64,128]{1,0:T(8,128)S(1)} %get-tuple-element.20), channel_id=1, source_target_pairs={{0,1},{1,2},{2,3},{3,4},{4,5},{5,6},{6,7},{8,9},{9,10},{10,11},{11... | collective-permute-start | bytes 98312 | tf_op jit(solution)/shard_map/ppermute | solution.py:381
  12.8 0.0 copy-done.3
  12.8 0.1 copy.6.lights_ref
  12.9 0.0 copy-done.2
  12.9 0.1 copy.7.curves_ref
  12.9 0.0 collective-permute-done.1.right_ref
  12.9 0.0 collective-permute-done.left_ref
  13.0 0.0 collective-permute-done.2._.refs_3_
  13.0 0.1 sides.1
  13.1 2.0 %collective-permute-start.6 = (f32[16,128]{1,0:T(8,128)S(1)}, f32[16,128]{1,0:T(8,128)S(1)}, u32[]{:S(2)}, u32[]{:S(2)}) collective-permute-start(f32[16,128]{1,0:T(8,128)S(1)} %get-tuple-element.29), channel_id=1, source_target_pairs={{0,8},{8,0},{16,24},{24,16},{1,9},{9,1},{17,25},{25,17},{2,10},{10... | collective-permute-start | bytes 24584 | tf_op jit(solution)/shard_map/ppermute | solution.py:385
  15.0 1.5 %collective-permute-start.7 = (f32[16,128]{1,0:T(8,128)S(1)}, f32[16,128]{1,0:T(8,128)S(1)}, u32[]{:S(2)}, u32[]{:S(2)}) collective-permute-start(f32[16,128]{1,0:T(8,128)S(1)} %get-tuple-element.30), channel_id=1, source_target_pairs={{0,16},{8,24},{16,0},{24,8},{1,17},{9,25},{17,1},{25,9},{2,18},{10... | collective-permute-start | bytes 24584 | tf_op jit(solution)/shard_map/ppermute | solution.py:385
  16.6 0.1 collective-permute-start.5
  16.6 0.0 copy-done.1
  16.6 4.3 %own.1 = (f32[16,64,128]{2,1,0:T(8,128)S(1)}, f32[4,3,8,128]{3,2,1,0:T(8,128)S(1)}, bf16[128,192]{1,0:T(8,128)(2,1)S(1)}) custom-call(s32[4]{0:T(128)S(1)} %copy-done.1, s32[1]{0:T(128)S(6)} %copy.9.flip_ref, f32[16,3]{1,0:T(8,128)S(1)} %copy.6.lights_ref, f32[16,4,8]{2,1,0:T(4,128)S(1)} %copy.7.curves_ref, ...), custom_call_target="tpu_custom_call" | custom-call | flops 4000000000 | tf_op jit(solution)/shard_map/own/pallas_call | solution.py:454
  21.0 0.7 %collective-permute-done.6.refs_5_ = f32[16,128]{1,0:T(8,128)S(1)} collective-permute-done((f32[16,128]{1,0:T(8,128)S(1)}, f32[16,128]{1,0:T(8,128)S(1)}, u32[]{:S(2)}, u32[]{:S(2)}) %collective-permute-start.6) | collective-permute-done | bytes 8224 | tf_op jit(solution)/shard_map/ppermute | solution.py:385
  21.7 0.0 collective-permute-done.7.refs_6_
  21.7 0.0 collective-permute-done.4.refs_2_
  21.7 0.0 collective-permute-done.3.refs_1_
  21.7 6.5 %near.1.refs_5_ = f32[3,16,64,128]{3,2,1,0:T(8,128)S(1)} custom-call(s32[1]{0:T(128)S(6)} %copy.9.flip_ref, f32[4,3,8,128]{3,2,1,0:T(8,128)S(1)} %get-tuple-element.23.vector_ref, bf16[128,192]{1,0:T(8,128)(2,1)S(1)} %get-tuple-element.24.weight_ref, f32[16,64,128]{2,1,0:T(8,128)S(1)} %get-tuple-element.28.inner_ref, ...), custom_call_target="tpu_custom_call" | custom-call | flops 60000002048 | tf_op jit(solution)/shard_map/near/pallas_call | solution.py:463
  28.1 3.1 %collective-permute-done.5.refs_4_ = f32[920,128]{1,0:T(8,128)S(1)} collective-permute-done((f32[920,128]{1,0:T(8,128)S(1)}, f32[920,128]{1,0:T(8,128)S(1)}, u32[]{:S(2)}, u32[]{:S(2)}) %collective-permute-start.5) | collective-permute-done | bytes 471072 | tf_op jit(solution)/shard_map/ppermute | solution.py:385
  31.2 4.1 %far.1 = f32[4,4,64,128]{3,2,1,0:T(8,128)} custom-call(s32[1]{0:T(128)S(6)} %copy.9.flip_ref, f32[4,3,8,128]{3,2,1,0:T(8,128)S(1)} %get-tuple-element.23.vector_ref, bf16[128,192]{1,0:T(8,128)(2,1)S(1)} %get-tuple-element.24.weight_ref, f32[1064,128]{1,0:T(8,128)S(1)} %get-tuple-element.19.own_ref.refs_0_, f32[1064,128]{1,0:T(8,128)S(1)} %collective-permute-done.3.refs_1_, ...), custom_call_target="tpu_custom_call" | custom-call | flops 5000000000 | tf_op jit(solution)/shard_map/far/pallas_call | solution.py:472
  (1 shorter events, 0.0 us)
Async XLA Ops:
  0.0 1.6 %copy-start = (f32[16,256,128]{2,1,0:T(8,128)S(1)}, f32[16,256,128]{2,1,0:T(8,128)}, u32[]{:S(2)}) copy-start(f32[16,256,128]{2,1,0:T(8,128)} %field_ref.3) | copy-start | bytes 6291460
  2.0 10.8 %copy-start.3 = (f32[16,3]{0,1:T(4,128)S(1)}, f32[16,3]{0,1:T(4,128)}, u32[]{:S(2)}) copy-start(f32[16,3]{0,1:T(4,128)} %param.6) | copy-start | bytes 580
  2.0 10.9 %copy-start.2 = (f32[16,4,8]{0,2,1:T(8,128)S(1)}, f32[16,4,8]{0,2,1:T(8,128)}, u32[]{:S(2)}) copy-start(f32[16,4,8]{0,2,1:T(8,128)} %param.7) | copy-start | bytes 6148
  2.0 14.6 %copy-start.1 = (s32[4]{0:T(128)S(1)}, s32[4]{0:T(128)}, u32[]{:S(2)}) copy-start(s32[4]{0:T(128)} %index_ref.1) | copy-start | bytes 52
  2.0 11.0 %collective-permute-start.2 = (f32[168,128]{1,0:T(8,128)S(1)}, f32[168,128]{1,0:T(8,128)S(1)}, u32[]{:S(2)}, u32[]{:S(2)}) collective-permute-start(f32[168,128]{1,0:T(8,128)S(1)} %get-tuple-element.21), channel_id=1, source_target_pairs={{0,24},{8,16},{16,8},{24,0},{1,25},{9,17},{17,9},{25,1},{2,26},{10... | collective-permute-start | bytes 258056 | tf_op jit(solution)/shard_map/ppermute | solution.py:385
  6.0 15.7 %collective-permute-start.4 = (f32[1064,128]{1,0:T(8,128)S(1)}, f32[1064,128]{1,0:T(8,128)S(1)}, u32[]{:S(2)}, u32[]{:S(2)}) collective-permute-start(f32[1064,128]{1,0:T(8,128)S(1)} %get-tuple-element.25), channel_id=1, source_target_pairs={{0,16},{8,24},{16,0},{24,8},{1,17},{9,25},{17,1},{25,9},{2,18},{10... | collective-permute-start | bytes 1634312 | tf_op jit(solution)/shard_map/ppermute | solution.py:385
  6.5 15.2 %collective-permute-start.3 = (f32[1064,128]{1,0:T(8,128)S(1)}, f32[1064,128]{1,0:T(8,128)S(1)}, u32[]{:S(2)}, u32[]{:S(2)}) collective-permute-start(f32[1064,128]{1,0:T(8,128)S(1)} %get-tuple-element.18._), channel_id=1, source_target_pairs={{0,8},{8,0},{16,24},{24,16},{1,9},{9,1},{17,25},{25,17},{2,10},{10... | collective-permute-start | bytes 1634312 | tf_op jit(solution)/shard_map/ppermute | solution.py:385
  7.8 5.2 %collective-permute-start.1 = (f32[64,128]{1,0:T(8,128)S(1)}, f32[64,128]{1,0:T(8,128)S(1)}, u32[]{:S(2)}, u32[]{:S(2)}) collective-permute-start(f32[64,128]{1,0:T(8,128)S(1)} %get-tuple-element.20), channel_id=1, source_target_pairs={{1,0},{2,1},{3,2},{4,3},{5,4},{6,5},{7,6},{9,8},{10,9},{11,10},{12... | collective-permute-start | bytes 98312 | tf_op jit(solution)/shard_map/ppermute | solution.py:381
  9.1 3.9 %collective-permute-start = (f32[64,128]{1,0:T(8,128)S(1)}, f32[64,128]{1,0:T(8,128)S(1)}, u32[]{:S(2)}, u32[]{:S(2)}) collective-permute-start(f32[64,128]{1,0:T(8,128)S(1)} %get-tuple-element.20), channel_id=1, source_target_pairs={{0,1},{1,2},{2,3},{3,4},{4,5},{5,6},{6,7},{8,9},{9,10},{10,11},{11... | collective-permute-start | bytes 98312 | tf_op jit(solution)/shard_map/ppermute | solution.py:381
  13.1 8.6 %collective-permute-start.6 = (f32[16,128]{1,0:T(8,128)S(1)}, f32[16,128]{1,0:T(8,128)S(1)}, u32[]{:S(2)}, u32[]{:S(2)}) collective-permute-start(f32[16,128]{1,0:T(8,128)S(1)} %get-tuple-element.29), channel_id=1, source_target_pairs={{0,8},{8,0},{16,24},{24,16},{1,9},{9,1},{17,25},{25,17},{2,10},{10... | collective-permute-start | bytes 24584 | tf_op jit(solution)/shard_map/ppermute | solution.py:385
  15.0 6.6 %collective-permute-start.7 = (f32[16,128]{1,0:T(8,128)S(1)}, f32[16,128]{1,0:T(8,128)S(1)}, u32[]{:S(2)}, u32[]{:S(2)}) collective-permute-start(f32[16,128]{1,0:T(8,128)S(1)} %get-tuple-element.30), channel_id=1, source_target_pairs={{0,16},{8,24},{16,0},{24,8},{1,17},{9,25},{17,1},{25,9},{2,18},{10... | collective-permute-start | bytes 24584 | tf_op jit(solution)/shard_map/ppermute | solution.py:385
  16.6 14.7 %collective-permute-start.5 = (f32[920,128]{1,0:T(8,128)S(1)}, f32[920,128]{1,0:T(8,128)S(1)}, u32[]{:S(2)}, u32[]{:S(2)}) collective-permute-start(f32[920,128]{1,0:T(8,128)S(1)} %constant_dynamic-update-slice_fusion), channel_id=1, source_target_pairs={{0,24},{8,16},{16,8},{24,0},{1,25},{9,17},{17,9},{25,1},{2,26},{10... | collective-permute-start | bytes 1413128 | tf_op jit(solution)/shard_map/ppermute | solution.py:385

commit v8 on v7

--- a/solution.py
+++ b/solution.py
@@ -52,7 +52,7 @@
         copy.wait()
 
 
-def edge_kernel(parts, field_ref, _, edge_ref, own_ref, body_ref):
+def edge_kernel(parts, split, field_ref, _, edge_ref, own_ref, body_ref, rest_ref):
     cells, all_rows, cols = field_ref.shape
     rows = all_rows // parts
     me = lax.axis_index("depth")
@@ -78,14 +78,18 @@
         own_ref[z : z + 1, :] = field_ref[z, pl.ds(jnp.maximum(low - 1, 0), 1), :] * above
         own_ref[cells + z : cells + z + 1, :] = field_ref[z, pl.ds(jnp.minimum(low + rows, all_rows - 1), 1), :] * below
     far_low = pl.multiple_of((me ^ (parts - 1)) * rows, SUB)
-    own_places = near_places(cells, rows, own_ref)
-    body_places = far_places(cells, rows, parts, None, body_ref)
+    own_places, _, _ = near_places(cells, rows, own_ref)
     for z in range(cells):
         ref, start = own_places[z]
         ref[start : start + rows, :] = field_ref[z, pl.ds(low, rows), :]
+    skip, more = rows // parts, rows - split
     for z in range(1, cells - 1):
-        ref, start = body_places[z]
-        ref[start : start + rows, :] = field_ref[z, pl.ds(far_low, rows), :]
+        at = skip + (z - 1) * split
+        body_ref[at : at + split, :] = field_ref[z, pl.ds(far_low, split), :]
+        next_row = skip + (cells - 2) * split + z - 1
+        body_ref[next_row : next_row + 1, :] = field_ref[z, pl.ds(far_low + split, 1), :]
+        at = SUB + (z - 1) * more
+        rest_ref[at : at + more, :] = field_ref[z, pl.ds(far_low + split, more), :]
 
 
 def side_kernel(parts, left_ref, right_ref, _, *outs):
@@ -104,13 +108,24 @@
 
 
 def near_places(cells, rows, head):
-    return [(head, 2 * cells + z * rows) for z in range(cells)]
-
-
-def far_places(cells, rows, parts, head, body):
-    skip = rows // parts
-    middle = [(body, skip + (z - 1) * rows) for z in range(1, cells - 1)]
-    return [(head, 2 * cells)] + middle + [(head, 2 * cells + rows)]
+    places = [(head, 2 * cells + z * rows) for z in range(cells)]
+    tops = [(0, head, z) for z in range(cells)]
+    bottoms = [(rows - SUB, head, cells + z) for z in range(cells)]
+    return places, tops, bottoms
+
+
+def far_places(cells, rows, parts, split, head, body, rest=None):
+    skip, more = rows // parts, rows - split
+    places, tops, bottoms = near_places(cells, rows, head)
+    places[0], places[-1] = (head, 2 * cells), (head, 2 * cells + rows)
+    for z in range(1, cells - 1):
+        if rest is None:
+            places[z] = (body, skip + (z - 1) * split)
+            bottoms[z] = (split - SUB, body, skip + (cells - 2) * split + z - 1)
+        else:
+            places[z] = (rest, SUB + (z - 1) * more - split)
+            tops[z] = (split, body, skip + z * split - 1)
+    return places, tops, bottoms
 
 
 def fill_ends(parts, cells, rows, heads, ends_ref):
@@ -151,7 +166,7 @@
         weight_ref[2 * pair * SUB : 2 * (pair + 1) * SUB, :] = value.astype(jnp.bfloat16)
 
 
-def prepare_steps(m, zs, head, places, lateral, base, cells, rows, parts, cols, ends_ref, weight_ref, cell_ref, mixed_ref):
+def prepare_steps(m, zs, where, lateral, base, cells, rows, parts, cols, ends_ref, weight_ref, cell_ref, mixed_ref):
     me = lax.axis_index("depth")
     part = me ^ m
     at = pl.ds(base, SUB)
@@ -159,8 +174,7 @@
     sublane = lax.broadcasted_iota(jnp.int32, (SUB, cols), 0)
     is_first = lane == 0
     is_last = lane == cols - 1
-    is_top = jnp.logical_and(sublane == 0, base == 0)
-    is_bottom = jnp.logical_and(sublane == SUB - 1, base == rows - SUB)
+    places, tops, bottoms = where
     group = rows // parts
     got = lateral[pl.ds(pl.multiple_of(base % group, SUB), SUB), :]
     sides = pltpu.roll(got, (2 * cols - 1 - base // group * (cols // parts)) % cols, 1)
@@ -176,8 +190,12 @@
     def step(z):
         ref, low = places[z]
         here = layer(z)
-        upper = jnp.where(is_top, head[z : z + 1, :], ref[pl.ds(low + base - 1, SUB), :])
-        lower = jnp.where(is_bottom, head[cells + z : cells + z + 1, :], ref[pl.ds(low + base + 1, SUB), :])
+        top_at, top_ref, top = tops[z]
+        bottom_at, bottom_ref, bottom = bottoms[z]
+        is_top = jnp.logical_and(sublane == 0, base == top_at)
+        is_bottom = jnp.logical_and(sublane == SUB - 1, base == bottom_at)
+        upper = jnp.where(is_top, top_ref[top : top + 1, :], ref[pl.ds(low + base - 1, SUB), :])
+        lower = jnp.where(is_bottom, bottom_ref[bottom : bottom + 1, :], ref[pl.ds(low + base + 1, SUB), :])
         edge = pltpu.roll(sides, (cols - 2 * z) % cols, 1) if z else sides
         grad_x = pltpu.roll(jnp.where(is_first, edge, here), cols - 1, 1) - pltpu.roll(
             jnp.where(is_last, edge, here), 1, 1
@@ -258,7 +276,7 @@
 
     def prepare(base, slot):
         return prepare_steps(
-            0, inner, own_ref, places, lateral_ref, base, cells, rows, parts, cols, None, weight_ref, cell_refs[slot], mixed_refs[slot]
+            0, inner, places, lateral_ref, base, cells, rows, parts, cols, None, weight_ref, cell_refs[slot], mixed_refs[slot]
         )
 
     for step in prepare(0, 0):
@@ -293,7 +311,7 @@
 
     def prepare(m, base):
         return prepare_steps(
-            m, zs[m], heads[m], places[m], laterals[m], base, cells, rows, parts, cols, ends_ref, weight_ref, cell_refs[m], mixed_refs[m]
+            m, zs[m], places[m], laterals[m], base, cells, rows, parts, cols, ends_ref, weight_ref, cell_refs[m], mixed_refs[m]
         )
 
     for step in prepare(0, 0):
@@ -323,21 +341,23 @@
     return [one[0] * other[0]] + [scale_one * a + scale_other * b for a, b in zip(one[1:], other[1:])]
 
 
-def far_kernel(parts, flip_ref, vector_ref, weight_ref, *refs):
-    heads, body, states, out_ref, picture_ref, ends_ref, sems = refs[:parts], *refs[parts : parts + 6]
-    cell_refs, mixed_refs = refs[parts + 6 : parts + 8], refs[parts + 8 :]
+def far_kernel(parts, split, low, high, flip_ref, vector_ref, weight_ref, *refs):
+    heads, body, refs = refs[:parts], refs[parts], refs[parts + 1 :]
+    rest, refs = (refs[0], refs[2:]) if low else (None, refs)
+    states, out_ref, picture_ref, ends_ref, sems = refs[:5]
+    cell_refs, mixed_refs = refs[5:7], refs[7:]
     channels, rows, cols = out_ref.shape[1:]
     cells = cell_refs[0].shape[1]
     passes = vector_ref.shape[0]
     flip = flip_ref[0]
     me = lax.axis_index("depth")
-    places = far_places(cells, rows, parts, heads[-1], body)
+    places = far_places(cells, rows, parts, split, heads[-1], body, rest)
     fill_ends(parts, cells, rows, heads, ends_ref)
-    tiles = rows // SUB
+    tiles = range(low // SUB, high // SUB)
 
     def prepare(base, slot):
         return prepare_steps(
-            parts - 1, range(cells), heads[-1], places, body, base, cells, rows, parts, cols, ends_ref, weight_ref, cell_refs[slot], mixed_refs[slot]
+            parts - 1, range(cells), places, body, base, cells, rows, parts, cols, ends_ref, weight_ref, cell_refs[slot], mixed_refs[slot]
         )
 
     def send(index):
@@ -359,19 +379,19 @@
             picture_ref[p, 3, at, :] = 1.0 - images[0][0]
         send(index).start()
 
-    for step in prepare(0, 0):
+    for step in prepare(low, 0):
         step()
 
     def pair(i, carry):
         for slot in range(2):
-            index = 2 * i + slot
-            after = pl.multiple_of(jnp.minimum(index + 1, tiles - 1) * SUB, SUB)
+            index = tiles[0] + 2 * i + slot
+            after = pl.multiple_of(jnp.minimum(index + 1, tiles[-1]) * SUB, SUB)
             result = march_unit(flip, vector_ref, range(cells), cells, cell_refs[slot], mixed_refs[slot], prepare(after, 1 - slot))
             finish(result, index)
         return carry
 
-    lax.fori_loop(0, tiles // 2, pair, 0)
-    for index in range(tiles):
+    lax.fori_loop(0, len(tiles) // 2, pair, 0)
+    for index in tiles:
         send(index).wait()
 
 
@@ -414,7 +434,9 @@
     near_rows = 2 * cells + cells * rows + SUB
     head_rows = 2 * cells + 2 * rows + SUB
     skip = rows // parts
-    body_rows = skip + (cells - 2) * rows + SUB
+    split = rows - rows // parts
+    body_rows = skip + (cells - 2) * split + cells
+    rest_rows = (cells - 2) * (rows - split) + 2 * SUB
     *packed, far_head = pl.pallas_call(
         functools.partial(pack_kernel, parts),
         out_shape=[array(near_rows, cols)] * (parts - 2) + [array(head_rows, cols)],
@@ -423,16 +445,16 @@
         scratch_shapes=[VMEM((parts - 1, 2, cells, SUB, cols), jnp.float32), pltpu.SemaphoreType.DMA((4, parts - 1))],
         name="pack",
         **settings(8, 1),
-    )(field)
+    )(pltpu.with_memory_space_constraint(field, pltpu.HBM))
     near = [swap_along(packed[m - 1], "depth", m) for m in range(1, parts - 1)]
 
     far_head = swap_along(far_head, "depth", parts - 1)
 
-    edges, own, far_body = pl.pallas_call(
-        functools.partial(edge_kernel, parts),
-        out_shape=[array(rows, cols), array(near_rows, cols), array(body_rows, cols)],
+    edges, own, far_body, far_rest = pl.pallas_call(
+        functools.partial(edge_kernel, parts, split),
+        out_shape=[array(rows, cols), array(near_rows, cols), array(body_rows, cols), array(rest_rows, cols)],
         in_specs=[in_vmem, in_any],
-        out_specs=[in_vmem] * 3,
+        out_specs=[in_vmem] * 4,
         name="edges",
         **settings(8, 1),
     )(field, packed[0])
@@ -446,6 +468,8 @@
     )(shift_along(edges, "tile", 1), shift_along(edges, "tile", -1), far_head)
     laterals = [swap_along(sides[m], "depth", m) for m in range(1, parts - 1)]
     far_body = swap_along(lax.dynamic_update_slice(far_body, sides[-1], (0, 0)), "depth", parts - 1)
+    *laterals, far_rest = lax.optimization_barrier((*laterals, far_rest))
+    far_rest = swap_along(far_rest, "depth", parts - 1)
 
     cell_shape = VMEM((3, cells, SUB, cols), jnp.float32)
     mixed_shape = VMEM((cells, values * SUB, cols), jnp.float32)
@@ -469,21 +493,26 @@
         name="near",
         **settings(16, 60),
     )(flips, vectors, weights, inner, own, *near, far_head, sides[0], *laterals)
-    return pl.pallas_call(
-        functools.partial(far_kernel, parts),
-        out_shape=array(passes, channels, rows, cols),
-        in_specs=[in_smem] + [in_vmem] * (parts + 4),
-        out_specs=in_any,
-        scratch_shapes=[
-            VMEM((passes, channels, rows, cols), jnp.float32),
-            ends_shape,
-            pltpu.SemaphoreType.DMA((tiles,)),
-        ]
-        + [cell_shape] * 2
-        + [mixed_shape] * 2,
-        name="far",
-        **settings(16, 5),
-    )(flips, vectors, weights, own, *near, far_head, far_body, states)
+    picture = None
+    for low, high in ((0, split), (split, rows)):
+        late = [far_rest, picture] if low else []
+        picture = pl.pallas_call(
+            functools.partial(far_kernel, parts, split, low, high),
+            out_shape=array(passes, channels, rows, cols),
+            in_specs=[in_smem] + [in_vmem] * (parts + 3) + [in_vmem, in_any][: len(late)] + [in_vmem],
+            out_specs=in_any,
+            scratch_shapes=[
+                VMEM((passes, channels, rows, cols), jnp.float32),
+                ends_shape,
+                pltpu.SemaphoreType.DMA((tiles,)),
+            ]
+            + [cell_shape] * 2
+            + [mixed_shape] * 2,
+            input_output_aliases={parts + 5: 0} if low else {},
+            name="late" if low else "far",
+            **settings(16, 2),
+        )(flips, vectors, weights, own, *near, far_head, far_body, *late, states)
+    return picture
 
 
 def solution(mesh):

time: 35.6 us -> 35.7 us (level)
  the two profiles are of different devices: /device:TPU:0 before, /device:TPU:24 now
where the time goes in v8:
time: 35.7 us; the launch traced here: 35.6 us
  Pallas kernels  18.6 us (52%)
  starting transfers between devices  14 us (39%)
  waiting for transfers between devices  2.02 us (6%)
  between operations  0.78 us (2%)
    ppermute x7, starting transfers between devices, swap_along(): lax.ppermute(block, axis, [(i, i ^ mask) for i in range(lax.axis_size(axi...  9.64 us
    pallas_call x1, Pallas kernels, on_device(): pl.pallas_call(functools.partial(near_kernel, parts), out_shape=array(par...  6.42 us
    pallas_call x2, Pallas kernels, on_device(): pl.pallas_call(functools.partial(far_kernel, parts, split, low, high), ou...  4.96 us
    pallas_call x1, Pallas kernels, on_device(): pl.pallas_call(functools.partial(own_kernel, parts), out_shape=[array(val...  4.33 us
    ppermute x2, starting transfers between devices, shift_along(): return lax.ppermute(block, axis, route)  4.32 us
    ppermute x2, waiting for transfers between devices, shift_along(): return lax.ppermute(block, axis, route)  2 us
    pallas_call x1, Pallas kernels, on_device(): pl.pallas_call(functools.partial(pack_kernel, parts), out_shape=[array(ne...  1.65 us
    pallas_call x1, Pallas kernels, on_device(): pl.pallas_call(functools.partial(edge_kernel, parts, split), out_shape=[a...  1.16 us
  transfers between devices with their start and end apart: 9, of which 1 were waited for; matrix products, arithmetic and copies ran while one was open for 0% of the time, Pallas kernels for 43%

profile of v8, /device:TPU:24, one launch (start us, length us, event | category | flops | bytes accessed | tf_op | source)
XLA Modules:
  0.0 35.6 jit_solution(12274282511622623326)
XLA Ops:
  0.0 1.7 %pack.1 = (f32[1064,128]{1,0:T(8,128)S(1)}, f32[1064,128]{1,0:T(8,128)S(1)}, f32[168,128]{1,0:T(8,128)S(1)}) custom-call(f32[16,256,128]{2,1,0:T(8,128)} %field_ref.3), custom_call_target="tpu_custom_call" | custom-call | flops 1000000000 | tf_op jit(solution)/shard_map/pack/pallas_call | solution.py:440
  1.7 0.0 copy-start.3
  1.7 0.0 copy-start.2
  1.7 0.0 copy-start.1
  1.7 2.5 %collective-permute-start.2 = (f32[168,128]{1,0:T(8,128)S(1)}, f32[168,128]{1,0:T(8,128)S(1)}, u32[]{:S(2)}, u32[]{:S(2)}) collective-permute-start(f32[168,128]{1,0:T(8,128)S(1)} %get-tuple-element.25), channel_id=1, source_target_pairs={{0,24},{8,16},{16,8},{24,0},{1,25},{9,17},{17,9},{25,1},{2,26},{10... | collective-permute-start | bytes 258056 | tf_op jit(solution)/shard_map/ppermute | solution.py:405
  4.2 0.5 %collective-permute-start.4 = (f32[1064,128]{1,0:T(8,128)S(1)}, f32[1064,128]{1,0:T(8,128)S(1)}, u32[]{:S(2)}, u32[]{:S(2)}) collective-permute-start(f32[1064,128]{1,0:T(8,128)S(1)} %get-tuple-element.29), channel_id=1, source_target_pairs={{0,16},{8,24},{16,0},{24,8},{1,17},{9,25},{17,1},{25,9},{2,18},{10... | collective-permute-start | bytes 1634312 | tf_op jit(solution)/shard_map/ppermute | solution.py:405
  4.7 0.5 %collective-permute-start.3 = (f32[1064,128]{1,0:T(8,128)S(1)}, f32[1064,128]{1,0:T(8,128)S(1)}, u32[]{:S(2)}, u32[]{:S(2)}) collective-permute-start(f32[1064,128]{1,0:T(8,128)S(1)} %get-tuple-element.22._), channel_id=1, source_target_pairs={{0,8},{8,0},{16,24},{24,16},{1,9},{9,1},{17,25},{25,17},{2,10},{10... | collective-permute-start | bytes 1634312 | tf_op jit(solution)/shard_map/ppermute | solution.py:405
  5.3 0.0 copy-done
  5.3 1.2 %edges.1 = (f32[64,128]{1,0:T(8,128)S(1)}, f32[1064,128]{1,0:T(8,128)S(1)}, f32[704,128]{1,0:T(8,128)S(1)}, f32[240,128]{1,0:T(8,128)S(1)}) custom-call(f32[16,256,128]{2,1,0:T(8,128)S(1)} %copy-done, f32[1064,128]{1,0:T(8,128)S(1)} %get-tuple-element.22._), custom_call_target="tpu_custom_call" | custom-call | flops 1000000000 | tf_op jit(solution)/shard_map/edges/pallas_call | solution.py:453
  6.4 1.9 %collective-permute-start.1 = (f32[64,128]{1,0:T(8,128)S(1)}, f32[64,128]{1,0:T(8,128)S(1)}, u32[]{:S(2)}, u32[]{:S(2)}) collective-permute-start(f32[64,128]{1,0:T(8,128)S(1)} %get-tuple-element.24), channel_id=1, source_target_pairs={{1,0},{2,1},{3,2},{4,3},{5,4},{6,5},{7,6},{9,8},{10,9},{11,10},{12... | collective-permute-start | bytes 98312 | tf_op jit(solution)/shard_map/ppermute | solution.py:401
  8.4 2.4 %collective-permute-start = (f32[64,128]{1,0:T(8,128)S(1)}, f32[64,128]{1,0:T(8,128)S(1)}, u32[]{:S(2)}, u32[]{:S(2)}) collective-permute-start(f32[64,128]{1,0:T(8,128)S(1)} %get-tuple-element.24), channel_id=1, source_target_pairs={{0,1},{1,2},{2,3},{3,4},{4,5},{5,6},{6,7},{8,9},{9,10},{10,11},{11... | collective-permute-start | bytes 98312 | tf_op jit(solution)/shard_map/ppermute | solution.py:401
  11.4 0.0 copy-done.3
  11.4 0.1 copy.7.lights_ref
  11.5 0.1 copy.8.curves_ref
  11.6 0.0 collective-permute-done.1.right_ref
  11.6 2.0 %collective-permute-done.left_ref = f32[64,128]{1,0:T(8,128)S(1)} collective-permute-done((f32[64,128]{1,0:T(8,128)S(1)}, f32[64,128]{1,0:T(8,128)S(1)}, u32[]{:S(2)}, u32[]{:S(2)}) %collective-permute-start) | collective-permute-done | bytes 32800 | tf_op jit(solution)/shard_map/ppermute | solution.py:401
  13.6 0.0 collective-permute-done.2._.refs_3_
  13.6 0.1 sides.1
  13.7 1.6 %collective-permute-start.6 = (f32[16,128]{1,0:T(8,128)S(1)}, f32[16,128]{1,0:T(8,128)S(1)}, u32[]{:S(2)}, u32[]{:S(2)}) collective-permute-start(f32[16,128]{1,0:T(8,128)S(1)} %get-tuple-element.32), channel_id=1, source_target_pairs={{0,8},{8,0},{16,24},{24,16},{1,9},{9,1},{17,25},{25,17},{2,10},{10... | collective-permute-start | bytes 24584 | tf_op jit(solution)/shard_map/ppermute | solution.py:405
  15.3 1.5 %collective-permute-start.7 = (f32[16,128]{1,0:T(8,128)S(1)}, f32[16,128]{1,0:T(8,128)S(1)}, u32[]{:S(2)}, u32[]{:S(2)}) collective-permute-start(f32[16,128]{1,0:T(8,128)S(1)} %get-tuple-element.33), channel_id=1, source_target_pairs={{0,16},{8,24},{16,0},{24,8},{1,17},{9,25},{17,1},{25,9},{2,18},{10... | collective-permute-start | bytes 24584 | tf_op jit(solution)/shard_map/ppermute | solution.py:405
  16.8 0.5 %collective-permute-start.5 = (f32[704,128]{1,0:T(8,128)S(1)}, f32[704,128]{1,0:T(8,128)S(1)}, u32[]{:S(2)}, u32[]{:S(2)}) collective-permute-start(f32[704,128]{1,0:T(8,128)S(1)} %constant_dynamic-update-slice_fusion), channel_id=1, source_target_pairs={{0,24},{8,16},{16,8},{24,0},{1,25},{9,17},{17,9},{25,1},{2,26},{10... | collective-permute-start | bytes 1081352 | tf_op jit(solution)/shard_map/ppermute | solution.py:405
  17.3 4.3 %own.1 = (f32[16,64,128]{2,1,0:T(8,128)S(1)}, f32[4,3,8,128]{3,2,1,0:T(8,128)S(1)}, bf16[128,192]{1,0:T(8,128)(2,1)S(1)}) custom-call(s32[4]{0:T(128)S(1)} %copy-done.1, s32[1]{0:T(128)S(6)} %copy.11.flip_ref, f32[16,3]{1,0:T(8,128)S(1)} %copy.7.lights_ref, f32[16,4,8]{2,1,0:T(4,128)S(1)} %copy.8.curves_ref, ...), custom_call_target="tpu_custom_call" | custom-call | flops 4000000000 | tf_op jit(solution)/shard_map/own/pallas_call | solution.py:478
  21.6 0.0 collective-permute-done.6.refs_5_
  21.6 0.0 collective-permute-done.7.refs_6_
  21.6 2.5 %collective-permute-start.8 = (f32[240,128]{1,0:T(8,128)S(1)}, f32[240,128]{1,0:T(8,128)S(1)}, u32[]{:S(2)}, u32[]{:S(2)}) collective-permute-start(f32[240,128]{1,0:T(8,128)S(1)} %get-tuple-element.35), channel_id=1, source_target_pairs={{0,24},{8,16},{16,8},{24,0},{1,25},{9,17},{17,9},{25,1},{2,26},{10... | collective-permute-start | bytes 368648 | tf_op jit(solution)/shard_map/ppermute | solution.py:405
  24.2 0.0 collective-permute-done.4.refs_2_
  24.2 0.0 collective-permute-done.3.refs_1_
  24.2 6.4 %near.1.refs_5_.refs_7_ = f32[3,16,64,128]{3,2,1,0:T(8,128)S(1)} custom-call(s32[1]{0:T(128)S(6)} %copy.11.flip_ref, f32[4,3,8,128]{3,2,1,0:T(8,128)S(1)} %get-tuple-element.27.vector_ref, bf16[128,192]{1,0:T(8,128)(2,1)S(1)} %get-tuple-element.28.weight_ref, f32[16,64,128]{2,1,0:T(8,128)S(1)} %get-tuple-element.36.inner_ref, ...), custom_call_target="tpu_custom_call" | custom-call | flops 60000002048 | tf_op jit(solution)/shard_map/near/pallas_call | solution.py:487
  30.6 0.0 collective-permute-done.5.refs_4_
  30.6 3.3 %far.1.refs_6_ = f32[4,4,64,128]{3,2,1,0:T(8,128)} custom-call(s32[1]{0:T(128)S(6)} %copy.11.flip_ref, f32[4,3,8,128]{3,2,1,0:T(8,128)S(1)} %get-tuple-element.27.vector_ref, bf16[128,192]{1,0:T(8,128)(2,1)S(1)} %get-tuple-element.28.weight_ref, f32[1064,128]{1,0:T(8,128)S(1)} %get-tuple-element.23.own_ref.refs_0_, ...), custom_call_target="tpu_custom_call" | custom-call | flops 2000000000 | tf_op jit(solution)/shard_map/far/pallas_call | solution.py:499
  34.0 0.0 collective-permute-done.8.refs_5_
  34.0 1.6 %late.1 = f32[4,4,64,128]{3,2,1,0:T(8,128)} custom-call(s32[1]{0:T(128)S(6)} %copy.11.flip_ref, f32[4,3,8,128]{3,2,1,0:T(8,128)S(1)} %get-tuple-element.27.vector_ref, bf16[128,192]{1,0:T(8,128)(2,1)S(1)} %get-tuple-element.28.weight_ref, f32[1064,128]{1,0:T(8,128)S(1)} %get-tuple-element.23.own_ref.refs_0_, ...), custom_call_target="tpu_custom_call", output_to_operand_aliasing={{}: (9, {})} | custom-call | flops 2000000000 | tf_op jit(solution)/shard_map/late/pallas_call | solution.py:499
  (4 shorter events, 0.0 us)
Async XLA Ops:
  0.0 5.3 %copy-start = (f32[16,256,128]{2,1,0:T(8,128)S(1)}, f32[16,256,128]{2,1,0:T(8,128)}, u32[]{:S(2)}) copy-start(f32[16,256,128]{2,1,0:T(8,128)} %field_ref.3) | copy-start | bytes 6291460
  1.7 9.8 %copy-start.3 = (f32[16,3]{0,1:T(4,128)S(1)}, f32[16,3]{0,1:T(4,128)}, u32[]{:S(2)}) copy-start(f32[16,3]{0,1:T(4,128)} %param.6) | copy-start | bytes 580
  1.7 9.8 %copy-start.2 = (f32[16,4,8]{0,2,1:T(8,128)S(1)}, f32[16,4,8]{0,2,1:T(8,128)}, u32[]{:S(2)}) copy-start(f32[16,4,8]{0,2,1:T(8,128)} %param.7) | copy-start | bytes 6148
  1.7 15.6 %copy-start.1 = (s32[4]{0:T(128)S(1)}, s32[4]{0:T(128)}, u32[]{:S(2)}) copy-start(s32[4]{0:T(128)} %index_ref.1) | copy-start | bytes 52
  1.7 11.9 %collective-permute-start.2 = (f32[168,128]{1,0:T(8,128)S(1)}, f32[168,128]{1,0:T(8,128)S(1)}, u32[]{:S(2)}, u32[]{:S(2)}) collective-permute-start(f32[168,128]{1,0:T(8,128)S(1)} %get-tuple-element.25), channel_id=1, source_target_pairs={{0,24},{8,16},{16,8},{24,0},{1,25},{9,17},{17,9},{25,1},{2,26},{10... | collective-permute-start | bytes 258056 | tf_op jit(solution)/shard_map/ppermute | solution.py:405
  4.2 20.0 %collective-permute-start.4 = (f32[1064,128]{1,0:T(8,128)S(1)}, f32[1064,128]{1,0:T(8,128)S(1)}, u32[]{:S(2)}, u32[]{:S(2)}) collective-permute-start(f32[1064,128]{1,0:T(8,128)S(1)} %get-tuple-element.29), channel_id=1, source_target_pairs={{0,16},{8,24},{16,0},{24,8},{1,17},{9,25},{17,1},{25,9},{2,18},{10... | collective-permute-start | bytes 1634312 | tf_op jit(solution)/shard_map/ppermute | solution.py:405
  4.7 19.5 %collective-permute-start.3 = (f32[1064,128]{1,0:T(8,128)S(1)}, f32[1064,128]{1,0:T(8,128)S(1)}, u32[]{:S(2)}, u32[]{:S(2)}) collective-permute-start(f32[1064,128]{1,0:T(8,128)S(1)} %get-tuple-element.22._), channel_id=1, source_target_pairs={{0,8},{8,0},{16,24},{24,16},{1,9},{9,1},{17,25},{25,17},{2,10},{10... | collective-permute-start | bytes 1634312 | tf_op jit(solution)/shard_map/ppermute | solution.py:405
  6.4 5.2 %collective-permute-start.1 = (f32[64,128]{1,0:T(8,128)S(1)}, f32[64,128]{1,0:T(8,128)S(1)}, u32[]{:S(2)}, u32[]{:S(2)}) collective-permute-start(f32[64,128]{1,0:T(8,128)S(1)} %get-tuple-element.24), channel_id=1, source_target_pairs={{1,0},{2,1},{3,2},{4,3},{5,4},{6,5},{7,6},{9,8},{10,9},{11,10},{12... | collective-permute-start | bytes 98312 | tf_op jit(solution)/shard_map/ppermute | solution.py:401
  8.4 5.2 %collective-permute-start = (f32[64,128]{1,0:T(8,128)S(1)}, f32[64,128]{1,0:T(8,128)S(1)}, u32[]{:S(2)}, u32[]{:S(2)}) collective-permute-start(f32[64,128]{1,0:T(8,128)S(1)} %get-tuple-element.24), channel_id=1, source_target_pairs={{0,1},{1,2},{2,3},{3,4},{4,5},{5,6},{6,7},{8,9},{9,10},{10,11},{11... | collective-permute-start | bytes 98312 | tf_op jit(solution)/shard_map/ppermute | solution.py:401
  13.7 7.9 %collective-permute-start.6 = (f32[16,128]{1,0:T(8,128)S(1)}, f32[16,128]{1,0:T(8,128)S(1)}, u32[]{:S(2)}, u32[]{:S(2)}) collective-permute-start(f32[16,128]{1,0:T(8,128)S(1)} %get-tuple-element.32), channel_id=1, source_target_pairs={{0,8},{8,0},{16,24},{24,16},{1,9},{9,1},{17,25},{25,17},{2,10},{10... | collective-permute-start | bytes 24584 | tf_op jit(solution)/shard_map/ppermute | solution.py:405
  15.3 6.3 %collective-permute-start.7 = (f32[16,128]{1,0:T(8,128)S(1)}, f32[16,128]{1,0:T(8,128)S(1)}, u32[]{:S(2)}, u32[]{:S(2)}) collective-permute-start(f32[16,128]{1,0:T(8,128)S(1)} %get-tuple-element.33), channel_id=1, source_target_pairs={{0,16},{8,24},{16,0},{24,8},{1,17},{9,25},{17,1},{25,9},{2,18},{10... | collective-permute-start | bytes 24584 | tf_op jit(solution)/shard_map/ppermute | solution.py:405
  16.8 13.8 %collective-permute-start.5 = (f32[704,128]{1,0:T(8,128)S(1)}, f32[704,128]{1,0:T(8,128)S(1)}, u32[]{:S(2)}, u32[]{:S(2)}) collective-permute-start(f32[704,128]{1,0:T(8,128)S(1)} %constant_dynamic-update-slice_fusion), channel_id=1, source_target_pairs={{0,24},{8,16},{16,8},{24,0},{1,25},{9,17},{17,9},{25,1},{2,26},{10... | collective-permute-start | bytes 1081352 | tf_op jit(solution)/shard_map/ppermute | solution.py:405
  21.6 12.3 %collective-permute-start.8 = (f32[240,128]{1,0:T(8,128)S(1)}, f32[240,128]{1,0:T(8,128)S(1)}, u32[]{:S(2)}, u32[]{:S(2)}) collective-permute-start(f32[240,128]{1,0:T(8,128)S(1)} %get-tuple-element.35), channel_id=1, source_target_pairs={{0,24},{8,16},{16,8},{24,0},{1,25},{9,17},{17,9},{25,1},{2,26},{10... | collective-permute-start | bytes 368648 | tf_op jit(solution)/shard_map/ppermute | solution.py:405

commit v9 on v8

--- a/solution.py
+++ b/solution.py
@@ -92,13 +92,14 @@
         rest_ref[at : at + more, :] = field_ref[z, pl.ds(far_low + split, more), :]
 
 
-def side_kernel(parts, left_ref, right_ref, _, *outs):
-    rows, cols = left_ref.shape
+def side_kernel(parts, even_ref, odd_ref, _, *outs):
+    rows, cols = even_ref.shape
     group = rows // parts
     width = cols // parts
     me = lax.axis_index("depth")
     lane = lax.broadcasted_iota(jnp.int32, (rows, cols), 1)
-    sides = jnp.where(lane % 2 == 0, left_ref[...], right_ref[...])
+    tile = lax.axis_index("tile")
+    sides = jnp.where((lane + tile) % 2 == 1, even_ref[...], odd_ref[...])
     for m in range(parts):
         acc = jnp.zeros((group, cols), jnp.float32)
         for j in range(parts):
@@ -141,26 +142,26 @@
 def fill_weights(index_ref, curves_ref, scale, weight_ref):
     passes = index_ref.shape[0]
     channels, knots = curves_ref.shape[1:]
-    shape = (2 * SUB, weight_ref.shape[1])
+    width = weight_ref.shape[1]
+    block = knots * SUB
+    points = jnp.concatenate([curves_ref[index_ref[p]] for p in range(passes)], axis=0)
+    channel = lax.broadcasted_iota(jnp.int32, points.shape, 0) % channels
+    points = jnp.where(channel == channels - 1, points * scale, points)
+    knot = lax.broadcasted_iota(jnp.int32, (knots, width), 0)
+    lane = lax.broadcasted_iota(jnp.int32, (knots, width), 1)
+    target = lane // SUB % knots
+    here = jnp.where(knot == target, 1.0, 0.0)
+    after = jnp.where(knot == target + 1, 1.0, 0.0)
+    is_slope = jnp.logical_and(lane >= block, lane < 2 * block)
+    spread = jnp.where(is_slope, after - here, here)
+    values = jnp.dot(points, spread, precision=lax.Precision.HIGHEST, preferred_element_type=jnp.float32)
+    shape = (2 * SUB, width)
     row = lax.broadcasted_iota(jnp.int32, shape, 0)
     lane = lax.broadcasted_iota(jnp.int32, shape, 1)
-    block = knots * SUB
-    knot = lane // SUB
     on_row = lane % SUB == row % SUB
-    zero = jnp.zeros(shape, jnp.float32)
     for pair in range(passes * channels // 2):
-        halves = []
-        for channel in (2 * pair, 2 * pair + 1):
-            chosen = index_ref[channel // channels]
-            factor = scale if channel % channels == channels - 1 else 1.0
-            points = [curves_ref[chosen, channel % channels, k] * factor for k in range(knots)]
-            half = zero
-            for k in range(knots):
-                half = jnp.where(jnp.logical_or(knot == k, knot == k + 2 * knots), points[k], half)
-                if k + 1 < knots:
-                    half = jnp.where(knot == k + knots, points[k + 1] - points[k], half)
-            halves.append(half)
-        value = jnp.where(on_row, jnp.where(row < SUB, halves[0], halves[1]), zero)
+        upper, lower = [jnp.broadcast_to(values[2 * pair + j : 2 * pair + j + 1], shape) for j in range(2)]
+        value = jnp.where(on_row, jnp.where(row < SUB, upper, lower), 0.0)
         coarse = value.astype(jnp.bfloat16).astype(jnp.float32)
         value = jnp.where(lane < 2 * block, value, value - coarse)
         weight_ref[2 * pair * SUB : 2 * (pair + 1) * SUB, :] = value.astype(jnp.bfloat16)
@@ -395,10 +396,9 @@
         send(index).wait()
 
 
-def shift_along(block, axis, amount):
-    count = lax.axis_size(axis)
-    route = [(i, i + amount) for i in range(count) if 0 <= i + amount < count]
-    return lax.ppermute(block, axis, route)
+def swap_pairs(block, axis, start):
+    pairs = [(i, i + 1) for i in range(start, lax.axis_size(axis) - 1, 2)]
+    return lax.ppermute(block, axis, pairs + [(j, i) for i, j in pairs])
 
 
 def swap_along(block, axis, mask):
@@ -465,7 +465,7 @@
         out_specs=[in_vmem] * parts,
         name="sides",
         **settings(4, 0.1),
-    )(shift_along(edges, "tile", 1), shift_along(edges, "tile", -1), far_head)
+    )(swap_pairs(edges, "tile", 0), swap_pairs(edges, "tile", 1), far_head)
     laterals = [swap_along(sides[m], "depth", m) for m in range(1, parts - 1)]
     far_body = swap_along(lax.dynamic_update_slice(far_body, sides[-1], (0, 0)), "depth", parts - 1)
     *laterals, far_rest = lax.optimization_barrier((*laterals, far_rest))
@@ -478,7 +478,7 @@
     inner, vectors, weights = pl.pallas_call(
         functools.partial(own_kernel, parts),
         out_shape=[array(values, rows, cols), array(passes, 3, SUB, cols), weight_shape],
-        in_specs=[in_smem] * 4 + [in_vmem] * 2,
+        in_specs=[in_smem] * 3 + [in_vmem] * 3,
         out_specs=[in_vmem] * 3,
         scratch_shapes=[cell_shape] * 2 + [mixed_shape] * 2,
         name="own",

time: 35.7 us -> 34.9 us (0.978)
  the two profiles are of different devices: /device:TPU:24 before, /device:TPU:0 now
where the time goes in v9:
time: 34.9 us; the launch traced here: 34.8 us
  Pallas kernels  18.1 us (52%)
  starting transfers between devices  13.7 us (39%)
  waiting for transfers between devices  2.01 us (6%)
  between operations  0.75 us (2%)
    ppermute x7, starting transfers between devices, swap_along(): lax.ppermute(block, axis, [(i, i ^ mask) for i in range(lax.axis_size(axi...  9.64 us
    pallas_call x1, Pallas kernels, on_device(): pl.pallas_call(functools.partial(near_kernel, parts), out_shape=array(par...  6.41 us
    pallas_call x2, Pallas kernels, on_device(): pl.pallas_call(functools.partial(far_kernel, parts, split, low, high), ou...  4.96 us
    ppermute x2, starting transfers between devices, swap_pairs(): return lax.ppermute(block, axis, pairs + [(j, i) for i, j in pairs])  4.06 us
    pallas_call x1, Pallas kernels, on_device(): pl.pallas_call(functools.partial(own_kernel, parts), out_shape=[array(val...  3.83 us
    ppermute x7, waiting for transfers between devices, swap_along(): lax.ppermute(block, axis, [(i, i ^ mask) for i in range(lax.axis_size(axi...  1.98 us
    pallas_call x1, Pallas kernels, on_device(): pl.pallas_call(functools.partial(pack_kernel, parts), out_shape=[array(ne...  1.65 us
    pallas_call x1, Pallas kernels, on_device(): pl.pallas_call(functools.partial(edge_kernel, parts, split), out_shape=[a...  1.16 us
  transfers between devices with their start and end apart: 9, of which 2 were waited for; matrix products, arithmetic and copies ran while one was open for 0% of the time, Pallas kernels for 43%

profile of v9, /device:TPU:0, one launch (start us, length us, event | category | flops | bytes accessed | tf_op | source)
XLA Modules:
  0.0 34.8 jit_solution(4499796758332659024)
XLA Ops:
  0.0 1.7 %pack.1 = (f32[1064,128]{1,0:T(8,128)S(1)}, f32[1064,128]{1,0:T(8,128)S(1)}, f32[168,128]{1,0:T(8,128)S(1)}) custom-call(f32[16,256,128]{2,1,0:T(8,128)} %field_ref.3), custom_call_target="tpu_custom_call" | custom-call | flops 1000000000 | tf_op jit(solution)/shard_map/pack/pallas_call | solution.py:440
  1.7 0.0 copy-start.3
  1.7 0.0 copy-start.2
  1.7 0.0 copy-start.1
  1.7 4.0 %collective-permute-start.2 = (f32[168,128]{1,0:T(8,128)S(1)}, f32[168,128]{1,0:T(8,128)S(1)}, u32[]{:S(2)}, u32[]{:S(2)}) collective-permute-start(f32[168,128]{1,0:T(8,128)S(1)} %get-tuple-element.25), channel_id=1, source_target_pairs={{0,24},{8,16},{16,8},{24,0},{1,25},{9,17},{17,9},{25,1},{2,26},{10... | collective-permute-start | bytes 258056 | tf_op jit(solution)/shard_map/ppermute | solution.py:405
  5.7 0.5 %collective-permute-start.4 = (f32[1064,128]{1,0:T(8,128)S(1)}, f32[1064,128]{1,0:T(8,128)S(1)}, u32[]{:S(2)}, u32[]{:S(2)}) collective-permute-start(f32[1064,128]{1,0:T(8,128)S(1)} %get-tuple-element.29), channel_id=1, source_target_pairs={{0,16},{8,24},{16,0},{24,8},{1,17},{9,25},{17,1},{25,9},{2,18},{10... | collective-permute-start | bytes 1634312 | tf_op jit(solution)/shard_map/ppermute | solution.py:405
  6.2 0.1 collective-permute-start.3
  6.3 0.0 copy-done
  6.3 1.2 %edges.1 = (f32[64,128]{1,0:T(8,128)S(1)}, f32[1064,128]{1,0:T(8,128)S(1)}, f32[704,128]{1,0:T(8,128)S(1)}, f32[240,128]{1,0:T(8,128)S(1)}) custom-call(f32[16,256,128]{2,1,0:T(8,128)S(1)} %copy-done, f32[1064,128]{1,0:T(8,128)S(1)} %get-tuple-element.22._), custom_call_target="tpu_custom_call" | custom-call | flops 1000000000 | tf_op jit(solution)/shard_map/edges/pallas_call | solution.py:453
  7.5 0.7 %collective-permute-start.1 = (f32[64,128]{1,0:T(8,128)S(1)}, f32[64,128]{1,0:T(8,128)S(1)}, u32[]{:S(2)}, u32[]{:S(2)}) collective-permute-start(f32[64,128]{1,0:T(8,128)S(1)} %get-tuple-element.24), channel_id=1, source_target_pairs={{1,2},{3,4},{5,6},{2,1},{4,3},{6,5},{9,10},{11,12},{13,14},{10,9},... | collective-permute-start | bytes 98312 | tf_op jit(solution)/shard_map/ppermute | solution.py:401
  8.1 3.4 %collective-permute-start = (f32[64,128]{1,0:T(8,128)S(1)}, f32[64,128]{1,0:T(8,128)S(1)}, u32[]{:S(2)}, u32[]{:S(2)}) collective-permute-start(f32[64,128]{1,0:T(8,128)S(1)} %get-tuple-element.24), channel_id=1, source_target_pairs={{0,1},{2,3},{4,5},{6,7},{1,0},{3,2},{5,4},{7,6},{8,9},{10,11},{12,... | collective-permute-start | bytes 98312 | tf_op jit(solution)/shard_map/ppermute | solution.py:401
  12.2 0.0 copy-done.3
  12.2 0.1 copy.7.lights_ref
  12.3 0.1 copy.8.curves_ref
  12.4 0.0 collective-permute-done.1.odd_ref
  12.4 0.0 collective-permute-done.even_ref
  12.4 0.0 collective-permute-done.2._.refs_3_
  12.4 0.1 sides.1
  12.5 1.6 %collective-permute-start.6 = (f32[16,128]{1,0:T(8,128)S(1)}, f32[16,128]{1,0:T(8,128)S(1)}, u32[]{:S(2)}, u32[]{:S(2)}) collective-permute-start(f32[16,128]{1,0:T(8,128)S(1)} %get-tuple-element.32), channel_id=1, source_target_pairs={{0,8},{8,0},{16,24},{24,16},{1,9},{9,1},{17,25},{25,17},{2,10},{10... | collective-permute-start | bytes 24584 | tf_op jit(solution)/shard_map/ppermute | solution.py:405
  14.1 1.5 %collective-permute-start.7 = (f32[16,128]{1,0:T(8,128)S(1)}, f32[16,128]{1,0:T(8,128)S(1)}, u32[]{:S(2)}, u32[]{:S(2)}) collective-permute-start(f32[16,128]{1,0:T(8,128)S(1)} %get-tuple-element.33), channel_id=1, source_target_pairs={{0,16},{8,24},{16,0},{24,8},{1,17},{9,25},{17,1},{25,9},{2,18},{10... | collective-permute-start | bytes 24584 | tf_op jit(solution)/shard_map/ppermute | solution.py:405
  15.6 0.5 %collective-permute-start.5 = (f32[704,128]{1,0:T(8,128)S(1)}, f32[704,128]{1,0:T(8,128)S(1)}, u32[]{:S(2)}, u32[]{:S(2)}) collective-permute-start(f32[704,128]{1,0:T(8,128)S(1)} %constant_dynamic-update-slice_fusion), channel_id=1, source_target_pairs={{0,24},{8,16},{16,8},{24,0},{1,25},{9,17},{17,9},{25,1},{2,26},{10... | collective-permute-start | bytes 1081352 | tf_op jit(solution)/shard_map/ppermute | solution.py:405
  16.1 3.8 %own.1 = (f32[16,64,128]{2,1,0:T(8,128)S(1)}, f32[4,3,8,128]{3,2,1,0:T(8,128)S(1)}, bf16[128,192]{1,0:T(8,128)(2,1)S(1)}) custom-call(s32[4]{0:T(128)S(1)} %copy-done.1, s32[1]{0:T(128)S(6)} %copy.11.flip_ref, f32[16,3]{1,0:T(8,128)S(1)} %copy.7.lights_ref, f32[16,4,8]{2,1,0:T(4,128)S(1)} %copy.8.curves_ref, ...), custom_call_target="tpu_custom_call" | custom-call | flops 4000000000 | tf_op jit(solution)/shard_map/own/pallas_call | solution.py:478
  19.9 1.7 %collective-permute-done.6.refs_5_ = f32[16,128]{1,0:T(8,128)S(1)} collective-permute-done((f32[16,128]{1,0:T(8,128)S(1)}, f32[16,128]{1,0:T(8,128)S(1)}, u32[]{:S(2)}, u32[]{:S(2)}) %collective-permute-start.6) | collective-permute-done | bytes 8224 | tf_op jit(solution)/shard_map/ppermute | solution.py:405
  21.6 0.0 collective-permute-done.7.refs_6_
  21.6 1.5 %collective-permute-start.8 = (f32[240,128]{1,0:T(8,128)S(1)}, f32[240,128]{1,0:T(8,128)S(1)}, u32[]{:S(2)}, u32[]{:S(2)}) collective-permute-start(f32[240,128]{1,0:T(8,128)S(1)} %get-tuple-element.35), channel_id=1, source_target_pairs={{0,24},{8,16},{16,8},{24,0},{1,25},{9,17},{17,9},{25,1},{2,26},{10... | collective-permute-start | bytes 368648 | tf_op jit(solution)/shard_map/ppermute | solution.py:405
  23.1 0.0 collective-permute-done.4.refs_2_
  23.1 0.0 collective-permute-done.3.refs_1_
  23.1 6.4 %near.1.refs_5_.refs_7_ = f32[3,16,64,128]{3,2,1,0:T(8,128)S(1)} custom-call(s32[1]{0:T(128)S(6)} %copy.11.flip_ref, f32[4,3,8,128]{3,2,1,0:T(8,128)S(1)} %get-tuple-element.27.vector_ref, bf16[128,192]{1,0:T(8,128)(2,1)S(1)} %get-tuple-element.28.weight_ref, f32[16,64,128]{2,1,0:T(8,128)S(1)} %get-tuple-element.36.inner_ref, ...), custom_call_target="tpu_custom_call" | custom-call | flops 60000002048 | tf_op jit(solution)/shard_map/near/pallas_call | solution.py:487
  29.6 0.2 collective-permute-done.5.refs_4_
  29.8 3.3 %far.1.refs_6_ = f32[4,4,64,128]{3,2,1,0:T(8,128)} custom-call(s32[1]{0:T(128)S(6)} %copy.11.flip_ref, f32[4,3,8,128]{3,2,1,0:T(8,128)S(1)} %get-tuple-element.27.vector_ref, bf16[128,192]{1,0:T(8,128)(2,1)S(1)} %get-tuple-element.28.weight_ref, f32[1064,128]{1,0:T(8,128)S(1)} %get-tuple-element.23.own_ref.refs_0_, ...), custom_call_target="tpu_custom_call" | custom-call | flops 2000000000 | tf_op jit(solution)/shard_map/far/pallas_call | solution.py:499
  33.1 0.0 collective-permute-done.8.refs_5_
  33.2 1.6 %late.1 = f32[4,4,64,128]{3,2,1,0:T(8,128)} custom-call(s32[1]{0:T(128)S(6)} %copy.11.flip_ref, f32[4,3,8,128]{3,2,1,0:T(8,128)S(1)} %get-tuple-element.27.vector_ref, bf16[128,192]{1,0:T(8,128)(2,1)S(1)} %get-tuple-element.28.weight_ref, f32[1064,128]{1,0:T(8,128)S(1)} %get-tuple-element.23.own_ref.refs_0_, ...), custom_call_target="tpu_custom_call", output_to_operand_aliasing={{}: (9, {})} | custom-call | flops 2000000000 | tf_op jit(solution)/shard_map/late/pallas_call | solution.py:499
  (4 shorter events, 0.0 us)
Async XLA Ops:
  0.0 6.3 %copy-start = (f32[16,256,128]{2,1,0:T(8,128)S(1)}, f32[16,256,128]{2,1,0:T(8,128)}, u32[]{:S(2)}) copy-start(f32[16,256,128]{2,1,0:T(8,128)} %field_ref.3) | copy-start | bytes 6291460
  1.7 10.5 %copy-start.3 = (f32[16,3]{0,1:T(4,128)S(1)}, f32[16,3]{0,1:T(4,128)}, u32[]{:S(2)}) copy-start(f32[16,3]{0,1:T(4,128)} %param.6) | copy-start | bytes 580
  1.7 10.6 %copy-start.2 = (f32[16,4,8]{0,2,1:T(8,128)S(1)}, f32[16,4,8]{0,2,1:T(8,128)}, u32[]{:S(2)}) copy-start(f32[16,4,8]{0,2,1:T(8,128)} %param.7) | copy-start | bytes 6148
  1.7 14.4 %copy-start.1 = (s32[4]{0:T(128)S(1)}, s32[4]{0:T(128)}, u32[]{:S(2)}) copy-start(s32[4]{0:T(128)} %index_ref.1) | copy-start | bytes 52
  1.7 10.7 %collective-permute-start.2 = (f32[168,128]{1,0:T(8,128)S(1)}, f32[168,128]{1,0:T(8,128)S(1)}, u32[]{:S(2)}, u32[]{:S(2)}) collective-permute-start(f32[168,128]{1,0:T(8,128)S(1)} %get-tuple-element.25), channel_id=1, source_target_pairs={{0,24},{8,16},{16,8},{24,0},{1,25},{9,17},{17,9},{25,1},{2,26},{10... | collective-permute-start | bytes 258056 | tf_op jit(solution)/shard_map/ppermute | solution.py:405
  5.7 17.5 %collective-permute-start.4 = (f32[1064,128]{1,0:T(8,128)S(1)}, f32[1064,128]{1,0:T(8,128)S(1)}, u32[]{:S(2)}, u32[]{:S(2)}) collective-permute-start(f32[1064,128]{1,0:T(8,128)S(1)} %get-tuple-element.29), channel_id=1, source_target_pairs={{0,16},{8,24},{16,0},{24,8},{1,17},{9,25},{17,1},{25,9},{2,18},{10... | collective-permute-start | bytes 1634312 | tf_op jit(solution)/shard_map/ppermute | solution.py:405
  6.2 17.0 %collective-permute-start.3 = (f32[1064,128]{1,0:T(8,128)S(1)}, f32[1064,128]{1,0:T(8,128)S(1)}, u32[]{:S(2)}, u32[]{:S(2)}) collective-permute-start(f32[1064,128]{1,0:T(8,128)S(1)} %get-tuple-element.22._), channel_id=1, source_target_pairs={{0,8},{8,0},{16,24},{24,16},{1,9},{9,1},{17,25},{25,17},{2,10},{10... | collective-permute-start | bytes 1634312 | tf_op jit(solution)/shard_map/ppermute | solution.py:405
  7.5 4.9 %collective-permute-start.1 = (f32[64,128]{1,0:T(8,128)S(1)}, f32[64,128]{1,0:T(8,128)S(1)}, u32[]{:S(2)}, u32[]{:S(2)}) collective-permute-start(f32[64,128]{1,0:T(8,128)S(1)} %get-tuple-element.24), channel_id=1, source_target_pairs={{1,2},{3,4},{5,6},{2,1},{4,3},{6,5},{9,10},{11,12},{13,14},{10,9},... | collective-permute-start | bytes 98312 | tf_op jit(solution)/shard_map/ppermute | solution.py:401
  8.1 4.3 %collective-permute-start = (f32[64,128]{1,0:T(8,128)S(1)}, f32[64,128]{1,0:T(8,128)S(1)}, u32[]{:S(2)}, u32[]{:S(2)}) collective-permute-start(f32[64,128]{1,0:T(8,128)S(1)} %get-tuple-element.24), channel_id=1, source_target_pairs={{0,1},{2,3},{4,5},{6,7},{1,0},{3,2},{5,4},{7,6},{8,9},{10,11},{12,... | collective-permute-start | bytes 98312 | tf_op jit(solution)/shard_map/ppermute | solution.py:401
  12.5 9.1 %collective-permute-start.6 = (f32[16,128]{1,0:T(8,128)S(1)}, f32[16,128]{1,0:T(8,128)S(1)}, u32[]{:S(2)}, u32[]{:S(2)}) collective-permute-start(f32[16,128]{1,0:T(8,128)S(1)} %get-tuple-element.32), channel_id=1, source_target_pairs={{0,8},{8,0},{16,24},{24,16},{1,9},{9,1},{17,25},{25,17},{2,10},{10... | collective-permute-start | bytes 24584 | tf_op jit(solution)/shard_map/ppermute | solution.py:405
  14.1 7.6 %collective-permute-start.7 = (f32[16,128]{1,0:T(8,128)S(1)}, f32[16,128]{1,0:T(8,128)S(1)}, u32[]{:S(2)}, u32[]{:S(2)}) collective-permute-start(f32[16,128]{1,0:T(8,128)S(1)} %get-tuple-element.33), channel_id=1, source_target_pairs={{0,16},{8,24},{16,0},{24,8},{1,17},{9,25},{17,1},{25,9},{2,18},{10... | collective-permute-start | bytes 24584 | tf_op jit(solution)/shard_map/ppermute | solution.py:405
  15.6 14.2 %collective-permute-start.5 = (f32[704,128]{1,0:T(8,128)S(1)}, f32[704,128]{1,0:T(8,128)S(1)}, u32[]{:S(2)}, u32[]{:S(2)}) collective-permute-start(f32[704,128]{1,0:T(8,128)S(1)} %constant_dynamic-update-slice_fusion), channel_id=1, source_target_pairs={{0,24},{8,16},{16,8},{24,0},{1,25},{9,17},{17,9},{25,1},{2,26},{10... | collective-permute-start | bytes 1081352 | tf_op jit(solution)/shard_map/ppermute | solution.py:405
  21.6 11.5 %collective-permute-start.8 = (f32[240,128]{1,0:T(8,128)S(1)}, f32[240,128]{1,0:T(8,128)S(1)}, u32[]{:S(2)}, u32[]{:S(2)}) collective-permute-start(f32[240,128]{1,0:T(8,128)S(1)} %get-tuple-element.35), channel_id=1, source_target_pairs={{0,24},{8,16},{16,8},{24,0},{1,25},{9,17},{17,9},{25,1},{2,26},{10... | collective-permute-start | bytes 368648 | tf_op jit(solution)/shard_map/ppermute | solution.py:405

commit v10 on v9

--- a/solution.py
+++ b/solution.py
@@ -31,11 +31,14 @@
             rims.append(pltpu.make_async_copy(source, rim_ref.at[j, side], sems.at[side, j]))
         block = field_ref.at[:, pl.ds(low, rows), :]
         if j < parts - 2:
-            centre = out.at[pl.ds(2 * cells, cells * rows), :].reshape(cells, rows, cols)
-            copies.append(pltpu.make_async_copy(block, centre, sems.at[2, j]))
+            centre = out.at[pl.ds(cells, cells * rows), :].reshape(cells, rows, cols)
+            quarter = cells // 4
+            for q in range(4):
+                layers = pl.ds(q * quarter, quarter)
+                copies.append(pltpu.make_async_copy(block.at[layers], centre.at[layers], sems.at[2 + q, j]))
         else:
             for side in range(2):
-                layer = out.at[pl.ds(2 * cells + side * rows, rows), :]
+                layer = out.at[pl.ds(cells + side * rows, rows), :]
                 copies.append(pltpu.make_async_copy(block.at[side * (cells - 1)], layer, sems.at[2 + side, j]))
     for copy in rims + copies:
         copy.start()
@@ -47,7 +50,8 @@
         below = jnp.where(part < parts - 1, 1.0, 0.0)
         for z in range(cells):
             out[z : z + 1, :] = rim_ref[j, 0, z, SUB - 1 : SUB, :] * above
-            out[cells + z : cells + z + 1, :] = rim_ref[j, 1, z, 0:1, :] * below
+            below_at = out.shape[0] - cells + z
+            out[below_at : below_at + 1, :] = rim_ref[j, 1, z, 0:1, :] * below
     for copy in copies:
         copy.wait()
 
@@ -76,7 +80,8 @@
     below = jnp.where(me < parts - 1, 1.0, 0.0)
     for z in range(cells):
         own_ref[z : z + 1, :] = field_ref[z, pl.ds(jnp.maximum(low - 1, 0), 1), :] * above
-        own_ref[cells + z : cells + z + 1, :] = field_ref[z, pl.ds(jnp.minimum(low + rows, all_rows - 1), 1), :] * below
+        below_at = cells + cells * rows + z
+        own_ref[below_at : below_at + 1, :] = field_ref[z, pl.ds(jnp.minimum(low + rows, all_rows - 1), 1), :] * below
     far_low = pl.multiple_of((me ^ (parts - 1)) * rows, SUB)
     own_places, _, _ = near_places(cells, rows, own_ref)
     for z in range(cells):
@@ -109,16 +114,17 @@
 
 
 def near_places(cells, rows, head):
-    places = [(head, 2 * cells + z * rows) for z in range(cells)]
+    count = head.shape[0]
+    places = [(head, cells + z * rows) for z in range(cells)]
     tops = [(0, head, z) for z in range(cells)]
-    bottoms = [(rows - SUB, head, cells + z) for z in range(cells)]
+    bottoms = [(rows - SUB, head, count - cells + z) for z in range(cells)]
     return places, tops, bottoms
 
 
 def far_places(cells, rows, parts, split, head, body, rest=None):
     skip, more = rows // parts, rows - split
     places, tops, bottoms = near_places(cells, rows, head)
-    places[0], places[-1] = (head, 2 * cells), (head, 2 * cells + rows)
+    places[0], places[-1] = (head, cells), (head, cells + rows)
     for z in range(1, cells - 1):
         if rest is None:
             places[z] = (body, skip + (z - 1) * split)
@@ -135,8 +141,8 @@
     ends_ref[parts + 1, 0] = jnp.zeros_like(ends_ref[0, 0])
     for m in range(parts):
         last = (cells - 1) * rows if m < parts - 1 else rows
-        ends_ref[(me ^ m) + 1, 0] = heads[m][2 * cells : 2 * cells + rows, :]
-        ends_ref[(me ^ m) + 1, 1] = heads[m][2 * cells + last : 2 * cells + last + rows, :]
+        ends_ref[(me ^ m) + 1, 0] = heads[m][cells : cells + rows, :]
+        ends_ref[(me ^ m) + 1, 1] = heads[m][cells + last : cells + last + rows, :]
 
 
 def fill_weights(index_ref, curves_ref, scale, weight_ref):
@@ -214,13 +220,16 @@
         rest = position - coarse
         right = coarse - segment
         left = 1.0 - right
-        zero = jnp.zeros_like(here)
-        is_at = [segment == k for k in range(knots - 1)]
-        tents = [jnp.where(is_at[0], left, zero)]
-        tents += [jnp.where(is_at[k], left, jnp.where(is_at[k - 1], right, zero)) for k in range(1, knots - 1)]
-        tents += [jnp.where(is_at[knots - 2], right, zero)]
-        rests = [jnp.where(is_at[k], rest, zero) for k in range(knots - 1)] + [zero]
-        return [jnp.concatenate(part, axis=0).astype(jnp.bfloat16) for part in (tents, rests)]
+        twice = lambda value: jnp.concatenate([value, value], axis=0).astype(jnp.bfloat16)
+        left, right, rest, segment = twice(left), twice(right), twice(rest), twice(segment)
+        zero = jnp.zeros_like(left)
+        tents, rests = [], []
+        for k in range(0, knots, 2):
+            is_here = segment == pair_at + k
+            is_before = segment == pair_at + (k - 1)
+            tents.append(jnp.where(is_here, left, jnp.where(is_before, right, zero)))
+            rests.append(jnp.where(is_here, rest, zero))
+        return [jnp.concatenate(part, axis=0) for part in (tents, rests)]
 
     def two(first, second):
         tents, rests = [jnp.concatenate(both, axis=1) for both in zip(step(first), step(second))]
@@ -230,6 +239,7 @@
         mixed_ref[second] = mixed[:, cols:]
 
     knots = weight_ref.shape[1] // (3 * SUB)
+    pair_at = jnp.where(lax.broadcasted_iota(jnp.int32, (2 * SUB, cols), 0) < SUB, 0.0, 1.0).astype(jnp.bfloat16)
     zs = list(zs)
     return [functools.partial(two, *zs[i : i + 2]) for i in range(0, len(zs), 2)]
 
@@ -260,6 +270,24 @@
     return [[keep] + sums for keep, sums in state]
 
 
+def march_tiles(count, start, prepare, unit):
+    def ahead(index, slot):
+        return prepare(pl.multiple_of((index + 1) * SUB, SUB), 1 - slot)
+
+    for step in prepare(start * SUB, 0):
+        step()
+
+    def pair(i, carry):
+        for slot in range(2):
+            index = start + 2 * i + slot
+            unit(index, slot, ahead(index, slot))
+        return carry
+
+    lax.fori_loop(0, count // 2 - 1, pair, 0)
+    unit(start + count - 2, 0, ahead(start + count - 2, 0))
+    unit(start + count - 1, 1, [])
+
+
 def own_kernel(parts, index_ref, flip_ref, lights_ref, curves_ref, own_ref, lateral_ref, out_ref, vector_ref, weight_ref, *refs):
     cell_refs, mixed_refs = refs[:2], refs[2:]
     rows, cols = out_ref.shape[1:]
@@ -280,20 +308,14 @@
             0, inner, places, lateral_ref, base, cells, rows, parts, cols, None, weight_ref, cell_refs[slot], mixed_refs[slot]
         )
 
-    for step in prepare(0, 0):
-        step()
-
-    def pair(i, carry):
-        for slot in range(2):
-            base = pl.multiple_of((2 * i + slot) * SUB, SUB)
-            after = pl.multiple_of(jnp.minimum(2 * i + slot + 1, tiles - 1) * SUB, SUB)
-            result = march_unit(flip, vector_ref, inner, cells, cell_refs[slot], mixed_refs[slot], prepare(after, 1 - slot))
-            for p in range(passes):
-                for j in range(channels):
-                    out_ref[p * channels + j, pl.ds(base, SUB), :] = result[p][j]
-        return carry
-
-    lax.fori_loop(0, tiles // 2, pair, 0)
+    def unit(index, slot, beside):
+        base = pl.multiple_of(index * SUB, SUB)
+        result = march_unit(flip, vector_ref, inner, cells, cell_refs[slot], mixed_refs[slot], beside)
+        for p in range(passes):
+            for j in range(channels):
+                out_ref[p * channels + j, pl.ds(base, SUB), :] = result[p][j]
+
+    march_tiles(tiles, 0, prepare, unit)
 
 
 def near_kernel(parts, flip_ref, vector_ref, weight_ref, inner_ref, *refs):
@@ -380,18 +402,10 @@
             picture_ref[p, 3, at, :] = 1.0 - images[0][0]
         send(index).start()
 
-    for step in prepare(low, 0):
-        step()
-
-    def pair(i, carry):
-        for slot in range(2):
-            index = tiles[0] + 2 * i + slot
-            after = pl.multiple_of(jnp.minimum(index + 1, tiles[-1]) * SUB, SUB)
-            result = march_unit(flip, vector_ref, range(cells), cells, cell_refs[slot], mixed_refs[slot], prepare(after, 1 - slot))
-            finish(result, index)
-        return carry
-
-    lax.fori_loop(0, len(tiles) // 2, pair, 0)
+    def unit(index, slot, beside):
+        finish(march_unit(flip, vector_ref, range(cells), cells, cell_refs[slot], mixed_refs[slot], beside), index)
+
+    march_tiles(len(tiles), tiles[0], prepare, unit)
     for index in tiles:
         send(index).wait()
 
@@ -431,8 +445,8 @@
             cost_estimate=pl.CostEstimate(flops=int(micros * 1e9), transcendentals=0, bytes_accessed=0),
         )
 
-    near_rows = 2 * cells + cells * rows + SUB
-    head_rows = 2 * cells + 2 * rows + SUB
+    near_rows = 2 * cells + cells * rows
+    head_rows = 2 * cells + 2 * rows
     skip = rows // parts
     split = rows - rows // parts
     body_rows = skip + (cells - 2) * split + cells
@@ -442,7 +456,7 @@
         out_shape=[array(near_rows, cols)] * (parts - 2) + [array(head_rows, cols)],
         in_specs=[in_hbm],
         out_specs=[in_vmem] * (parts - 1),
-        scratch_shapes=[VMEM((parts - 1, 2, cells, SUB, cols), jnp.float32), pltpu.SemaphoreType.DMA((4, parts - 1))],
+        scratch_shapes=[VMEM((parts - 1, 2, cells, SUB, cols), jnp.float32), pltpu.SemaphoreType.DMA((6, parts - 1))],
         name="pack",
         **settings(8, 1),
     )(pltpu.with_memory_space_constraint(field, pltpu.HBM))

time: 34.9 us -> 34.4 us (0.986)
  Pallas kernels: 18.1 us -> 17.4 us
    pallas_call x2, Pallas kernels: 4.96 us -> 4.55 us  [on_device(): pl.pallas_call(functools.partial(far_kernel, parts, split, low, high), ou...]
  transfers between devices with their start and end apart: 9 -> 9, of which waited for: 2 -> 2; matrix products, arithmetic and copies ran while one was open for 0% -> 0% of each run, Pallas kernels for 43% -> 42%
where the time goes in v10:
time: 34.4 us; the launch traced here: 34.2 us
  Pallas kernels  17.4 us (51%)
  starting transfers between devices  13.7 us (40%)
  waiting for transfers between devices  2.21 us (6%)
  between operations  0.75 us (2%)
    ppermute x7, starting transfers between devices, swap_along(): lax.ppermute(block, axis, [(i, i ^ mask) for i in range(lax.axis_size(axi...  9.64 us
    pallas_call x1, Pallas kernels, on_device(): pl.pallas_call(functools.partial(near_kernel, parts), out_shape=array(par...  6.24 us
    pallas_call x2, Pallas kernels, on_device(): pl.pallas_call(functools.partial(far_kernel, parts, split, low, high), ou...  4.55 us
    ppermute x2, starting transfers between devices, swap_pairs(): return lax.ppermute(block, axis, pairs + [(j, i) for i, j in pairs])  4.06 us
    pallas_call x1, Pallas kernels, on_device(): pl.pallas_call(functools.partial(own_kernel, parts), out_shape=[array(val...  3.62 us
    ppermute x7, waiting for transfers between devices, swap_along(): lax.ppermute(block, axis, [(i, i ^ mask) for i in range(lax.axis_size(axi...  2.18 us
    pallas_call x1, Pallas kernels, on_device(): pl.pallas_call(functools.partial(pack_kernel, parts), out_shape=[array(ne...  1.71 us
    pallas_call x1, Pallas kernels, on_device(): pl.pallas_call(functools.partial(edge_kernel, parts, split), out_shape=[a...  1.16 us
  transfers between devices with their start and end apart: 9, of which 2 were waited for; matrix products, arithmetic and copies ran while one was open for 0% of the time, Pallas kernels for 42%

profile of v10, /device:TPU:0, one launch (start us, length us, event | category | flops | bytes accessed | tf_op | source)
XLA Modules:
  0.0 34.2 jit_solution(10659776355557346653)
XLA Ops:
  0.0 1.7 %pack.1 = (f32[1056,128]{1,0:T(8,128)S(1)}, f32[1056,128]{1,0:T(8,128)S(1)}, f32[160,128]{1,0:T(8,128)S(1)}) custom-call(f32[16,256,128]{2,1,0:T(8,128)} %field_ref.3), custom_call_target="tpu_custom_call" | custom-call | flops 1000000000 | tf_op jit(solution)/shard_map/pack/pallas_call | solution.py:454
  1.7 0.0 copy-start.3
  1.7 0.0 copy-start.2
  1.7 0.0 copy-start.1
  1.8 4.0 %collective-permute-start.2 = (f32[160,128]{1,0:T(8,128)S(1)}, f32[160,128]{1,0:T(8,128)S(1)}, u32[]{:S(2)}, u32[]{:S(2)}) collective-permute-start(f32[160,128]{1,0:T(8,128)S(1)} %get-tuple-element.25), channel_id=1, source_target_pairs={{0,24},{8,16},{16,8},{24,0},{1,25},{9,17},{17,9},{25,1},{2,26},{10... | collective-permute-start | bytes 245768 | tf_op jit(solution)/shard_map/ppermute | solution.py:419
  5.7 0.5 %collective-permute-start.4 = (f32[1056,128]{1,0:T(8,128)S(1)}, f32[1056,128]{1,0:T(8,128)S(1)}, u32[]{:S(2)}, u32[]{:S(2)}) collective-permute-start(f32[1056,128]{1,0:T(8,128)S(1)} %get-tuple-element.29), channel_id=1, source_target_pairs={{0,16},{8,24},{16,0},{24,8},{1,17},{9,25},{17,1},{25,9},{2,18},{10... | collective-permute-start | bytes 1622024 | tf_op jit(solution)/shard_map/ppermute | solution.py:419
  6.2 0.1 collective-permute-start.3
  6.4 0.0 copy-done
  6.4 1.2 %edges.1 = (f32[64,128]{1,0:T(8,128)S(1)}, f32[1056,128]{1,0:T(8,128)S(1)}, f32[704,128]{1,0:T(8,128)S(1)}, f32[240,128]{1,0:T(8,128)S(1)}) custom-call(f32[16,256,128]{2,1,0:T(8,128)S(1)} %copy-done, f32[1056,128]{1,0:T(8,128)S(1)} %get-tuple-element.22._), custom_call_target="tpu_custom_call" | custom-call | flops 1000000000 | tf_op jit(solution)/shard_map/edges/pallas_call | solution.py:467
  7.5 0.7 %collective-permute-start.1 = (f32[64,128]{1,0:T(8,128)S(1)}, f32[64,128]{1,0:T(8,128)S(1)}, u32[]{:S(2)}, u32[]{:S(2)}) collective-permute-start(f32[64,128]{1,0:T(8,128)S(1)} %get-tuple-element.24), channel_id=1, source_target_pairs={{1,2},{3,4},{5,6},{2,1},{4,3},{6,5},{9,10},{11,12},{13,14},{10,9},... | collective-permute-start | bytes 98312 | tf_op jit(solution)/shard_map/ppermute | solution.py:415
  8.2 3.4 %collective-permute-start = (f32[64,128]{1,0:T(8,128)S(1)}, f32[64,128]{1,0:T(8,128)S(1)}, u32[]{:S(2)}, u32[]{:S(2)}) collective-permute-start(f32[64,128]{1,0:T(8,128)S(1)} %get-tuple-element.24), channel_id=1, source_target_pairs={{0,1},{2,3},{4,5},{6,7},{1,0},{3,2},{5,4},{7,6},{8,9},{10,11},{12,... | collective-permute-start | bytes 98312 | tf_op jit(solution)/shard_map/ppermute | solution.py:415
  12.3 0.0 copy-done.3
  12.3 0.1 copy.7.lights_ref
  12.4 0.1 copy.8.curves_ref
  12.4 0.0 collective-permute-done.1.odd_ref
  12.4 0.0 collective-permute-done.even_ref
  12.5 0.0 collective-permute-done.2._.refs_3_
  12.5 0.1 sides.1
  12.6 1.6 %collective-permute-start.6 = (f32[16,128]{1,0:T(8,128)S(1)}, f32[16,128]{1,0:T(8,128)S(1)}, u32[]{:S(2)}, u32[]{:S(2)}) collective-permute-start(f32[16,128]{1,0:T(8,128)S(1)} %get-tuple-element.32), channel_id=1, source_target_pairs={{0,8},{8,0},{16,24},{24,16},{1,9},{9,1},{17,25},{25,17},{2,10},{10... | collective-permute-start | bytes 24584 | tf_op jit(solution)/shard_map/ppermute | solution.py:419
  14.1 1.5 %collective-permute-start.7 = (f32[16,128]{1,0:T(8,128)S(1)}, f32[16,128]{1,0:T(8,128)S(1)}, u32[]{:S(2)}, u32[]{:S(2)}) collective-permute-start(f32[16,128]{1,0:T(8,128)S(1)} %get-tuple-element.33), channel_id=1, source_target_pairs={{0,16},{8,24},{16,0},{24,8},{1,17},{9,25},{17,1},{25,9},{2,18},{10... | collective-permute-start | bytes 24584 | tf_op jit(solution)/shard_map/ppermute | solution.py:419
  15.7 0.5 %collective-permute-start.5 = (f32[704,128]{1,0:T(8,128)S(1)}, f32[704,128]{1,0:T(8,128)S(1)}, u32[]{:S(2)}, u32[]{:S(2)}) collective-permute-start(f32[704,128]{1,0:T(8,128)S(1)} %constant_dynamic-update-slice_fusion), channel_id=1, source_target_pairs={{0,24},{8,16},{16,8},{24,0},{1,25},{9,17},{17,9},{25,1},{2,26},{10... | collective-permute-start | bytes 1081352 | tf_op jit(solution)/shard_map/ppermute | solution.py:419
  16.1 3.6 %own.1 = (f32[16,64,128]{2,1,0:T(8,128)S(1)}, f32[4,3,8,128]{3,2,1,0:T(8,128)S(1)}, bf16[128,192]{1,0:T(8,128)(2,1)S(1)}) custom-call(s32[4]{0:T(128)S(1)} %copy-done.1, s32[1]{0:T(128)S(6)} %copy.11.flip_ref, f32[16,3]{1,0:T(8,128)S(1)} %copy.7.lights_ref, f32[16,4,8]{2,1,0:T(4,128)S(1)} %copy.8.curves_ref, ...), custom_call_target="tpu_custom_call" | custom-call | flops 4000000000 | tf_op jit(solution)/shard_map/own/pallas_call | solution.py:492
  19.8 1.8 %collective-permute-done.6.refs_5_ = f32[16,128]{1,0:T(8,128)S(1)} collective-permute-done((f32[16,128]{1,0:T(8,128)S(1)}, f32[16,128]{1,0:T(8,128)S(1)}, u32[]{:S(2)}, u32[]{:S(2)}) %collective-permute-start.6) | collective-permute-done | bytes 8224 | tf_op jit(solution)/shard_map/ppermute | solution.py:419
  21.6 0.0 collective-permute-done.7.refs_6_
  21.6 1.5 %collective-permute-start.8 = (f32[240,128]{1,0:T(8,128)S(1)}, f32[240,128]{1,0:T(8,128)S(1)}, u32[]{:S(2)}, u32[]{:S(2)}) collective-permute-start(f32[240,128]{1,0:T(8,128)S(1)} %get-tuple-element.35), channel_id=1, source_target_pairs={{0,24},{8,16},{16,8},{24,0},{1,25},{9,17},{17,9},{25,1},{2,26},{10... | collective-permute-start | bytes 368648 | tf_op jit(solution)/shard_map/ppermute | solution.py:419
  23.1 0.0 collective-permute-done.4.refs_2_
  23.1 0.0 collective-permute-done.3.refs_1_
  23.1 6.2 %near.1.refs_5_.refs_7_ = f32[3,16,64,128]{3,2,1,0:T(8,128)S(1)} custom-call(s32[1]{0:T(128)S(6)} %copy.11.flip_ref, f32[4,3,8,128]{3,2,1,0:T(8,128)S(1)} %get-tuple-element.27.vector_ref, bf16[128,192]{1,0:T(8,128)(2,1)S(1)} %get-tuple-element.28.weight_ref, f32[16,64,128]{2,1,0:T(8,128)S(1)} %get-tuple-element.36.inner_ref, ...), custom_call_target="tpu_custom_call" | custom-call | flops 60000002048 | tf_op jit(solution)/shard_map/near/pallas_call | solution.py:501
  29.4 0.3 collective-permute-done.5.refs_4_
  29.7 3.1 %far.1.refs_6_ = f32[4,4,64,128]{3,2,1,0:T(8,128)} custom-call(s32[1]{0:T(128)S(6)} %copy.11.flip_ref, f32[4,3,8,128]{3,2,1,0:T(8,128)S(1)} %get-tuple-element.27.vector_ref, bf16[128,192]{1,0:T(8,128)(2,1)S(1)} %get-tuple-element.28.weight_ref, f32[1056,128]{1,0:T(8,128)S(1)} %get-tuple-element.23.own_ref.refs_0_, ...), custom_call_target="tpu_custom_call" | custom-call | flops 2000000000 | tf_op jit(solution)/shard_map/far/pallas_call | solution.py:513
  32.8 0.0 collective-permute-done.8.refs_5_
  32.8 1.4 %late.1 = f32[4,4,64,128]{3,2,1,0:T(8,128)} custom-call(s32[1]{0:T(128)S(6)} %copy.11.flip_ref, f32[4,3,8,128]{3,2,1,0:T(8,128)S(1)} %get-tuple-element.27.vector_ref, bf16[128,192]{1,0:T(8,128)(2,1)S(1)} %get-tuple-element.28.weight_ref, f32[1056,128]{1,0:T(8,128)S(1)} %get-tuple-element.23.own_ref.refs_0_, ...), custom_call_target="tpu_custom_call", output_to_operand_aliasing={{}: (9, {})} | custom-call | flops 2000000000 | tf_op jit(solution)/shard_map/late/pallas_call | solution.py:513
  (4 shorter events, 0.0 us)
Async XLA Ops:
  0.0 6.4 %copy-start = (f32[16,256,128]{2,1,0:T(8,128)S(1)}, f32[16,256,128]{2,1,0:T(8,128)}, u32[]{:S(2)}) copy-start(f32[16,256,128]{2,1,0:T(8,128)} %field_ref.3) | copy-start | bytes 6291460
  1.7 10.5 %copy-start.3 = (f32[16,3]{0,1:T(4,128)S(1)}, f32[16,3]{0,1:T(4,128)}, u32[]{:S(2)}) copy-start(f32[16,3]{0,1:T(4,128)} %param.6) | copy-start | bytes 580
  1.7 10.6 %copy-start.2 = (f32[16,4,8]{0,2,1:T(8,128)S(1)}, f32[16,4,8]{0,2,1:T(8,128)}, u32[]{:S(2)}) copy-start(f32[16,4,8]{0,2,1:T(8,128)} %param.7) | copy-start | bytes 6148
  1.7 14.4 %copy-start.1 = (s32[4]{0:T(128)S(1)}, s32[4]{0:T(128)}, u32[]{:S(2)}) copy-start(s32[4]{0:T(128)} %index_ref.1) | copy-start | bytes 52
  1.8 10.7 %collective-permute-start.2 = (f32[160,128]{1,0:T(8,128)S(1)}, f32[160,128]{1,0:T(8,128)S(1)}, u32[]{:S(2)}, u32[]{:S(2)}) collective-permute-start(f32[160,128]{1,0:T(8,128)S(1)} %get-tuple-element.25), channel_id=1, source_target_pairs={{0,24},{8,16},{16,8},{24,0},{1,25},{9,17},{17,9},{25,1},{2,26},{10... | collective-permute-start | bytes 245768 | tf_op jit(solution)/shard_map/ppermute | solution.py:419
  5.7 17.4 %collective-permute-start.4 = (f32[1056,128]{1,0:T(8,128)S(1)}, f32[1056,128]{1,0:T(8,128)S(1)}, u32[]{:S(2)}, u32[]{:S(2)}) collective-permute-start(f32[1056,128]{1,0:T(8,128)S(1)} %get-tuple-element.29), channel_id=1, source_target_pairs={{0,16},{8,24},{16,0},{24,8},{1,17},{9,25},{17,1},{25,9},{2,18},{10... | collective-permute-start | bytes 1622024 | tf_op jit(solution)/shard_map/ppermute | solution.py:419
  6.2 16.9 %collective-permute-start.3 = (f32[1056,128]{1,0:T(8,128)S(1)}, f32[1056,128]{1,0:T(8,128)S(1)}, u32[]{:S(2)}, u32[]{:S(2)}) collective-permute-start(f32[1056,128]{1,0:T(8,128)S(1)} %get-tuple-element.22._), channel_id=1, source_target_pairs={{0,8},{8,0},{16,24},{24,16},{1,9},{9,1},{17,25},{25,17},{2,10},{10... | collective-permute-start | bytes 1622024 | tf_op jit(solution)/shard_map/ppermute | solution.py:419
  7.5 4.9 %collective-permute-start.1 = (f32[64,128]{1,0:T(8,128)S(1)}, f32[64,128]{1,0:T(8,128)S(1)}, u32[]{:S(2)}, u32[]{:S(2)}) collective-permute-start(f32[64,128]{1,0:T(8,128)S(1)} %get-tuple-element.24), channel_id=1, source_target_pairs={{1,2},{3,4},{5,6},{2,1},{4,3},{6,5},{9,10},{11,12},{13,14},{10,9},... | collective-permute-start | bytes 98312 | tf_op jit(solution)/shard_map/ppermute | solution.py:415
  8.2 4.3 %collective-permute-start = (f32[64,128]{1,0:T(8,128)S(1)}, f32[64,128]{1,0:T(8,128)S(1)}, u32[]{:S(2)}, u32[]{:S(2)}) collective-permute-start(f32[64,128]{1,0:T(8,128)S(1)} %get-tuple-element.24), channel_id=1, source_target_pairs={{0,1},{2,3},{4,5},{6,7},{1,0},{3,2},{5,4},{7,6},{8,9},{10,11},{12,... | collective-permute-start | bytes 98312 | tf_op jit(solution)/shard_map/ppermute | solution.py:415
  12.6 9.0 %collective-permute-start.6 = (f32[16,128]{1,0:T(8,128)S(1)}, f32[16,128]{1,0:T(8,128)S(1)}, u32[]{:S(2)}, u32[]{:S(2)}) collective-permute-start(f32[16,128]{1,0:T(8,128)S(1)} %get-tuple-element.32), channel_id=1, source_target_pairs={{0,8},{8,0},{16,24},{24,16},{1,9},{9,1},{17,25},{25,17},{2,10},{10... | collective-permute-start | bytes 24584 | tf_op jit(solution)/shard_map/ppermute | solution.py:419
  14.1 7.5 %collective-permute-start.7 = (f32[16,128]{1,0:T(8,128)S(1)}, f32[16,128]{1,0:T(8,128)S(1)}, u32[]{:S(2)}, u32[]{:S(2)}) collective-permute-start(f32[16,128]{1,0:T(8,128)S(1)} %get-tuple-element.33), channel_id=1, source_target_pairs={{0,16},{8,24},{16,0},{24,8},{1,17},{9,25},{17,1},{25,9},{2,18},{10... | collective-permute-start | bytes 24584 | tf_op jit(solution)/shard_map/ppermute | solution.py:419
  15.7 14.0 %collective-permute-start.5 = (f32[704,128]{1,0:T(8,128)S(1)}, f32[704,128]{1,0:T(8,128)S(1)}, u32[]{:S(2)}, u32[]{:S(2)}) collective-permute-start(f32[704,128]{1,0:T(8,128)S(1)} %constant_dynamic-update-slice_fusion), channel_id=1, source_target_pairs={{0,24},{8,16},{16,8},{24,0},{1,25},{9,17},{17,9},{25,1},{2,26},{10... | collective-permute-start | bytes 1081352 | tf_op jit(solution)/shard_map/ppermute | solution.py:419
  21.6 11.2 %collective-permute-start.8 = (f32[240,128]{1,0:T(8,128)S(1)}, f32[240,128]{1,0:T(8,128)S(1)}, u32[]{:S(2)}, u32[]{:S(2)}) collective-permute-start(f32[240,128]{1,0:T(8,128)S(1)} %get-tuple-element.35), channel_id=1, source_target_pairs={{0,24},{8,16},{16,8},{24,0},{1,25},{9,17},{17,9},{25,1},{2,26},{10... | collective-permute-start | bytes 368648 | tf_op jit(solution)/shard_map/ppermute | solution.py:419

commit v11 on v10

--- a/solution.py
+++ b/solution.py
@@ -14,6 +14,7 @@
 SMEM = pltpu.SMEM
 MIB = 1 << 20
 FINE = 49152.0
+WHOLE = 12582912.0
 
 
 def pack_kernel(parts, field_ref, *refs):
@@ -173,7 +174,46 @@
         weight_ref[2 * pair * SUB : 2 * (pair + 1) * SUB, :] = value.astype(jnp.bfloat16)
 
 
-def prepare_steps(m, zs, where, lateral, base, cells, rows, parts, cols, ends_ref, weight_ref, cell_ref, mixed_ref):
+def mix_steps(zs, places, base, cols, weight_ref, mixed_ref):
+    knots = weight_ref.shape[1] // (3 * SUB)
+    half = 0.5 * (knots - 1)
+    row = lax.broadcasted_iota(jnp.int32, (2 * SUB, cols), 0)
+    knot_at = [jnp.where(row < SUB, 0.0 + k, 1.0 + k).astype(jnp.bfloat16) for k in range(0, knots, 2)]
+    zero = jnp.zeros((2 * SUB, cols), jnp.bfloat16)
+
+    def twice(value):
+        return jnp.concatenate([value, value], axis=0).astype(jnp.bfloat16)
+
+    def basis(z):
+        ref, low = places[z]
+        scaled = half * jnp.tanh(0.5 * ref[pl.ds(low + base, SUB), :])
+        position = scaled + half
+        segment = ((scaled + (half - 0.5)) + WHOLE) - WHOLE
+        coarse = (position + FINE) - FINE
+        right = coarse - segment
+        left, right, rest = twice(1.0 - right), twice(right), twice(position - coarse)
+        here = twice(segment)
+        after = twice(segment + 1.0)
+        tents, rests = [], []
+        for at in knot_at:
+            is_here = here == at
+            tents.append(jnp.where(is_here, left, jnp.where(after == at, right, zero)))
+            rests.append(jnp.where(is_here, rest, zero))
+        return [jnp.concatenate(part, axis=0) for part in (tents, rests)]
+
+    def two(first, second):
+        tents, rests = [jnp.concatenate(both, axis=1) for both in zip(basis(first), basis(second))]
+        right = jnp.concatenate([tents, rests, tents], axis=0)
+        mixed = jnp.dot(weight_ref[...], right, preferred_element_type=jnp.float32)
+        mixed_ref[first] = mixed[:, :cols]
+        mixed_ref[second] = mixed[:, cols:]
+
+    zs = list(zs)
+    return [functools.partial(two, *zs[i : i + 2]) for i in range(0, len(zs), 2)]
+
+
+def slope_steps(m, zs, where, lateral, base, cells, rows, parts, cols, ends_ref, cell_ref):
+    places, tops, bottoms = where
     me = lax.axis_index("depth")
     part = me ^ m
     at = pl.ds(base, SUB)
@@ -181,7 +221,10 @@
     sublane = lax.broadcasted_iota(jnp.int32, (SUB, cols), 0)
     is_first = lane == 0
     is_last = lane == cols - 1
-    places, tops, bottoms = where
+    is_top = {low: jnp.logical_and(sublane == 0, base == low) for low in sorted({top[0] for top in tops})}
+    is_bottom = {
+        low: jnp.logical_and(sublane == SUB - 1, base == low) for low in sorted({bottom[0] for bottom in bottoms})
+    }
     group = rows // parts
     got = lateral[pl.ds(pl.multiple_of(base % group, SUB), SUB), :]
     sides = pltpu.roll(got, (2 * cols - 1 - base // group * (cols // parts)) % cols, 1)
@@ -199,10 +242,8 @@
         here = layer(z)
         top_at, top_ref, top = tops[z]
         bottom_at, bottom_ref, bottom = bottoms[z]
-        is_top = jnp.logical_and(sublane == 0, base == top_at)
-        is_bottom = jnp.logical_and(sublane == SUB - 1, base == bottom_at)
-        upper = jnp.where(is_top, top_ref[top : top + 1, :], ref[pl.ds(low + base - 1, SUB), :])
-        lower = jnp.where(is_bottom, bottom_ref[bottom : bottom + 1, :], ref[pl.ds(low + base + 1, SUB), :])
+        upper = jnp.where(is_top[top_at], top_ref[top : top + 1, :], ref[pl.ds(low + base - 1, SUB), :])
+        lower = jnp.where(is_bottom[bottom_at], bottom_ref[bottom : bottom + 1, :], ref[pl.ds(low + base + 1, SUB), :])
         edge = pltpu.roll(sides, (cols - 2 * z) % cols, 1) if z else sides
         grad_x = pltpu.roll(jnp.where(is_first, edge, here), cols - 1, 1) - pltpu.roll(
             jnp.where(is_last, edge, here), 1, 1
@@ -213,35 +254,20 @@
         cell_ref[0, z] = grad_x * inverse
         cell_ref[1, z] = grad_y * inverse
         cell_ref[2, z] = grad_z * inverse
-        half = 0.5 * (knots - 1)
-        position = half + half * jnp.tanh(0.5 * here)
-        coarse = (position + FINE) - FINE
-        segment = jnp.minimum(jnp.floor(position), knots - 2.0)
-        rest = position - coarse
-        right = coarse - segment
-        left = 1.0 - right
-        twice = lambda value: jnp.concatenate([value, value], axis=0).astype(jnp.bfloat16)
-        left, right, rest, segment = twice(left), twice(right), twice(rest), twice(segment)
-        zero = jnp.zeros_like(left)
-        tents, rests = [], []
-        for k in range(0, knots, 2):
-            is_here = segment == pair_at + k
-            is_before = segment == pair_at + (k - 1)
-            tents.append(jnp.where(is_here, left, jnp.where(is_before, right, zero)))
-            rests.append(jnp.where(is_here, rest, zero))
-        return [jnp.concatenate(part, axis=0) for part in (tents, rests)]
-
-    def two(first, second):
-        tents, rests = [jnp.concatenate(both, axis=1) for both in zip(step(first), step(second))]
-        right = jnp.concatenate([tents, rests, tents], axis=0)
-        mixed = jnp.dot(weight_ref[...], right, preferred_element_type=jnp.float32)
-        mixed_ref[first] = mixed[:, :cols]
-        mixed_ref[second] = mixed[:, cols:]
-
-    knots = weight_ref.shape[1] // (3 * SUB)
-    pair_at = jnp.where(lax.broadcasted_iota(jnp.int32, (2 * SUB, cols), 0) < SUB, 0.0, 1.0).astype(jnp.bfloat16)
-    zs = list(zs)
-    return [functools.partial(two, *zs[i : i + 2]) for i in range(0, len(zs), 2)]
+
+    return [functools.partial(step, z) for z in zs]
+
+
+def prepare_steps(m, zs, where, lateral, base, cells, rows, parts, cols, ends_ref, weight_ref, cell_ref, mixed_ref):
+    slopes = slope_steps(m, zs, where, lateral, base, cells, rows, parts, cols, ends_ref, cell_ref)
+    mixes = mix_steps(zs, where[0], base, cols, weight_ref, mixed_ref)
+
+    def both(i):
+        mixes[i]()
+        for step in slopes[2 * i : 2 * i + 2]:
+            step()
+
+    return [functools.partial(both, i) for i in range(len(mixes))]
 
 
 def march_unit(flip, vector_ref, zs, cells, cell_ref, mixed_ref, beside, inner=None):
@@ -288,34 +314,44 @@
     unit(start + count - 1, 1, [])
 
 
-def own_kernel(parts, index_ref, flip_ref, lights_ref, curves_ref, own_ref, lateral_ref, out_ref, vector_ref, weight_ref, *refs):
-    cell_refs, mixed_refs = refs[:2], refs[2:]
-    rows, cols = out_ref.shape[1:]
-    channels = curves_ref.shape[1]
+def mix_kernel(parts, index_ref, lights_ref, curves_ref, own_ref, vector_ref, weight_ref, mixed_ref):
+    tiles, cells, _, cols = mixed_ref.shape
     passes = index_ref.shape[0]
-    cells = cell_refs[0].shape[1]
-    flip = flip_ref[0]
-    tiles = rows // SUB
-    inner = range(1, cells - 1)
     for p in range(passes):
         for axis in range(3):
             vector_ref[p, axis] = jnp.full((SUB, cols), lights_ref[index_ref[p], axis])
     fill_weights(index_ref, curves_ref, OPACITY / (parts * cells), weight_ref)
-    places = near_places(cells, rows, own_ref)
+    places, _, _ = near_places(cells, tiles * SUB, own_ref)
+
+    def tile(i, carry):
+        base = pl.multiple_of(i * SUB, SUB)
+        for step in mix_steps(range(1, cells - 1), places, base, cols, weight_ref, mixed_ref.at[i]):
+            step()
+        return carry
+
+    lax.fori_loop(0, tiles, tile, 0)
+
+
+def own_kernel(parts, flip_ref, vector_ref, own_ref, mixed_ref, lateral_ref, out_ref, *cell_refs):
+    rows, cols = out_ref.shape[1:]
+    passes = vector_ref.shape[0]
+    channels = out_ref.shape[0] // passes
+    cells = cell_refs[0].shape[1]
+    flip = flip_ref[0]
+    inner = range(1, cells - 1)
+    where = near_places(cells, rows, own_ref)
 
     def prepare(base, slot):
-        return prepare_steps(
-            0, inner, places, lateral_ref, base, cells, rows, parts, cols, None, weight_ref, cell_refs[slot], mixed_refs[slot]
-        )
+        return slope_steps(0, inner, where, lateral_ref, base, cells, rows, parts, cols, None, cell_refs[slot])
 
     def unit(index, slot, beside):
         base = pl.multiple_of(index * SUB, SUB)
-        result = march_unit(flip, vector_ref, inner, cells, cell_refs[slot], mixed_refs[slot], beside)
+        result = march_unit(flip, vector_ref, inner, cells, cell_refs[slot], mixed_ref.at[index], beside)
         for p in range(passes):
             for j in range(channels):
                 out_ref[p * channels + j, pl.ds(base, SUB), :] = result[p][j]
 
-    march_tiles(tiles, 0, prepare, unit)
+    march_tiles(rows // SUB, 0, prepare, unit)
 
 
 def near_kernel(parts, flip_ref, vector_ref, weight_ref, inner_ref, *refs):
@@ -489,15 +525,23 @@
     mixed_shape = VMEM((cells, values * SUB, cols), jnp.float32)
     ends_shape = VMEM((parts + 2, 2, rows, cols), jnp.float32)
     weight_shape = jax.ShapeDtypeStruct((values * SUB, 3 * knots * SUB), jnp.bfloat16)
-    inner, vectors, weights = pl.pallas_call(
+    vectors, weights, mixed = pl.pallas_call(
+        functools.partial(mix_kernel, parts),
+        out_shape=[array(passes, 3, SUB, cols), weight_shape, array(tiles, cells, values * SUB, cols)],
+        in_specs=[in_smem] * 2 + [in_vmem] * 2,
+        out_specs=[in_vmem] * 3,
+        name="mix",
+        **settings(8, 0.5),
+    )(light_index, light_vectors, transfer, own)
+    inner = pl.pallas_call(
         functools.partial(own_kernel, parts),
-        out_shape=[array(values, rows, cols), array(passes, 3, SUB, cols), weight_shape],
-        in_specs=[in_smem] * 3 + [in_vmem] * 3,
-        out_specs=[in_vmem] * 3,
-        scratch_shapes=[cell_shape] * 2 + [mixed_shape] * 2,
+        out_shape=array(values, rows, cols),
+        in_specs=[in_smem] + [in_vmem] * 4,
+        out_specs=in_vmem,
+        scratch_shapes=[cell_shape] * 2,
         name="own",
-        **settings(12, 4),
-    )(light_index, flips, light_vectors, transfer, own, sides[0])
+        **settings(8, 2),
+    )(flips, vectors, own, mixed, sides[0])
     states = pl.pallas_call(
         functools.partial(near_kernel, parts),
         out_shape=array(parts - 1, values, rows, cols),

time: 34.4 us -> 39.6 us (1.15)
  waiting for transfers between devices: 2.21 us -> 4.91 us
  Pallas kernels: 17.4 us -> 19.3 us
  starting transfers between devices: 13.7 us -> 14.3 us
    ppermute x7, waiting for transfers between devices: 2.18 us -> 4.91 us  [swap_along(): lax.ppermute(block, axis, [(i, i ^ mask) for i in range(lax.axis_size(axi...]
    pallas_call x1 -> x2, Pallas kernels: 3.62 us -> 5.3 us  [the longest x1 3.31 us: on_device(): pl.pallas_call(functools.partial(mix_kernel, parts), out_shape=[array(pas...]
    ppermute x7, starting transfers between devices: 9.64 us -> 10.2 us  [swap_along(): lax.ppermute(block, axis, [(i, i ^ mask) for i in range(lax.axis_size(axi...]
  transfers between devices with their start and end apart: 9 -> 9, of which waited for: 2 -> 2; matrix products, arithmetic and copies ran while one was open for 0% -> 0% of each run, Pallas kernels for 42% -> 41%
where the time goes in v11:
time: 39.6 us; the launch traced here: 39.5 us
  Pallas kernels  19.3 us (49%)
  starting transfers between devices  14.3 us (36%)
  waiting for transfers between devices  4.91 us (12%)
  between operations  0.79 us (2%)
    ppermute x7, starting transfers between devices, swap_along(): lax.ppermute(block, axis, [(i, i ^ mask) for i in range(lax.axis_size(axi...  10.2 us
    pallas_call x1, Pallas kernels, on_device(): pl.pallas_call(functools.partial(near_kernel, parts), out_shape=array(par...  6.43 us
    ppermute x7, waiting for transfers between devices, swap_along(): lax.ppermute(block, axis, [(i, i ^ mask) for i in range(lax.axis_size(axi...  4.91 us
    pallas_call x2, Pallas kernels, on_device(): pl.pallas_call(functools.partial(far_kernel, parts, split, low, high), ou...  4.58 us
    ppermute x2, starting transfers between devices, swap_pairs(): return lax.ppermute(block, axis, pairs + [(j, i) for i, j in pairs])  4.09 us
    pallas_call x1, Pallas kernels, on_device(): pl.pallas_call(functools.partial(mix_kernel, parts), out_shape=[array(pas...  3.31 us
    pallas_call x1, Pallas kernels, on_device(): pl.pallas_call(functools.partial(own_kernel, parts), out_shape=array(valu...  1.99 us
    pallas_call x1, Pallas kernels, on_device(): pl.pallas_call(functools.partial(pack_kernel, parts), out_shape=[array(ne...  1.71 us
  transfers between devices with their start and end apart: 9, of which 2 were waited for; matrix products, arithmetic and copies ran while one was open for 0% of the time, Pallas kernels for 41%

profile of v11, /device:TPU:0, one launch (start us, length us, event | category | flops | bytes accessed | tf_op | source)
XLA Modules:
  0.0 39.5 jit_solution(4060428806935111508)
XLA Ops:
  0.0 1.7 %pack.1 = (f32[1056,128]{1,0:T(8,128)S(1)}, f32[1056,128]{1,0:T(8,128)S(1)}, f32[160,128]{1,0:T(8,128)S(1)}) custom-call(f32[16,256,128]{2,1,0:T(8,128)} %field_ref.3), custom_call_target="tpu_custom_call" | custom-call | flops 1000000000 | tf_op jit(solution)/shard_map/pack/pallas_call | solution.py:490
  1.7 0.0 copy-start.3
  1.7 0.0 copy-start.2
  1.7 0.0 copy-start.1
  1.8 3.0 %collective-permute-start.1 = (f32[1056,128]{1,0:T(8,128)S(1)}, f32[1056,128]{1,0:T(8,128)S(1)}, u32[]{:S(2)}, u32[]{:S(2)}) collective-permute-start(f32[1056,128]{1,0:T(8,128)S(1)} %get-tuple-element.26), channel_id=1, source_target_pairs={{0,16},{8,24},{16,0},{24,8},{1,17},{9,25},{17,1},{25,9},{2,18},{10... | collective-permute-start | bytes 1622024 | tf_op jit(solution)/shard_map/ppermute | solution.py:455
  4.8 1.5 %collective-permute-start = (f32[1056,128]{1,0:T(8,128)S(1)}, f32[1056,128]{1,0:T(8,128)S(1)}, u32[]{:S(2)}, u32[]{:S(2)}) collective-permute-start(f32[1056,128]{1,0:T(8,128)S(1)} %get-tuple-element.22._), channel_id=1, source_target_pairs={{0,8},{8,0},{16,24},{24,16},{1,9},{9,1},{17,25},{25,17},{2,10},{10... | collective-permute-start | bytes 1622024 | tf_op jit(solution)/shard_map/ppermute | solution.py:455
  6.3 0.0 collective-permute-start.2
  6.3 1.2 %edges.1 = (f32[64,128]{1,0:T(8,128)S(1)}, f32[1056,128]{1,0:T(8,128)S(1)}, f32[704,128]{1,0:T(8,128)S(1)}, f32[240,128]{1,0:T(8,128)S(1)}) custom-call(f32[16,256,128]{2,1,0:T(8,128)S(1)} %copy-done, f32[1056,128]{1,0:T(8,128)S(1)} %get-tuple-element.22._), custom_call_target="tpu_custom_call" | custom-call | flops 1000000000 | tf_op jit(solution)/shard_map/edges/pallas_call | solution.py:503
  7.5 0.7 %collective-permute-start.4 = (f32[64,128]{1,0:T(8,128)S(1)}, f32[64,128]{1,0:T(8,128)S(1)}, u32[]{:S(2)}, u32[]{:S(2)}) collective-permute-start(f32[64,128]{1,0:T(8,128)S(1)} %get-tuple-element.29), channel_id=1, source_target_pairs={{1,2},{3,4},{5,6},{2,1},{4,3},{6,5},{9,10},{11,12},{13,14},{10,9},... | collective-permute-start | bytes 98312 | tf_op jit(solution)/shard_map/ppermute | solution.py:451
  8.2 3.4 %collective-permute-start.3 = (f32[64,128]{1,0:T(8,128)S(1)}, f32[64,128]{1,0:T(8,128)S(1)}, u32[]{:S(2)}, u32[]{:S(2)}) collective-permute-start(f32[64,128]{1,0:T(8,128)S(1)} %get-tuple-element.29), channel_id=1, source_target_pairs={{0,1},{2,3},{4,5},{6,7},{1,0},{3,2},{5,4},{7,6},{8,9},{10,11},{12,... | collective-permute-start | bytes 98312 | tf_op jit(solution)/shard_map/ppermute | solution.py:451
  12.3 0.1 copy.7.lights_ref
  12.3 0.0 copy-done.2
  12.4 0.1 copy.8.curves_ref
  12.4 3.3 %mix.1 = (f32[4,3,8,128]{3,2,1,0:T(8,128)S(1)}, bf16[128,192]{1,0:T(8,128)(2,1)S(1)}, f32[8,16,128,128]{3,2,1,0:T(8,128)S(1)}) custom-call(s32[4]{0:T(128)S(1)} %copy-done.1, f32[16,3]{1,0:T(8,128)S(1)} %copy.7.lights_ref, f32[16,4,8]{2,1,0:T(4,128)S(1)} %copy.8.curves_ref, f32[1056,128]{1,0:T(8,128)S(1)} %get-tuple-element.23.own_ref.refs_0_), custom_call_target="tpu_custom_call" | custom-call | flops 500000000 | tf_op jit(solution)/shard_map/mix/pallas_call | solution.py:528
  15.8 0.0 collective-permute-done.4.odd_ref
  15.8 0.0 collective-permute-done.3.even_ref
  15.8 4.3 %collective-permute-done.2._.refs_3_ = f32[160,128]{1,0:T(8,128)S(1)} collective-permute-done((f32[160,128]{1,0:T(8,128)S(1)}, f32[160,128]{1,0:T(8,128)S(1)}, u32[]{:S(2)}, u32[]{:S(2)}) %collective-permute-start.2) | collective-permute-done | bytes 81952 | tf_op jit(solution)/shard_map/ppermute | solution.py:455
  20.1 0.1 sides.1
  20.2 1.7 %collective-permute-start.6 = (f32[16,128]{1,0:T(8,128)S(1)}, f32[16,128]{1,0:T(8,128)S(1)}, u32[]{:S(2)}, u32[]{:S(2)}) collective-permute-start(f32[16,128]{1,0:T(8,128)S(1)} %get-tuple-element.31), channel_id=1, source_target_pairs={{0,8},{8,0},{16,24},{24,16},{1,9},{9,1},{17,25},{25,17},{2,10},{10... | collective-permute-start | bytes 24584 | tf_op jit(solution)/shard_map/ppermute | solution.py:455
  21.9 1.5 %collective-permute-start.7 = (f32[16,128]{1,0:T(8,128)S(1)}, f32[16,128]{1,0:T(8,128)S(1)}, u32[]{:S(2)}, u32[]{:S(2)}) collective-permute-start(f32[16,128]{1,0:T(8,128)S(1)} %get-tuple-element.32), channel_id=1, source_target_pairs={{0,16},{8,24},{16,0},{24,8},{1,17},{9,25},{17,1},{25,9},{2,18},{10... | collective-permute-start | bytes 24584 | tf_op jit(solution)/shard_map/ppermute | solution.py:455
  23.4 0.3 collective-permute-start.5
  23.7 2.0 %own.1.inner_ref = f32[16,64,128]{2,1,0:T(8,128)S(1)} custom-call(s32[1]{0:T(128)S(6)} %copy.11.flip_ref, f32[4,3,8,128]{3,2,1,0:T(8,128)S(1)} %get-tuple-element.24.vector_ref, f32[1056,128]{1,0:T(8,128)S(1)} %get-tuple-element.23.own_ref.refs_0_, f32[8,16,128,128]{3,2,1,0:T(8,128)S(1)} %get-tuple-element.35.mixed_ref, ...), custom_call_target="tpu_custom_call" | custom-call | flops 2000000000 | tf_op jit(solution)/shard_map/own/pallas_call | solution.py:536
  25.7 0.0 collective-permute-done.6.refs_5_
  25.7 0.6 %collective-permute-done.7.refs_6_ = f32[16,128]{1,0:T(8,128)S(1)} collective-permute-done((f32[16,128]{1,0:T(8,128)S(1)}, f32[16,128]{1,0:T(8,128)S(1)}, u32[]{:S(2)}, u32[]{:S(2)}) %collective-permute-start.7) | collective-permute-done | bytes 8224 | tf_op jit(solution)/shard_map/ppermute | solution.py:455
  26.3 2.1 %collective-permute-start.8 = (f32[240,128]{1,0:T(8,128)S(1)}, f32[240,128]{1,0:T(8,128)S(1)}, u32[]{:S(2)}, u32[]{:S(2)}) collective-permute-start(f32[240,128]{1,0:T(8,128)S(1)} %get-tuple-element.34), channel_id=1, source_target_pairs={{0,24},{8,16},{16,8},{24,0},{1,25},{9,17},{17,9},{25,1},{2,26},{10... | collective-permute-start | bytes 368648 | tf_op jit(solution)/shard_map/ppermute | solution.py:455
  28.4 0.0 collective-permute-done.1.refs_2_
  28.4 0.0 collective-permute-done.refs_1_
  28.4 6.4 %near.1.refs_5_.refs_7_ = f32[3,16,64,128]{3,2,1,0:T(8,128)S(1)} custom-call(s32[1]{0:T(128)S(6)} %copy.11.flip_ref, f32[4,3,8,128]{3,2,1,0:T(8,128)S(1)} %get-tuple-element.24.vector_ref, bf16[128,192]{1,0:T(8,128)(2,1)S(1)} %get-tuple-element.25.weight_ref, f32[16,64,128]{2,1,0:T(8,128)S(1)} %own.1.inner_ref, ...), custom_call_target="tpu_custom_call" | custom-call | flops 60000002048 | tf_op jit(solution)/shard_map/near/pallas_call | solution.py:545
  34.9 0.0 collective-permute-done.5.refs_4_
  34.9 3.2 %far.1.refs_6_ = f32[4,4,64,128]{3,2,1,0:T(8,128)} custom-call(s32[1]{0:T(128)S(6)} %copy.11.flip_ref, f32[4,3,8,128]{3,2,1,0:T(8,128)S(1)} %get-tuple-element.24.vector_ref, bf16[128,192]{1,0:T(8,128)(2,1)S(1)} %get-tuple-element.25.weight_ref, f32[1056,128]{1,0:T(8,128)S(1)} %get-tuple-element.23.own_ref.refs_0_, ...), custom_call_target="tpu_custom_call" | custom-call | flops 2000000000 | tf_op jit(solution)/shard_map/far/pallas_call | solution.py:557
  38.1 0.0 collective-permute-done.8.refs_5_
  38.1 1.4 %late.1 = f32[4,4,64,128]{3,2,1,0:T(8,128)} custom-call(s32[1]{0:T(128)S(6)} %copy.11.flip_ref, f32[4,3,8,128]{3,2,1,0:T(8,128)S(1)} %get-tuple-element.24.vector_ref, bf16[128,192]{1,0:T(8,128)(2,1)S(1)} %get-tuple-element.25.weight_ref, f32[1056,128]{1,0:T(8,128)S(1)} %get-tuple-element.23.own_ref.refs_0_, ...), custom_call_target="tpu_custom_call", output_to_operand_aliasing={{}: (9, {})} | custom-call | flops 2000000000 | tf_op jit(solution)/shard_map/late/pallas_call | solution.py:557
  (5 shorter events, 0.0 us)
Async XLA Ops:
  0.0 6.3 %copy-start = (f32[16,256,128]{2,1,0:T(8,128)S(1)}, f32[16,256,128]{2,1,0:T(8,128)}, u32[]{:S(2)}) copy-start(f32[16,256,128]{2,1,0:T(8,128)} %field_ref.3) | copy-start | bytes 6291460
  1.7 10.5 %copy-start.3 = (f32[16,3]{0,1:T(4,128)S(1)}, f32[16,3]{0,1:T(4,128)}, u32[]{:S(2)}) copy-start(f32[16,3]{0,1:T(4,128)} %param.6) | copy-start | bytes 580
  1.7 10.6 %copy-start.2 = (f32[16,4,8]{0,2,1:T(8,128)S(1)}, f32[16,4,8]{0,2,1:T(8,128)}, u32[]{:S(2)}) copy-start(f32[16,4,8]{0,2,1:T(8,128)} %param.7) | copy-start | bytes 6148
  1.7 10.7 %copy-start.1 = (s32[4]{0:T(128)S(1)}, s32[4]{0:T(128)}, u32[]{:S(2)}) copy-start(s32[4]{0:T(128)} %index_ref.1) | copy-start | bytes 52
  1.8 26.7 %collective-permute-start.1 = (f32[1056,128]{1,0:T(8,128)S(1)}, f32[1056,128]{1,0:T(8,128)S(1)}, u32[]{:S(2)}, u32[]{:S(2)}) collective-permute-start(f32[1056,128]{1,0:T(8,128)S(1)} %get-tuple-element.26), channel_id=1, source_target_pairs={{0,16},{8,24},{16,0},{24,8},{1,17},{9,25},{17,1},{25,9},{2,18},{10... | collective-permute-start | bytes 1622024 | tf_op jit(solution)/shard_map/ppermute | solution.py:455
  4.8 23.6 %collective-permute-start = (f32[1056,128]{1,0:T(8,128)S(1)}, f32[1056,128]{1,0:T(8,128)S(1)}, u32[]{:S(2)}, u32[]{:S(2)}) collective-permute-start(f32[1056,128]{1,0:T(8,128)S(1)} %get-tuple-element.22._), channel_id=1, source_target_pairs={{0,8},{8,0},{16,24},{24,16},{1,9},{9,1},{17,25},{25,17},{2,10},{10... | collective-permute-start | bytes 1622024 | tf_op jit(solution)/shard_map/ppermute | solution.py:455
  6.3 13.8 %collective-permute-start.2 = (f32[160,128]{1,0:T(8,128)S(1)}, f32[160,128]{1,0:T(8,128)S(1)}, u32[]{:S(2)}, u32[]{:S(2)}) collective-permute-start(f32[160,128]{1,0:T(8,128)S(1)} %get-tuple-element.27), channel_id=1, source_target_pairs={{0,24},{8,16},{16,8},{24,0},{1,25},{9,17},{17,9},{25,1},{2,26},{10... | collective-permute-start | bytes 245768 | tf_op jit(solution)/shard_map/ppermute | solution.py:455
  7.5 8.3 %collective-permute-start.4 = (f32[64,128]{1,0:T(8,128)S(1)}, f32[64,128]{1,0:T(8,128)S(1)}, u32[]{:S(2)}, u32[]{:S(2)}) collective-permute-start(f32[64,128]{1,0:T(8,128)S(1)} %get-tuple-element.29), channel_id=1, source_target_pairs={{1,2},{3,4},{5,6},{2,1},{4,3},{6,5},{9,10},{11,12},{13,14},{10,9},... | collective-permute-start | bytes 98312 | tf_op jit(solution)/shard_map/ppermute | solution.py:451
  8.2 7.6 %collective-permute-start.3 = (f32[64,128]{1,0:T(8,128)S(1)}, f32[64,128]{1,0:T(8,128)S(1)}, u32[]{:S(2)}, u32[]{:S(2)}) collective-permute-start(f32[64,128]{1,0:T(8,128)S(1)} %get-tuple-element.29), channel_id=1, source_target_pairs={{0,1},{2,3},{4,5},{6,7},{1,0},{3,2},{5,4},{7,6},{8,9},{10,11},{12,... | collective-permute-start | bytes 98312 | tf_op jit(solution)/shard_map/ppermute | solution.py:451
  20.2 5.5 %collective-permute-start.6 = (f32[16,128]{1,0:T(8,128)S(1)}, f32[16,128]{1,0:T(8,128)S(1)}, u32[]{:S(2)}, u32[]{:S(2)}) collective-permute-start(f32[16,128]{1,0:T(8,128)S(1)} %get-tuple-element.31), channel_id=1, source_target_pairs={{0,8},{8,0},{16,24},{24,16},{1,9},{9,1},{17,25},{25,17},{2,10},{10... | collective-permute-start | bytes 24584 | tf_op jit(solution)/shard_map/ppermute | solution.py:455
  21.9 4.5 %collective-permute-start.7 = (f32[16,128]{1,0:T(8,128)S(1)}, f32[16,128]{1,0:T(8,128)S(1)}, u32[]{:S(2)}, u32[]{:S(2)}) collective-permute-start(f32[16,128]{1,0:T(8,128)S(1)} %get-tuple-element.32), channel_id=1, source_target_pairs={{0,16},{8,24},{16,0},{24,8},{1,17},{9,25},{17,1},{25,9},{2,18},{10... | collective-permute-start | bytes 24584 | tf_op jit(solution)/shard_map/ppermute | solution.py:455
  23.4 11.5 %collective-permute-start.5 = (f32[704,128]{1,0:T(8,128)S(1)}, f32[704,128]{1,0:T(8,128)S(1)}, u32[]{:S(2)}, u32[]{:S(2)}) collective-permute-start(f32[704,128]{1,0:T(8,128)S(1)} %constant_dynamic-update-slice_fusion), channel_id=1, source_target_pairs={{0,24},{8,16},{16,8},{24,0},{1,25},{9,17},{17,9},{25,1},{2,26},{10... | collective-permute-start | bytes 1081352 | tf_op jit(solution)/shard_map/ppermute | solution.py:455
  26.3 11.7 %collective-permute-start.8 = (f32[240,128]{1,0:T(8,128)S(1)}, f32[240,128]{1,0:T(8,128)S(1)}, u32[]{:S(2)}, u32[]{:S(2)}) collective-permute-start(f32[240,128]{1,0:T(8,128)S(1)} %get-tuple-element.34), channel_id=1, source_target_pairs={{0,24},{8,16},{16,8},{24,0},{1,25},{9,17},{17,9},{25,1},{2,26},{10... | collective-permute-start | bytes 368648 | tf_op jit(solution)/shard_map/ppermute | solution.py:455

commit v12 on v11

--- a/solution.py
+++ b/solution.py
@@ -10,6 +10,7 @@
 AMBIENT = 0.3
 OPACITY = 2.0
 SUB = 8
+GROUP = 4
 VMEM = pltpu.VMEM
 SMEM = pltpu.SMEM
 MIB = 1 << 20
@@ -201,15 +202,15 @@
             rests.append(jnp.where(is_here, rest, zero))
         return [jnp.concatenate(part, axis=0) for part in (tents, rests)]
 
-    def two(first, second):
-        tents, rests = [jnp.concatenate(both, axis=1) for both in zip(basis(first), basis(second))]
+    def several(group):
+        tents, rests = [jnp.concatenate(parts, axis=1) for parts in zip(*[basis(z) for z in group])]
         right = jnp.concatenate([tents, rests, tents], axis=0)
         mixed = jnp.dot(weight_ref[...], right, preferred_element_type=jnp.float32)
-        mixed_ref[first] = mixed[:, :cols]
-        mixed_ref[second] = mixed[:, cols:]
+        for j, z in enumerate(group):
+            mixed_ref[z] = mixed[:, j * cols : (j + 1) * cols]
 
     zs = list(zs)
-    return [functools.partial(two, *zs[i : i + 2]) for i in range(0, len(zs), 2)]
+    return [functools.partial(several, zs[i : i + GROUP]) for i in range(0, len(zs), GROUP)]
 
 
 def slope_steps(m, zs, where, lateral, base, cells, rows, parts, cols, ends_ref, cell_ref):
@@ -264,7 +265,7 @@
 
     def both(i):
         mixes[i]()
-        for step in slopes[2 * i : 2 * i + 2]:
+        for step in slopes[GROUP * i : GROUP * (i + 1)]:
             step()
 
     return [functools.partial(both, i) for i in range(len(mixes))]
@@ -531,7 +532,7 @@
         in_specs=[in_smem] * 2 + [in_vmem] * 2,
         out_specs=[in_vmem] * 3,
         name="mix",
-        **settings(8, 0.5),
+        **settings(8, 0.01),
     )(light_index, light_vectors, transfer, own)
     inner = pl.pallas_call(
         functools.partial(own_kernel, parts),
@@ -540,7 +541,7 @@
         out_specs=in_vmem,
         scratch_shapes=[cell_shape] * 2,
         name="own",
-        **settings(8, 2),
+        **settings(8, 4),
     )(flips, vectors, own, mixed, sides[0])
     states = pl.pallas_call(
         functools.partial(near_kernel, parts),

time: 39.6 us -> 35.8 us (0.904)
  waiting for transfers between devices: 4.91 us -> 0.58 us
  starting transfers between devices: 14.3 us -> 14.7 us
    ppermute x7, waiting for transfers between devices: 4.91 us -> 0.57 us  [swap_along(): lax.ppermute(block, axis, [(i, i ^ mask) for i in range(lax.axis_size(axi...]
    ppermute x7, starting transfers between devices: 10.2 us -> 10.7 us  [swap_along(): lax.ppermute(block, axis, [(i, i ^ mask) for i in range(lax.axis_size(axi...]
  transfers between devices with their start and end apart: 9 -> 9, of which waited for: 2 -> 1; matrix products, arithmetic and copies ran while one was open for 0% -> 0% of each run, Pallas kernels for 41% -> 46%
where the time goes in v12:
time: 35.8 us; the launch traced here: 35.6 us
  Pallas kernels  19.3 us (54%)
  starting transfers between devices  14.7 us (41%)
  between operations  0.8 us (2%)
  waiting for transfers between devices  0.58 us (2%)
    ppermute x7, starting transfers between devices, swap_along(): lax.ppermute(block, axis, [(i, i ^ mask) for i in range(lax.axis_size(axi...  10.7 us
    pallas_call x1, Pallas kernels, on_device(): pl.pallas_call(functools.partial(near_kernel, parts), out_shape=array(par...  6.42 us
    pallas_call x2, Pallas kernels, on_device(): pl.pallas_call(functools.partial(far_kernel, parts, split, low, high), ou...  4.62 us
    ppermute x2, starting transfers between devices, swap_pairs(): return lax.ppermute(block, axis, pairs + [(j, i) for i, j in pairs])  4.06 us
    pallas_call x1, Pallas kernels, on_device(): pl.pallas_call(functools.partial(mix_kernel, parts), out_shape=[array(pas...  3.31 us
    pallas_call x1, Pallas kernels, on_device(): pl.pallas_call(functools.partial(own_kernel, parts), out_shape=array(valu...  1.99 us
    pallas_call x1, Pallas kernels, on_device(): pl.pallas_call(functools.partial(pack_kernel, parts), out_shape=[array(ne...  1.71 us
    pallas_call x1, Pallas kernels, on_device(): pl.pallas_call(functools.partial(edge_kernel, parts, split), out_shape=[a...  1.16 us
  transfers between devices with their start and end apart: 9, of which 1 were waited for; matrix products, arithmetic and copies ran while one was open for 0% of the time, Pallas kernels for 46%

profile of v12, /device:TPU:0, one launch (start us, length us, event | category | flops | bytes accessed | tf_op | source)
XLA Modules:
  0.0 35.6 jit_solution(2229660546820492565)
XLA Ops:
  0.0 1.7 %pack.1 = (f32[1056,128]{1,0:T(8,128)S(1)}, f32[1056,128]{1,0:T(8,128)S(1)}, f32[160,128]{1,0:T(8,128)S(1)}) custom-call(f32[16,256,128]{2,1,0:T(8,128)} %field_ref.3), custom_call_target="tpu_custom_call" | custom-call | flops 1000000000 | tf_op jit(solution)/shard_map/pack/pallas_call | solution.py:491
  1.7 0.0 copy-start.3
  1.7 0.0 copy-start.2
  1.7 0.0 copy-start
  1.8 4.0 %collective-permute-start.2 = (f32[160,128]{1,0:T(8,128)S(1)}, f32[160,128]{1,0:T(8,128)S(1)}, u32[]{:S(2)}, u32[]{:S(2)}) collective-permute-start(f32[160,128]{1,0:T(8,128)S(1)} %get-tuple-element.27), channel_id=1, source_target_pairs={{0,24},{8,16},{16,8},{24,0},{1,25},{9,17},{17,9},{25,1},{2,26},{10... | collective-permute-start | bytes 245768 | tf_op jit(solution)/shard_map/ppermute | solution.py:456
  5.7 0.5 %collective-permute-start.1 = (f32[1056,128]{1,0:T(8,128)S(1)}, f32[1056,128]{1,0:T(8,128)S(1)}, u32[]{:S(2)}, u32[]{:S(2)}) collective-permute-start(f32[1056,128]{1,0:T(8,128)S(1)} %get-tuple-element.26), channel_id=1, source_target_pairs={{0,16},{8,24},{16,0},{24,8},{1,17},{9,25},{17,1},{25,9},{2,18},{10... | collective-permute-start | bytes 1622024 | tf_op jit(solution)/shard_map/ppermute | solution.py:456
  6.2 0.1 collective-permute-start
  6.4 1.2 %edges.1 = (f32[64,128]{1,0:T(8,128)S(1)}, f32[1056,128]{1,0:T(8,128)S(1)}, f32[704,128]{1,0:T(8,128)S(1)}, f32[240,128]{1,0:T(8,128)S(1)}) custom-call(f32[16,256,128]{2,1,0:T(8,128)S(1)} %copy-done.1, f32[1056,128]{1,0:T(8,128)S(1)} %get-tuple-element.22._), custom_call_target="tpu_custom_call" | custom-call | flops 1000000000 | tf_op jit(solution)/shard_map/edges/pallas_call | solution.py:504
  7.5 0.7 %collective-permute-start.4 = (f32[64,128]{1,0:T(8,128)S(1)}, f32[64,128]{1,0:T(8,128)S(1)}, u32[]{:S(2)}, u32[]{:S(2)}) collective-permute-start(f32[64,128]{1,0:T(8,128)S(1)} %get-tuple-element.29), channel_id=1, source_target_pairs={{1,2},{3,4},{5,6},{2,1},{4,3},{6,5},{9,10},{11,12},{13,14},{10,9},... | collective-permute-start | bytes 98312 | tf_op jit(solution)/shard_map/ppermute | solution.py:452
  8.2 3.4 %collective-permute-start.3 = (f32[64,128]{1,0:T(8,128)S(1)}, f32[64,128]{1,0:T(8,128)S(1)}, u32[]{:S(2)}, u32[]{:S(2)}) collective-permute-start(f32[64,128]{1,0:T(8,128)S(1)} %get-tuple-element.29), channel_id=1, source_target_pairs={{0,1},{2,3},{4,5},{6,7},{1,0},{3,2},{5,4},{7,6},{8,9},{10,11},{12,... | collective-permute-start | bytes 98312 | tf_op jit(solution)/shard_map/ppermute | solution.py:452
  12.3 0.1 copy.7.lights_ref
  12.3 0.0 copy-done.2
  12.4 0.1 copy.8.curves_ref
  12.4 3.3 %mix.1 = (f32[4,3,8,128]{3,2,1,0:T(8,128)S(1)}, bf16[128,192]{1,0:T(8,128)(2,1)S(1)}, f32[8,16,128,128]{3,2,1,0:T(8,128)S(1)}) custom-call(s32[4]{0:T(128)S(1)} %copy-done, f32[16,3]{1,0:T(8,128)S(1)} %copy.7.lights_ref, f32[16,4,8]{2,1,0:T(4,128)S(1)} %copy.8.curves_ref, f32[1056,128]{1,0:T(8,128)S(1)} %get-tuple-element.23.own_ref.refs_0_), custom_call_target="tpu_custom_call" | custom-call | flops 10000000 | tf_op jit(solution)/shard_map/mix/pallas_call | solution.py:529
  15.8 0.0 collective-permute-done.4.odd_ref
  15.8 0.0 collective-permute-done.3.even_ref
  15.8 0.0 collective-permute-done.2._.refs_3_
  15.8 0.1 sides.1
  15.9 1.6 %collective-permute-start.6 = (f32[16,128]{1,0:T(8,128)S(1)}, f32[16,128]{1,0:T(8,128)S(1)}, u32[]{:S(2)}, u32[]{:S(2)}) collective-permute-start(f32[16,128]{1,0:T(8,128)S(1)} %get-tuple-element.31), channel_id=1, source_target_pairs={{0,8},{8,0},{16,24},{24,16},{1,9},{9,1},{17,25},{25,17},{2,10},{10... | collective-permute-start | bytes 24584 | tf_op jit(solution)/shard_map/ppermute | solution.py:456
  17.5 1.5 %collective-permute-start.7 = (f32[16,128]{1,0:T(8,128)S(1)}, f32[16,128]{1,0:T(8,128)S(1)}, u32[]{:S(2)}, u32[]{:S(2)}) collective-permute-start(f32[16,128]{1,0:T(8,128)S(1)} %get-tuple-element.32), channel_id=1, source_target_pairs={{0,16},{8,24},{16,0},{24,8},{1,17},{9,25},{17,1},{25,9},{2,18},{10... | collective-permute-start | bytes 24584 | tf_op jit(solution)/shard_map/ppermute | solution.py:456
  19.0 0.5 %collective-permute-start.5 = (f32[704,128]{1,0:T(8,128)S(1)}, f32[704,128]{1,0:T(8,128)S(1)}, u32[]{:S(2)}, u32[]{:S(2)}) collective-permute-start(f32[704,128]{1,0:T(8,128)S(1)} %constant_dynamic-update-slice_fusion), channel_id=1, source_target_pairs={{0,24},{8,16},{16,8},{24,0},{1,25},{9,17},{17,9},{25,1},{2,26},{10... | collective-permute-start | bytes 1081352 | tf_op jit(solution)/shard_map/ppermute | solution.py:456
  19.5 2.0 %own.1.inner_ref = f32[16,64,128]{2,1,0:T(8,128)S(1)} custom-call(s32[1]{0:T(128)S(6)} %copy.11.flip_ref, f32[4,3,8,128]{3,2,1,0:T(8,128)S(1)} %get-tuple-element.24.vector_ref, f32[1056,128]{1,0:T(8,128)S(1)} %get-tuple-element.23.own_ref.refs_0_, f32[8,16,128,128]{3,2,1,0:T(8,128)S(1)} %get-tuple-element.35.mixed_ref, ...), custom_call_target="tpu_custom_call" | custom-call | flops 4000000000 | tf_op jit(solution)/shard_map/own/pallas_call | solution.py:537
  21.5 0.0 collective-permute-done.6.refs_5_
  21.5 0.0 collective-permute-done.7.refs_6_
  21.5 2.5 %collective-permute-start.8 = (f32[240,128]{1,0:T(8,128)S(1)}, f32[240,128]{1,0:T(8,128)S(1)}, u32[]{:S(2)}, u32[]{:S(2)}) collective-permute-start(f32[240,128]{1,0:T(8,128)S(1)} %get-tuple-element.34), channel_id=1, source_target_pairs={{0,24},{8,16},{16,8},{24,0},{1,25},{9,17},{17,9},{25,1},{2,26},{10... | collective-permute-start | bytes 368648 | tf_op jit(solution)/shard_map/ppermute | solution.py:456
  24.0 0.0 collective-permute-done.1.refs_2_
  24.0 0.0 collective-permute-done.refs_1_
  24.0 6.4 %near.1.refs_5_.refs_7_ = f32[3,16,64,128]{3,2,1,0:T(8,128)S(1)} custom-call(s32[1]{0:T(128)S(6)} %copy.11.flip_ref, f32[4,3,8,128]{3,2,1,0:T(8,128)S(1)} %get-tuple-element.24.vector_ref, bf16[128,192]{1,0:T(8,128)(2,1)S(1)} %get-tuple-element.25.weight_ref, f32[16,64,128]{2,1,0:T(8,128)S(1)} %own.1.inner_ref, ...), custom_call_target="tpu_custom_call" | custom-call | flops 60000002048 | tf_op jit(solution)/shard_map/near/pallas_call | solution.py:546
  30.4 0.6 %collective-permute-done.5.refs_4_ = f32[704,128]{1,0:T(8,128)S(1)} collective-permute-done((f32[704,128]{1,0:T(8,128)S(1)}, f32[704,128]{1,0:T(8,128)S(1)}, u32[]{:S(2)}, u32[]{:S(2)}) %collective-permute-start.5) | collective-permute-done | bytes 360480 | tf_op jit(solution)/shard_map/ppermute | solution.py:456
  31.0 3.2 %far.1.refs_6_ = f32[4,4,64,128]{3,2,1,0:T(8,128)} custom-call(s32[1]{0:T(128)S(6)} %copy.11.flip_ref, f32[4,3,8,128]{3,2,1,0:T(8,128)S(1)} %get-tuple-element.24.vector_ref, bf16[128,192]{1,0:T(8,128)(2,1)S(1)} %get-tuple-element.25.weight_ref, f32[1056,128]{1,0:T(8,128)S(1)} %get-tuple-element.23.own_ref.refs_0_, ...), custom_call_target="tpu_custom_call" | custom-call | flops 2000000000 | tf_op jit(solution)/shard_map/far/pallas_call | solution.py:558
  34.2 0.0 collective-permute-done.8.refs_5_
  34.2 1.4 %late.1 = f32[4,4,64,128]{3,2,1,0:T(8,128)} custom-call(s32[1]{0:T(128)S(6)} %copy.11.flip_ref, f32[4,3,8,128]{3,2,1,0:T(8,128)S(1)} %get-tuple-element.24.vector_ref, bf16[128,192]{1,0:T(8,128)(2,1)S(1)} %get-tuple-element.25.weight_ref, f32[1056,128]{1,0:T(8,128)S(1)} %get-tuple-element.23.own_ref.refs_0_, ...), custom_call_target="tpu_custom_call", output_to_operand_aliasing={{}: (9, {})} | custom-call | flops 2000000000 | tf_op jit(solution)/shard_map/late/pallas_call | solution.py:558
  (5 shorter events, 0.0 us)
Async XLA Ops:
  0.0 6.4 %copy-start.1 = (f32[16,256,128]{2,1,0:T(8,128)S(1)}, f32[16,256,128]{2,1,0:T(8,128)}, u32[]{:S(2)}) copy-start(f32[16,256,128]{2,1,0:T(8,128)} %field_ref.3) | copy-start | bytes 6291460
  1.7 10.5 %copy-start.3 = (f32[16,3]{0,1:T(4,128)S(1)}, f32[16,3]{0,1:T(4,128)}, u32[]{:S(2)}) copy-start(f32[16,3]{0,1:T(4,128)} %param.6) | copy-start | bytes 580
  1.7 10.6 %copy-start.2 = (f32[16,4,8]{0,2,1:T(8,128)S(1)}, f32[16,4,8]{0,2,1:T(8,128)}, u32[]{:S(2)}) copy-start(f32[16,4,8]{0,2,1:T(8,128)} %param.7) | copy-start | bytes 6148
  1.7 10.7 %copy-start = (s32[4]{0:T(128)S(1)}, s32[4]{0:T(128)}, u32[]{:S(2)}) copy-start(s32[4]{0:T(128)} %index_ref.1) | copy-start | bytes 52
  1.8 14.0 %collective-permute-start.2 = (f32[160,128]{1,0:T(8,128)S(1)}, f32[160,128]{1,0:T(8,128)S(1)}, u32[]{:S(2)}, u32[]{:S(2)}) collective-permute-start(f32[160,128]{1,0:T(8,128)S(1)} %get-tuple-element.27), channel_id=1, source_target_pairs={{0,24},{8,16},{16,8},{24,0},{1,25},{9,17},{17,9},{25,1},{2,26},{10... | collective-permute-start | bytes 245768 | tf_op jit(solution)/shard_map/ppermute | solution.py:456
  5.7 18.3 %collective-permute-start.1 = (f32[1056,128]{1,0:T(8,128)S(1)}, f32[1056,128]{1,0:T(8,128)S(1)}, u32[]{:S(2)}, u32[]{:S(2)}) collective-permute-start(f32[1056,128]{1,0:T(8,128)S(1)} %get-tuple-element.26), channel_id=1, source_target_pairs={{0,16},{8,24},{16,0},{24,8},{1,17},{9,25},{17,1},{25,9},{2,18},{10... | collective-permute-start | bytes 1622024 | tf_op jit(solution)/shard_map/ppermute | solution.py:456
  6.2 17.8 %collective-permute-start = (f32[1056,128]{1,0:T(8,128)S(1)}, f32[1056,128]{1,0:T(8,128)S(1)}, u32[]{:S(2)}, u32[]{:S(2)}) collective-permute-start(f32[1056,128]{1,0:T(8,128)S(1)} %get-tuple-element.22._), channel_id=1, source_target_pairs={{0,8},{8,0},{16,24},{24,16},{1,9},{9,1},{17,25},{25,17},{2,10},{10... | collective-permute-start | bytes 1622024 | tf_op jit(solution)/shard_map/ppermute | solution.py:456
  7.5 8.2 %collective-permute-start.4 = (f32[64,128]{1,0:T(8,128)S(1)}, f32[64,128]{1,0:T(8,128)S(1)}, u32[]{:S(2)}, u32[]{:S(2)}) collective-permute-start(f32[64,128]{1,0:T(8,128)S(1)} %get-tuple-element.29), channel_id=1, source_target_pairs={{1,2},{3,4},{5,6},{2,1},{4,3},{6,5},{9,10},{11,12},{13,14},{10,9},... | collective-permute-start | bytes 98312 | tf_op jit(solution)/shard_map/ppermute | solution.py:452
  8.2 7.6 %collective-permute-start.3 = (f32[64,128]{1,0:T(8,128)S(1)}, f32[64,128]{1,0:T(8,128)S(1)}, u32[]{:S(2)}, u32[]{:S(2)}) collective-permute-start(f32[64,128]{1,0:T(8,128)S(1)} %get-tuple-element.29), channel_id=1, source_target_pairs={{0,1},{2,3},{4,5},{6,7},{1,0},{3,2},{5,4},{7,6},{8,9},{10,11},{12,... | collective-permute-start | bytes 98312 | tf_op jit(solution)/shard_map/ppermute | solution.py:452
  15.9 5.5 %collective-permute-start.6 = (f32[16,128]{1,0:T(8,128)S(1)}, f32[16,128]{1,0:T(8,128)S(1)}, u32[]{:S(2)}, u32[]{:S(2)}) collective-permute-start(f32[16,128]{1,0:T(8,128)S(1)} %get-tuple-element.31), channel_id=1, source_target_pairs={{0,8},{8,0},{16,24},{24,16},{1,9},{9,1},{17,25},{25,17},{2,10},{10... | collective-permute-start | bytes 24584 | tf_op jit(solution)/shard_map/ppermute | solution.py:456
  17.5 4.0 %collective-permute-start.7 = (f32[16,128]{1,0:T(8,128)S(1)}, f32[16,128]{1,0:T(8,128)S(1)}, u32[]{:S(2)}, u32[]{:S(2)}) collective-permute-start(f32[16,128]{1,0:T(8,128)S(1)} %get-tuple-element.32), channel_id=1, source_target_pairs={{0,16},{8,24},{16,0},{24,8},{1,17},{9,25},{17,1},{25,9},{2,18},{10... | collective-permute-start | bytes 24584 | tf_op jit(solution)/shard_map/ppermute | solution.py:456
  19.0 12.0 %collective-permute-start.5 = (f32[704,128]{1,0:T(8,128)S(1)}, f32[704,128]{1,0:T(8,128)S(1)}, u32[]{:S(2)}, u32[]{:S(2)}) collective-permute-start(f32[704,128]{1,0:T(8,128)S(1)} %constant_dynamic-update-slice_fusion), channel_id=1, source_target_pairs={{0,24},{8,16},{16,8},{24,0},{1,25},{9,17},{17,9},{25,1},{2,26},{10... | collective-permute-start | bytes 1081352 | tf_op jit(solution)/shard_map/ppermute | solution.py:456
  21.5 12.7 %collective-permute-start.8 = (f32[240,128]{1,0:T(8,128)S(1)}, f32[240,128]{1,0:T(8,128)S(1)}, u32[]{:S(2)}, u32[]{:S(2)}) collective-permute-start(f32[240,128]{1,0:T(8,128)S(1)} %get-tuple-element.34), channel_id=1, source_target_pairs={{0,24},{8,16},{16,8},{24,0},{1,25},{9,17},{17,9},{25,1},{2,26},{10... | collective-permute-start | bytes 368648 | tf_op jit(solution)/shard_map/ppermute | solution.py:456

commit v13 on v12

--- a/solution.py
+++ b/solution.py
@@ -58,10 +58,16 @@
         copy.wait()
 
 
-def edge_kernel(parts, split, field_ref, _, edge_ref, own_ref, body_ref, rest_ref):
+def edge_kernel(parts, split, source_ref, _, edge_ref, own_ref, body_ref, rest_ref, field_ref, sems):
     cells, all_rows, cols = field_ref.shape
     rows = all_rows // parts
     me = lax.axis_index("depth")
+    quarter = cells // 4
+    copies = []
+    for q in range(4):
+        layers = pl.ds(q * quarter, quarter)
+        copies.append(pltpu.make_async_copy(source_ref.at[layers], field_ref.at[layers], sems.at[q]))
+        copies[-1].start()
     lane_pair = lax.broadcasted_iota(jnp.int32, (SUB, cols), 1) // 2
 
     def tile(i, carry):
@@ -76,11 +82,12 @@
         edge_ref[pl.ds(pl.multiple_of(i * SUB, SUB), SUB), :] = acc
         return carry
 
-    lax.fori_loop(0, rows // SUB, tile, 0)
     low = pl.multiple_of(me * rows, SUB)
     above = jnp.where(me > 0, 1.0, 0.0)
     below = jnp.where(me < parts - 1, 1.0, 0.0)
     for z in range(cells):
+        if z % quarter == 0:
+            copies[z // quarter].wait()
         own_ref[z : z + 1, :] = field_ref[z, pl.ds(jnp.maximum(low - 1, 0), 1), :] * above
         below_at = cells + cells * rows + z
         own_ref[below_at : below_at + 1, :] = field_ref[z, pl.ds(jnp.minimum(low + rows, all_rows - 1), 1), :] * below
@@ -97,6 +104,7 @@
         body_ref[next_row : next_row + 1, :] = field_ref[z, pl.ds(far_low + split, 1), :]
         at = SUB + (z - 1) * more
         rest_ref[at : at + more, :] = field_ref[z, pl.ds(far_low + split, more), :]
+    lax.fori_loop(0, rows // SUB, tile, 0)
 
 
 def side_kernel(parts, even_ref, odd_ref, _, *outs):
@@ -358,7 +366,7 @@
 def near_kernel(parts, flip_ref, vector_ref, weight_ref, inner_ref, *refs):
     count = parts - 1
     heads, laterals, out_ref, ends_ref = refs[:parts], refs[parts : 2 * parts - 1], refs[2 * parts - 1], refs[2 * parts]
-    cell_refs, mixed_refs = refs[2 * parts + 1 : 2 * parts + 1 + count], refs[2 * parts + 1 + count :]
+    cell_refs, mixed_refs = refs[2 * parts + 1 : 2 * parts + 1 + 2 * count], refs[2 * parts + 1 + 2 * count :]
     rows, cols = out_ref.shape[2:]
     cells = cell_refs[0].shape[1]
     passes = vector_ref.shape[0]
@@ -369,28 +377,32 @@
     places = [near_places(cells, rows, head) for head in heads[:count]]
     fill_ends(parts, cells, rows, heads, ends_ref)
 
-    def prepare(m, base):
+    def prepare(m, base, slot):
+        spot = slot * count + m
         return prepare_steps(
-            m, zs[m], places[m], laterals[m], base, cells, rows, parts, cols, ends_ref, weight_ref, cell_refs[m], mixed_refs[m]
+            m, zs[m], places[m], laterals[m], base, cells, rows, parts, cols, ends_ref, weight_ref, cell_refs[spot], mixed_refs[spot]
         )
 
-    for step in prepare(0, 0):
-        step()
-
-    def tile(i, carry):
-        base = pl.multiple_of(i * SUB, SUB)
-        after = pl.multiple_of(jnp.minimum(i + 1, tiles - 1) * SUB, SUB)
+    marches = [len(z) for z in zs]
+    ends = [sum(marches[: m + 1]) for m in range(count)]
+
+    def unit(index, slot, beside):
+        base = pl.multiple_of(index * SUB, SUB)
         at = pl.ds(base, SUB)
+        cuts = [0] + [len(beside) * end // ends[-1] for end in ends]
         for m in range(count):
-            beside = prepare(m + 1, base) if m + 1 < count else prepare(0, after)
             inner = (lambda p, j: inner_ref[p * channels + j, at, :]) if m == 0 else None
-            result = march_unit(flip, vector_ref, zs[m], cells, cell_refs[m], mixed_refs[m], beside, inner)
+            mine = beside[cuts[m] : cuts[m + 1]]
+            spot = slot * count + m
+            result = march_unit(flip, vector_ref, zs[m], cells, cell_refs[spot], mixed_refs[spot], mine, inner)
             for p in range(passes):
                 for j in range(channels):
                     out_ref[m, p * channels + j, at, :] = result[p][j]
-        return carry
-
-    lax.fori_loop(0, tiles, tile, 0)
+
+    def prepare_all(base, slot):
+        return [step for m in range(count) for step in prepare(m, base, slot)]
+
+    march_tiles(tiles, 0, prepare_all, unit)
 
 
 def over_either(first_leads, one, other):
@@ -485,7 +497,7 @@
     near_rows = 2 * cells + cells * rows
     head_rows = 2 * cells + 2 * rows
     skip = rows // parts
-    split = rows - rows // parts
+    split = rows // 2
     body_rows = skip + (cells - 2) * split + cells
     rest_rows = (cells - 2) * (rows - split) + 2 * SUB
     *packed, far_head = pl.pallas_call(
@@ -504,11 +516,12 @@
     edges, own, far_body, far_rest = pl.pallas_call(
         functools.partial(edge_kernel, parts, split),
         out_shape=[array(rows, cols), array(near_rows, cols), array(body_rows, cols), array(rest_rows, cols)],
-        in_specs=[in_vmem, in_any],
+        in_specs=[in_hbm, in_any],
         out_specs=[in_vmem] * 4,
+        scratch_shapes=[VMEM(field.shape, jnp.float32), pltpu.SemaphoreType.DMA((4,))],
         name="edges",
         **settings(8, 1),
-    )(field, packed[0])
+    )(pltpu.with_memory_space_constraint(field, pltpu.HBM), packed[0])
     sides = pl.pallas_call(
         functools.partial(side_kernel, parts),
         out_shape=[array(skip, cols)] * parts,
@@ -548,9 +561,9 @@
         out_shape=array(parts - 1, values, rows, cols),
         in_specs=[in_smem] + [in_vmem] * (2 * parts + 2),
         out_specs=in_vmem,
-        scratch_shapes=[ends_shape] + [cell_shape] * (parts - 1) + [mixed_shape] * (parts - 1),
+        scratch_shapes=[ends_shape] + [cell_shape] * (2 * parts - 2) + [mixed_shape] * (2 * parts - 2),
         name="near",
-        **settings(16, 60),
+        **settings(20, 60),
     )(flips, vectors, weights, inner, own, *near, far_head, sides[0], *laterals)
     picture = None
     for low, high in ((0, split), (split, rows)):

time: 35.8 us -> 36.5 us (1.020)
  Pallas kernels: 19.3 us -> 20.6 us
  waiting for transfers between devices: 0.58 us -> 0.02 us
    pallas_call x1, Pallas kernels: 1.16 us -> 2.71 us  [on_device(): pl.pallas_call(functools.partial(edge_kernel, parts, split), out_shape=[a...]
    ppermute x7, waiting for transfers between devices: 0.57 us -> 0.02 us  [swap_along(): lax.ppermute(block, axis, [(i, i ^ mask) for i in range(lax.axis_size(axi...]
  transfers between devices with their start and end apart: 9 -> 9, of which waited for: 1 -> 0; matrix products, arithmetic and copies ran while one was open for 0% -> 0% of each run, Pallas kernels for 46% -> 46%
where the time goes in v13:
time: 36.5 us; the launch traced here: 36.3 us
  Pallas kernels  20.6 us (56%)
  starting transfers between devices  14.7 us (40%)
  between operations  0.8 us (2%)
    ppermute x7, starting transfers between devices, swap_along(): lax.ppermute(block, axis, [(i, i ^ mask) for i in range(lax.axis_size(axi...  10.7 us
    pallas_call x1, Pallas kernels, on_device(): pl.pallas_call(functools.partial(near_kernel, parts), out_shape=array(par...  6.32 us
    pallas_call x2, Pallas kernels, on_device(): pl.pallas_call(functools.partial(far_kernel, parts, split, low, high), ou...  4.57 us
    ppermute x2, starting transfers between devices, swap_pairs(): return lax.ppermute(block, axis, pairs + [(j, i) for i, j in pairs])  4.06 us
    pallas_call x1, Pallas kernels, on_device(): pl.pallas_call(functools.partial(mix_kernel, parts), out_shape=[array(pas...  3.31 us
    pallas_call x1, Pallas kernels, on_device(): pl.pallas_call(functools.partial(edge_kernel, parts, split), out_shape=[a...  2.71 us
    pallas_call x1, Pallas kernels, on_device(): pl.pallas_call(functools.partial(own_kernel, parts), out_shape=array(valu...  1.99 us
    pallas_call x1, Pallas kernels, on_device(): pl.pallas_call(functools.partial(pack_kernel, parts), out_shape=[array(ne...  1.57 us
  transfers between devices with their start and end apart: 9, of which 0 were waited for; matrix products, arithmetic and copies ran while one was open for 0% of the time, Pallas kernels for 46%

profile of v13, /device:TPU:0, one launch (start us, length us, event | category | flops | bytes accessed | tf_op | source)
XLA Modules:
  0.0 36.3 jit_solution(18290531759615328502)
XLA Ops:
  0.0 1.6 %pack.1 = (f32[1056,128]{1,0:T(8,128)S(1)}, f32[1056,128]{1,0:T(8,128)S(1)}, f32[160,128]{1,0:T(8,128)S(1)}) custom-call(f32[16,256,128]{2,1,0:T(8,128)} %source_ref.1), custom_call_target="tpu_custom_call" | custom-call | flops 1000000000 | tf_op jit(solution)/shard_map/pack/pallas_call | solution.py:503
  1.6 0.0 copy-start.2
  1.6 0.0 copy-start.1
  1.6 0.0 copy-start
  1.6 4.0 %collective-permute-start.2 = (f32[160,128]{1,0:T(8,128)S(1)}, f32[160,128]{1,0:T(8,128)S(1)}, u32[]{:S(2)}, u32[]{:S(2)}) collective-permute-start(f32[160,128]{1,0:T(8,128)S(1)} %get-tuple-element.27), channel_id=1, source_target_pairs={{0,24},{8,16},{16,8},{24,0},{1,25},{9,17},{17,9},{25,1},{2,26},{10... | collective-permute-start | bytes 245768 | tf_op jit(solution)/shard_map/ppermute | solution.py:468
  5.6 0.5 %collective-permute-start.1 = (f32[1056,128]{1,0:T(8,128)S(1)}, f32[1056,128]{1,0:T(8,128)S(1)}, u32[]{:S(2)}, u32[]{:S(2)}) collective-permute-start(f32[1056,128]{1,0:T(8,128)S(1)} %get-tuple-element.26), channel_id=1, source_target_pairs={{0,16},{8,24},{16,0},{24,8},{1,17},{9,25},{17,1},{25,9},{2,18},{10... | collective-permute-start | bytes 1622024 | tf_op jit(solution)/shard_map/ppermute | solution.py:468
  6.1 0.1 collective-permute-start
  6.2 2.7 %edges.1 = (f32[64,128]{1,0:T(8,128)S(1)}, f32[1056,128]{1,0:T(8,128)S(1)}, f32[480,128]{1,0:T(8,128)S(1)}, f32[464,128]{1,0:T(8,128)S(1)}) custom-call(f32[16,256,128]{2,1,0:T(8,128)} %source_ref.1, f32[1056,128]{1,0:T(8,128)S(1)} %get-tuple-element.22._), custom_call_target="tpu_custom_call" | custom-call | flops 1000000000 | tf_op jit(solution)/shard_map/edges/pallas_call | solution.py:516
  8.9 0.7 %collective-permute-start.4 = (f32[64,128]{1,0:T(8,128)S(1)}, f32[64,128]{1,0:T(8,128)S(1)}, u32[]{:S(2)}, u32[]{:S(2)}) collective-permute-start(f32[64,128]{1,0:T(8,128)S(1)} %get-tuple-element.29), channel_id=1, source_target_pairs={{1,2},{3,4},{5,6},{2,1},{4,3},{6,5},{9,10},{11,12},{13,14},{10,9},... | collective-permute-start | bytes 98312 | tf_op jit(solution)/shard_map/ppermute | solution.py:464
  9.6 3.4 %collective-permute-start.3 = (f32[64,128]{1,0:T(8,128)S(1)}, f32[64,128]{1,0:T(8,128)S(1)}, u32[]{:S(2)}, u32[]{:S(2)}) collective-permute-start(f32[64,128]{1,0:T(8,128)S(1)} %get-tuple-element.29), channel_id=1, source_target_pairs={{0,1},{2,3},{4,5},{6,7},{1,0},{3,2},{5,4},{7,6},{8,9},{10,11},{12,... | collective-permute-start | bytes 98312 | tf_op jit(solution)/shard_map/ppermute | solution.py:464
  13.7 0.1 copy.7.lights_ref
  13.8 0.1 copy.8.curves_ref
  13.8 0.0 copy-done
  13.8 3.3 %mix.1 = (f32[4,3,8,128]{3,2,1,0:T(8,128)S(1)}, bf16[128,192]{1,0:T(8,128)(2,1)S(1)}, f32[8,16,128,128]{3,2,1,0:T(8,128)S(1)}) custom-call(s32[4]{0:T(128)S(1)} %copy-done, f32[16,3]{1,0:T(8,128)S(1)} %copy.7.lights_ref, f32[16,4,8]{2,1,0:T(4,128)S(1)} %copy.8.curves_ref, f32[1056,128]{1,0:T(8,128)S(1)} %get-tuple-element.23.own_ref.refs_0_), custom_call_target="tpu_custom_call" | custom-call | flops 10000000 | tf_op jit(solution)/shard_map/mix/pallas_call | solution.py:542
  17.2 0.0 collective-permute-done.4.odd_ref
  17.2 0.0 collective-permute-done.3.even_ref
  17.2 0.0 collective-permute-done.2._.refs_3_
  17.2 0.1 sides.1
  17.3 1.6 %collective-permute-start.6 = (f32[16,128]{1,0:T(8,128)S(1)}, f32[16,128]{1,0:T(8,128)S(1)}, u32[]{:S(2)}, u32[]{:S(2)}) collective-permute-start(f32[16,128]{1,0:T(8,128)S(1)} %get-tuple-element.31), channel_id=1, source_target_pairs={{0,8},{8,0},{16,24},{24,16},{1,9},{9,1},{17,25},{25,17},{2,10},{10... | collective-permute-start | bytes 24584 | tf_op jit(solution)/shard_map/ppermute | solution.py:468
  18.9 1.5 %collective-permute-start.7 = (f32[16,128]{1,0:T(8,128)S(1)}, f32[16,128]{1,0:T(8,128)S(1)}, u32[]{:S(2)}, u32[]{:S(2)}) collective-permute-start(f32[16,128]{1,0:T(8,128)S(1)} %get-tuple-element.32), channel_id=1, source_target_pairs={{0,16},{8,24},{16,0},{24,8},{1,17},{9,25},{17,1},{25,9},{2,18},{10... | collective-permute-start | bytes 24584 | tf_op jit(solution)/shard_map/ppermute | solution.py:468
  20.4 0.5 %collective-permute-start.5 = (f32[480,128]{1,0:T(8,128)S(1)}, f32[480,128]{1,0:T(8,128)S(1)}, u32[]{:S(2)}, u32[]{:S(2)}) collective-permute-start(f32[480,128]{1,0:T(8,128)S(1)} %constant_dynamic-update-slice_fusion), channel_id=1, source_target_pairs={{0,24},{8,16},{16,8},{24,0},{1,25},{9,17},{17,9},{25,1},{2,26},{10... | collective-permute-start | bytes 737288 | tf_op jit(solution)/shard_map/ppermute | solution.py:468
  20.9 2.0 %own.1.inner_ref = f32[16,64,128]{2,1,0:T(8,128)S(1)} custom-call(s32[1]{0:T(128)S(6)} %copy.11.flip_ref, f32[4,3,8,128]{3,2,1,0:T(8,128)S(1)} %get-tuple-element.24.vector_ref, f32[1056,128]{1,0:T(8,128)S(1)} %get-tuple-element.23.own_ref.refs_0_, f32[8,16,128,128]{3,2,1,0:T(8,128)S(1)} %get-tuple-element.35.mixed_ref, ...), custom_call_target="tpu_custom_call" | custom-call | flops 4000000000 | tf_op jit(solution)/shard_map/own/pallas_call | solution.py:550
  22.9 0.0 collective-permute-done.6.refs_5_
  22.9 0.0 collective-permute-done.7.refs_6_
  22.9 2.5 %collective-permute-start.8 = (f32[464,128]{1,0:T(8,128)S(1)}, f32[464,128]{1,0:T(8,128)S(1)}, u32[]{:S(2)}, u32[]{:S(2)}) collective-permute-start(f32[464,128]{1,0:T(8,128)S(1)} %get-tuple-element.34), channel_id=1, source_target_pairs={{0,24},{8,16},{16,8},{24,0},{1,25},{9,17},{17,9},{25,1},{2,26},{10... | collective-permute-start | bytes 712712 | tf_op jit(solution)/shard_map/ppermute | solution.py:468
  25.4 0.0 collective-permute-done.1.refs_2_
  25.4 0.0 collective-permute-done.refs_1_
  25.4 6.3 %near.1.refs_5_.refs_7_ = f32[3,16,64,128]{3,2,1,0:T(8,128)S(1)} custom-call(s32[1]{0:T(128)S(6)} %copy.11.flip_ref, f32[4,3,8,128]{3,2,1,0:T(8,128)S(1)} %get-tuple-element.24.vector_ref, bf16[128,192]{1,0:T(8,128)(2,1)S(1)} %get-tuple-element.25.weight_ref, f32[16,64,128]{2,1,0:T(8,128)S(1)} %own.1.inner_ref, ...), custom_call_target="tpu_custom_call" | custom-call | flops 60000002048 | tf_op jit(solution)/shard_map/near/pallas_call | solution.py:559
  31.7 0.0 collective-permute-done.5.refs_4_
  31.8 2.3 %far.1.refs_6_ = f32[4,4,64,128]{3,2,1,0:T(8,128)} custom-call(s32[1]{0:T(128)S(6)} %copy.11.flip_ref, f32[4,3,8,128]{3,2,1,0:T(8,128)S(1)} %get-tuple-element.24.vector_ref, bf16[128,192]{1,0:T(8,128)(2,1)S(1)} %get-tuple-element.25.weight_ref, f32[1056,128]{1,0:T(8,128)S(1)} %get-tuple-element.23.own_ref.refs_0_, ...), custom_call_target="tpu_custom_call" | custom-call | flops 2000000000 | tf_op jit(solution)/shard_map/far/pallas_call | solution.py:571
  34.1 0.0 collective-permute-done.8.refs_5_
  34.1 2.3 %late.1 = f32[4,4,64,128]{3,2,1,0:T(8,128)} custom-call(s32[1]{0:T(128)S(6)} %copy.11.flip_ref, f32[4,3,8,128]{3,2,1,0:T(8,128)S(1)} %get-tuple-element.24.vector_ref, bf16[128,192]{1,0:T(8,128)(2,1)S(1)} %get-tuple-element.25.weight_ref, f32[1056,128]{1,0:T(8,128)S(1)} %get-tuple-element.23.own_ref.refs_0_, ...), custom_call_target="tpu_custom_call", output_to_operand_aliasing={{}: (9, {})} | custom-call | flops 2000000000 | tf_op jit(solution)/shard_map/late/pallas_call | solution.py:571
  (3 shorter events, 0.0 us)
Async XLA Ops:
  1.6 12.1 %copy-start.2 = (f32[16,3]{0,1:T(4,128)S(1)}, f32[16,3]{0,1:T(4,128)}, u32[]{:S(2)}) copy-start(f32[16,3]{0,1:T(4,128)} %param.6) | copy-start | bytes 580
  1.6 12.2 %copy-start.1 = (f32[16,4,8]{0,2,1:T(8,128)S(1)}, f32[16,4,8]{0,2,1:T(8,128)}, u32[]{:S(2)}) copy-start(f32[16,4,8]{0,2,1:T(8,128)} %param.7) | copy-start | bytes 6148
  1.6 12.2 %copy-start = (s32[4]{0:T(128)S(1)}, s32[4]{0:T(128)}, u32[]{:S(2)}) copy-start(s32[4]{0:T(128)} %index_ref.1) | copy-start | bytes 52
  1.6 15.6 %collective-permute-start.2 = (f32[160,128]{1,0:T(8,128)S(1)}, f32[160,128]{1,0:T(8,128)S(1)}, u32[]{:S(2)}, u32[]{:S(2)}) collective-permute-start(f32[160,128]{1,0:T(8,128)S(1)} %get-tuple-element.27), channel_id=1, source_target_pairs={{0,24},{8,16},{16,8},{24,0},{1,25},{9,17},{17,9},{25,1},{2,26},{10... | collective-permute-start | bytes 245768 | tf_op jit(solution)/shard_map/ppermute | solution.py:468
  5.6 19.8 %collective-permute-start.1 = (f32[1056,128]{1,0:T(8,128)S(1)}, f32[1056,128]{1,0:T(8,128)S(1)}, u32[]{:S(2)}, u32[]{:S(2)}) collective-permute-start(f32[1056,128]{1,0:T(8,128)S(1)} %get-tuple-element.26), channel_id=1, source_target_pairs={{0,16},{8,24},{16,0},{24,8},{1,17},{9,25},{17,1},{25,9},{2,18},{10... | collective-permute-start | bytes 1622024 | tf_op jit(solution)/shard_map/ppermute | solution.py:468
  6.1 19.3 %collective-permute-start = (f32[1056,128]{1,0:T(8,128)S(1)}, f32[1056,128]{1,0:T(8,128)S(1)}, u32[]{:S(2)}, u32[]{:S(2)}) collective-permute-start(f32[1056,128]{1,0:T(8,128)S(1)} %get-tuple-element.22._), channel_id=1, source_target_pairs={{0,8},{8,0},{16,24},{24,16},{1,9},{9,1},{17,25},{25,17},{2,10},{10... | collective-permute-start | bytes 1622024 | tf_op jit(solution)/shard_map/ppermute | solution.py:468
  8.9 8.2 %collective-permute-start.4 = (f32[64,128]{1,0:T(8,128)S(1)}, f32[64,128]{1,0:T(8,128)S(1)}, u32[]{:S(2)}, u32[]{:S(2)}) collective-permute-start(f32[64,128]{1,0:T(8,128)S(1)} %get-tuple-element.29), channel_id=1, source_target_pairs={{1,2},{3,4},{5,6},{2,1},{4,3},{6,5},{9,10},{11,12},{13,14},{10,9},... | collective-permute-start | bytes 98312 | tf_op jit(solution)/shard_map/ppermute | solution.py:464
  9.6 7.6 %collective-permute-start.3 = (f32[64,128]{1,0:T(8,128)S(1)}, f32[64,128]{1,0:T(8,128)S(1)}, u32[]{:S(2)}, u32[]{:S(2)}) collective-permute-start(f32[64,128]{1,0:T(8,128)S(1)} %get-tuple-element.29), channel_id=1, source_target_pairs={{0,1},{2,3},{4,5},{6,7},{1,0},{3,2},{5,4},{7,6},{8,9},{10,11},{12,... | collective-permute-start | bytes 98312 | tf_op jit(solution)/shard_map/ppermute | solution.py:464
  17.3 5.5 %collective-permute-start.6 = (f32[16,128]{1,0:T(8,128)S(1)}, f32[16,128]{1,0:T(8,128)S(1)}, u32[]{:S(2)}, u32[]{:S(2)}) collective-permute-start(f32[16,128]{1,0:T(8,128)S(1)} %get-tuple-element.31), channel_id=1, source_target_pairs={{0,8},{8,0},{16,24},{24,16},{1,9},{9,1},{17,25},{25,17},{2,10},{10... | collective-permute-start | bytes 24584 | tf_op jit(solution)/shard_map/ppermute | solution.py:468
  18.9 4.0 %collective-permute-start.7 = (f32[16,128]{1,0:T(8,128)S(1)}, f32[16,128]{1,0:T(8,128)S(1)}, u32[]{:S(2)}, u32[]{:S(2)}) collective-permute-start(f32[16,128]{1,0:T(8,128)S(1)} %get-tuple-element.32), channel_id=1, source_target_pairs={{0,16},{8,24},{16,0},{24,8},{1,17},{9,25},{17,1},{25,9},{2,18},{10... | collective-permute-start | bytes 24584 | tf_op jit(solution)/shard_map/ppermute | solution.py:468
  20.4 11.3 %collective-permute-start.5 = (f32[480,128]{1,0:T(8,128)S(1)}, f32[480,128]{1,0:T(8,128)S(1)}, u32[]{:S(2)}, u32[]{:S(2)}) collective-permute-start(f32[480,128]{1,0:T(8,128)S(1)} %constant_dynamic-update-slice_fusion), channel_id=1, source_target_pairs={{0,24},{8,16},{16,8},{24,0},{1,25},{9,17},{17,9},{25,1},{2,26},{10... | collective-permute-start | bytes 737288 | tf_op jit(solution)/shard_map/ppermute | solution.py:468
  22.9 11.2 %collective-permute-start.8 = (f32[464,128]{1,0:T(8,128)S(1)}, f32[464,128]{1,0:T(8,128)S(1)}, u32[]{:S(2)}, u32[]{:S(2)}) collective-permute-start(f32[464,128]{1,0:T(8,128)S(1)} %get-tuple-element.34), channel_id=1, source_target_pairs={{0,24},{8,16},{16,8},{24,0},{1,25},{9,17},{17,9},{25,1},{2,26},{10... | collective-permute-start | bytes 712712 | tf_op jit(solution)/shard_map/ppermute | solution.py:468

commit v14 on v10

--- a/solution.py
+++ b/solution.py
@@ -24,10 +24,10 @@
     copies, rims = [], []
     for j, out in enumerate(outs):
         low = pl.multiple_of((me ^ (j + 1)) * rows, SUB)
-        before = pl.multiple_of(jnp.maximum(low - SUB, 0), SUB)
-        after = pl.multiple_of(jnp.minimum(low + rows, all_rows - SUB), SUB)
+        before = jnp.maximum(low - 1, 0)
+        after = jnp.minimum(low + rows, all_rows - 1)
         for side, start in enumerate((before, after)):
-            source = field_ref.at[:, pl.ds(start, SUB), :]
+            source = field_ref.at[:, pl.ds(start, 1), :]
             rims.append(pltpu.make_async_copy(source, rim_ref.at[j, side], sems.at[side, j]))
         block = field_ref.at[:, pl.ds(low, rows), :]
         if j < parts - 2:
@@ -49,7 +49,7 @@
         above = jnp.where(part > 0, 1.0, 0.0)
         below = jnp.where(part < parts - 1, 1.0, 0.0)
         for z in range(cells):
-            out[z : z + 1, :] = rim_ref[j, 0, z, SUB - 1 : SUB, :] * above
+            out[z : z + 1, :] = rim_ref[j, 0, z, 0:1, :] * above
             below_at = out.shape[0] - cells + z
             out[below_at : below_at + 1, :] = rim_ref[j, 1, z, 0:1, :] * below
     for copy in copies:
@@ -456,7 +456,7 @@
         out_shape=[array(near_rows, cols)] * (parts - 2) + [array(head_rows, cols)],
         in_specs=[in_hbm],
         out_specs=[in_vmem] * (parts - 1),
-        scratch_shapes=[VMEM((parts - 1, 2, cells, SUB, cols), jnp.float32), pltpu.SemaphoreType.DMA((6, parts - 1))],
+        scratch_shapes=[VMEM((parts - 1, 2, cells, 1, cols), jnp.float32), pltpu.SemaphoreType.DMA((6, parts - 1))],
         name="pack",
         **settings(8, 1),
     )(pltpu.with_memory_space_constraint(field, pltpu.HBM))

time: 34.4 us -> 34.4 us (level)
  no operation moved by 1% of the time
where the time goes in v14:
time: 34.4 us; the launch traced here: 34.3 us
  Pallas kernels  17.5 us (51%)
  starting transfers between devices  13.7 us (40%)
  waiting for transfers between devices  2.17 us (6%)
  between operations  0.75 us (2%)
    ppermute x7, starting transfers between devices, swap_along(): lax.ppermute(block, axis, [(i, i ^ mask) for i in range(lax.axis_size(axi...  9.64 us
    pallas_call x1, Pallas kernels, on_device(): pl.pallas_call(functools.partial(near_kernel, parts), out_shape=array(par...  6.27 us
    pallas_call x2, Pallas kernels, on_device(): pl.pallas_call(functools.partial(far_kernel, parts, split, low, high), ou...  4.6 us
    ppermute x2, starting transfers between devices, swap_pairs(): return lax.ppermute(block, axis, pairs + [(j, i) for i, j in pairs])  4.06 us
    pallas_call x1, Pallas kernels, on_device(): pl.pallas_call(functools.partial(own_kernel, parts), out_shape=[array(val...  3.64 us
    ppermute x7, waiting for transfers between devices, swap_along(): lax.ppermute(block, axis, [(i, i ^ mask) for i in range(lax.axis_size(axi...  2.14 us
    pallas_call x1, Pallas kernels, on_device(): pl.pallas_call(functools.partial(pack_kernel, parts), out_shape=[array(ne...  1.68 us
    pallas_call x1, Pallas kernels, on_device(): pl.pallas_call(functools.partial(edge_kernel, parts, split), out_shape=[a...  1.16 us
  transfers between devices with their start and end apart: 9, of which 2 were waited for; matrix products, arithmetic and copies ran while one was open for 0% of the time, Pallas kernels for 42%

profile of v14, /device:TPU:0, one launch (start us, length us, event | category | flops | bytes accessed | tf_op | source)
XLA Modules:
  0.0 34.3 jit_solution(3644372586874691428)
XLA Ops:
  0.0 1.7 %pack.1 = (f32[1056,128]{1,0:T(8,128)S(1)}, f32[1056,128]{1,0:T(8,128)S(1)}, f32[160,128]{1,0:T(8,128)S(1)}) custom-call(f32[16,256,128]{2,1,0:T(8,128)} %field_ref.3), custom_call_target="tpu_custom_call" | custom-call | flops 1000000000 | tf_op jit(solution)/shard_map/pack/pallas_call | solution.py:454
  1.7 0.0 copy-start.3
  1.7 0.0 copy-start.2
  1.7 0.0 copy-start.1
  1.7 4.0 %collective-permute-start.2 = (f32[160,128]{1,0:T(8,128)S(1)}, f32[160,128]{1,0:T(8,128)S(1)}, u32[]{:S(2)}, u32[]{:S(2)}) collective-permute-start(f32[160,128]{1,0:T(8,128)S(1)} %get-tuple-element.25), channel_id=1, source_target_pairs={{0,24},{8,16},{16,8},{24,0},{1,25},{9,17},{17,9},{25,1},{2,26},{10... | collective-permute-start | bytes 245768 | tf_op jit(solution)/shard_map/ppermute | solution.py:419
  5.7 0.5 %collective-permute-start.4 = (f32[1056,128]{1,0:T(8,128)S(1)}, f32[1056,128]{1,0:T(8,128)S(1)}, u32[]{:S(2)}, u32[]{:S(2)}) collective-permute-start(f32[1056,128]{1,0:T(8,128)S(1)} %get-tuple-element.29), channel_id=1, source_target_pairs={{0,16},{8,24},{16,0},{24,8},{1,17},{9,25},{17,1},{25,9},{2,18},{10... | collective-permute-start | bytes 1622024 | tf_op jit(solution)/shard_map/ppermute | solution.py:419
  6.2 0.1 collective-permute-start.3
  6.3 0.0 copy-done
  6.3 1.2 %edges.1 = (f32[64,128]{1,0:T(8,128)S(1)}, f32[1056,128]{1,0:T(8,128)S(1)}, f32[704,128]{1,0:T(8,128)S(1)}, f32[240,128]{1,0:T(8,128)S(1)}) custom-call(f32[16,256,128]{2,1,0:T(8,128)S(1)} %copy-done, f32[1056,128]{1,0:T(8,128)S(1)} %get-tuple-element.22._), custom_call_target="tpu_custom_call" | custom-call | flops 1000000000 | tf_op jit(solution)/shard_map/edges/pallas_call | solution.py:467
  7.5 0.7 %collective-permute-start.1 = (f32[64,128]{1,0:T(8,128)S(1)}, f32[64,128]{1,0:T(8,128)S(1)}, u32[]{:S(2)}, u32[]{:S(2)}) collective-permute-start(f32[64,128]{1,0:T(8,128)S(1)} %get-tuple-element.24), channel_id=1, source_target_pairs={{1,2},{3,4},{5,6},{2,1},{4,3},{6,5},{9,10},{11,12},{13,14},{10,9},... | collective-permute-start | bytes 98312 | tf_op jit(solution)/shard_map/ppermute | solution.py:415
  8.2 3.4 %collective-permute-start = (f32[64,128]{1,0:T(8,128)S(1)}, f32[64,128]{1,0:T(8,128)S(1)}, u32[]{:S(2)}, u32[]{:S(2)}) collective-permute-start(f32[64,128]{1,0:T(8,128)S(1)} %get-tuple-element.24), channel_id=1, source_target_pairs={{0,1},{2,3},{4,5},{6,7},{1,0},{3,2},{5,4},{7,6},{8,9},{10,11},{12,... | collective-permute-start | bytes 98312 | tf_op jit(solution)/shard_map/ppermute | solution.py:415
  12.2 0.1 copy.7.lights_ref
  12.3 0.1 copy.8.curves_ref
  12.4 0.0 collective-permute-done.1.odd_ref
  12.4 0.0 collective-permute-done.even_ref
  12.4 0.0 collective-permute-done.2._.refs_3_
  12.4 0.1 sides.1
  12.6 1.6 %collective-permute-start.6 = (f32[16,128]{1,0:T(8,128)S(1)}, f32[16,128]{1,0:T(8,128)S(1)}, u32[]{:S(2)}, u32[]{:S(2)}) collective-permute-start(f32[16,128]{1,0:T(8,128)S(1)} %get-tuple-element.32), channel_id=1, source_target_pairs={{0,8},{8,0},{16,24},{24,16},{1,9},{9,1},{17,25},{25,17},{2,10},{10... | collective-permute-start | bytes 24584 | tf_op jit(solution)/shard_map/ppermute | solution.py:419
  14.1 1.5 %collective-permute-start.7 = (f32[16,128]{1,0:T(8,128)S(1)}, f32[16,128]{1,0:T(8,128)S(1)}, u32[]{:S(2)}, u32[]{:S(2)}) collective-permute-start(f32[16,128]{1,0:T(8,128)S(1)} %get-tuple-element.33), channel_id=1, source_target_pairs={{0,16},{8,24},{16,0},{24,8},{1,17},{9,25},{17,1},{25,9},{2,18},{10... | collective-permute-start | bytes 24584 | tf_op jit(solution)/shard_map/ppermute | solution.py:419
  15.6 0.5 %collective-permute-start.5 = (f32[704,128]{1,0:T(8,128)S(1)}, f32[704,128]{1,0:T(8,128)S(1)}, u32[]{:S(2)}, u32[]{:S(2)}) collective-permute-start(f32[704,128]{1,0:T(8,128)S(1)} %constant_dynamic-update-slice_fusion), channel_id=1, source_target_pairs={{0,24},{8,16},{16,8},{24,0},{1,25},{9,17},{17,9},{25,1},{2,26},{10... | collective-permute-start | bytes 1081352 | tf_op jit(solution)/shard_map/ppermute | solution.py:419
  16.1 0.0 copy-done.1
  16.1 3.6 %own.1 = (f32[16,64,128]{2,1,0:T(8,128)S(1)}, f32[4,3,8,128]{3,2,1,0:T(8,128)S(1)}, bf16[128,192]{1,0:T(8,128)(2,1)S(1)}) custom-call(s32[4]{0:T(128)S(1)} %copy-done.1, s32[1]{0:T(128)S(6)} %copy.11.flip_ref, f32[16,3]{1,0:T(8,128)S(1)} %copy.7.lights_ref, f32[16,4,8]{2,1,0:T(4,128)S(1)} %copy.8.curves_ref, ...), custom_call_target="tpu_custom_call" | custom-call | flops 4000000000 | tf_op jit(solution)/shard_map/own/pallas_call | solution.py:492
  19.8 1.8 %collective-permute-done.6.refs_5_ = f32[16,128]{1,0:T(8,128)S(1)} collective-permute-done((f32[16,128]{1,0:T(8,128)S(1)}, f32[16,128]{1,0:T(8,128)S(1)}, u32[]{:S(2)}, u32[]{:S(2)}) %collective-permute-start.6) | collective-permute-done | bytes 8224 | tf_op jit(solution)/shard_map/ppermute | solution.py:419
  21.6 0.0 collective-permute-done.7.refs_6_
  21.6 1.5 %collective-permute-start.8 = (f32[240,128]{1,0:T(8,128)S(1)}, f32[240,128]{1,0:T(8,128)S(1)}, u32[]{:S(2)}, u32[]{:S(2)}) collective-permute-start(f32[240,128]{1,0:T(8,128)S(1)} %get-tuple-element.35), channel_id=1, source_target_pairs={{0,24},{8,16},{16,8},{24,0},{1,25},{9,17},{17,9},{25,1},{2,26},{10... | collective-permute-start | bytes 368648 | tf_op jit(solution)/shard_map/ppermute | solution.py:419
  23.1 0.0 collective-permute-done.4.refs_2_
  23.1 0.0 collective-permute-done.3.refs_1_
  23.1 6.3 %near.1.refs_5_.refs_7_ = f32[3,16,64,128]{3,2,1,0:T(8,128)S(1)} custom-call(s32[1]{0:T(128)S(6)} %copy.11.flip_ref, f32[4,3,8,128]{3,2,1,0:T(8,128)S(1)} %get-tuple-element.27.vector_ref, bf16[128,192]{1,0:T(8,128)(2,1)S(1)} %get-tuple-element.28.weight_ref, f32[16,64,128]{2,1,0:T(8,128)S(1)} %get-tuple-element.36.inner_ref, ...), custom_call_target="tpu_custom_call" | custom-call | flops 60000002048 | tf_op jit(solution)/shard_map/near/pallas_call | solution.py:501
  29.4 0.3 collective-permute-done.5.refs_4_
  29.7 3.2 %far.1.refs_6_ = f32[4,4,64,128]{3,2,1,0:T(8,128)} custom-call(s32[1]{0:T(128)S(6)} %copy.11.flip_ref, f32[4,3,8,128]{3,2,1,0:T(8,128)S(1)} %get-tuple-element.27.vector_ref, bf16[128,192]{1,0:T(8,128)(2,1)S(1)} %get-tuple-element.28.weight_ref, f32[1056,128]{1,0:T(8,128)S(1)} %get-tuple-element.23.own_ref.refs_0_, ...), custom_call_target="tpu_custom_call" | custom-call | flops 2000000000 | tf_op jit(solution)/shard_map/far/pallas_call | solution.py:513
  32.8 0.0 collective-permute-done.8.refs_5_
  32.8 1.4 %late.1 = f32[4,4,64,128]{3,2,1,0:T(8,128)} custom-call(s32[1]{0:T(128)S(6)} %copy.11.flip_ref, f32[4,3,8,128]{3,2,1,0:T(8,128)S(1)} %get-tuple-element.27.vector_ref, bf16[128,192]{1,0:T(8,128)(2,1)S(1)} %get-tuple-element.28.weight_ref, f32[1056,128]{1,0:T(8,128)S(1)} %get-tuple-element.23.own_ref.refs_0_, ...), custom_call_target="tpu_custom_call", output_to_operand_aliasing={{}: (9, {})} | custom-call | flops 2000000000 | tf_op jit(solution)/shard_map/late/pallas_call | solution.py:513
  (4 shorter events, 0.0 us)
Async XLA Ops:
  0.0 6.3 %copy-start = (f32[16,256,128]{2,1,0:T(8,128)S(1)}, f32[16,256,128]{2,1,0:T(8,128)}, u32[]{:S(2)}) copy-start(f32[16,256,128]{2,1,0:T(8,128)} %field_ref.3) | copy-start | bytes 6291460
  1.7 10.5 %copy-start.3 = (f32[16,3]{0,1:T(4,128)S(1)}, f32[16,3]{0,1:T(4,128)}, u32[]{:S(2)}) copy-start(f32[16,3]{0,1:T(4,128)} %param.6) | copy-start | bytes 580
  1.7 10.6 %copy-start.2 = (f32[16,4,8]{0,2,1:T(8,128)S(1)}, f32[16,4,8]{0,2,1:T(8,128)}, u32[]{:S(2)}) copy-start(f32[16,4,8]{0,2,1:T(8,128)} %param.7) | copy-start | bytes 6148
  1.7 14.4 %copy-start.1 = (s32[4]{0:T(128)S(1)}, s32[4]{0:T(128)}, u32[]{:S(2)}) copy-start(s32[4]{0:T(128)} %index_ref.1) | copy-start | bytes 52
  1.7 10.7 %collective-permute-start.2 = (f32[160,128]{1,0:T(8,128)S(1)}, f32[160,128]{1,0:T(8,128)S(1)}, u32[]{:S(2)}, u32[]{:S(2)}) collective-permute-start(f32[160,128]{1,0:T(8,128)S(1)} %get-tuple-element.25), channel_id=1, source_target_pairs={{0,24},{8,16},{16,8},{24,0},{1,25},{9,17},{17,9},{25,1},{2,26},{10... | collective-permute-start | bytes 245768 | tf_op jit(solution)/shard_map/ppermute | solution.py:419
  5.7 17.4 %collective-permute-start.4 = (f32[1056,128]{1,0:T(8,128)S(1)}, f32[1056,128]{1,0:T(8,128)S(1)}, u32[]{:S(2)}, u32[]{:S(2)}) collective-permute-start(f32[1056,128]{1,0:T(8,128)S(1)} %get-tuple-element.29), channel_id=1, source_target_pairs={{0,16},{8,24},{16,0},{24,8},{1,17},{9,25},{17,1},{25,9},{2,18},{10... | collective-permute-start | bytes 1622024 | tf_op jit(solution)/shard_map/ppermute | solution.py:419
  6.2 16.9 %collective-permute-start.3 = (f32[1056,128]{1,0:T(8,128)S(1)}, f32[1056,128]{1,0:T(8,128)S(1)}, u32[]{:S(2)}, u32[]{:S(2)}) collective-permute-start(f32[1056,128]{1,0:T(8,128)S(1)} %get-tuple-element.22._), channel_id=1, source_target_pairs={{0,8},{8,0},{16,24},{24,16},{1,9},{9,1},{17,25},{25,17},{2,10},{10... | collective-permute-start | bytes 1622024 | tf_op jit(solution)/shard_map/ppermute | solution.py:419
  7.5 4.9 %collective-permute-start.1 = (f32[64,128]{1,0:T(8,128)S(1)}, f32[64,128]{1,0:T(8,128)S(1)}, u32[]{:S(2)}, u32[]{:S(2)}) collective-permute-start(f32[64,128]{1,0:T(8,128)S(1)} %get-tuple-element.24), channel_id=1, source_target_pairs={{1,2},{3,4},{5,6},{2,1},{4,3},{6,5},{9,10},{11,12},{13,14},{10,9},... | collective-permute-start | bytes 98312 | tf_op jit(solution)/shard_map/ppermute | solution.py:415
  8.2 4.3 %collective-permute-start = (f32[64,128]{1,0:T(8,128)S(1)}, f32[64,128]{1,0:T(8,128)S(1)}, u32[]{:S(2)}, u32[]{:S(2)}) collective-permute-start(f32[64,128]{1,0:T(8,128)S(1)} %get-tuple-element.24), channel_id=1, source_target_pairs={{0,1},{2,3},{4,5},{6,7},{1,0},{3,2},{5,4},{7,6},{8,9},{10,11},{12,... | collective-permute-start | bytes 98312 | tf_op jit(solution)/shard_map/ppermute | solution.py:415
  12.6 9.0 %collective-permute-start.6 = (f32[16,128]{1,0:T(8,128)S(1)}, f32[16,128]{1,0:T(8,128)S(1)}, u32[]{:S(2)}, u32[]{:S(2)}) collective-permute-start(f32[16,128]{1,0:T(8,128)S(1)} %get-tuple-element.32), channel_id=1, source_target_pairs={{0,8},{8,0},{16,24},{24,16},{1,9},{9,1},{17,25},{25,17},{2,10},{10... | collective-permute-start | bytes 24584 | tf_op jit(solution)/shard_map/ppermute | solution.py:419
  14.1 7.5 %collective-permute-start.7 = (f32[16,128]{1,0:T(8,128)S(1)}, f32[16,128]{1,0:T(8,128)S(1)}, u32[]{:S(2)}, u32[]{:S(2)}) collective-permute-start(f32[16,128]{1,0:T(8,128)S(1)} %get-tuple-element.33), channel_id=1, source_target_pairs={{0,16},{8,24},{16,0},{24,8},{1,17},{9,25},{17,1},{25,9},{2,18},{10... | collective-permute-start | bytes 24584 | tf_op jit(solution)/shard_map/ppermute | solution.py:419
  15.6 14.0 %collective-permute-start.5 = (f32[704,128]{1,0:T(8,128)S(1)}, f32[704,128]{1,0:T(8,128)S(1)}, u32[]{:S(2)}, u32[]{:S(2)}) collective-permute-start(f32[704,128]{1,0:T(8,128)S(1)} %constant_dynamic-update-slice_fusion), channel_id=1, source_target_pairs={{0,24},{8,16},{16,8},{24,0},{1,25},{9,17},{17,9},{25,1},{2,26},{10... | collective-permute-start | bytes 1081352 | tf_op jit(solution)/shard_map/ppermute | solution.py:419
  21.6 11.2 %collective-permute-start.8 = (f32[240,128]{1,0:T(8,128)S(1)}, f32[240,128]{1,0:T(8,128)S(1)}, u32[]{:S(2)}, u32[]{:S(2)}) collective-permute-start(f32[240,128]{1,0:T(8,128)S(1)} %get-tuple-element.35), channel_id=1, source_target_pairs={{0,24},{8,16},{16,8},{24,0},{1,25},{9,17},{17,9},{25,1},{2,26},{10... | collective-permute-start | bytes 368648 | tf_op jit(solution)/shard_map/ppermute | solution.py:419

commit v15 on v10

--- a/solution.py
+++ b/solution.py
@@ -337,23 +337,31 @@
             m, zs[m], places[m], laterals[m], base, cells, rows, parts, cols, ends_ref, weight_ref, cell_refs[m], mixed_refs[m]
         )
 
-    for step in prepare(0, 0):
-        step()
-
-    def tile(i, carry):
+    def others(base):
+        return [step for m in range(count - 1) for step in prepare(m, base)]
+
+    def unit(i, ahead):
         base = pl.multiple_of(i * SUB, SUB)
-        after = pl.multiple_of(jnp.minimum(i + 1, tiles - 1) * SUB, SUB)
         at = pl.ds(base, SUB)
+        last = prepare(count - 1, base)
+        lengths = [len(z) for z in zs[:-1]]
+        cuts = [len(last) * sum(lengths[:m]) // sum(lengths) for m in range(count)]
         for m in range(count):
-            beside = prepare(m + 1, base) if m + 1 < count else prepare(0, after)
+            beside = ahead if m == count - 1 else last[cuts[m] : cuts[m + 1]]
             inner = (lambda p, j: inner_ref[p * channels + j, at, :]) if m == 0 else None
             result = march_unit(flip, vector_ref, zs[m], cells, cell_refs[m], mixed_refs[m], beside, inner)
             for p in range(passes):
                 for j in range(channels):
                     out_ref[m, p * channels + j, at, :] = result[p][j]
+
+    def tile(i, carry):
+        unit(i, others(pl.multiple_of((i + 1) * SUB, SUB)))
         return carry
 
-    lax.fori_loop(0, tiles, tile, 0)
+    for step in others(0):
+        step()
+    lax.fori_loop(0, tiles - 1, tile, 0)
+    unit(tiles - 1, [])
 
 
 def over_either(first_leads, one, other):
@@ -448,7 +456,7 @@
     near_rows = 2 * cells + cells * rows
     head_rows = 2 * cells + 2 * rows
     skip = rows // parts
-    split = rows - rows // parts
+    split = rows // 2
     body_rows = skip + (cells - 2) * split + cells
     rest_rows = (cells - 2) * (rows - split) + 2 * SUB
     *packed, far_head = pl.pallas_call(

time: 34.4 us -> 34.6 us (level)
  Pallas kernels: 17.4 us -> 17.8 us
    pallas_call x1, Pallas kernels: 6.24 us -> 6.66 us  [on_device(): pl.pallas_call(functools.partial(near_kernel, parts), out_shape=array(par...]
  transfers between devices with their start and end apart: 9 -> 9, of which waited for: 2 -> 1; matrix products, arithmetic and copies ran while one was open for 0% -> 0% of each run, Pallas kernels for 42% -> 40%
where the time goes in v15:
time: 34.6 us; the launch traced here: 34.3 us
  Pallas kernels  17.8 us (51%)
  starting transfers between devices  13.7 us (40%)
  waiting for transfers between devices  1.89 us (5%)
  between operations  0.76 us (2%)
    ppermute x7, starting transfers between devices, swap_along(): lax.ppermute(block, axis, [(i, i ^ mask) for i in range(lax.axis_size(axi...  9.64 us
    pallas_call x1, Pallas kernels, on_device(): pl.pallas_call(functools.partial(near_kernel, parts), out_shape=array(par...  6.66 us
    pallas_call x2, Pallas kernels, on_device(): pl.pallas_call(functools.partial(far_kernel, parts, split, low, high), ou...  4.52 us
    ppermute x2, starting transfers between devices, swap_pairs(): return lax.ppermute(block, axis, pairs + [(j, i) for i, j in pairs])  4.06 us
    pallas_call x1, Pallas kernels, on_device(): pl.pallas_call(functools.partial(own_kernel, parts), out_shape=[array(val...  3.62 us
    ppermute x7, waiting for transfers between devices, swap_along(): lax.ppermute(block, axis, [(i, i ^ mask) for i in range(lax.axis_size(axi...  1.86 us
    pallas_call x1, Pallas kernels, on_device(): pl.pallas_call(functools.partial(pack_kernel, parts), out_shape=[array(ne...  1.71 us
    pallas_call x1, Pallas kernels, on_device(): pl.pallas_call(functools.partial(edge_kernel, parts, split), out_shape=[a...  1.16 us
  transfers between devices with their start and end apart: 9, of which 1 were waited for; matrix products, arithmetic and copies ran while one was open for 0% of the time, Pallas kernels for 40%

profile of v15, /device:TPU:0, one launch (start us, length us, event | category | flops | bytes accessed | tf_op | source)
XLA Modules:
  0.0 34.3 jit_solution(15841262576144360333)
XLA Ops:
  0.0 1.7 %pack.1 = (f32[1056,128]{1,0:T(8,128)S(1)}, f32[1056,128]{1,0:T(8,128)S(1)}, f32[160,128]{1,0:T(8,128)S(1)}) custom-call(f32[16,256,128]{2,1,0:T(8,128)} %field_ref.3), custom_call_target="tpu_custom_call" | custom-call | flops 1000000000 | tf_op jit(solution)/shard_map/pack/pallas_call | solution.py:462
  1.7 0.0 copy-start.3
  1.7 0.0 copy-start.2
  1.7 0.0 copy-start.1
  1.8 4.0 %collective-permute-start.2 = (f32[160,128]{1,0:T(8,128)S(1)}, f32[160,128]{1,0:T(8,128)S(1)}, u32[]{:S(2)}, u32[]{:S(2)}) collective-permute-start(f32[160,128]{1,0:T(8,128)S(1)} %get-tuple-element.25), channel_id=1, source_target_pairs={{0,24},{8,16},{16,8},{24,0},{1,25},{9,17},{17,9},{25,1},{2,26},{10... | collective-permute-start | bytes 245768 | tf_op jit(solution)/shard_map/ppermute | solution.py:427
  5.7 0.5 %collective-permute-start.4 = (f32[1056,128]{1,0:T(8,128)S(1)}, f32[1056,128]{1,0:T(8,128)S(1)}, u32[]{:S(2)}, u32[]{:S(2)}) collective-permute-start(f32[1056,128]{1,0:T(8,128)S(1)} %get-tuple-element.29), channel_id=1, source_target_pairs={{0,16},{8,24},{16,0},{24,8},{1,17},{9,25},{17,1},{25,9},{2,18},{10... | collective-permute-start | bytes 1622024 | tf_op jit(solution)/shard_map/ppermute | solution.py:427
  6.2 0.1 collective-permute-start.3
  6.4 0.0 copy-done
  6.4 1.2 %edges.1 = (f32[64,128]{1,0:T(8,128)S(1)}, f32[1056,128]{1,0:T(8,128)S(1)}, f32[480,128]{1,0:T(8,128)S(1)}, f32[464,128]{1,0:T(8,128)S(1)}) custom-call(f32[16,256,128]{2,1,0:T(8,128)S(1)} %copy-done, f32[1056,128]{1,0:T(8,128)S(1)} %get-tuple-element.22._), custom_call_target="tpu_custom_call" | custom-call | flops 1000000000 | tf_op jit(solution)/shard_map/edges/pallas_call | solution.py:475
  7.5 0.7 %collective-permute-start.1 = (f32[64,128]{1,0:T(8,128)S(1)}, f32[64,128]{1,0:T(8,128)S(1)}, u32[]{:S(2)}, u32[]{:S(2)}) collective-permute-start(f32[64,128]{1,0:T(8,128)S(1)} %get-tuple-element.24), channel_id=1, source_target_pairs={{1,2},{3,4},{5,6},{2,1},{4,3},{6,5},{9,10},{11,12},{13,14},{10,9},... | collective-permute-start | bytes 98312 | tf_op jit(solution)/shard_map/ppermute | solution.py:423
  8.2 3.4 %collective-permute-start = (f32[64,128]{1,0:T(8,128)S(1)}, f32[64,128]{1,0:T(8,128)S(1)}, u32[]{:S(2)}, u32[]{:S(2)}) collective-permute-start(f32[64,128]{1,0:T(8,128)S(1)} %get-tuple-element.24), channel_id=1, source_target_pairs={{0,1},{2,3},{4,5},{6,7},{1,0},{3,2},{5,4},{7,6},{8,9},{10,11},{12,... | collective-permute-start | bytes 98312 | tf_op jit(solution)/shard_map/ppermute | solution.py:423
  12.3 0.0 copy-done.3
  12.3 0.1 copy.7.lights_ref
  12.4 0.1 copy.8.curves_ref
  12.4 0.0 collective-permute-done.1.odd_ref
  12.4 0.0 collective-permute-done.even_ref
  12.5 0.0 collective-permute-done.2._.refs_3_
  12.5 0.1 sides.1
  12.6 1.6 %collective-permute-start.6 = (f32[16,128]{1,0:T(8,128)S(1)}, f32[16,128]{1,0:T(8,128)S(1)}, u32[]{:S(2)}, u32[]{:S(2)}) collective-permute-start(f32[16,128]{1,0:T(8,128)S(1)} %get-tuple-element.32), channel_id=1, source_target_pairs={{0,8},{8,0},{16,24},{24,16},{1,9},{9,1},{17,25},{25,17},{2,10},{10... | collective-permute-start | bytes 24584 | tf_op jit(solution)/shard_map/ppermute | solution.py:427
  14.1 1.5 %collective-permute-start.7 = (f32[16,128]{1,0:T(8,128)S(1)}, f32[16,128]{1,0:T(8,128)S(1)}, u32[]{:S(2)}, u32[]{:S(2)}) collective-permute-start(f32[16,128]{1,0:T(8,128)S(1)} %get-tuple-element.33), channel_id=1, source_target_pairs={{0,16},{8,24},{16,0},{24,8},{1,17},{9,25},{17,1},{25,9},{2,18},{10... | collective-permute-start | bytes 24584 | tf_op jit(solution)/shard_map/ppermute | solution.py:427
  15.7 0.5 %collective-permute-start.5 = (f32[480,128]{1,0:T(8,128)S(1)}, f32[480,128]{1,0:T(8,128)S(1)}, u32[]{:S(2)}, u32[]{:S(2)}) collective-permute-start(f32[480,128]{1,0:T(8,128)S(1)} %constant_dynamic-update-slice_fusion), channel_id=1, source_target_pairs={{0,24},{8,16},{16,8},{24,0},{1,25},{9,17},{17,9},{25,1},{2,26},{10... | collective-permute-start | bytes 737288 | tf_op jit(solution)/shard_map/ppermute | solution.py:427
  16.1 3.6 %own.1 = (f32[16,64,128]{2,1,0:T(8,128)S(1)}, f32[4,3,8,128]{3,2,1,0:T(8,128)S(1)}, bf16[128,192]{1,0:T(8,128)(2,1)S(1)}) custom-call(s32[4]{0:T(128)S(1)} %copy-done.1, s32[1]{0:T(128)S(6)} %copy.11.flip_ref, f32[16,3]{1,0:T(8,128)S(1)} %copy.7.lights_ref, f32[16,4,8]{2,1,0:T(4,128)S(1)} %copy.8.curves_ref, ...), custom_call_target="tpu_custom_call" | custom-call | flops 4000000000 | tf_op jit(solution)/shard_map/own/pallas_call | solution.py:500
  19.8 1.8 %collective-permute-done.6.refs_5_ = f32[16,128]{1,0:T(8,128)S(1)} collective-permute-done((f32[16,128]{1,0:T(8,128)S(1)}, f32[16,128]{1,0:T(8,128)S(1)}, u32[]{:S(2)}, u32[]{:S(2)}) %collective-permute-start.6) | collective-permute-done | bytes 8224 | tf_op jit(solution)/shard_map/ppermute | solution.py:427
  21.6 0.0 collective-permute-done.7.refs_6_
  21.6 1.5 %collective-permute-start.8 = (f32[464,128]{1,0:T(8,128)S(1)}, f32[464,128]{1,0:T(8,128)S(1)}, u32[]{:S(2)}, u32[]{:S(2)}) collective-permute-start(f32[464,128]{1,0:T(8,128)S(1)} %get-tuple-element.35), channel_id=1, source_target_pairs={{0,24},{8,16},{16,8},{24,0},{1,25},{9,17},{17,9},{25,1},{2,26},{10... | collective-permute-start | bytes 712712 | tf_op jit(solution)/shard_map/ppermute | solution.py:427
  23.1 0.0 collective-permute-done.4.refs_2_
  23.1 0.0 collective-permute-done.3.refs_1_
  23.1 6.7 %near.1.refs_5_.refs_7_ = f32[3,16,64,128]{3,2,1,0:T(8,128)S(1)} custom-call(s32[1]{0:T(128)S(6)} %copy.11.flip_ref, f32[4,3,8,128]{3,2,1,0:T(8,128)S(1)} %get-tuple-element.27.vector_ref, bf16[128,192]{1,0:T(8,128)(2,1)S(1)} %get-tuple-element.28.weight_ref, f32[16,64,128]{2,1,0:T(8,128)S(1)} %get-tuple-element.36.inner_ref, ...), custom_call_target="tpu_custom_call" | custom-call | flops 60000002048 | tf_op jit(solution)/shard_map/near/pallas_call | solution.py:509
  29.8 0.0 collective-permute-done.5.refs_4_
  29.8 2.3 %far.1.refs_6_ = f32[4,4,64,128]{3,2,1,0:T(8,128)} custom-call(s32[1]{0:T(128)S(6)} %copy.11.flip_ref, f32[4,3,8,128]{3,2,1,0:T(8,128)S(1)} %get-tuple-element.27.vector_ref, bf16[128,192]{1,0:T(8,128)(2,1)S(1)} %get-tuple-element.28.weight_ref, f32[1056,128]{1,0:T(8,128)S(1)} %get-tuple-element.23.own_ref.refs_0_, ...), custom_call_target="tpu_custom_call" | custom-call | flops 2000000000 | tf_op jit(solution)/shard_map/far/pallas_call | solution.py:521
  32.1 0.0 collective-permute-done.8.refs_5_
  32.1 2.3 %late.1 = f32[4,4,64,128]{3,2,1,0:T(8,128)} custom-call(s32[1]{0:T(128)S(6)} %copy.11.flip_ref, f32[4,3,8,128]{3,2,1,0:T(8,128)S(1)} %get-tuple-element.27.vector_ref, bf16[128,192]{1,0:T(8,128)(2,1)S(1)} %get-tuple-element.28.weight_ref, f32[1056,128]{1,0:T(8,128)S(1)} %get-tuple-element.23.own_ref.refs_0_, ...), custom_call_target="tpu_custom_call", output_to_operand_aliasing={{}: (9, {})} | custom-call | flops 2000000000 | tf_op jit(solution)/shard_map/late/pallas_call | solution.py:521
  (4 shorter events, 0.0 us)
Async XLA Ops:
  0.0 6.4 %copy-start = (f32[16,256,128]{2,1,0:T(8,128)S(1)}, f32[16,256,128]{2,1,0:T(8,128)}, u32[]{:S(2)}) copy-start(f32[16,256,128]{2,1,0:T(8,128)} %field_ref.3) | copy-start | bytes 6291460
  1.7 10.5 %copy-start.3 = (f32[16,3]{0,1:T(4,128)S(1)}, f32[16,3]{0,1:T(4,128)}, u32[]{:S(2)}) copy-start(f32[16,3]{0,1:T(4,128)} %param.6) | copy-start | bytes 580
  1.7 10.6 %copy-start.2 = (f32[16,4,8]{0,2,1:T(8,128)S(1)}, f32[16,4,8]{0,2,1:T(8,128)}, u32[]{:S(2)}) copy-start(f32[16,4,8]{0,2,1:T(8,128)} %param.7) | copy-start | bytes 6148
  1.7 14.4 %copy-start.1 = (s32[4]{0:T(128)S(1)}, s32[4]{0:T(128)}, u32[]{:S(2)}) copy-start(s32[4]{0:T(128)} %index_ref.1) | copy-start | bytes 52
  1.8 10.7 %collective-permute-start.2 = (f32[160,128]{1,0:T(8,128)S(1)}, f32[160,128]{1,0:T(8,128)S(1)}, u32[]{:S(2)}, u32[]{:S(2)}) collective-permute-start(f32[160,128]{1,0:T(8,128)S(1)} %get-tuple-element.25), channel_id=1, source_target_pairs={{0,24},{8,16},{16,8},{24,0},{1,25},{9,17},{17,9},{25,1},{2,26},{10... | collective-permute-start | bytes 245768 | tf_op jit(solution)/shard_map/ppermute | solution.py:427
  5.7 17.4 %collective-permute-start.4 = (f32[1056,128]{1,0:T(8,128)S(1)}, f32[1056,128]{1,0:T(8,128)S(1)}, u32[]{:S(2)}, u32[]{:S(2)}) collective-permute-start(f32[1056,128]{1,0:T(8,128)S(1)} %get-tuple-element.29), channel_id=1, source_target_pairs={{0,16},{8,24},{16,0},{24,8},{1,17},{9,25},{17,1},{25,9},{2,18},{10... | collective-permute-start | bytes 1622024 | tf_op jit(solution)/shard_map/ppermute | solution.py:427
  6.2 16.9 %collective-permute-start.3 = (f32[1056,128]{1,0:T(8,128)S(1)}, f32[1056,128]{1,0:T(8,128)S(1)}, u32[]{:S(2)}, u32[]{:S(2)}) collective-permute-start(f32[1056,128]{1,0:T(8,128)S(1)} %get-tuple-element.22._), channel_id=1, source_target_pairs={{0,8},{8,0},{16,24},{24,16},{1,9},{9,1},{17,25},{25,17},{2,10},{10... | collective-permute-start | bytes 1622024 | tf_op jit(solution)/shard_map/ppermute | solution.py:427
  7.5 4.9 %collective-permute-start.1 = (f32[64,128]{1,0:T(8,128)S(1)}, f32[64,128]{1,0:T(8,128)S(1)}, u32[]{:S(2)}, u32[]{:S(2)}) collective-permute-start(f32[64,128]{1,0:T(8,128)S(1)} %get-tuple-element.24), channel_id=1, source_target_pairs={{1,2},{3,4},{5,6},{2,1},{4,3},{6,5},{9,10},{11,12},{13,14},{10,9},... | collective-permute-start | bytes 98312 | tf_op jit(solution)/shard_map/ppermute | solution.py:423
  8.2 4.3 %collective-permute-start = (f32[64,128]{1,0:T(8,128)S(1)}, f32[64,128]{1,0:T(8,128)S(1)}, u32[]{:S(2)}, u32[]{:S(2)}) collective-permute-start(f32[64,128]{1,0:T(8,128)S(1)} %get-tuple-element.24), channel_id=1, source_target_pairs={{0,1},{2,3},{4,5},{6,7},{1,0},{3,2},{5,4},{7,6},{8,9},{10,11},{12,... | collective-permute-start | bytes 98312 | tf_op jit(solution)/shard_map/ppermute | solution.py:423
  12.6 9.0 %collective-permute-start.6 = (f32[16,128]{1,0:T(8,128)S(1)}, f32[16,128]{1,0:T(8,128)S(1)}, u32[]{:S(2)}, u32[]{:S(2)}) collective-permute-start(f32[16,128]{1,0:T(8,128)S(1)} %get-tuple-element.32), channel_id=1, source_target_pairs={{0,8},{8,0},{16,24},{24,16},{1,9},{9,1},{17,25},{25,17},{2,10},{10... | collective-permute-start | bytes 24584 | tf_op jit(solution)/shard_map/ppermute | solution.py:427
  14.1 7.5 %collective-permute-start.7 = (f32[16,128]{1,0:T(8,128)S(1)}, f32[16,128]{1,0:T(8,128)S(1)}, u32[]{:S(2)}, u32[]{:S(2)}) collective-permute-start(f32[16,128]{1,0:T(8,128)S(1)} %get-tuple-element.33), channel_id=1, source_target_pairs={{0,16},{8,24},{16,0},{24,8},{1,17},{9,25},{17,1},{25,9},{2,18},{10... | collective-permute-start | bytes 24584 | tf_op jit(solution)/shard_map/ppermute | solution.py:427
  15.7 14.1 %collective-permute-start.5 = (f32[480,128]{1,0:T(8,128)S(1)}, f32[480,128]{1,0:T(8,128)S(1)}, u32[]{:S(2)}, u32[]{:S(2)}) collective-permute-start(f32[480,128]{1,0:T(8,128)S(1)} %constant_dynamic-update-slice_fusion), channel_id=1, source_target_pairs={{0,24},{8,16},{16,8},{24,0},{1,25},{9,17},{17,9},{25,1},{2,26},{10... | collective-permute-start | bytes 737288 | tf_op jit(solution)/shard_map/ppermute | solution.py:427
  21.6 10.4 %collective-permute-start.8 = (f32[464,128]{1,0:T(8,128)S(1)}, f32[464,128]{1,0:T(8,128)S(1)}, u32[]{:S(2)}, u32[]{:S(2)}) collective-permute-start(f32[464,128]{1,0:T(8,128)S(1)} %get-tuple-element.35), channel_id=1, source_target_pairs={{0,24},{8,16},{16,8},{24,0},{1,25},{9,17},{17,9},{25,1},{2,26},{10... | collective-permute-start | bytes 712712 | tf_op jit(solution)/shard_map/ppermute | solution.py:427

commit v16 on v10

--- a/solution.py
+++ b/solution.py
@@ -448,7 +448,7 @@
     near_rows = 2 * cells + cells * rows
     head_rows = 2 * cells + 2 * rows
     skip = rows // parts
-    split = rows - rows // parts
+    split = rows // 2
     body_rows = skip + (cells - 2) * split + cells
     rest_rows = (cells - 2) * (rows - split) + 2 * SUB
     *packed, far_head = pl.pallas_call(

time: 34.4 us -> 34.1 us (level)
  transfers between devices with their start and end apart: 9 -> 9, of which waited for: 2 -> 1; matrix products, arithmetic and copies ran while one was open for 0% -> 0% of each run, Pallas kernels for 42% -> 40%
where the time goes in v16:
time: 34.1 us; the launch traced here: 33.9 us
  Pallas kernels  17.4 us (51%)
  starting transfers between devices  13.7 us (40%)
  waiting for transfers between devices  1.89 us (6%)
  between operations  0.76 us (2%)
    ppermute x7, starting transfers between devices, swap_along(): lax.ppermute(block, axis, [(i, i ^ mask) for i in range(lax.axis_size(axi...  9.64 us
    pallas_call x1, Pallas kernels, on_device(): pl.pallas_call(functools.partial(near_kernel, parts), out_shape=array(par...  6.24 us
    pallas_call x2, Pallas kernels, on_device(): pl.pallas_call(functools.partial(far_kernel, parts, split, low, high), ou...  4.52 us
    ppermute x2, starting transfers between devices, swap_pairs(): return lax.ppermute(block, axis, pairs + [(j, i) for i, j in pairs])  4.06 us
    pallas_call x1, Pallas kernels, on_device(): pl.pallas_call(functools.partial(own_kernel, parts), out_shape=[array(val...  3.62 us
    ppermute x7, waiting for transfers between devices, swap_along(): lax.ppermute(block, axis, [(i, i ^ mask) for i in range(lax.axis_size(axi...  1.86 us
    pallas_call x1, Pallas kernels, on_device(): pl.pallas_call(functools.partial(pack_kernel, parts), out_shape=[array(ne...  1.71 us
    pallas_call x1, Pallas kernels, on_device(): pl.pallas_call(functools.partial(edge_kernel, parts, split), out_shape=[a...  1.16 us
  transfers between devices with their start and end apart: 9, of which 1 were waited for; matrix products, arithmetic and copies ran while one was open for 0% of the time, Pallas kernels for 40%

profile of v16, /device:TPU:0, one launch (start us, length us, event | category | flops | bytes accessed | tf_op | source)
XLA Modules:
  0.0 33.9 jit_solution(16085057274725780544)
XLA Ops:
  0.0 1.7 %pack.1 = (f32[1056,128]{1,0:T(8,128)S(1)}, f32[1056,128]{1,0:T(8,128)S(1)}, f32[160,128]{1,0:T(8,128)S(1)}) custom-call(f32[16,256,128]{2,1,0:T(8,128)} %field_ref.3), custom_call_target="tpu_custom_call" | custom-call | flops 1000000000 | tf_op jit(solution)/shard_map/pack/pallas_call | solution.py:454
  1.7 0.0 copy-start.3
  1.7 0.0 copy-start.2
  1.7 0.0 copy-start.1
  1.8 4.0 %collective-permute-start.2 = (f32[160,128]{1,0:T(8,128)S(1)}, f32[160,128]{1,0:T(8,128)S(1)}, u32[]{:S(2)}, u32[]{:S(2)}) collective-permute-start(f32[160,128]{1,0:T(8,128)S(1)} %get-tuple-element.25), channel_id=1, source_target_pairs={{0,24},{8,16},{16,8},{24,0},{1,25},{9,17},{17,9},{25,1},{2,26},{10... | collective-permute-start | bytes 245768 | tf_op jit(solution)/shard_map/ppermute | solution.py:419
  5.7 0.5 %collective-permute-start.4 = (f32[1056,128]{1,0:T(8,128)S(1)}, f32[1056,128]{1,0:T(8,128)S(1)}, u32[]{:S(2)}, u32[]{:S(2)}) collective-permute-start(f32[1056,128]{1,0:T(8,128)S(1)} %get-tuple-element.29), channel_id=1, source_target_pairs={{0,16},{8,24},{16,0},{24,8},{1,17},{9,25},{17,1},{25,9},{2,18},{10... | collective-permute-start | bytes 1622024 | tf_op jit(solution)/shard_map/ppermute | solution.py:419
  6.2 0.1 collective-permute-start.3
  6.4 0.0 copy-done
  6.4 1.2 %edges.1 = (f32[64,128]{1,0:T(8,128)S(1)}, f32[1056,128]{1,0:T(8,128)S(1)}, f32[480,128]{1,0:T(8,128)S(1)}, f32[464,128]{1,0:T(8,128)S(1)}) custom-call(f32[16,256,128]{2,1,0:T(8,128)S(1)} %copy-done, f32[1056,128]{1,0:T(8,128)S(1)} %get-tuple-element.22._), custom_call_target="tpu_custom_call" | custom-call | flops 1000000000 | tf_op jit(solution)/shard_map/edges/pallas_call | solution.py:467
  7.5 0.7 %collective-permute-start.1 = (f32[64,128]{1,0:T(8,128)S(1)}, f32[64,128]{1,0:T(8,128)S(1)}, u32[]{:S(2)}, u32[]{:S(2)}) collective-permute-start(f32[64,128]{1,0:T(8,128)S(1)} %get-tuple-element.24), channel_id=1, source_target_pairs={{1,2},{3,4},{5,6},{2,1},{4,3},{6,5},{9,10},{11,12},{13,14},{10,9},... | collective-permute-start | bytes 98312 | tf_op jit(solution)/shard_map/ppermute | solution.py:415
  8.2 3.4 %collective-permute-start = (f32[64,128]{1,0:T(8,128)S(1)}, f32[64,128]{1,0:T(8,128)S(1)}, u32[]{:S(2)}, u32[]{:S(2)}) collective-permute-start(f32[64,128]{1,0:T(8,128)S(1)} %get-tuple-element.24), channel_id=1, source_target_pairs={{0,1},{2,3},{4,5},{6,7},{1,0},{3,2},{5,4},{7,6},{8,9},{10,11},{12,... | collective-permute-start | bytes 98312 | tf_op jit(solution)/shard_map/ppermute | solution.py:415
  12.3 0.1 copy.7.lights_ref
  12.3 0.0 copy-done.2
  12.4 0.1 copy.8.curves_ref
  12.4 0.0 collective-permute-done.1.odd_ref
  12.4 0.0 collective-permute-done.even_ref
  12.5 0.0 collective-permute-done.2._.refs_3_
  12.5 0.1 sides.1
  12.6 1.6 %collective-permute-start.6 = (f32[16,128]{1,0:T(8,128)S(1)}, f32[16,128]{1,0:T(8,128)S(1)}, u32[]{:S(2)}, u32[]{:S(2)}) collective-permute-start(f32[16,128]{1,0:T(8,128)S(1)} %get-tuple-element.32), channel_id=1, source_target_pairs={{0,8},{8,0},{16,24},{24,16},{1,9},{9,1},{17,25},{25,17},{2,10},{10... | collective-permute-start | bytes 24584 | tf_op jit(solution)/shard_map/ppermute | solution.py:419
  14.1 1.5 %collective-permute-start.7 = (f32[16,128]{1,0:T(8,128)S(1)}, f32[16,128]{1,0:T(8,128)S(1)}, u32[]{:S(2)}, u32[]{:S(2)}) collective-permute-start(f32[16,128]{1,0:T(8,128)S(1)} %get-tuple-element.33), channel_id=1, source_target_pairs={{0,16},{8,24},{16,0},{24,8},{1,17},{9,25},{17,1},{25,9},{2,18},{10... | collective-permute-start | bytes 24584 | tf_op jit(solution)/shard_map/ppermute | solution.py:419
  15.7 0.5 %collective-permute-start.5 = (f32[480,128]{1,0:T(8,128)S(1)}, f32[480,128]{1,0:T(8,128)S(1)}, u32[]{:S(2)}, u32[]{:S(2)}) collective-permute-start(f32[480,128]{1,0:T(8,128)S(1)} %constant_dynamic-update-slice_fusion), channel_id=1, source_target_pairs={{0,24},{8,16},{16,8},{24,0},{1,25},{9,17},{17,9},{25,1},{2,26},{10... | collective-permute-start | bytes 737288 | tf_op jit(solution)/shard_map/ppermute | solution.py:419
  16.1 3.6 %own.1 = (f32[16,64,128]{2,1,0:T(8,128)S(1)}, f32[4,3,8,128]{3,2,1,0:T(8,128)S(1)}, bf16[128,192]{1,0:T(8,128)(2,1)S(1)}) custom-call(s32[4]{0:T(128)S(1)} %copy-done.1, s32[1]{0:T(128)S(6)} %copy.11.flip_ref, f32[16,3]{1,0:T(8,128)S(1)} %copy.7.lights_ref, f32[16,4,8]{2,1,0:T(4,128)S(1)} %copy.8.curves_ref, ...), custom_call_target="tpu_custom_call" | custom-call | flops 4000000000 | tf_op jit(solution)/shard_map/own/pallas_call | solution.py:492
  19.8 1.8 %collective-permute-done.6.refs_5_ = f32[16,128]{1,0:T(8,128)S(1)} collective-permute-done((f32[16,128]{1,0:T(8,128)S(1)}, f32[16,128]{1,0:T(8,128)S(1)}, u32[]{:S(2)}, u32[]{:S(2)}) %collective-permute-start.6) | collective-permute-done | bytes 8224 | tf_op jit(solution)/shard_map/ppermute | solution.py:419
  21.6 0.0 collective-permute-done.7.refs_6_
  21.6 1.5 %collective-permute-start.8 = (f32[464,128]{1,0:T(8,128)S(1)}, f32[464,128]{1,0:T(8,128)S(1)}, u32[]{:S(2)}, u32[]{:S(2)}) collective-permute-start(f32[464,128]{1,0:T(8,128)S(1)} %get-tuple-element.35), channel_id=1, source_target_pairs={{0,24},{8,16},{16,8},{24,0},{1,25},{9,17},{17,9},{25,1},{2,26},{10... | collective-permute-start | bytes 712712 | tf_op jit(solution)/shard_map/ppermute | solution.py:419
  23.1 0.0 collective-permute-done.4.refs_2_
  23.1 0.0 collective-permute-done.3.refs_1_
  23.1 6.2 %near.1.refs_5_.refs_7_ = f32[3,16,64,128]{3,2,1,0:T(8,128)S(1)} custom-call(s32[1]{0:T(128)S(6)} %copy.11.flip_ref, f32[4,3,8,128]{3,2,1,0:T(8,128)S(1)} %get-tuple-element.27.vector_ref, bf16[128,192]{1,0:T(8,128)(2,1)S(1)} %get-tuple-element.28.weight_ref, f32[16,64,128]{2,1,0:T(8,128)S(1)} %get-tuple-element.36.inner_ref, ...), custom_call_target="tpu_custom_call" | custom-call | flops 60000002048 | tf_op jit(solution)/shard_map/near/pallas_call | solution.py:501
  29.4 0.0 collective-permute-done.5.refs_4_
  29.4 2.3 %far.1.refs_6_ = f32[4,4,64,128]{3,2,1,0:T(8,128)} custom-call(s32[1]{0:T(128)S(6)} %copy.11.flip_ref, f32[4,3,8,128]{3,2,1,0:T(8,128)S(1)} %get-tuple-element.27.vector_ref, bf16[128,192]{1,0:T(8,128)(2,1)S(1)} %get-tuple-element.28.weight_ref, f32[1056,128]{1,0:T(8,128)S(1)} %get-tuple-element.23.own_ref.refs_0_, ...), custom_call_target="tpu_custom_call" | custom-call | flops 2000000000 | tf_op jit(solution)/shard_map/far/pallas_call | solution.py:513
  31.6 0.0 collective-permute-done.8.refs_5_
  31.6 2.3 %late.1 = f32[4,4,64,128]{3,2,1,0:T(8,128)} custom-call(s32[1]{0:T(128)S(6)} %copy.11.flip_ref, f32[4,3,8,128]{3,2,1,0:T(8,128)S(1)} %get-tuple-element.27.vector_ref, bf16[128,192]{1,0:T(8,128)(2,1)S(1)} %get-tuple-element.28.weight_ref, f32[1056,128]{1,0:T(8,128)S(1)} %get-tuple-element.23.own_ref.refs_0_, ...), custom_call_target="tpu_custom_call", output_to_operand_aliasing={{}: (9, {})} | custom-call | flops 2000000000 | tf_op jit(solution)/shard_map/late/pallas_call | solution.py:513
  (4 shorter events, 0.0 us)
Async XLA Ops:
  0.0 6.4 %copy-start = (f32[16,256,128]{2,1,0:T(8,128)S(1)}, f32[16,256,128]{2,1,0:T(8,128)}, u32[]{:S(2)}) copy-start(f32[16,256,128]{2,1,0:T(8,128)} %field_ref.3) | copy-start | bytes 6291460
  1.7 10.5 %copy-start.3 = (f32[16,3]{0,1:T(4,128)S(1)}, f32[16,3]{0,1:T(4,128)}, u32[]{:S(2)}) copy-start(f32[16,3]{0,1:T(4,128)} %param.6) | copy-start | bytes 580
  1.7 10.6 %copy-start.2 = (f32[16,4,8]{0,2,1:T(8,128)S(1)}, f32[16,4,8]{0,2,1:T(8,128)}, u32[]{:S(2)}) copy-start(f32[16,4,8]{0,2,1:T(8,128)} %param.7) | copy-start | bytes 6148
  1.7 14.4 %copy-start.1 = (s32[4]{0:T(128)S(1)}, s32[4]{0:T(128)}, u32[]{:S(2)}) copy-start(s32[4]{0:T(128)} %index_ref.1) | copy-start | bytes 52
  1.8 10.7 %collective-permute-start.2 = (f32[160,128]{1,0:T(8,128)S(1)}, f32[160,128]{1,0:T(8,128)S(1)}, u32[]{:S(2)}, u32[]{:S(2)}) collective-permute-start(f32[160,128]{1,0:T(8,128)S(1)} %get-tuple-element.25), channel_id=1, source_target_pairs={{0,24},{8,16},{16,8},{24,0},{1,25},{9,17},{17,9},{25,1},{2,26},{10... | collective-permute-start | bytes 245768 | tf_op jit(solution)/shard_map/ppermute | solution.py:419
  5.7 17.4 %collective-permute-start.4 = (f32[1056,128]{1,0:T(8,128)S(1)}, f32[1056,128]{1,0:T(8,128)S(1)}, u32[]{:S(2)}, u32[]{:S(2)}) collective-permute-start(f32[1056,128]{1,0:T(8,128)S(1)} %get-tuple-element.29), channel_id=1, source_target_pairs={{0,16},{8,24},{16,0},{24,8},{1,17},{9,25},{17,1},{25,9},{2,18},{10... | collective-permute-start | bytes 1622024 | tf_op jit(solution)/shard_map/ppermute | solution.py:419
  6.2 16.9 %collective-permute-start.3 = (f32[1056,128]{1,0:T(8,128)S(1)}, f32[1056,128]{1,0:T(8,128)S(1)}, u32[]{:S(2)}, u32[]{:S(2)}) collective-permute-start(f32[1056,128]{1,0:T(8,128)S(1)} %get-tuple-element.22._), channel_id=1, source_target_pairs={{0,8},{8,0},{16,24},{24,16},{1,9},{9,1},{17,25},{25,17},{2,10},{10... | collective-permute-start | bytes 1622024 | tf_op jit(solution)/shard_map/ppermute | solution.py:419
  7.5 4.9 %collective-permute-start.1 = (f32[64,128]{1,0:T(8,128)S(1)}, f32[64,128]{1,0:T(8,128)S(1)}, u32[]{:S(2)}, u32[]{:S(2)}) collective-permute-start(f32[64,128]{1,0:T(8,128)S(1)} %get-tuple-element.24), channel_id=1, source_target_pairs={{1,2},{3,4},{5,6},{2,1},{4,3},{6,5},{9,10},{11,12},{13,14},{10,9},... | collective-permute-start | bytes 98312 | tf_op jit(solution)/shard_map/ppermute | solution.py:415
  8.2 4.3 %collective-permute-start = (f32[64,128]{1,0:T(8,128)S(1)}, f32[64,128]{1,0:T(8,128)S(1)}, u32[]{:S(2)}, u32[]{:S(2)}) collective-permute-start(f32[64,128]{1,0:T(8,128)S(1)} %get-tuple-element.24), channel_id=1, source_target_pairs={{0,1},{2,3},{4,5},{6,7},{1,0},{3,2},{5,4},{7,6},{8,9},{10,11},{12,... | collective-permute-start | bytes 98312 | tf_op jit(solution)/shard_map/ppermute | solution.py:415
  12.6 9.0 %collective-permute-start.6 = (f32[16,128]{1,0:T(8,128)S(1)}, f32[16,128]{1,0:T(8,128)S(1)}, u32[]{:S(2)}, u32[]{:S(2)}) collective-permute-start(f32[16,128]{1,0:T(8,128)S(1)} %get-tuple-element.32), channel_id=1, source_target_pairs={{0,8},{8,0},{16,24},{24,16},{1,9},{9,1},{17,25},{25,17},{2,10},{10... | collective-permute-start | bytes 24584 | tf_op jit(solution)/shard_map/ppermute | solution.py:419
  14.1 7.5 %collective-permute-start.7 = (f32[16,128]{1,0:T(8,128)S(1)}, f32[16,128]{1,0:T(8,128)S(1)}, u32[]{:S(2)}, u32[]{:S(2)}) collective-permute-start(f32[16,128]{1,0:T(8,128)S(1)} %get-tuple-element.33), channel_id=1, source_target_pairs={{0,16},{8,24},{16,0},{24,8},{1,17},{9,25},{17,1},{25,9},{2,18},{10... | collective-permute-start | bytes 24584 | tf_op jit(solution)/shard_map/ppermute | solution.py:419
  15.7 13.7 %collective-permute-start.5 = (f32[480,128]{1,0:T(8,128)S(1)}, f32[480,128]{1,0:T(8,128)S(1)}, u32[]{:S(2)}, u32[]{:S(2)}) collective-permute-start(f32[480,128]{1,0:T(8,128)S(1)} %constant_dynamic-update-slice_fusion), channel_id=1, source_target_pairs={{0,24},{8,16},{16,8},{24,0},{1,25},{9,17},{17,9},{25,1},{2,26},{10... | collective-permute-start | bytes 737288 | tf_op jit(solution)/shard_map/ppermute | solution.py:419
  21.6 10.0 %collective-permute-start.8 = (f32[464,128]{1,0:T(8,128)S(1)}, f32[464,128]{1,0:T(8,128)S(1)}, u32[]{:S(2)}, u32[]{:S(2)}) collective-permute-start(f32[464,128]{1,0:T(8,128)S(1)} %get-tuple-element.35), channel_id=1, source_target_pairs={{0,24},{8,16},{16,8},{24,0},{1,25},{9,17},{17,9},{25,1},{2,26},{10... | collective-permute-start | bytes 712712 | tf_op jit(solution)/shard_map/ppermute | solution.py:419
